TPU v7x, 32 devices: a whole 2x2x4 slice. The times are simulated.
32 devices in a mesh: loop: 16 (over z, x, core), row: 2 (over y).
Axes of the slice: x: 2, y: 2, z: 4, core: 2. Of those that a mesh axis runs over, the one named last changes fastest.
Arguments:
- features: bfloat16 [4096, 256], P(('loop', 'row')), may hold values from -6 to 6
- weight: bfloat16 [256, 256], replicated, may hold values from -0.375 to 0.375
- bias_vector: float32 [256], replicated, may hold values from -3 to 3
- cotangent: bfloat16 [4096, 256], P(('loop', 'row')), may hold values from -6 to 6
- tile_values: bfloat16 [1024, 128, 128], P(('loop', 'row')), as said below
- tile_rows: int32 [1024], P(('loop', 'row')), may hold values from 0 to 1, as said below
- counts: int32 [512], P(('loop', 'row')), may hold values from 0 to 2, as said below
Outputs:
- output: bfloat16 [4096, 256], P(('loop', 'row'))
- grad_features: bfloat16 [4096, 256], P(('loop', 'row'))
- grad_weight: float32 [256, 256], replicated
- grad_bias: float32 [256], replicated
Inputs may be any that keep to these rules, and one draw needn't show every extreme that they name: Within one group the 2 tile_rows are distinct. `counts`: in every device's group j = l (destination and source blocks of the same 2 blocks) all slots are live. `tile_values`: A is symmetric and nonnegative: a live tile for destination block a and source block b exists exactly when one for destination block b and source block a does, and the two are transposes of each other.
All inputs are finite; a program needn't handle non-finite values.
Results may differ from a plain program's by a relative error of at most 0.014.
Values may be sent and summed in bfloat16 or wider, within the bound.
No kernel may reach another device: no remote copies, remote signals or barrier semaphores. Data moves between devices by JAX's collectives and lax.ppermute only.
A program may use at most 128 MiB of HBM per device.

v0:
```python
import jax
import jax.numpy as jnp
from jax import lax
from jax.sharding import PartitionSpec as P


def expand_groups(tile_values, tile_rows, counts):
    tile_size = tile_values.shape[-1]
    groups = counts.shape[0]
    slots = tile_rows.shape[0] // groups
    matrices = tile_values.reshape(groups, slots, tile_size, tile_size)
    dest_rows = tile_rows.reshape(groups, slots)
    slot_ids = jnp.arange(slots, dtype=jnp.int32)
    live_slots = slot_ids[None, :] < counts[:, None]
    onehot = ((dest_rows[:, :, None] == slot_ids[None, None, :]) & live_slots[:, :, None]).astype(
        jnp.bfloat16
    )
    expanded = jnp.einsum("gsd,gsac->gdac", onehot, matrices, preferred_element_type=jnp.float32)
    return expanded.astype(jnp.bfloat16)


def aggregate_into(tile_values, tile_rows, counts, shard_piece):
    tile_size = tile_values.shape[-1]
    group_count = shard_piece.shape[0] // tile_size
    expanded = expand_groups(tile_values, tile_rows, counts)
    sources = shard_piece.reshape(group_count, tile_size, shard_piece.shape[1])
    return jnp.einsum("gdac,gch->dah", expanded, sources, preferred_element_type=jnp.float32)


def shards(features, weight, bias_vector, cotangent, tile_values, tile_rows, counts):
    tile_size = features.shape[0]
    feature_width = features.shape[1]
    slots = tile_rows.shape[0] // counts.shape[0]
    partial_sums = aggregate_into(
        tile_values, tile_rows, counts, lax.all_gather(features, "loop", axis=0, tiled=True)
    )
    hidden_sum = lax.psum_scatter(
        partial_sums.reshape(slots * tile_size, feature_width),
        "row",
        scatter_dimension=0,
        tiled=True,
    )
    hidden = hidden_sum.astype(jnp.bfloat16)
    preact = jnp.dot(hidden, weight, preferred_element_type=jnp.float32) + bias_vector
    sigmoid_z = jax.nn.sigmoid(preact)
    output = (preact * sigmoid_z).astype(jnp.bfloat16)
    grad_z = cotangent.astype(jnp.float32) * sigmoid_z * (1.0 + preact * (1.0 - sigmoid_z))
    grad_z_half = grad_z.astype(jnp.bfloat16)
    weight_term = jnp.einsum("nk,nh->kh", hidden, grad_z_half, preferred_element_type=jnp.float32)
    bias_term = jnp.sum(grad_z, axis=0)
    weight_total, bias_total = lax.psum((weight_term, bias_term), ("loop", "row"))
    node_total = tile_size * lax.axis_size("loop") * lax.axis_size("row")
    norm_factor = 1.0 / node_total**0.5
    grad_hidden = jnp.einsum(
        "nh,kh->nk", grad_z_half, weight, preferred_element_type=jnp.float32
    ).astype(jnp.bfloat16)
    group_grads = lax.all_gather(grad_hidden, "row", axis=0, tiled=True)
    group_grads = group_grads.reshape(slots, tile_size, feature_width)
    expanded = expand_groups(tile_values, tile_rows, counts)
    term = jnp.einsum("gdac,dah->gch", expanded, group_grads, preferred_element_type=jnp.float32)
    grad_sum = lax.psum_scatter(
        term.reshape(lax.axis_size("loop") * tile_size, feature_width).astype(jnp.bfloat16),
        "loop",
        scatter_dimension=0,
        tiled=True,
    )
    return (output, grad_sum, weight_total * norm_factor, bias_total * norm_factor)


def solution(mesh):
    in_specs = (
        P(("loop", "row"), None),
        P(),
        P(),
        P(("loop", "row"), None),
        P(("loop", "row"), None, None),
        P(("loop", "row")),
        P(("loop", "row")),
    )
    out_specs = (P(("loop", "row"), None), P(("loop", "row"), None), P(), P())
    return jax.shard_map(shards, mesh=mesh, in_specs=in_specs, out_specs=out_specs, check_vma=False)
```

profile of v0, /device:TPU:0, one launch (start us, length us, event | category | flops | bytes accessed | tf_op | source)
XLA Modules:
  0.0 263.9 jit_solution(1600943621714882078)
XLA Ops:
  7.2 0.0 copy-start
  7.2 0.0 all-gather.2.cloned.1.call-start
  7.2 0.7 all-gather.2.cloned.1.call-update
  7.9 0.0 reduce-scatter.3.cloned.1.call-start
  8.0 0.7 eq.8
  8.7 0.7 iota_compare_fusion
  9.4 0.0 copy-done
  9.4 1.2 convolution_convert_fusion
  10.7 0.2 copy.17
  10.9 39.9 %all-gather.2.cloned.1.call-done = bf16[2048,256]{1,0:T(8,128)(2,1)} async-done(((bf16[128,256]{1,0:T(8,128)(2,1)}), bf16[2048,256]{1,0:T(8,128)(2,1)}) %all-gather.2.cloned.1.call-update) | async-done | bytes 1048592 | tf_op jit(solution)/shard_map/all_gather | solution.py:35
  50.8 2.4 convolution_bitcast_fusion.1
  53.2 0.0 reduce-scatter.3.cloned.1.call-update
  53.2 0.0 all-reduce.2.cloned.1.call-start
  53.3 0.0 copy-start.2
  53.3 0.0 copy-start.3
  53.3 0.0 copy-start.4
  53.3 0.9 copy.15
  54.3 10.0 %reduce-scatter.3.cloned.1.call-done = f32[128,256]{1,0:T(8,128)} async-done(((f32[256,256]{1,0:T(8,128)}), f32[128,256]{1,0:T(8,128)}) %reduce-scatter.3.cloned.1.call-update) | async-done | bytes 131088 | tf_op jit(solution)/shard_map/reduce_scatter | solution.py:37
  64.3 0.0 copy-done.2
  64.3 1.8 fusion.11
  66.1 0.2 convolution_convert_fusion.1
  66.3 0.9 fusion.2
  67.2 0.0 all-reduce.2.cloned.1.call-update
  67.3 0.0 reduce-scatter.5.cloned.1.call-start
  67.3 4.9 %all_gather.7 = bf16[256,256]{1,0:T(8,128)(2,1)S(1)} all-gather(bf16[128,256]{1,0:T(8,128)(2,1)S(1)} %convolution_convert_fusion.1), channel_id=1, replica_groups=mesh['loop'=16,'row'=2] {'row'}, dimensions={0}, use_global_device_ids=true | all-gather | bytes 196608 | tf_op jit(solution)/shard_map/all_gather | solution.py:57
  72.2 1.4 fusion
  73.6 0.0 reduce-scatter.5.cloned.1.call-update
  73.7 39.5 %psum.15 = f32[256]{0:T(256)S(1)} all-reduce(f32[256]{0:T(256)S(1)} %get-tuple-element.4), channel_id=1, replica_groups=mesh['loop'=16,'row'=2] {'loop','row'}, use_global_device_ids=true, to_apply=%region_4.0 | all-reduce | flops 256 | bytes 2048 | tf_op jit(solution)/shard_map/psum | solution.py:51
  113.2 0.6 broadcast_multiply_fusion.1
  113.7 82.7 %all-reduce.2.cloned.1.call-done = f32[256,256]{1,0:T(8,128)} async-done(((f32[256,256]{1,0:T(8,128)}), f32[256,256]{1,0:T(8,128)}) %all-reduce.2.cloned.1.call-update) | async-done | bytes 262160 | tf_op jit(solution)/shard_map/psum | solution.py:51
  196.4 1.7 broadcast_multiply_fusion
  198.1 59.3 %reduce-scatter.5.cloned.1.call-done = bf16[128,256]{1,0:T(8,128)(2,1)} async-done(((bf16[2048,256]{1,0:T(8,128)(2,1)}), bf16[128,256]{1,0:T(8,128)(2,1)}) %reduce-scatter.5.cloned.1.call-update) | async-done | bytes 65552 | tf_op jit(solution)/shard_map/reduce_scatter | solution.py:61
  (4 shorter events, 0.0 us)
Async XLA Ops:
  7.2 2.3 copy-start
  7.2 43.7 %all-gather.2.cloned.1.call-start = ((), (), s32[]{:S(2)}) async-start(), calls=%async_computation.2 | async-start | bytes 1114112 | tf_op jit(solution)/shard_map/all_gather | solution.py:35
  7.9 56.4 %reduce-scatter.3.cloned.1.call-start = ((), (), s32[]{:S(2)}) async-start(), calls=%async_computation.3 | async-start | bytes 393216 | tf_op jit(solution)/shard_map/reduce_scatter | solution.py:37
  53.2 143.2 %all-reduce.2.cloned.1.call-start = ((), (), s32[]{:S(2)}) async-start(), calls=%async_computation.5 | async-start | bytes 524288 | tf_op jit(solution)/shard_map/psum | solution.py:51
  53.3 11.0 %copy-start.2 = (bf16[256,256]{1,0:T(8,128)(2,1)S(1)}, bf16[256,256]{1,0:T(8,128)(2,1)}, u32[]{:S(2)}) copy-start(bf16[256,256]{1,0:T(8,128)(2,1)} %param.8) | copy-start | bytes 393220
  53.3 11.0 %copy-start.3 = (bf16[128,256]{1,0:T(8,128)(2,1)S(1)}, bf16[128,256]{1,0:T(8,128)(2,1)}, u32[]{:S(2)}) copy-start(bf16[128,256]{1,0:T(8,128)(2,1)} %param.10) | copy-start | bytes 196612
  53.3 11.0 %copy-start.4 = (f32[256]{0:T(256)S(1)}, f32[256]{0:T(256)}, u32[]{:S(2)}) copy-start(f32[256]{0:T(256)} %param.9) | copy-start | bytes 3076
  64.3 2.0 copy-start.1
  67.3 190.1 %reduce-scatter.5.cloned.1.call-start = ((), (), s32[]{:S(2)}) async-start(), calls=%async_computation.4 | async-start | bytes 1114112 | tf_op jit(solution)/shard_map/reduce_scatter | solution.py:61
Sparse Core Ops, SparseCore 0:
  10.2 40.6 all-gather.1
  53.6 10.5 reduce-scatter.2
  71.3 125.1 all-reduce.1
  200.9 56.3 reduce-scatter.4
where the time goes:
time: 264 us
  waiting for transfers between devices  193 us (73%)
  blocking collectives  44.4 us (17%)
  between operations  13.8 us (5%)
  matrix products  7.93 us (3%)
  other arithmetic  2.97 us (1%)
    psum x1, waiting for transfers between devices, shards(): lax.psum((weight_term, bias_term), ('loop', 'row'))  82.7 us
    reduce_scatter x1, waiting for transfers between devices, shards(): lax.psum_scatter(term.reshape(lax.axis_size('loop') * tile_size, feature_...  59.3 us
    all_gather x1, waiting for transfers between devices, shards(): lax.all_gather(features, 'loop', axis=0, tiled=True)  39.9 us
    psum x1, blocking collectives, shards(): lax.psum((weight_term, bias_term), ('loop', 'row'))  39.5 us
    reduce_scatter x1, waiting for transfers between devices, shards(): lax.psum_scatter(partial_sums.reshape(slots * tile_size, feature_width),...  10 us
  transfers between devices with their start and end apart: 4, of which 4 were waited for; matrix products, arithmetic and copies ran while one was open for 3% of the time, Pallas kernels for 0%

commit v1 on v0

v1 whole, which is shorter than its diff:
```python
import functools

import jax
import jax.numpy as jnp
from jax import lax
from jax.experimental import pallas as pl
from jax.experimental.pallas import tpu as pltpu
from jax.sharding import PartitionSpec as P

BF16 = jnp.bfloat16
F32 = jnp.float32
VMEM = pl.BlockSpec(memory_space=pltpu.VMEM)
SMEM = pl.BlockSpec(memory_space=pltpu.SMEM)
PARAMS = pltpu.CompilerParams(vmem_limit_bytes=56 * 1024 * 1024)


def gather_stages(n_loop):
    top = [m for m in range(4, n_loop, 4)]
    stages = [top] if top else []
    return stages + [[b] for b in (2, 1) if b < n_loop]


def block_masks(n_loop):
    masks = [0]
    for stage in gather_stages(n_loop):
        masks = masks + [c ^ m for c in stage for m in masks]
    return masks


def xor_permute(x, axis, mask, n):
    return lax.ppermute(x, axis, [(i, i ^ mask) for i in range(n)])


def gather_stage(blocks, stage, n_loop):
    return blocks + [xor_permute(b, "loop", c, n_loop) for c in stage for b in blocks]


def expand_kernel(n_loop, n_row, tile, rows_ref, counts_ref, tiles_ref, out_ref):
    me = lax.axis_index("row")

    def body(j, carry):
        for s in range(n_row):
            slot = j * n_row + s
            place = jnp.bitwise_xor(rows_ref[slot], me)
            live = s < counts_ref[j]
            value = tiles_ref[slot]
            value = jnp.where(live, value, jnp.zeros_like(value))
            out_ref[
                pl.ds(pl.multiple_of(place * tile, tile), tile),
                pl.ds(pl.multiple_of(j * tile, tile), tile),
            ] = value
        return carry

    lax.fori_loop(0, n_loop, body, 0)


def place_blocks(masks, tile, block_refs, out_ref):
    me = lax.axis_index("loop")
    for mask, ref in zip(masks, block_refs):
        j = jnp.bitwise_xor(me, mask)
        out_ref[pl.ds(pl.multiple_of(j * tile, tile), tile), :] = ref[...]


def rows_product(a_ref, x, n_row, tile, own_ref, send_refs):
    step = min(2, n_row)
    for q in range(0, n_row, step):
        product = jnp.dot(
            a_ref[q * tile : (q + step) * tile, :], x, preferred_element_type=F32
        )
        for k in range(step):
            part = product[k * tile : (k + 1) * tile, :]
            if q + k == 0:
                own_ref[...] = part
            else:
                send_refs[q + k - 1][...] = part.astype(BF16)


def forward_kernel(masks, n_row, tile, a_ref, *refs):
    n = len(masks)
    block_refs, own_ref, send_refs, x_ref = refs[:n], refs[n], refs[n + 1 : -1], refs[-1]
    place_blocks(masks, tile, block_refs, x_ref)
    rows_product(a_ref, x_ref[...], n_row, tile, own_ref, send_refs)


def backward_kernel(masks, n_row, tile, a_ref, w_ref, b_ref, *refs):
    n = len(masks)
    h_refs, c_refs = refs[:n], refs[n : 2 * n]
    out_ref, gw_ref, gf_ref = refs[2 * n : 2 * n + 3]
    send_refs = refs[2 * n + 3 : 2 * n + 3 + n_row - 1]
    h_all, c_all, gh_all, out_all = refs[-4:]
    place_blocks(masks, tile, h_refs, h_all)
    place_blocks(masks, tile, c_refs, c_all)
    width = w_ref.shape[0]
    step = min(2, n) * tile

    def body(i, carry):
        grad_w, grad_b = carry
        at = pl.ds(pl.multiple_of(i * step, step), step)
        hidden = h_all[at, :]
        preact = jnp.dot(hidden, w_ref[...], preferred_element_type=F32) + b_ref[...]
        sig = jax.nn.sigmoid(preact)
        out_all[at, :] = (preact * sig).astype(BF16)
        grad_z = c_all[at, :].astype(F32) * sig * (1.0 + preact * (1.0 - sig))
        half = grad_z.astype(BF16)
        grad_b = grad_b + jnp.sum(grad_z, axis=0, keepdims=True)
        grad_w = grad_w + lax.dot_general(
            hidden, half, (((0,), (0,)), ((), ())), preferred_element_type=F32
        )
        gh_all[at, :] = lax.dot_general(
            half, w_ref[...], (((1,), (1,)), ((), ())), preferred_element_type=F32
        ).astype(BF16)
        return grad_w, grad_b

    grad_w, grad_b = lax.fori_loop(
        0,
        n * tile // step,
        body,
        (jnp.zeros((width, width), F32), jnp.zeros((1, width), F32)),
    )
    mine = lax.axis_index("loop")
    out_ref[...] = out_all[pl.ds(pl.multiple_of(mine * tile, tile), tile), :]
    high = grad_b.astype(BF16)
    low = (grad_b - high.astype(F32)).astype(BF16)
    gw_ref[:width, :] = grad_w.astype(BF16)
    row = lax.broadcasted_iota(jnp.int32, (16, width), 0)
    high = jnp.broadcast_to(high.astype(F32), (16, width))
    low = jnp.broadcast_to(low.astype(F32), (16, width))
    gw_ref[width:, :] = jnp.where(row == 0, high, jnp.where(row == 1, low, 0.0)).astype(BF16)
    rows_product(a_ref, gh_all[...], n_row, tile, gf_ref, send_refs)


def call(kernel, outs, scratch=(), specs=None):
    return pl.pallas_call(
        kernel,
        out_shape=outs,
        in_specs=specs,
        out_specs=jax.tree.map(lambda _: VMEM, outs),
        scratch_shapes=scratch,
        compiler_params=PARAMS,
    )


def shards(n_loop, n_row, features, weight, bias_vector, cotangent, tile_values, tile_rows, counts):
    tile, width = features.shape
    masks = block_masks(n_loop)
    stages = gather_stages(n_loop)
    nodes = tile * n_loop * n_row
    shape = jax.ShapeDtypeStruct

    blocks = [features]
    cots = [cotangent]
    for stage in stages:
        blocks = gather_stage(blocks, stage, n_loop)
        blocks, cots = lax.optimization_barrier((blocks, cots))
        cots = gather_stage(cots, stage, n_loop)

    adjacency = call(
        functools.partial(expand_kernel, n_loop, n_row, tile),
        shape((n_row * tile, n_loop * tile), BF16),
        specs=[SMEM, SMEM, VMEM],
    )(tile_rows, counts, tile_values)

    sends = [shape((tile, width), BF16)] * (n_row - 1)
    own, *parts = call(
        functools.partial(forward_kernel, masks, n_row, tile),
        [shape((tile, width), F32)] + sends,
        scratch=[pltpu.VMEM((n_loop * tile, width), BF16)],
        specs=[VMEM] * (1 + n_loop),
    )(adjacency, *blocks)
    for q, part in enumerate(parts):
        own = own + xor_permute(part, "row", q + 1, n_row).astype(F32)
    hidden = own.astype(BF16)

    hiddens = [hidden]
    for stage in stages:
        hiddens = gather_stage(hiddens, stage, n_loop)

    big = pltpu.VMEM((n_loop * tile, width), BF16)
    output, grad_w, own, *parts = call(
        functools.partial(backward_kernel, masks, n_row, tile),
        [shape((tile, width), BF16), shape((width + 16, width), BF16), shape((tile, width), F32)]
        + sends,
        scratch=[big] * 4,
        specs=[VMEM] * (3 + 2 * n_loop),
    )(adjacency, weight, bias_vector.reshape(1, width), *hiddens, *cots)

    for q, part in enumerate(parts):
        own = own + xor_permute(part, "row", q + 1, n_row).astype(F32)
    grad_features = own.astype(BF16)

    norm_factor = 1.0 / nodes**0.5
    bit = 1
    while bit < n_row:
        other = xor_permute(grad_w, "row", bit, n_row)
        total = grad_w.astype(F32) + other.astype(F32)
        bias_total = total[width : width + 1, :] + total[width + 1 : width + 2, :]
        bit *= 2
        if bit < n_row:
            high = bias_total.astype(BF16)
            low = (bias_total - high.astype(F32)).astype(BF16)
            rest = jnp.zeros((14, width), BF16)
            grad_w = jnp.concatenate([total[:width].astype(BF16), high, low, rest], axis=0)
    return (
        output,
        grad_features,
        total[:width] * norm_factor,
        bias_total.reshape(width) * norm_factor,
    )


def solution(mesh):
    in_specs = (
        P(("loop", "row"), None),
        P(),
        P(),
        P(("loop", "row"), None),
        P(("loop", "row"), None, None),
        P(("loop", "row")),
        P(("loop", "row")),
    )
    out_specs = (P(("loop", "row"), None), P(("loop", "row"), None), P(), P())
    return jax.shard_map(
        functools.partial(shards, mesh.shape["loop"], mesh.shape["row"]),
        mesh=mesh,
        in_specs=in_specs,
        out_specs=out_specs,
        check_vma=False,
    )
```

time: 264 us -> 78.4 us (0.30)
  waiting for transfers between devices: 193 us -> 25.6 us
  blocking collectives: 44.4 us -> 0 us
  starting transfers between devices: 0.16 us -> 34.6 us
  between operations: 13.8 us -> 1.17 us
  Pallas kernels: 0 us -> 12.3 us
  matrix products: 7.93 us -> 0 us
    psum x1 -> x0, waiting for transfers between devices: 82.7 us -> none  [shards(): lax.psum((weight_term, bias_term), ('loop', 'row'))]
    reduce_scatter x2 -> x0, waiting for transfers between devices: 69.3 us -> none  [the longest x1 59.3 us: shards(): lax.psum_scatter(term.reshape(lax.axis_size('loop') * tile_size, feature_...]
    all_gather x1 -> x0, waiting for transfers between devices: 39.9 us -> none  [shards(): lax.all_gather(features, 'loop', axis=0, tiled=True)]
    psum x1 -> x0, blocking collectives: 39.5 us -> none  [shards(): lax.psum((weight_term, bias_term), ('loop', 'row'))]
    ppermute x0 -> x48, starting transfers between devices: none -> 34.6 us  [xor_permute(): return lax.ppermute(x, axis, [(i, i ^ mask) for i in range(n)])]
    ppermute x0 -> x48, waiting for transfers between devices: none -> 25.6 us  [xor_permute(): return lax.ppermute(x, axis, [(i, i ^ mask) for i in range(n)])]
    pallas_call x0 -> x3, Pallas kernels: none -> 12.3 us  [the longest x1 7.02 us: shards(): call(functools.partial(backward_kernel, masks, n_row, tile), [shape((tile...]
    dot_general x6 -> x0, matrix products: 7.93 us -> none  [the longest x1 2.36 us: aggregate_into(): jnp.einsum('gdac,gch->dah', expanded, sources, preferred_element_type=jnp...]
  transfers between devices with their start and end apart: 4 -> 48, of which waited for: 4 -> 17; matrix products, arithmetic and copies ran while one was open for 3% -> 3% of each run, Pallas kernels for 0% -> 7%
where the time goes in v1:
time: 78.4 us; the launch traced here: 78.1 us
  starting transfers between devices  34.6 us (44%)
  waiting for transfers between devices  25.6 us (33%)
  Pallas kernels  12.3 us (16%)
  other arithmetic  3.79 us (5%)
  between operations  1.17 us (1%)
    ppermute x48, starting transfers between devices, xor_permute(): return lax.ppermute(x, axis, [(i, i ^ mask) for i in range(n)])  34.6 us
    ppermute x48, waiting for transfers between devices, xor_permute(): return lax.ppermute(x, axis, [(i, i ^ mask) for i in range(n)])  25.6 us
    pallas_call x1, Pallas kernels, shards(): call(functools.partial(backward_kernel, masks, n_row, tile), [shape((tile...  7.02 us
    pallas_call x1, Pallas kernels, shards(): call(functools.partial(forward_kernel, masks, n_row, tile), [shape((tile,...  2.69 us
    pallas_call x1, Pallas kernels, shards(): call(functools.partial(expand_kernel, n_loop, n_row, tile), shape((n_row...  2.57 us
  transfers between devices with their start and end apart: 48, of which 17 were waited for; matrix products, arithmetic and copies ran while one was open for 3% of the time, Pallas kernels for 7%

profile of v1, /device:TPU:0, one launch (start us, length us, event | category | flops | bytes accessed | tf_op | source)
XLA Modules:
  0.0 78.1 jit_solution(3500874727348429907)
XLA Ops:
  0.6 4.1 %collective-permute-start.1 = (bf16[128,256]{1,0:T(8,128)(2,1)}, bf16[128,256]{1,0:T(8,128)(2,1)S(1)}, u32[]{:S(2)}, u32[]{:S(2)}) collective-permute-start(bf16[128,256]{1,0:T(8,128)(2,1)} %refs_0_), channel_id=1, source_target_pairs={{0,16},{2,18},{4,20},{6,22},{8,24},{10,26},{12,28},{14,30},{16,0},... | collective-permute-start | bytes 196616 | tf_op jit(solution)/shard_map/ppermute | solution.py:31
  4.7 1.6 %collective-permute-start = (bf16[128,256]{1,0:T(8,128)(2,1)}, bf16[128,256]{1,0:T(8,128)(2,1)S(1)}, u32[]{:S(2)}, u32[]{:S(2)}) collective-permute-start(bf16[128,256]{1,0:T(8,128)(2,1)} %refs_0_), channel_id=1, source_target_pairs={{0,8},{2,10},{4,12},{6,14},{8,0},{10,2},{12,4},{14,6},{16,24},{18,... | collective-permute-start | bytes 196616 | tf_op jit(solution)/shard_map/ppermute | solution.py:31
  6.3 1.7 %collective-permute-done.1.refs_2_ = bf16[128,256]{1,0:T(8,128)(2,1)S(1)} collective-permute-done((bf16[128,256]{1,0:T(8,128)(2,1)}, bf16[128,256]{1,0:T(8,128)(2,1)S(1)}, u32[]{:S(2)}, u32[]{:S(2)}) %collective-permute-start.1) | collective-permute-done | bytes 65568 | tf_op jit(solution)/shard_map/ppermute | solution.py:31
  8.0 1.2 %collective-permute-done.refs_1_ = bf16[128,256]{1,0:T(8,128)(2,1)S(1)} collective-permute-done((bf16[128,256]{1,0:T(8,128)(2,1)}, bf16[128,256]{1,0:T(8,128)(2,1)S(1)}, u32[]{:S(2)}, u32[]{:S(2)}) %collective-permute-start) | collective-permute-done | bytes 65568 | tf_op jit(solution)/shard_map/ppermute | solution.py:31
  9.2 3.4 %collective-permute-done.2.refs_3_ = bf16[128,256]{1,0:T(8,128)(2,1)S(1)} collective-permute-done((bf16[128,256]{1,0:T(8,128)(2,1)}, bf16[128,256]{1,0:T(8,128)(2,1)S(1)}, u32[]{:S(2)}, u32[]{:S(2)}) %collective-permute-start.2) | collective-permute-done | bytes 65568 | tf_op jit(solution)/shard_map/ppermute | solution.py:31
  12.6 1.5 %collective-permute-start.3 = (bf16[128,256]{1,0:T(8,128)(2,1)}, bf16[128,256]{1,0:T(8,128)(2,1)S(1)}, u32[]{:S(2)}, u32[]{:S(2)}) collective-permute-start(bf16[128,256]{1,0:T(8,128)(2,1)} %refs_0_), channel_id=1, source_target_pairs={{0,4},{2,6},{4,0},{6,2},{8,12},{10,14},{12,8},{14,10},{16,20},{18,... | collective-permute-start | bytes 196616 | tf_op jit(solution)/shard_map/ppermute | solution.py:31
  14.6 1.5 %collective-permute-start.5 = (bf16[128,256]{1,0:T(8,128)(2,1)S(1)}, bf16[128,256]{1,0:T(8,128)(2,1)S(1)}, u32[]{:S(2)}, u32[]{:S(2)}) collective-permute-start(bf16[128,256]{1,0:T(8,128)(2,1)S(1)} %collective-permute-done.1.refs_2_), channel_id=1, source_target_pairs={{0,4},{2,6},{4,0},{6,2},{8,12},{10,14},{12,8},{14,10},{16,20},{18,... | collective-permute-start | bytes 196616 | tf_op jit(solution)/shard_map/ppermute | solution.py:31
  16.7 1.3 %collective-permute-start.9 = (bf16[128,256]{1,0:T(8,128)(2,1)}, bf16[128,256]{1,0:T(8,128)(2,1)S(1)}, u32[]{:S(2)}, u32[]{:S(2)}) collective-permute-start(bf16[128,256]{1,0:T(8,128)(2,1)} %refs_16_), channel_id=1, source_target_pairs={{0,24},{2,26},{4,28},{6,30},{8,16},{10,18},{12,20},{14,22},{16,8},... | collective-permute-start | bytes 196616 | tf_op jit(solution)/shard_map/ppermute | solution.py:31
  18.0 1.1 %collective-permute-start.8 = (bf16[128,256]{1,0:T(8,128)(2,1)}, bf16[128,256]{1,0:T(8,128)(2,1)S(1)}, u32[]{:S(2)}, u32[]{:S(2)}) collective-permute-start(bf16[128,256]{1,0:T(8,128)(2,1)} %refs_16_), channel_id=1, source_target_pairs={{0,16},{2,18},{4,20},{6,22},{8,24},{10,26},{12,28},{14,30},{16,0},... | collective-permute-start | bytes 196616 | tf_op jit(solution)/shard_map/ppermute | solution.py:31
  19.1 2.0 %collective-permute-start.7 = (bf16[128,256]{1,0:T(8,128)(2,1)}, bf16[128,256]{1,0:T(8,128)(2,1)S(1)}, u32[]{:S(2)}, u32[]{:S(2)}) collective-permute-start(bf16[128,256]{1,0:T(8,128)(2,1)} %refs_16_), channel_id=1, source_target_pairs={{0,8},{2,10},{4,12},{6,14},{8,0},{10,2},{12,4},{14,6},{16,24},{18,... | collective-permute-start | bytes 196616 | tf_op jit(solution)/shard_map/ppermute | solution.py:31
  21.1 1.9 %collective-permute-done.9.refs_19_ = bf16[128,256]{1,0:T(8,128)(2,1)S(1)} collective-permute-done((bf16[128,256]{1,0:T(8,128)(2,1)}, bf16[128,256]{1,0:T(8,128)(2,1)S(1)}, u32[]{:S(2)}, u32[]{:S(2)}) %collective-permute-start.9) | collective-permute-done | bytes 65568 | tf_op jit(solution)/shard_map/ppermute | solution.py:31
  23.0 1.4 %collective-permute-done.8.refs_18_ = bf16[128,256]{1,0:T(8,128)(2,1)S(1)} collective-permute-done((bf16[128,256]{1,0:T(8,128)(2,1)}, bf16[128,256]{1,0:T(8,128)(2,1)S(1)}, u32[]{:S(2)}, u32[]{:S(2)}) %collective-permute-start.8) | collective-permute-done | bytes 65568 | tf_op jit(solution)/shard_map/ppermute | solution.py:31
  26.6 1.5 %collective-permute-start.18 = (bf16[128,256]{1,0:T(8,128)(2,1)}, bf16[128,256]{1,0:T(8,128)(2,1)S(1)}, u32[]{:S(2)}, u32[]{:S(2)}) collective-permute-start(bf16[128,256]{1,0:T(8,128)(2,1)} %refs_16_), channel_id=1, source_target_pairs={{0,4},{2,6},{4,0},{6,2},{8,12},{10,14},{12,8},{14,10},{16,20},{18,... | collective-permute-start | bytes 196616 | tf_op jit(solution)/shard_map/ppermute | solution.py:31
  28.6 1.5 %collective-permute-start.20 = (bf16[128,256]{1,0:T(8,128)(2,1)S(1)}, bf16[128,256]{1,0:T(8,128)(2,1)S(1)}, u32[]{:S(2)}, u32[]{:S(2)}) collective-permute-start(bf16[128,256]{1,0:T(8,128)(2,1)S(1)} %collective-permute-done.8.refs_18_), channel_id=1, source_target_pairs={{0,4},{2,6},{4,0},{6,2},{8,12},{10,14},{12,8},{14,10},{16,20},{18,... | collective-permute-start | bytes 196616 | tf_op jit(solution)/shard_map/ppermute | solution.py:31
  30.6 2.6 %shard_map.102.a_ref = bf16[256,2048]{1,0:T(8,128)(2,1)} custom-call(s32[32]{0:T(128)} %rows_ref.1, s32[16]{0:T(128)} %counts_ref.1, bf16[32,128,128]{2,1,0:T(8,128)(2,1)} %tiles_ref.1), custom_call_target="tpu_custom_call" | custom-call | tf_op jit(solution)/shard_map/pallas_call | solution.py:157
  33.4 1.0 %collective-permute-done.20.refs_22_ = bf16[128,256]{1,0:T(8,128)(2,1)S(1)} collective-permute-done((bf16[128,256]{1,0:T(8,128)(2,1)S(1)}, bf16[128,256]{1,0:T(8,128)(2,1)S(1)}, u32[]{:S(2)}, u32[]{:S(2)}) %collective-permute-start.20) | collective-permute-done | bytes 65568 | tf_op jit(solution)/shard_map/ppermute | solution.py:31
  35.9 2.7 %shard_map.103 = (f32[128,256]{1,0:T(8,128)}, bf16[128,256]{1,0:T(8,128)(2,1)}) custom-call(bf16[256,2048]{1,0:T(8,128)(2,1)} %shard_map.102.a_ref, bf16[128,256]{1,0:T(8,128)(2,1)} %refs_0_, bf16[128,256]{1,0:T(8,128)(2,1)} %copy-done.15, bf16[128,256]{1,0:T(8,128)(2,1)} %copy-done.14, bf16[128,256]{1,0:T(8,128)(2,1)} %copy-done.17, ...), custom_call_target="tpu_custom_call" | custom-call | tf_op jit(solution)/shard_map/pallas_call | solution.py:164
  38.6 1.5 %collective-permute-start.22 = (bf16[128,256]{1,0:T(8,128)(2,1)}, bf16[128,256]{1,0:T(8,128)(2,1)S(1)}, u32[]{:S(2)}, u32[]{:S(2)}) collective-permute-start(bf16[128,256]{1,0:T(8,128)(2,1)} %get-tuple-element.85), channel_id=1, source_target_pairs={{0,1},{1,0},{2,3},{3,2},{4,5},{5,4},{6,7},{7,6},{8,9},{9,8},{10,11... | collective-permute-start | bytes 196616 | tf_op jit(solution)/shard_map/ppermute | solution.py:31
  41.4 1.9 %collective-permute-done.22 = bf16[128,256]{1,0:T(8,128)(2,1)S(1)} collective-permute-done((bf16[128,256]{1,0:T(8,128)(2,1)}, bf16[128,256]{1,0:T(8,128)(2,1)S(1)}, u32[]{:S(2)}, u32[]{:S(2)}) %collective-permute-start.22) | collective-permute-done | bytes 65568 | tf_op jit(solution)/shard_map/ppermute | solution.py:31
  44.3 1.6 %collective-permute-start.26 = (bf16[128,256]{1,0:T(8,128)(2,1)S(1)}, bf16[128,256]{1,0:T(8,128)(2,1)S(1)}, u32[]{:S(2)}, u32[]{:S(2)}) collective-permute-start(bf16[128,256]{1,0:T(8,128)(2,1)S(1)} %add_convert_fusion.1.refs_0_), channel_id=1, source_target_pairs={{0,4},{2,6},{4,0},{6,2},{8,12},{10,14},{12,8},{14,10},{16,20},{18,... | collective-permute-start | bytes 196616 | tf_op jit(solution)/shard_map/ppermute | solution.py:31
  45.8 1.8 %collective-permute-start.25 = (bf16[128,256]{1,0:T(8,128)(2,1)S(1)}, bf16[128,256]{1,0:T(8,128)(2,1)S(1)}, u32[]{:S(2)}, u32[]{:S(2)}) collective-permute-start(bf16[128,256]{1,0:T(8,128)(2,1)S(1)} %add_convert_fusion.1.refs_0_), channel_id=1, source_target_pairs={{0,24},{2,26},{4,28},{6,30},{8,16},{10,18},{12,20},{14,22},{16,8},... | collective-permute-start | bytes 196616 | tf_op jit(solution)/shard_map/ppermute | solution.py:31
  47.6 1.0 %collective-permute-start.24 = (bf16[128,256]{1,0:T(8,128)(2,1)S(1)}, bf16[128,256]{1,0:T(8,128)(2,1)S(1)}, u32[]{:S(2)}, u32[]{:S(2)}) collective-permute-start(bf16[128,256]{1,0:T(8,128)(2,1)S(1)} %add_convert_fusion.1.refs_0_), channel_id=1, source_target_pairs={{0,16},{2,18},{4,20},{6,22},{8,24},{10,26},{12,28},{14,30},{16,0},... | collective-permute-start | bytes 196616 | tf_op jit(solution)/shard_map/ppermute | solution.py:31
  48.6 1.7 %collective-permute-start.23 = (bf16[128,256]{1,0:T(8,128)(2,1)S(1)}, bf16[128,256]{1,0:T(8,128)(2,1)S(1)}, u32[]{:S(2)}, u32[]{:S(2)}) collective-permute-start(bf16[128,256]{1,0:T(8,128)(2,1)S(1)} %add_convert_fusion.1.refs_0_), channel_id=1, source_target_pairs={{0,8},{2,10},{4,12},{6,14},{8,0},{10,2},{12,4},{14,6},{16,24},{18,... | collective-permute-start | bytes 196616 | tf_op jit(solution)/shard_map/ppermute | solution.py:31
  50.3 2.3 %collective-permute-done.25.refs_3_ = bf16[128,256]{1,0:T(8,128)(2,1)S(1)} collective-permute-done((bf16[128,256]{1,0:T(8,128)(2,1)S(1)}, bf16[128,256]{1,0:T(8,128)(2,1)S(1)}, u32[]{:S(2)}, u32[]{:S(2)}) %collective-permute-start.25) | collective-permute-done | bytes 65568 | tf_op jit(solution)/shard_map/ppermute | solution.py:31
  53.3 1.7 %collective-permute-done.24.refs_2_ = bf16[128,256]{1,0:T(8,128)(2,1)S(1)} collective-permute-done((bf16[128,256]{1,0:T(8,128)(2,1)S(1)}, bf16[128,256]{1,0:T(8,128)(2,1)S(1)}, u32[]{:S(2)}, u32[]{:S(2)}) %collective-permute-start.24) | collective-permute-done | bytes 65568 | tf_op jit(solution)/shard_map/ppermute | solution.py:31
  55.5 1.5 %collective-permute-start.27 = (bf16[128,256]{1,0:T(8,128)(2,1)S(1)}, bf16[128,256]{1,0:T(8,128)(2,1)S(1)}, u32[]{:S(2)}, u32[]{:S(2)}) collective-permute-start(bf16[128,256]{1,0:T(8,128)(2,1)S(1)} %collective-permute-done.23.refs_1_), channel_id=1, source_target_pairs={{0,4},{2,6},{4,0},{6,2},{8,12},{10,14},{12,8},{14,10},{16,20},{18,... | collective-permute-start | bytes 196616 | tf_op jit(solution)/shard_map/ppermute | solution.py:31
  57.6 2.1 %collective-permute-done.28.refs_6_ = bf16[128,256]{1,0:T(8,128)(2,1)S(1)} collective-permute-done((bf16[128,256]{1,0:T(8,128)(2,1)S(1)}, bf16[128,256]{1,0:T(8,128)(2,1)S(1)}, u32[]{:S(2)}, u32[]{:S(2)}) %collective-permute-start.28) | collective-permute-done | bytes 65568 | tf_op jit(solution)/shard_map/ppermute | solution.py:31
  62.2 7.0 %shard_map.104 = (bf16[128,256]{1,0:T(8,128)(2,1)}, bf16[272,256]{1,0:T(8,128)(2,1)}, f32[128,256]{1,0:T(8,128)}, bf16[128,256]{1,0:T(8,128)(2,1)}) custom-call(bf16[256,2048]{1,0:T(8,128)(2,1)} %shard_map.102.a_ref, bf16[256,256]{1,0:T(8,128)(2,1)} %w_ref.1, f32[1,256]{1,0:T(1,128)} %bitcast.2, bf16[128,256]{1,0:T(8,128)(2,1)} %copy-done, ...), custom_call_target="tpu_custom_call" | custom-call | tf_op jit(solution)/shard_map/pallas_call | solution.py:179
  69.3 1.6 %collective-permute-start.46 = (bf16[128,256]{1,0:T(8,128)(2,1)}, bf16[128,256]{1,0:T(8,128)(2,1)S(1)}, u32[]{:S(2)}, u32[]{:S(2)}) collective-permute-start(bf16[128,256]{1,0:T(8,128)(2,1)} %get-tuple-element.96), channel_id=1, source_target_pairs={{0,1},{1,0},{2,3},{3,2},{4,5},{5,4},{6,7},{7,6},{8,9},{9,8},{10,11... | collective-permute-start | bytes 196616 | tf_op jit(solution)/shard_map/ppermute | solution.py:31
  71.4 2.8 %collective-permute-done.46 = bf16[128,256]{1,0:T(8,128)(2,1)S(1)} collective-permute-done((bf16[128,256]{1,0:T(8,128)(2,1)}, bf16[128,256]{1,0:T(8,128)(2,1)S(1)}, u32[]{:S(2)}, u32[]{:S(2)}) %collective-permute-start.46) | collective-permute-done | bytes 65568 | tf_op jit(solution)/shard_map/ppermute | solution.py:31
  74.2 1.5 %add_convert_fusion = bf16[128,256]{1,0:T(8,128)(2,1)} fusion(f32[128,256]{1,0:T(8,128)} %get-tuple-element.95, bf16[128,256]{1,0:T(8,128)(2,1)S(1)} %collective-permute-done.46), kind=kLoop, calls=%fused_computation.2 | loop fusion | flops 98304 | bytes 262144 | tf_op jit(solution)/shard_map/convert_element_type | solution.py:189
  75.7 1.1 %collective-permute-done.47 = bf16[272,256]{1,0:T(8,128)(2,1)S(1)} collective-permute-done((bf16[272,256]{1,0:T(8,128)(2,1)}, bf16[272,256]{1,0:T(8,128)(2,1)S(1)}, u32[]{:S(2)}, u32[]{:S(2)}) %collective-permute-start.47) | collective-permute-done | bytes 139296 | tf_op jit(solution)/shard_map/ppermute | solution.py:31
  (168 shorter events, 14.1 us)
Async XLA Ops:
  0.6 7.4 %collective-permute-start.1 = (bf16[128,256]{1,0:T(8,128)(2,1)}, bf16[128,256]{1,0:T(8,128)(2,1)S(1)}, u32[]{:S(2)}, u32[]{:S(2)}) collective-permute-start(bf16[128,256]{1,0:T(8,128)(2,1)} %refs_0_), channel_id=1, source_target_pairs={{0,16},{2,18},{4,20},{6,22},{8,24},{10,26},{12,28},{14,30},{16,0},... | collective-permute-start | bytes 196616 | tf_op jit(solution)/shard_map/ppermute | solution.py:31
  6.3 6.3 %collective-permute-start.2 = (bf16[128,256]{1,0:T(8,128)(2,1)}, bf16[128,256]{1,0:T(8,128)(2,1)S(1)}, u32[]{:S(2)}, u32[]{:S(2)}) collective-permute-start(bf16[128,256]{1,0:T(8,128)(2,1)} %refs_0_), channel_id=1, source_target_pairs={{0,24},{2,26},{4,28},{6,30},{8,16},{10,18},{12,20},{14,22},{16,8},... | collective-permute-start | bytes 196616 | tf_op jit(solution)/shard_map/ppermute | solution.py:31
  12.6 5.4 %collective-permute-start.3 = (bf16[128,256]{1,0:T(8,128)(2,1)}, bf16[128,256]{1,0:T(8,128)(2,1)S(1)}, u32[]{:S(2)}, u32[]{:S(2)}) collective-permute-start(bf16[128,256]{1,0:T(8,128)(2,1)} %refs_0_), channel_id=1, source_target_pairs={{0,4},{2,6},{4,0},{6,2},{8,12},{10,14},{12,8},{14,10},{16,20},{18,... | collective-permute-start | bytes 196616 | tf_op jit(solution)/shard_map/ppermute | solution.py:31
  14.1 5.0 %collective-permute-start.4 = (bf16[128,256]{1,0:T(8,128)(2,1)S(1)}, bf16[128,256]{1,0:T(8,128)(2,1)S(1)}, u32[]{:S(2)}, u32[]{:S(2)}) collective-permute-start(bf16[128,256]{1,0:T(8,128)(2,1)S(1)} %collective-permute-done.refs_1_), channel_id=1, source_target_pairs={{0,4},{2,6},{4,0},{6,2},{8,12},{10,14},{12,8},{14,10},{16,20},{18,... | collective-permute-start | bytes 196616 | tf_op jit(solution)/shard_map/ppermute | solution.py:31
  14.6 6.4 %collective-permute-start.5 = (bf16[128,256]{1,0:T(8,128)(2,1)S(1)}, bf16[128,256]{1,0:T(8,128)(2,1)S(1)}, u32[]{:S(2)}, u32[]{:S(2)}) collective-permute-start(bf16[128,256]{1,0:T(8,128)(2,1)S(1)} %collective-permute-done.1.refs_2_), channel_id=1, source_target_pairs={{0,4},{2,6},{4,0},{6,2},{8,12},{10,14},{12,8},{14,10},{16,20},{18,... | collective-permute-start | bytes 196616 | tf_op jit(solution)/shard_map/ppermute | solution.py:31
  16.1 4.9 %collective-permute-start.6 = (bf16[128,256]{1,0:T(8,128)(2,1)S(1)}, bf16[128,256]{1,0:T(8,128)(2,1)S(1)}, u32[]{:S(2)}, u32[]{:S(2)}) collective-permute-start(bf16[128,256]{1,0:T(8,128)(2,1)S(1)} %collective-permute-done.2.refs_3_), channel_id=1, source_target_pairs={{0,4},{2,6},{4,0},{6,2},{8,12},{10,14},{12,8},{14,10},{16,20},{18,... | collective-permute-start | bytes 196616 | tf_op jit(solution)/shard_map/ppermute | solution.py:31
  16.7 6.3 %collective-permute-start.9 = (bf16[128,256]{1,0:T(8,128)(2,1)}, bf16[128,256]{1,0:T(8,128)(2,1)S(1)}, u32[]{:S(2)}, u32[]{:S(2)}) collective-permute-start(bf16[128,256]{1,0:T(8,128)(2,1)} %refs_16_), channel_id=1, source_target_pairs={{0,24},{2,26},{4,28},{6,30},{8,16},{10,18},{12,20},{14,22},{16,8},... | collective-permute-start | bytes 196616 | tf_op jit(solution)/shard_map/ppermute | solution.py:31
  18.0 6.3 %collective-permute-start.8 = (bf16[128,256]{1,0:T(8,128)(2,1)}, bf16[128,256]{1,0:T(8,128)(2,1)S(1)}, u32[]{:S(2)}, u32[]{:S(2)}) collective-permute-start(bf16[128,256]{1,0:T(8,128)(2,1)} %refs_16_), channel_id=1, source_target_pairs={{0,16},{2,18},{4,20},{6,22},{8,24},{10,26},{12,28},{14,30},{16,0},... | collective-permute-start | bytes 196616 | tf_op jit(solution)/shard_map/ppermute | solution.py:31
  19.1 5.2 %collective-permute-start.7 = (bf16[128,256]{1,0:T(8,128)(2,1)}, bf16[128,256]{1,0:T(8,128)(2,1)S(1)}, u32[]{:S(2)}, u32[]{:S(2)}) collective-permute-start(bf16[128,256]{1,0:T(8,128)(2,1)} %refs_16_), channel_id=1, source_target_pairs={{0,8},{2,10},{4,12},{6,14},{8,0},{10,2},{12,4},{14,6},{16,24},{18,... | collective-permute-start | bytes 196616 | tf_op jit(solution)/shard_map/ppermute | solution.py:31
  26.4 6.9 %collective-permute-start.17 = (bf16[128,256]{1,0:T(8,128)(2,1)S(1)}, bf16[128,256]{1,0:T(8,128)(2,1)S(1)}, u32[]{:S(2)}, u32[]{:S(2)}) collective-permute-start(bf16[128,256]{1,0:T(8,128)(2,1)S(1)} %collective-permute-done.6.refs_7_), channel_id=1, source_target_pairs={{0,2},{2,0},{4,6},{6,4},{8,10},{10,8},{12,14},{14,12},{16,18},{18,... | collective-permute-start | bytes 196616 | tf_op jit(solution)/shard_map/ppermute | solution.py:31
  26.6 6.8 %collective-permute-start.18 = (bf16[128,256]{1,0:T(8,128)(2,1)}, bf16[128,256]{1,0:T(8,128)(2,1)S(1)}, u32[]{:S(2)}, u32[]{:S(2)}) collective-permute-start(bf16[128,256]{1,0:T(8,128)(2,1)} %refs_16_), channel_id=1, source_target_pairs={{0,4},{2,6},{4,0},{6,2},{8,12},{10,14},{12,8},{14,10},{16,20},{18,... | collective-permute-start | bytes 196616 | tf_op jit(solution)/shard_map/ppermute | solution.py:31
  28.1 5.3 %collective-permute-start.19 = (bf16[128,256]{1,0:T(8,128)(2,1)S(1)}, bf16[128,256]{1,0:T(8,128)(2,1)S(1)}, u32[]{:S(2)}, u32[]{:S(2)}) collective-permute-start(bf16[128,256]{1,0:T(8,128)(2,1)S(1)} %collective-permute-done.7.refs_17_), channel_id=1, source_target_pairs={{0,4},{2,6},{4,0},{6,2},{8,12},{10,14},{12,8},{14,10},{16,20},{18,... | collective-permute-start | bytes 196616 | tf_op jit(solution)/shard_map/ppermute | solution.py:31
  28.6 5.8 %collective-permute-start.20 = (bf16[128,256]{1,0:T(8,128)(2,1)S(1)}, bf16[128,256]{1,0:T(8,128)(2,1)S(1)}, u32[]{:S(2)}, u32[]{:S(2)}) collective-permute-start(bf16[128,256]{1,0:T(8,128)(2,1)S(1)} %collective-permute-done.8.refs_18_), channel_id=1, source_target_pairs={{0,4},{2,6},{4,0},{6,2},{8,12},{10,14},{12,8},{14,10},{16,20},{18,... | collective-permute-start | bytes 196616 | tf_op jit(solution)/shard_map/ppermute | solution.py:31
  30.1 5.2 %collective-permute-start.21 = (bf16[128,256]{1,0:T(8,128)(2,1)S(1)}, bf16[128,256]{1,0:T(8,128)(2,1)S(1)}, u32[]{:S(2)}, u32[]{:S(2)}) collective-permute-start(bf16[128,256]{1,0:T(8,128)(2,1)S(1)} %collective-permute-done.9.refs_19_), channel_id=1, source_target_pairs={{0,4},{2,6},{4,0},{6,2},{8,12},{10,14},{12,8},{14,10},{16,20},{18,... | collective-permute-start | bytes 196616 | tf_op jit(solution)/shard_map/ppermute | solution.py:31
  35.3 5.0 %collective-permute-start.38 = (bf16[128,256]{1,0:T(8,128)(2,1)S(1)}, bf16[128,256]{1,0:T(8,128)(2,1)S(1)}, u32[]{:S(2)}, u32[]{:S(2)}) collective-permute-start(bf16[128,256]{1,0:T(8,128)(2,1)S(1)} %copy-done.2), channel_id=1, source_target_pairs={{0,2},{2,0},{4,6},{6,4},{8,10},{10,8},{12,14},{14,12},{16,18},{18,... | collective-permute-start | bytes 196616 | tf_op jit(solution)/shard_map/ppermute | solution.py:31
  35.3 5.4 %collective-permute-start.39 = (bf16[128,256]{1,0:T(8,128)(2,1)S(1)}, bf16[128,256]{1,0:T(8,128)(2,1)S(1)}, u32[]{:S(2)}, u32[]{:S(2)}) collective-permute-start(bf16[128,256]{1,0:T(8,128)(2,1)S(1)} %collective-permute-done.7.refs_17_), channel_id=1, source_target_pairs={{0,2},{2,0},{4,6},{6,4},{8,10},{10,8},{12,14},{14,12},{16,18},{18,... | collective-permute-start | bytes 196616 | tf_op jit(solution)/shard_map/ppermute | solution.py:31
  35.9 5.1 %collective-permute-start.40 = (bf16[128,256]{1,0:T(8,128)(2,1)S(1)}, bf16[128,256]{1,0:T(8,128)(2,1)S(1)}, u32[]{:S(2)}, u32[]{:S(2)}) collective-permute-start(bf16[128,256]{1,0:T(8,128)(2,1)S(1)} %collective-permute-done.8.refs_18_), channel_id=1, source_target_pairs={{0,2},{2,0},{4,6},{6,4},{8,10},{10,8},{12,14},{14,12},{16,18},{18,... | collective-permute-start | bytes 196616 | tf_op jit(solution)/shard_map/ppermute | solution.py:31
  40.3 5.5 %collective-permute-start.42 = (bf16[128,256]{1,0:T(8,128)(2,1)S(1)}, bf16[128,256]{1,0:T(8,128)(2,1)S(1)}, u32[]{:S(2)}, u32[]{:S(2)}) collective-permute-start(bf16[128,256]{1,0:T(8,128)(2,1)S(1)} %collective-permute-done.18.refs_20_), channel_id=1, source_target_pairs={{0,2},{2,0},{4,6},{6,4},{8,10},{10,8},{12,14},{14,12},{16,18},{18,... | collective-permute-start | bytes 196616 | tf_op jit(solution)/shard_map/ppermute | solution.py:31
  40.7 6.9 %collective-permute-start.43 = (bf16[128,256]{1,0:T(8,128)(2,1)S(1)}, bf16[128,256]{1,0:T(8,128)(2,1)S(1)}, u32[]{:S(2)}, u32[]{:S(2)}) collective-permute-start(bf16[128,256]{1,0:T(8,128)(2,1)S(1)} %collective-permute-done.19.refs_21_), channel_id=1, source_target_pairs={{0,2},{2,0},{4,6},{6,4},{8,10},{10,8},{12,14},{14,12},{16,18},{18,... | collective-permute-start | bytes 196616 | tf_op jit(solution)/shard_map/ppermute | solution.py:31
  41.0 6.6 %collective-permute-start.44 = (bf16[128,256]{1,0:T(8,128)(2,1)S(1)}, bf16[128,256]{1,0:T(8,128)(2,1)S(1)}, u32[]{:S(2)}, u32[]{:S(2)}) collective-permute-start(bf16[128,256]{1,0:T(8,128)(2,1)S(1)} %collective-permute-done.20.refs_22_), channel_id=1, source_target_pairs={{0,2},{2,0},{4,6},{6,4},{8,10},{10,8},{12,14},{14,12},{16,18},{18,... | collective-permute-start | bytes 196616 | tf_op jit(solution)/shard_map/ppermute | solution.py:31
  43.3 5.3 %collective-permute-start.45 = (bf16[128,256]{1,0:T(8,128)(2,1)S(1)}, bf16[128,256]{1,0:T(8,128)(2,1)S(1)}, u32[]{:S(2)}, u32[]{:S(2)}) collective-permute-start(bf16[128,256]{1,0:T(8,128)(2,1)S(1)} %collective-permute-done.21.refs_23_), channel_id=1, source_target_pairs={{0,2},{2,0},{4,6},{6,4},{8,10},{10,8},{12,14},{14,12},{16,18},{18,... | collective-permute-start | bytes 196616 | tf_op jit(solution)/shard_map/ppermute | solution.py:31
  44.3 6.1 %collective-permute-start.26 = (bf16[128,256]{1,0:T(8,128)(2,1)S(1)}, bf16[128,256]{1,0:T(8,128)(2,1)S(1)}, u32[]{:S(2)}, u32[]{:S(2)}) collective-permute-start(bf16[128,256]{1,0:T(8,128)(2,1)S(1)} %add_convert_fusion.1.refs_0_), channel_id=1, source_target_pairs={{0,4},{2,6},{4,0},{6,2},{8,12},{10,14},{12,8},{14,10},{16,20},{18,... | collective-permute-start | bytes 196616 | tf_op jit(solution)/shard_map/ppermute | solution.py:31
  45.8 6.8 %collective-permute-start.25 = (bf16[128,256]{1,0:T(8,128)(2,1)S(1)}, bf16[128,256]{1,0:T(8,128)(2,1)S(1)}, u32[]{:S(2)}, u32[]{:S(2)}) collective-permute-start(bf16[128,256]{1,0:T(8,128)(2,1)S(1)} %add_convert_fusion.1.refs_0_), channel_id=1, source_target_pairs={{0,24},{2,26},{4,28},{6,30},{8,16},{10,18},{12,20},{14,22},{16,8},... | collective-permute-start | bytes 196616 | tf_op jit(solution)/shard_map/ppermute | solution.py:31
  47.6 5.1 %collective-permute-start.30 = (bf16[128,256]{1,0:T(8,128)(2,1)S(1)}, bf16[128,256]{1,0:T(8,128)(2,1)S(1)}, u32[]{:S(2)}, u32[]{:S(2)}) collective-permute-start(bf16[128,256]{1,0:T(8,128)(2,1)S(1)} %add_convert_fusion.1.refs_0_), channel_id=1, source_target_pairs={{0,2},{2,0},{4,6},{6,4},{8,10},{10,8},{12,14},{14,12},{16,18},{18,... | collective-permute-start | bytes 196616 | tf_op jit(solution)/shard_map/ppermute | solution.py:31
  47.6 7.3 %collective-permute-start.24 = (bf16[128,256]{1,0:T(8,128)(2,1)S(1)}, bf16[128,256]{1,0:T(8,128)(2,1)S(1)}, u32[]{:S(2)}, u32[]{:S(2)}) collective-permute-start(bf16[128,256]{1,0:T(8,128)(2,1)S(1)} %add_convert_fusion.1.refs_0_), channel_id=1, source_target_pairs={{0,16},{2,18},{4,20},{6,22},{8,24},{10,26},{12,28},{14,30},{16,0},... | collective-permute-start | bytes 196616 | tf_op jit(solution)/shard_map/ppermute | solution.py:31
  48.6 6.9 %collective-permute-start.23 = (bf16[128,256]{1,0:T(8,128)(2,1)S(1)}, bf16[128,256]{1,0:T(8,128)(2,1)S(1)}, u32[]{:S(2)}, u32[]{:S(2)}) collective-permute-start(bf16[128,256]{1,0:T(8,128)(2,1)S(1)} %add_convert_fusion.1.refs_0_), channel_id=1, source_target_pairs={{0,8},{2,10},{4,12},{6,14},{8,0},{10,2},{12,4},{14,6},{16,24},{18,... | collective-permute-start | bytes 196616 | tf_op jit(solution)/shard_map/ppermute | solution.py:31
  50.3 6.6 %collective-permute-start.34 = (bf16[128,256]{1,0:T(8,128)(2,1)S(1)}, bf16[128,256]{1,0:T(8,128)(2,1)S(1)}, u32[]{:S(2)}, u32[]{:S(2)}) collective-permute-start(bf16[128,256]{1,0:T(8,128)(2,1)S(1)} %collective-permute-done.26.refs_4_), channel_id=1, source_target_pairs={{0,2},{2,0},{4,6},{6,4},{8,10},{10,8},{12,14},{14,12},{16,18},{18,... | collective-permute-start | bytes 196616 | tf_op jit(solution)/shard_map/ppermute | solution.py:31
  52.7 4.8 %collective-permute-start.29 = (bf16[128,256]{1,0:T(8,128)(2,1)S(1)}, bf16[128,256]{1,0:T(8,128)(2,1)S(1)}, u32[]{:S(2)}, u32[]{:S(2)}) collective-permute-start(bf16[128,256]{1,0:T(8,128)(2,1)S(1)} %collective-permute-done.25.refs_3_), channel_id=1, source_target_pairs={{0,4},{2,6},{4,0},{6,2},{8,12},{10,14},{12,8},{14,10},{16,20},{18,... | collective-permute-start | bytes 196616 | tf_op jit(solution)/shard_map/ppermute | solution.py:31
  54.9 4.7 %collective-permute-start.28 = (bf16[128,256]{1,0:T(8,128)(2,1)S(1)}, bf16[128,256]{1,0:T(8,128)(2,1)S(1)}, u32[]{:S(2)}, u32[]{:S(2)}) collective-permute-start(bf16[128,256]{1,0:T(8,128)(2,1)S(1)} %collective-permute-done.24.refs_2_), channel_id=1, source_target_pairs={{0,4},{2,6},{4,0},{6,2},{8,12},{10,14},{12,8},{14,10},{16,20},{18,... | collective-permute-start | bytes 196616 | tf_op jit(solution)/shard_map/ppermute | solution.py:31
  55.5 4.9 %collective-permute-start.27 = (bf16[128,256]{1,0:T(8,128)(2,1)S(1)}, bf16[128,256]{1,0:T(8,128)(2,1)S(1)}, u32[]{:S(2)}, u32[]{:S(2)}) collective-permute-start(bf16[128,256]{1,0:T(8,128)(2,1)S(1)} %collective-permute-done.23.refs_1_), channel_id=1, source_target_pairs={{0,4},{2,6},{4,0},{6,2},{8,12},{10,14},{12,8},{14,10},{16,20},{18,... | collective-permute-start | bytes 196616 | tf_op jit(solution)/shard_map/ppermute | solution.py:31
  69.3 4.9 %collective-permute-start.46 = (bf16[128,256]{1,0:T(8,128)(2,1)}, bf16[128,256]{1,0:T(8,128)(2,1)S(1)}, u32[]{:S(2)}, u32[]{:S(2)}) collective-permute-start(bf16[128,256]{1,0:T(8,128)(2,1)} %get-tuple-element.96), channel_id=1, source_target_pairs={{0,1},{1,0},{2,3},{3,2},{4,5},{5,4},{6,7},{7,6},{8,9},{9,8},{10,11... | collective-permute-start | bytes 196616 | tf_op jit(solution)/shard_map/ppermute | solution.py:31
  70.9 5.9 %collective-permute-start.47 = (bf16[272,256]{1,0:T(8,128)(2,1)}, bf16[272,256]{1,0:T(8,128)(2,1)S(1)}, u32[]{:S(2)}, u32[]{:S(2)}) collective-permute-start(bf16[272,256]{1,0:T(8,128)(2,1)} %get-tuple-element.97), channel_id=1, source_target_pairs={{0,1},{1,0},{2,3},{3,2},{4,5},{5,4},{6,7},{7,6},{8,9},{9,8},{10,11... | collective-permute-start | bytes 417800 | tf_op jit(solution)/shard_map/ppermute | solution.py:31
  (64 other events, 490.9 us)

commit v2 on v1

v2 whole, which is shorter than its diff:
```python
import functools
import math

import jax
import jax.numpy as jnp
from jax import lax
from jax.experimental import pallas as pl
from jax.experimental.pallas import tpu as pltpu
from jax.sharding import Mesh
from jax.sharding import PartitionSpec as P

BF16 = jnp.bfloat16
F32 = jnp.float32
VMEM = pl.BlockSpec(memory_space=pltpu.VMEM)
SMEM = pl.BlockSpec(memory_space=pltpu.SMEM)
MIB = 1024 * 1024


def swap(x, axis):
    return lax.ppermute(x, axis, [(0, 1), (1, 0)])


def gather_far(block, n_far):
    copies = jnp.broadcast_to(block, (n_far,) + block.shape)
    return lax.all_to_all(copies, "far", 0, 0).reshape(n_far * block.shape[0], block.shape[1])


def after(x, *others):
    return lax.optimization_barrier((x,) + others)[0]


def expand_kernel(n_loop, n_row, tile, rows_ref, counts_ref, tiles_ref, out_ref):
    n_far = n_loop // 4
    me = lax.axis_index("row")
    my_near = 2 * lax.axis_index("mid") + lax.axis_index("core")

    def body(j, carry):
        piece = jnp.bitwise_xor(lax.rem(j, 4), my_near)
        column = piece * n_far + lax.div(j, 4)
        for s in range(n_row):
            slot = j * n_row + s
            place = jnp.bitwise_xor(rows_ref[slot], me)
            value = tiles_ref[slot]
            value = jnp.where(s < counts_ref[j], value, jnp.zeros_like(value))
            out_ref[
                pl.ds(pl.multiple_of(place * tile, tile), tile),
                pl.ds(pl.multiple_of(column * tile, tile), tile),
            ] = value
        return carry

    lax.fori_loop(0, n_loop, body, 0)


def columns_product(a_ref, first, pieces, row_slice):
    total = None
    for k, piece in enumerate(pieces):
        depth = piece.shape[0]
        at = (first + k) * depth
        product = jnp.dot(
            a_ref[row_slice, at : at + depth], piece[...], preferred_element_type=F32
        )
        total = product if total is None else total + product
    return total


def forward_half_kernel(tile, n_row, a_ref, p0_ref, p1_ref, out_ref):
    step = min(2, n_row) * tile
    for at in range(0, n_row * tile, step):
        rows = slice(at, at + step)
        out_ref[rows, :] = columns_product(a_ref, 0, (p0_ref, p1_ref), rows)


def split_rows(total_of, tile, n_row, own_ref, send_refs):
    step = min(2, n_row)
    for q in range(0, n_row, step):
        total = total_of(slice(q * tile, (q + step) * tile))
        for k in range(step):
            part = total[k * tile : (k + 1) * tile, :]
            if q + k == 0:
                own_ref[...] = part
            else:
                send_refs[q + k - 1][...] = part.astype(BF16)


def forward_kernel(tile, n_row, a_ref, p2_ref, p3_ref, half_ref, own_ref, *send_refs):
    split_rows(
        lambda rows: half_ref[rows, :] + columns_product(a_ref, 2, (p2_ref, p3_ref), rows),
        tile,
        n_row,
        own_ref,
        send_refs,
    )


def backward_piece(h_ref, c_ref, w_ref, b_ref, gh_ref):
    depth, width = h_ref.shape
    step = min(depth, 256)

    def body(i, carry):
        grad_w, grad_b = carry
        at = pl.ds(pl.multiple_of(i * step, step), step)
        hidden = h_ref[at, :]
        preact = jnp.dot(hidden, w_ref[...], preferred_element_type=F32) + b_ref[...]
        sig = 0.5 * jnp.tanh(0.5 * preact) + 0.5
        grad_z = c_ref[at, :].astype(F32) * sig * (1.0 + preact * (1.0 - sig))
        half = grad_z.astype(BF16)
        grad_b = grad_b + jnp.sum(grad_z.reshape(step // 8, 8, width), axis=0)
        grad_w = grad_w + lax.dot_general(
            hidden, half, (((0,), (0,)), ((), ())), preferred_element_type=F32
        )
        gh_ref[at, :] = lax.dot_general(
            half, w_ref[...], (((1,), (1,)), ((), ())), preferred_element_type=F32
        ).astype(BF16)
        return grad_w, grad_b

    carry = (jnp.zeros((width, width), F32), jnp.zeros((8, width), F32))
    for i in range(depth // step):
        carry = body(i, carry)
    return carry


def backward_half_kernel(
    tile, n_row, a_ref, w_ref, b_ref, h0_ref, h1_ref, c0_ref, c1_ref,
    out_ref, gw_ref, gb_ref, gf_ref, gh0_ref, gh1_ref,
):
    mine = pl.ds(pl.multiple_of(lax.axis_index("far") * tile, tile), tile)
    preact = jnp.dot(h0_ref[mine, :], w_ref[...], preferred_element_type=F32) + b_ref[...]
    out_ref[...] = (preact * (0.5 * jnp.tanh(0.5 * preact) + 0.5)).astype(BF16)
    gw0, gb0 = backward_piece(h0_ref, c0_ref, w_ref, b_ref, gh0_ref)
    gw1, gb1 = backward_piece(h1_ref, c1_ref, w_ref, b_ref, gh1_ref)
    gw_ref[...] = gw0 + gw1
    gb_ref[...] = gb0 + gb1
    step = min(2, n_row) * tile
    for at in range(0, n_row * tile, step):
        rows = slice(at, at + step)
        gf_ref[rows, :] = columns_product(a_ref, 0, (gh0_ref, gh1_ref), rows)


def backward_weight_kernel(
    w_ref, b_ref, h2_ref, h3_ref, c2_ref, c3_ref, gw_ref, gb_ref,
    gh2_ref, gh3_ref, message_ref,
):
    width = w_ref.shape[0]
    gw2, gb2 = backward_piece(h2_ref, c2_ref, w_ref, b_ref, gh2_ref)
    gw3, gb3 = backward_piece(h3_ref, c3_ref, w_ref, b_ref, gh3_ref)
    message_ref[:width, :] = (gw_ref[...] + (gw2 + gw3)).astype(BF16)
    bias = jnp.sum(gb_ref[...] + (gb2 + gb3), axis=0, keepdims=True)
    high = bias.astype(BF16).astype(F32)
    low = bias - high
    row = lax.broadcasted_iota(jnp.int32, (16, width), 0)
    high = jnp.broadcast_to(high, (16, width))
    low = jnp.broadcast_to(low, (16, width))
    message_ref[width:, :] = jnp.where(row == 0, high, jnp.where(row == 1, low, 0.0)).astype(BF16)


def call(kernel, name, outs, operands, scratch=(), specs=None, flops=0):
    size = sum(o.size * o.dtype.itemsize for o in list(operands) + list(outs))
    held = size + sum(math.prod(s.shape) * jnp.dtype(s.dtype).itemsize for s in scratch)
    return pl.pallas_call(
        kernel,
        name=name,
        out_shape=outs,
        in_specs=specs or [VMEM] * len(operands),
        out_specs=[VMEM] * len(outs),
        scratch_shapes=scratch,
        cost_estimate=pl.CostEstimate(flops=flops, bytes_accessed=size, transcendentals=0),
        compiler_params=pltpu.CompilerParams(vmem_limit_bytes=2 * held + 4 * MIB),
    )(*operands)


def shards(n_loop, n_row, features, weight, bias_vector, cotangent, tile_values, tile_rows, counts):
    tile, width = features.shape
    n_far = n_loop // 4
    nodes = tile * n_loop * n_row
    rows, depth = n_row * tile, n_far * tile
    shape = jax.ShapeDtypeStruct
    product = 2 * rows * 2 * depth * width

    f0 = gather_far(features, n_far)
    f2 = swap(f0, "mid")
    f1 = swap(f0, "core")
    c0 = gather_far(after(cotangent, f0), n_far)

    (adjacency,) = call(
        functools.partial(expand_kernel, n_loop, n_row, tile),
        "expand",
        [shape((rows, n_loop * tile), BF16)],
        (tile_rows, counts, tile_values),
        specs=[SMEM, SMEM, VMEM],
    )
    (half,) = call(
        functools.partial(forward_half_kernel, tile, n_row),
        "forward_near",
        [shape((rows, width), F32)],
        (adjacency, f0, f1),
        flops=product,
    )
    f3 = swap(after(f2, c0, half), "core")
    c2 = swap(after(c0, f2), "mid")
    c1 = swap(after(c0, f2), "core")

    sends = [shape((tile, width), BF16)] * (n_row - 1)
    own, *parts = call(
        functools.partial(forward_kernel, tile, n_row),
        "forward_rest",
        [shape((tile, width), F32)] + sends,
        (adjacency, f2, f3, half),
        flops=product,
    )
    for q, part in enumerate(parts):
        own = own + row_swap(part, q + 1, n_row).astype(F32)
    hidden = own.astype(BF16)
    c3 = swap(after(c2, parts[0]), "core")

    h0 = gather_far(hidden, n_far)
    h1 = swap(h0, "core")
    h2 = swap(h0, "mid")

    bias_row = bias_vector.reshape(1, width)
    gh = pltpu.VMEM((depth, width), BF16)
    elements = 2 * 6 * depth * width * width
    output, grad_w, grad_b, half = call(
        functools.partial(backward_half_kernel, tile, n_row),
        "backward_near",
        [
            shape((tile, width), BF16),
            shape((width, width), F32),
            shape((8, width), F32),
            shape((rows, width), F32),
        ],
        (adjacency, weight, bias_row, h0, h1, c0, c1),
        scratch=[gh, gh],
        flops=product + elements,
    )
    h3 = swap(after(h2, half), "core")
    gh2, gh3, message = call(
        backward_weight_kernel,
        "backward_rest",
        [shape((depth, width), BF16)] * 2 + [shape((width + 16, width), BF16)],
        (weight, bias_row, h2, h3, c2, c3, grad_w, grad_b),
        flops=elements,
    )
    own, *parts = call(
        functools.partial(forward_kernel, tile, n_row),
        "features_rest",
        [shape((tile, width), F32)] + sends,
        (adjacency, gh2, gh3, half),
        flops=product,
    )

    norm_factor = 1.0 / nodes**0.5
    bit = 1
    while bit < n_row:
        other = row_swap(message, bit, n_row)
        total = message.astype(F32) + other.astype(F32)
        bias_total = total[width : width + 1, :] + total[width + 1 : width + 2, :]
        bit *= 2
        if bit < n_row:
            high = bias_total.astype(BF16)
            low = (bias_total - high.astype(F32)).astype(BF16)
            rest = jnp.zeros((14, width), BF16)
            message = jnp.concatenate([total[:width].astype(BF16), high, low, rest], axis=0)

    for q, part in enumerate(parts):
        own = own + row_swap(part, q + 1, n_row).astype(F32)
    grad_features = own.astype(BF16)
    return (
        output,
        grad_features,
        total[:width] * norm_factor,
        bias_total.reshape(width) * norm_factor,
    )


def row_swap(x, mask, n_row):
    return lax.ppermute(x, "row", [(i, i ^ mask) for i in range(n_row)])


def solution(mesh):
    n_loop, n_row = mesh.shape["loop"], mesh.shape["row"]
    fine = Mesh(mesh.devices.reshape(n_loop // 4, 2, 2, n_row), ("far", "mid", "core", "row"))
    every = ("far", "mid", "core", "row")
    in_specs = (
        P(every, None),
        P(),
        P(),
        P(every, None),
        P(every, None, None),
        P(every),
        P(every),
    )
    out_specs = (P(every, None), P(every, None), P(), P())
    return jax.shard_map(
        functools.partial(shards, n_loop, n_row),
        mesh=fine,
        in_specs=in_specs,
        out_specs=out_specs,
        check_vma=False,
    )
```

time: 78.4 us -> 71.3 us (0.909)
  starting transfers between devices: 34.6 us -> 17.2 us
  blocking collectives: 0 us -> 15 us
  Pallas kernels: 12.3 us -> 4.03 us
  waiting for transfers between devices: 25.6 us -> 28.8 us
  local copies, waits for them, and re-layouts: 0.64 us -> 3.24 us
  other arithmetic: 3.79 us -> 1.98 us
    ppermute x48 -> x12, starting transfers between devices: 34.6 us -> 8.52 us  [the longest x9 4.85 us: swap(): return lax.ppermute(x, axis, [(0, 1), (1, 0)])]
    all_to_all x0 -> x1, blocking collectives: none -> 15 us  [gather_far(): lax.all_to_all(copies, 'far', 0, 0)]
    all_to_all x0 -> x2, starting transfers between devices: none -> 8.65 us  [gather_far(): lax.all_to_all(copies, 'far', 0, 0)]
    pallas_call x3 -> x6, Pallas kernels: 12.3 us -> 4.03 us  [call(): pl.pallas_call(kernel, name=name, out_shape=outs, in_specs=specs or [VMEM...]
    all_to_all x0 -> x2, waiting for transfers between devices: none -> 6.69 us  [gather_far(): lax.all_to_all(copies, 'far', 0, 0)]
    ppermute x48 -> x12, waiting for transfers between devices: 25.6 us -> 22.1 us  [the longest x9 14.7 us: swap(): return lax.ppermute(x, axis, [(0, 1), (1, 0)])]
    broadcast_in_dim x0 -> x3, local copies, waits for them, and re-layouts: none -> 3.22 us  [gather_far(): copies = jnp.broadcast_to(block, (n_far,) + block.shape)]
    convert_element_type x1, other arithmetic: 0.92 us -> 0.01 us  [shards(): hidden = own.astype(BF16)]
  transfers between devices with their start and end apart: 48 -> 14, of which waited for: 17 -> 8; matrix products, arithmetic and copies ran while one was open for 3% -> 1% of each run, Pallas kernels for 7% -> 3%
where the time goes in v2:
time: 71.3 us; the launch traced here: 70.9 us
  waiting for transfers between devices  28.8 us (40%)
  starting transfers between devices  17.2 us (24%)
  blocking collectives  15 us (21%)
  Pallas kernels  4.03 us (6%)
  local copies, waits for them, and re-layouts  3.24 us (5%)
  other arithmetic  1.98 us (3%)
  between operations  0.74 us (1%)
    all_to_all x1, blocking collectives, gather_far(): lax.all_to_all(copies, 'far', 0, 0)  15 us
    ppermute x9, waiting for transfers between devices, swap(): return lax.ppermute(x, axis, [(0, 1), (1, 0)])  14.7 us
    all_to_all x2, starting transfers between devices, gather_far(): lax.all_to_all(copies, 'far', 0, 0)  8.65 us
    ppermute x3, waiting for transfers between devices, row_swap(): return lax.ppermute(x, 'row', [(i, i ^ mask) for i in range(n_row)])  7.32 us
    all_to_all x2, waiting for transfers between devices, gather_far(): lax.all_to_all(copies, 'far', 0, 0)  6.69 us
    ppermute x9, starting transfers between devices, swap(): return lax.ppermute(x, axis, [(0, 1), (1, 0)])  4.85 us
    pallas_call x6, Pallas kernels, call(): pl.pallas_call(kernel, name=name, out_shape=outs, in_specs=specs or [VMEM...  4.03 us
    ppermute x3, starting transfers between devices, row_swap(): return lax.ppermute(x, 'row', [(i, i ^ mask) for i in range(n_row)])  3.68 us
  transfers between devices with their start and end apart: 14, of which 8 were waited for; matrix products, arithmetic and copies ran while one was open for 1% of the time, Pallas kernels for 3%

profile of v2, /device:TPU:0, one launch (start us, length us, event | category | flops | bytes accessed | tf_op | source)
XLA Modules:
  0.0 70.9 jit_solution(12033440856964367767)
XLA Ops:
  0.6 0.9 %broadcast_in_dim.9 = bf16[4,128,256]{2,1,0:T(8,128)(2,1)S(1)} broadcast(bf16[128,256]{1,0:T(8,128)(2,1)} %param.7), dimensions={1,2} | broadcast | bytes 327680 | tf_op jit(solution)/shard_map/broadcast_in_dim | solution.py:24
  1.6 15.0 %all_to_all.15 = bf16[4,128,256]{2,1,0:T(8,128)(2,1)S(1)} all-to-all(bf16[4,128,256]{2,1,0:T(8,128)(2,1)S(1)} %broadcast_in_dim.9), channel_id=1, replica_groups=mesh['far'=4,'mid'=2,'core'=2,'row'=2] {'far'}, dimensions={0} | all-to-all | bytes 524288 | tf_op jit(solution)/shard_map/all_to_all | solution.py:25
  16.6 1.6 %broadcast_in_dim.10 = bf16[4,128,256]{2,1,0:T(8,128)(2,1)} broadcast(bf16[128,256]{1,0:T(8,128)(2,1)} %param.10), dimensions={1,2} | broadcast | bytes 327680 | tf_op jit(solution)/shard_map/broadcast_in_dim | solution.py:24
  18.1 3.5 %all-to-all-start.1 = ((bf16[4,128,256]{2,1,0:T(8,128)(2,1)}), bf16[4,128,256]{2,1,0:T(8,128)(2,1)S(1)}, u32[]{:S(2)}, u32[]{:S(2)}) async-start(bf16[4,128,256]{2,1,0:T(8,128)(2,1)} %broadcast_in_dim.10), calls=%async_computation.1 | async-start | bytes 524288 | tf_op jit(solution)/shard_map/all_to_all | solution.py:25
  21.7 0.1 collective-permute-start.1
  21.8 1.6 %collective-permute-start = (bf16[512,256]{1,0:T(8,128)(2,1)S(1)}, bf16[512,256]{1,0:T(8,128)(2,1)S(1)}, u32[]{:S(2)}, u32[]{:S(2)}) collective-permute-start(bf16[512,256]{1,0:T(8,128)(2,1)S(1)} %bitcast.6), channel_id=1, source_target_pairs={{0,4},{4,0},{1,5},{5,1},{2,6},{6,2},{3,7},{7,3},{8,12},{12,8},{9,1... | collective-permute-start | bytes 786440 | tf_op jit(solution)/shard_map/ppermute | solution.py:20
  23.3 0.9 %expand.1.a_ref = bf16[256,2048]{1,0:T(8,128)(2,1)S(1)} custom-call(s32[32]{0:T(128)S(1)} %copy-done.3, s32[16]{0:T(128)S(1)} %copy-done.4, bf16[32,128,128]{2,1,0:T(8,128)(2,1)S(1)} %copy-done), custom_call_target="tpu_custom_call" | custom-call | bytes 2097344 | tf_op jit(solution)/shard_map/expand/pallas_call | solution.py:159
  24.3 0.3 forward_near.1.half_ref
  24.6 5.9 %collective-permute-done.p2_ref = bf16[512,256]{1,0:T(8,128)(2,1)S(1)} collective-permute-done((bf16[512,256]{1,0:T(8,128)(2,1)S(1)}, bf16[512,256]{1,0:T(8,128)(2,1)S(1)}, u32[]{:S(2)}, u32[]{:S(2)}) %collective-permute-start) | collective-permute-done | bytes 262176 | tf_op jit(solution)/shard_map/ppermute | solution.py:20
  30.5 0.0 all-to-all-done.1
  30.5 1.5 %collective-permute-done.2.p3_ref = bf16[512,256]{1,0:T(8,128)(2,1)S(1)} collective-permute-done((bf16[512,256]{1,0:T(8,128)(2,1)S(1)}, bf16[512,256]{1,0:T(8,128)(2,1)S(1)}, u32[]{:S(2)}, u32[]{:S(2)}) %collective-permute-start.2) | collective-permute-done | bytes 262176 | tf_op jit(solution)/shard_map/ppermute | solution.py:20
  32.0 0.3 forward_rest.1
  32.3 1.6 %collective-permute-start.3 = (bf16[128,256]{1,0:T(8,128)(2,1)S(1)}, bf16[128,256]{1,0:T(8,128)(2,1)S(1)}, u32[]{:S(2)}, u32[]{:S(2)}) collective-permute-start(bf16[128,256]{1,0:T(8,128)(2,1)S(1)} %get-tuple-element.23), channel_id=1, source_target_pairs={{0,1},{1,0},{2,3},{3,2},{4,5},{5,4},{6,7},{7,6},{8,9},{9,8},{10,11... | collective-permute-start | bytes 196616 | tf_op jit(solution)/shard_map/ppermute | solution.py:276
  33.9 2.7 %collective-permute-done.3 = bf16[128,256]{1,0:T(8,128)(2,1)S(1)} collective-permute-done((bf16[128,256]{1,0:T(8,128)(2,1)S(1)}, bf16[128,256]{1,0:T(8,128)(2,1)S(1)}, u32[]{:S(2)}, u32[]{:S(2)}) %collective-permute-start.3) | collective-permute-done | bytes 65568 | tf_op jit(solution)/shard_map/ppermute | solution.py:276
  36.7 0.7 %broadcast_in_dim.11 = bf16[4,128,256]{2,1,0:T(8,128)(2,1)} broadcast(bf16[128,256]{1,0:T(8,128)(2,1)S(1)} %add_convert_fusion.1), dimensions={1,2} | broadcast | bytes 327680 | tf_op jit(solution)/shard_map/broadcast_in_dim | solution.py:24
  37.4 5.1 %all-to-all-start.2 = ((bf16[4,128,256]{2,1,0:T(8,128)(2,1)}), bf16[4,128,256]{2,1,0:T(8,128)(2,1)S(1)}, u32[]{:S(2)}, u32[]{:S(2)}) async-start(bf16[4,128,256]{2,1,0:T(8,128)(2,1)} %broadcast_in_dim.11), calls=%async_computation.2 | async-start | bytes 524288 | tf_op jit(solution)/shard_map/all_to_all | solution.py:25
  42.5 1.5 %collective-permute-start.8 = (bf16[512,256]{1,0:T(8,128)(2,1)S(1)}, bf16[512,256]{1,0:T(8,128)(2,1)S(1)}, u32[]{:S(2)}, u32[]{:S(2)}) collective-permute-start(bf16[512,256]{1,0:T(8,128)(2,1)S(1)} %bitcast.8), channel_id=1, source_target_pairs={{0,4},{4,0},{1,5},{5,1},{2,6},{6,2},{3,7},{7,3},{8,12},{12,8},{9,1... | collective-permute-start | bytes 786440 | tf_op jit(solution)/shard_map/ppermute | solution.py:20
  44.0 6.7 %all-to-all-done.2 = bf16[4,128,256]{2,1,0:T(8,128)(2,1)S(1)} async-done(((bf16[4,128,256]{2,1,0:T(8,128)(2,1)}), bf16[4,128,256]{2,1,0:T(8,128)(2,1)S(1)}, u32[]{:S(2)}, u32[]{:S(2)}) %all-to-all-start.2) | async-done | bytes 262176 | tf_op jit(solution)/shard_map/all_to_all | solution.py:25
  50.7 1.5 %collective-permute-start.6 = (bf16[512,256]{1,0:T(8,128)(2,1)S(1)}, bf16[512,256]{1,0:T(8,128)(2,1)S(1)}, u32[]{:S(2)}, u32[]{:S(2)}) collective-permute-start(bf16[512,256]{1,0:T(8,128)(2,1)S(1)} %bitcast.12), channel_id=1, source_target_pairs={{0,4},{4,0},{1,5},{5,1},{2,6},{6,2},{3,7},{7,3},{8,12},{12,8},{9,1... | collective-permute-start | bytes 786440 | tf_op jit(solution)/shard_map/ppermute | solution.py:20
  52.2 0.2 collective-permute-start.9
  52.5 1.2 %backward_near.1 = (bf16[128,256]{1,0:T(8,128)(2,1)}, f32[256,256]{1,0:T(8,128)S(1)}, f32[8,256]{1,0:T(8,128)S(1)}, f32[256,256]{1,0:T(8,128)S(1)}) custom-call(bf16[256,2048]{1,0:T(8,128)(2,1)S(1)} %expand.1.a_ref, bf16[256,256]{1,0:T(8,128)(2,1)S(1)} %copy-done.1, f32[1,256]{1,0:T(1,128)S(1)} %bitcast.14, bf16[512,256]{1,0:T(8,128)(2,1)S(1)} %bitcast.13, ...), custom_call_target="tpu_custom_call" | custom-call | flops 536870912 | bytes 2827264 | tf_op jit(solution)/shard_map/backward_near/pallas_call | solution.py:159
  53.7 5.8 %collective-permute-done.6.h2_ref = bf16[512,256]{1,0:T(8,128)(2,1)S(1)} collective-permute-done((bf16[512,256]{1,0:T(8,128)(2,1)S(1)}, bf16[512,256]{1,0:T(8,128)(2,1)S(1)}, u32[]{:S(2)}, u32[]{:S(2)}) %collective-permute-start.6) | collective-permute-done | bytes 262176 | tf_op jit(solution)/shard_map/ppermute | solution.py:20
  59.4 1.5 %collective-permute-done.7.h3_ref = bf16[512,256]{1,0:T(8,128)(2,1)S(1)} collective-permute-done((bf16[512,256]{1,0:T(8,128)(2,1)S(1)}, bf16[512,256]{1,0:T(8,128)(2,1)S(1)}, u32[]{:S(2)}, u32[]{:S(2)}) %collective-permute-start.7) | collective-permute-done | bytes 262176 | tf_op jit(solution)/shard_map/ppermute | solution.py:20
  61.0 1.0 %backward_rest.1 = (bf16[512,256]{1,0:T(8,128)(2,1)S(1)}, bf16[512,256]{1,0:T(8,128)(2,1)S(1)}, bf16[272,256]{1,0:T(8,128)(2,1)S(1)}) custom-call(bf16[256,256]{1,0:T(8,128)(2,1)S(1)} %copy-done.1, f32[1,256]{1,0:T(1,128)S(1)} %bitcast.15, bf16[512,256]{1,0:T(8,128)(2,1)S(1)} %collective-permute-done.6.h2_ref, ...), custom_call_target="tpu_custom_call" | custom-call | flops 402653184 | bytes 2114560 | tf_op jit(solution)/shard_map/backward_rest/pallas_call | solution.py:159
  62.0 0.3 features_rest.1
  62.3 1.6 %collective-permute-start.10 = (bf16[128,256]{1,0:T(8,128)(2,1)S(1)}, bf16[128,256]{1,0:T(8,128)(2,1)S(1)}, u32[]{:S(2)}, u32[]{:S(2)}) collective-permute-start(bf16[128,256]{1,0:T(8,128)(2,1)S(1)} %get-tuple-element.34), channel_id=1, source_target_pairs={{0,1},{1,0},{2,3},{3,2},{4,5},{5,4},{6,7},{7,6},{8,9},{9,8},{10,11... | collective-permute-start | bytes 196616 | tf_op jit(solution)/shard_map/ppermute | solution.py:276
  63.9 0.5 collective-permute-start.11
  64.4 2.6 %collective-permute-done.10 = bf16[128,256]{1,0:T(8,128)(2,1)S(1)} collective-permute-done((bf16[128,256]{1,0:T(8,128)(2,1)S(1)}, bf16[128,256]{1,0:T(8,128)(2,1)S(1)}, u32[]{:S(2)}, u32[]{:S(2)}) %collective-permute-start.10) | collective-permute-done | bytes 65568 | tf_op jit(solution)/shard_map/ppermute | solution.py:276
  67.0 0.6 add_convert_fusion
  67.6 2.0 %collective-permute-done.11 = bf16[272,256]{1,0:T(8,128)(2,1)S(1)} collective-permute-done((bf16[272,256]{1,0:T(8,128)(2,1)S(1)}, bf16[272,256]{1,0:T(8,128)(2,1)S(1)}, u32[]{:S(2)}, u32[]{:S(2)}) %collective-permute-start.11) | collective-permute-done | bytes 139296 | tf_op jit(solution)/shard_map/ppermute | solution.py:276
  69.6 0.6 fusion
  70.2 0.7 %slice_multiply_fusion = f32[256,256]{1,0:T(8,128)} fusion(f32[272,256]{1,0:T(8,128)S(1)} %convert_add_fusion), kind=kLoop, calls=%fused_computation.1 | loop fusion | flops 65536 | bytes 524288 | tf_op jit(solution)/shard_map/mul | solution.py:270
  (21 shorter events, 0.1 us)
Async XLA Ops:
  0.6 22.7 %copy-start = (bf16[32,128,128]{2,1,0:T(8,128)(2,1)S(1)}, bf16[32,128,128]{2,1,0:T(8,128)(2,1)}, u32[]{:S(2)}) copy-start(bf16[32,128,128]{2,1,0:T(8,128)(2,1)} %tiles_ref.1) | copy-start | bytes 3145732
  18.1 5.2 %copy-start.3 = (s32[32]{0:T(128)S(1)}, s32[32]{0:T(128)}, u32[]{:S(2)}) copy-start(s32[32]{0:T(128)} %rows_ref.1) | copy-start | bytes 388
  18.1 5.2 %copy-start.4 = (s32[16]{0:T(128)S(1)}, s32[16]{0:T(128)}, u32[]{:S(2)}) copy-start(s32[16]{0:T(128)} %counts_ref.1) | copy-start | bytes 196
  18.1 12.4 %all-to-all-start.1 = ((bf16[4,128,256]{2,1,0:T(8,128)(2,1)}), bf16[4,128,256]{2,1,0:T(8,128)(2,1)S(1)}, u32[]{:S(2)}, u32[]{:S(2)}) async-start(bf16[4,128,256]{2,1,0:T(8,128)(2,1)} %broadcast_in_dim.10), calls=%async_computation.1 | async-start | bytes 524288 | tf_op jit(solution)/shard_map/all_to_all | solution.py:25
  21.7 2.6 %collective-permute-start.1 = (bf16[512,256]{1,0:T(8,128)(2,1)S(1)}, bf16[512,256]{1,0:T(8,128)(2,1)S(1)}, u32[]{:S(2)}, u32[]{:S(2)}) collective-permute-start(bf16[512,256]{1,0:T(8,128)(2,1)S(1)} %bitcast.5), channel_id=1, source_target_pairs={{0,2},{2,0},{1,3},{3,1},{4,6},{6,4},{5,7},{7,5},{8,10},{10,8},{9,1... | collective-permute-start | bytes 786440 | tf_op jit(solution)/shard_map/ppermute | solution.py:20
  21.8 8.7 %collective-permute-start = (bf16[512,256]{1,0:T(8,128)(2,1)S(1)}, bf16[512,256]{1,0:T(8,128)(2,1)S(1)}, u32[]{:S(2)}, u32[]{:S(2)}) collective-permute-start(bf16[512,256]{1,0:T(8,128)(2,1)S(1)} %bitcast.6), channel_id=1, source_target_pairs={{0,4},{4,0},{1,5},{5,1},{2,6},{6,2},{3,7},{7,3},{8,12},{12,8},{9,1... | collective-permute-start | bytes 786440 | tf_op jit(solution)/shard_map/ppermute | solution.py:20
  30.5 1.5 %collective-permute-start.2 = (bf16[512,256]{1,0:T(8,128)(2,1)S(1)}, bf16[512,256]{1,0:T(8,128)(2,1)S(1)}, u32[]{:S(2)}, u32[]{:S(2)}) collective-permute-start(bf16[512,256]{1,0:T(8,128)(2,1)S(1)} %collective-permute-done.p2_ref), channel_id=1, source_target_pairs={{0,2},{2,0},{1,3},{3,1},{4,6},{6,4},{5,7},{7,5},{8,10},{10,8},{9,1... | collective-permute-start | bytes 786440 | tf_op jit(solution)/shard_map/ppermute | solution.py:20
  32.3 4.3 %collective-permute-start.3 = (bf16[128,256]{1,0:T(8,128)(2,1)S(1)}, bf16[128,256]{1,0:T(8,128)(2,1)S(1)}, u32[]{:S(2)}, u32[]{:S(2)}) collective-permute-start(bf16[128,256]{1,0:T(8,128)(2,1)S(1)} %get-tuple-element.23), channel_id=1, source_target_pairs={{0,1},{1,0},{2,3},{3,2},{4,5},{5,4},{6,7},{7,6},{8,9},{9,8},{10,11... | collective-permute-start | bytes 196616 | tf_op jit(solution)/shard_map/ppermute | solution.py:276
  37.4 15.0 %copy-start.1 = (bf16[256,256]{1,0:T(8,128)(2,1)S(1)}, bf16[256,256]{1,0:T(8,128)(2,1)}, u32[]{:S(2)}) copy-start(bf16[256,256]{1,0:T(8,128)(2,1)} %w_ref.3) | copy-start | bytes 393220
  37.4 13.3 %all-to-all-start.2 = ((bf16[4,128,256]{2,1,0:T(8,128)(2,1)}), bf16[4,128,256]{2,1,0:T(8,128)(2,1)S(1)}, u32[]{:S(2)}, u32[]{:S(2)}) async-start(bf16[4,128,256]{2,1,0:T(8,128)(2,1)} %broadcast_in_dim.11), calls=%async_computation.2 | async-start | bytes 524288 | tf_op jit(solution)/shard_map/all_to_all | solution.py:25
  42.5 9.7 %collective-permute-start.8 = (bf16[512,256]{1,0:T(8,128)(2,1)S(1)}, bf16[512,256]{1,0:T(8,128)(2,1)S(1)}, u32[]{:S(2)}, u32[]{:S(2)}) collective-permute-start(bf16[512,256]{1,0:T(8,128)(2,1)S(1)} %bitcast.8), channel_id=1, source_target_pairs={{0,4},{4,0},{1,5},{5,1},{2,6},{6,2},{3,7},{7,3},{8,12},{12,8},{9,1... | collective-permute-start | bytes 786440 | tf_op jit(solution)/shard_map/ppermute | solution.py:20
  44.0 8.4 %collective-permute-start.5 = (bf16[512,256]{1,0:T(8,128)(2,1)S(1)}, bf16[512,256]{1,0:T(8,128)(2,1)S(1)}, u32[]{:S(2)}, u32[]{:S(2)}) collective-permute-start(bf16[512,256]{1,0:T(8,128)(2,1)S(1)} %bitcast.9), channel_id=1, source_target_pairs={{0,2},{2,0},{1,3},{3,1},{4,6},{6,4},{5,7},{7,5},{8,10},{10,8},{9,1... | collective-permute-start | bytes 786440 | tf_op jit(solution)/shard_map/ppermute | solution.py:20
  50.7 1.7 %copy-start.2 = (f32[256]{0:T(256)S(1)}, f32[256]{0:T(256)}, u32[]{:S(2)}) copy-start(f32[256]{0:T(256)} %param.9) | copy-start | bytes 3076
  50.7 1.7 %collective-permute-start.4 = (bf16[512,256]{1,0:T(8,128)(2,1)S(1)}, bf16[512,256]{1,0:T(8,128)(2,1)S(1)}, u32[]{:S(2)}, u32[]{:S(2)}) collective-permute-start(bf16[512,256]{1,0:T(8,128)(2,1)S(1)} %bitcast.11), channel_id=1, source_target_pairs={{0,2},{2,0},{1,3},{3,1},{4,6},{6,4},{5,7},{7,5},{8,10},{10,8},{9,1... | collective-permute-start | bytes 786440 | tf_op jit(solution)/shard_map/ppermute | solution.py:20
  50.7 8.7 %collective-permute-start.6 = (bf16[512,256]{1,0:T(8,128)(2,1)S(1)}, bf16[512,256]{1,0:T(8,128)(2,1)S(1)}, u32[]{:S(2)}, u32[]{:S(2)}) collective-permute-start(bf16[512,256]{1,0:T(8,128)(2,1)S(1)} %bitcast.12), channel_id=1, source_target_pairs={{0,4},{4,0},{1,5},{5,1},{2,6},{6,2},{3,7},{7,3},{8,12},{12,8},{9,1... | collective-permute-start | bytes 786440 | tf_op jit(solution)/shard_map/ppermute | solution.py:20
  52.2 7.2 %collective-permute-start.9 = (bf16[512,256]{1,0:T(8,128)(2,1)S(1)}, bf16[512,256]{1,0:T(8,128)(2,1)S(1)}, u32[]{:S(2)}, u32[]{:S(2)}) collective-permute-start(bf16[512,256]{1,0:T(8,128)(2,1)S(1)} %collective-permute-done.8.c2_ref), channel_id=1, source_target_pairs={{0,2},{2,0},{1,3},{3,1},{4,6},{6,4},{5,7},{7,5},{8,10},{10,8},{9,1... | collective-permute-start | bytes 786440 | tf_op jit(solution)/shard_map/ppermute | solution.py:20
  59.4 1.5 %collective-permute-start.7 = (bf16[512,256]{1,0:T(8,128)(2,1)S(1)}, bf16[512,256]{1,0:T(8,128)(2,1)S(1)}, u32[]{:S(2)}, u32[]{:S(2)}) collective-permute-start(bf16[512,256]{1,0:T(8,128)(2,1)S(1)} %collective-permute-done.6.h2_ref), channel_id=1, source_target_pairs={{0,2},{2,0},{1,3},{3,1},{4,6},{6,4},{5,7},{7,5},{8,10},{10,8},{9,1... | collective-permute-start | bytes 786440 | tf_op jit(solution)/shard_map/ppermute | solution.py:20
  62.3 4.7 %collective-permute-start.10 = (bf16[128,256]{1,0:T(8,128)(2,1)S(1)}, bf16[128,256]{1,0:T(8,128)(2,1)S(1)}, u32[]{:S(2)}, u32[]{:S(2)}) collective-permute-start(bf16[128,256]{1,0:T(8,128)(2,1)S(1)} %get-tuple-element.34), channel_id=1, source_target_pairs={{0,1},{1,0},{2,3},{3,2},{4,5},{5,4},{6,7},{7,6},{8,9},{9,8},{10,11... | collective-permute-start | bytes 196616 | tf_op jit(solution)/shard_map/ppermute | solution.py:276
  63.9 5.7 %collective-permute-start.11 = (bf16[272,256]{1,0:T(8,128)(2,1)S(1)}, bf16[272,256]{1,0:T(8,128)(2,1)S(1)}, u32[]{:S(2)}, u32[]{:S(2)}) collective-permute-start(bf16[272,256]{1,0:T(8,128)(2,1)S(1)} %get-tuple-element.35), channel_id=1, source_target_pairs={{0,1},{1,0},{2,3},{3,2},{4,5},{5,4},{6,7},{7,6},{8,9},{9,8},{10,11... | collective-permute-start | bytes 417800 | tf_op jit(solution)/shard_map/ppermute | solution.py:276

commit v3 on v0

v3 whole, which is shorter than its diff:
```python
import functools
import math

import jax
import jax.numpy as jnp
from jax import lax
from jax.experimental import pallas as pl
from jax.experimental.pallas import tpu as pltpu
from jax.sharding import Mesh
from jax.sharding import PartitionSpec as P

BF16 = jnp.bfloat16
F32 = jnp.float32
VMEM = pl.BlockSpec(memory_space=pltpu.VMEM)
SMEM = pl.BlockSpec(memory_space=pltpu.SMEM)
MIB = 1024 * 1024
PAD = 16


def partner(x, axis, mask, n):
    return lax.ppermute(x, axis, [(i, i ^ mask) for i in range(n)])


def swap(x, axis):
    return partner(x, axis, 1, 2)


def after(x, *others):
    return lax.optimization_barrier((x,) + others)[0]


def shape(*dims, dtype=BF16):
    return jax.ShapeDtypeStruct(dims, dtype)


def dot(a, b, contract=((1,), (0,))):
    return lax.dot_general(a, b, (contract, ((), ())), preferred_element_type=F32)


def sigmoid(x):
    return 0.5 * jnp.tanh(0.5 * x) + 0.5


def tree_sum(parts):
    while len(parts) > 1:
        parts = [parts[i] + parts[i + 1] for i in range(0, len(parts), 2)]
    return parts[0]


def expand_kernel(n_loop, n_row, tile, rows_ref, counts_ref, tiles_ref, out_ref):
    n_far = n_loop // 4
    my_row, my_far = lax.axis_index("row"), lax.axis_index("far")
    my_near = 2 * lax.axis_index("mid") + lax.axis_index("core")

    def body(j, carry):
        near = jnp.bitwise_xor(lax.rem(j, 4), my_near)
        column = near * n_far + jnp.bitwise_xor(lax.div(j, 4), my_far)
        for s in range(n_row):
            slot = j * n_row + s
            place = jnp.bitwise_xor(rows_ref[slot], my_row)
            value = tiles_ref[slot]
            value = jnp.where(s < counts_ref[j], value, jnp.zeros_like(value))
            out_ref[
                pl.ds(pl.multiple_of(place * tile, tile), tile),
                pl.ds(pl.multiple_of(column * tile, tile), tile),
            ] = value
        return carry

    lax.fori_loop(0, n_loop, body, 0)


def product_rows(a_ref, first, block_refs, rows):
    x = jnp.concatenate([ref[...] for ref in block_refs], axis=0)
    return dot(a_ref[rows, first : first + x.shape[0]], x)


def near_kernel(tile, n_row, a_ref, *refs):
    block_refs, out_ref = refs[:-1], refs[-1]
    step = min(2, n_row) * tile
    for at in range(0, n_row * tile, step):
        rows = slice(at, at + step)
        out_ref[rows, :] = product_rows(a_ref, 0, block_refs, rows)


def rest_kernel(tile, n_row, n_blocks, a_ref, half_ref, *refs):
    block_refs, own_ref, send_refs = refs[:n_blocks], refs[n_blocks], refs[n_blocks + 1 :]
    first = a_ref.shape[1] // 2
    step = min(2, n_row)
    for q in range(0, n_row, step):
        rows = slice(q * tile, (q + step) * tile)
        total = half_ref[rows, :] + product_rows(a_ref, first, block_refs, rows)
        for k in range(step):
            part = total[k * tile : (k + 1) * tile, :]
            if q + k == 0:
                own_ref[...] = part
            else:
                send_refs[q + k - 1][...] = part.astype(BF16)


def sum_kernel(own_ref, *refs):
    part_refs, out_ref = refs[:-1], refs[-1]
    total = own_ref[...]
    for ref in part_refs:
        total = total + ref[...].astype(F32)
    out_ref[...] = total.astype(BF16)


def chunk_grads(w_ref, b_ref, h_refs, c_refs, gh_ref, out_ref=None):
    tile, width = h_refs[0].shape
    weight_sums, bias_sums = [], []
    for k, (h_ref, c_ref) in enumerate(zip(h_refs, c_refs)):
        hidden = h_ref[...]
        preact = dot(hidden, w_ref[...]) + b_ref[...]
        sig = sigmoid(preact)
        if k == 0 and out_ref is not None:
            out_ref[...] = (preact * sig).astype(BF16)
        grad_z = c_ref[...].astype(F32) * sig * (1.0 + preact * (1.0 - sig))
        half = grad_z.astype(BF16)
        gh_ref[k * tile : (k + 1) * tile, :] = dot(half, w_ref[...], ((1,), (1,))).astype(BF16)
        bias_sums.append(jnp.sum(grad_z.reshape(tile // 8, 8, width), axis=0))
        weight_sums.append(dot(hidden, half, ((0,), (0,))))
    return tree_sum(weight_sums), tree_sum(bias_sums)


def first_chunk_kernel(n, w_ref, b_ref, *refs):
    h_refs, c_refs = refs[:n], refs[n : 2 * n]
    gh_ref, out_ref, gw_ref, gb_ref = refs[2 * n :]
    gw_ref[...], gb_ref[...] = chunk_grads(w_ref, b_ref, h_refs, c_refs, gh_ref, out_ref)


def write_message(ref, grad_w, bias):
    rows, width = grad_w.shape
    ref[:rows, :] = grad_w.astype(BF16)
    high = bias.astype(BF16).astype(F32)
    row = lax.broadcasted_iota(jnp.int32, (PAD, width), 0)
    low = jnp.broadcast_to(bias - high, (PAD, width))
    high = jnp.broadcast_to(high, (PAD, width))
    ref[rows:, :] = jnp.where(row == 0, high, jnp.where(row == 1, low, 0.0)).astype(BF16)


def read_message(ref):
    rows = ref.shape[0] - PAD
    tail = ref[rows:, :].astype(F32)
    return ref[:rows, :].astype(F32), tail[0:1, :] + tail[1:2, :]


def last_chunk_kernel(n, w_ref, b_ref, *refs):
    h_refs, c_refs = refs[:n], refs[n : 2 * n]
    gw_ref, gb_ref, gh_ref, keep_ref, send_ref, sum_ref = refs[2 * n :]
    half = keep_ref.shape[0] - PAD
    grad_w, grad_b = chunk_grads(w_ref, b_ref, h_refs, c_refs, gh_ref)
    sum_ref[...] = gw_ref[...] + grad_w
    bias = jnp.sum(gb_ref[...] + grad_b, axis=0, keepdims=True)
    core = lax.axis_index("core")
    kept = sum_ref[pl.ds(pl.multiple_of(core * half, half), half), :]
    sent = sum_ref[pl.ds(pl.multiple_of((1 - core) * half, half), half), :]
    write_message(keep_ref, kept, bias)
    write_message(send_ref, sent, bias)


def message_kernel(own_ref, other_ref, out_ref):
    own_w, own_b = read_message(own_ref)
    other_w, other_b = read_message(other_ref)
    write_message(out_ref, own_w + other_w, own_b + other_b)


def scale_kernel(factor, own_ref, other_ref, half_ref, bias_ref):
    own_w, own_b = read_message(own_ref)
    other_w, other_b = read_message(other_ref)
    half_ref[...] = (own_w + other_w) * factor
    bias_ref[...] = (own_b + other_b) * factor


def halves_kernel(own_ref, other_ref, out_ref):
    half = own_ref.shape[0]
    core = lax.axis_index("core")
    out_ref[pl.ds(pl.multiple_of(core * half, half), half), :] = own_ref[...]
    out_ref[pl.ds(pl.multiple_of((1 - core) * half, half), half), :] = other_ref[...]


def call(kernel, name, outs, operands, scratch=(), specs=None, flops=0):
    size = sum(o.size * o.dtype.itemsize for o in list(operands) + list(outs))
    held = size + sum(math.prod(s.shape) * jnp.dtype(s.dtype).itemsize for s in scratch)
    return pl.pallas_call(
        kernel,
        name=name,
        out_shape=outs,
        in_specs=specs or [VMEM] * len(operands),
        out_specs=[VMEM] * len(outs),
        scratch_shapes=scratch,
        cost_estimate=pl.CostEstimate(flops=flops, bytes_accessed=size, transcendentals=0),
        compiler_params=pltpu.CompilerParams(vmem_limit_bytes=2 * held + 4 * MIB),
    )(*operands)


def shards(n_loop, n_row, features, weight, bias_vector, cotangent, tile_values, tile_rows, counts):
    tile, width = features.shape
    n_far = n_loop // 4
    nodes = tile * n_loop * n_row
    rows = n_row * tile
    flops = rows * n_loop * tile * width

    def far_blocks(block):
        return [block] + [partner(block, "far", m, n_far) for m in range(1, n_far)]

    def product(near, rest, name):
        (half,) = call(
            functools.partial(near_kernel, tile, n_row),
            name + "_near",
            [shape(rows, width, dtype=F32)],
            [adjacency] + near,
            flops=flops,
        )
        own, *parts = call(
            functools.partial(rest_kernel, tile, n_row, len(rest)),
            name + "_rest",
            [shape(tile, width, dtype=F32)] + [shape(tile, width)] * (n_row - 1),
            [adjacency, half] + rest,
            flops=flops,
        )
        others = [partner(part, "row", q + 1, n_row) for q, part in enumerate(parts)]
        (total,) = call(sum_kernel, name + "_sum", [shape(tile, width)], [own] + others)
        return total

    (adjacency,) = call(
        functools.partial(expand_kernel, n_loop, n_row, tile),
        "expand",
        [shape(rows, n_loop * tile)],
        (tile_rows, counts, tile_values),
        specs=[SMEM, SMEM, VMEM],
    )

    f00 = far_blocks(features)
    f10 = [swap(block, "mid") for block in f00]
    f01 = [swap(block, "core") for block in f00]
    f11 = [swap(block, "core") for block in f10]
    cots = far_blocks(after(cotangent, *f00[1:]))
    hidden = product(f00 + f01, f10 + f11, "forward")

    hiddens = far_blocks(hidden)
    bias_row = bias_vector.reshape(1, width)
    n = n_far // 2
    chunk_flops = n * tile * 6 * width * width
    gh_a, output, grad_w, grad_b = call(
        functools.partial(first_chunk_kernel, n),
        "first_chunk",
        [
            shape(n * tile, width),
            shape(tile, width),
            shape(width, width, dtype=F32),
            shape(8, width, dtype=F32),
        ],
        [weight, bias_row] + hiddens[:n] + cots[:n],
        flops=chunk_flops,
    )
    half_rows = width // 2 + PAD
    gh_b, keep, send = call(
        functools.partial(last_chunk_kernel, n),
        "last_chunk",
        [shape(n * tile, width), shape(half_rows, width), shape(half_rows, width)],
        [weight, bias_row] + hiddens[n:] + cots[n:] + [grad_w, grad_b],
        scratch=[pltpu.VMEM((width, width), F32)],
        flops=chunk_flops,
    )
    g00 = [gh_a, gh_b]
    g10 = [swap(chunk, "mid") for chunk in g00]
    g01 = [swap(chunk, "core") for chunk in g00]
    g11 = [swap(chunk, "core") for chunk in g10]
    grad_features = product(g00 + g01, g10 + g11, "backward")

    (message,) = call(
        message_kernel, "sum_core", [shape(half_rows, width)], [keep, swap(send, "core")]
    )
    bit = 1
    while bit < n_row:
        (message,) = call(
            message_kernel,
            "sum_row",
            [shape(half_rows, width)],
            [message, partner(message, "row", bit, n_row)],
        )
        bit *= 2
    half, bias_grad = call(
        functools.partial(scale_kernel, 1.0 / nodes**0.5),
        "sum_mid",
        [shape(width // 2, width, dtype=F32), shape(1, width, dtype=F32)],
        [message, swap(message, "mid")],
    )
    (weight_grad,) = call(
        halves_kernel, "halves", [shape(width, width, dtype=F32)], [half, swap(half, "core")]
    )
    return output, grad_features, weight_grad, bias_grad.reshape(width)


def solution(mesh):
    n_loop, n_row = mesh.shape["loop"], mesh.shape["row"]
    every = ("far", "mid", "core", "row")
    fine = Mesh(mesh.devices.reshape(n_loop // 4, 2, 2, n_row), every)
    in_specs = (
        P(every, None),
        P(),
        P(),
        P(every, None),
        P(every, None, None),
        P(every),
        P(every),
    )
    out_specs = (P(every, None), P(every, None), P(), P())
    return jax.shard_map(
        functools.partial(shards, n_loop, n_row),
        mesh=fine,
        in_specs=in_specs,
        out_specs=out_specs,
        check_vma=False,
    )
```

time: 264 us -> 63.7 us (0.24)
  waiting for transfers between devices: 193 us -> 26.5 us
  blocking collectives: 44.4 us -> 0 us
  starting transfers between devices: 0.16 us -> 28 us
  between operations: 13.8 us -> 0.82 us
  matrix products: 7.93 us -> 0 us
  Pallas kernels: 0 us -> 5.72 us
  other arithmetic: 2.97 us -> 0 us
    psum x1 -> x0, waiting for transfers between devices: 82.7 us -> none  [shards(): lax.psum((weight_term, bias_term), ('loop', 'row'))]
    reduce_scatter x2 -> x0, waiting for transfers between devices: 69.3 us -> none  [the longest x1 59.3 us: shards(): lax.psum_scatter(term.reshape(lax.axis_size('loop') * tile_size, feature_...]
    all_gather x1 -> x0, waiting for transfers between devices: 39.9 us -> none  [shards(): lax.all_gather(features, 'loop', axis=0, tiled=True)]
    psum x1 -> x0, blocking collectives: 39.5 us -> none  [shards(): lax.psum((weight_term, bias_term), ('loop', 'row'))]
    ppermute x0 -> x33, starting transfers between devices: none -> 28 us  [partner(): return lax.ppermute(x, axis, [(i, i ^ mask) for i in range(n)])]
    ppermute x0 -> x33, waiting for transfers between devices: none -> 26.5 us  [partner(): return lax.ppermute(x, axis, [(i, i ^ mask) for i in range(n)])]
    dot_general x6 -> x0, matrix products: 7.93 us -> none  [the longest x1 2.36 us: aggregate_into(): jnp.einsum('gdac,gch->dah', expanded, sources, preferred_element_type=jnp...]
    pallas_call x0 -> x13, Pallas kernels: none -> 5.72 us  [call(): pl.pallas_call(kernel, name=name, out_shape=outs, in_specs=specs or [VMEM...]
  transfers between devices with their start and end apart: 4 -> 33, of which waited for: 4 -> 12; matrix products, arithmetic and copies ran while one was open for 3% -> 0% of each run, Pallas kernels for 0% -> 7%
where the time goes in v3:
time: 63.7 us; the launch traced here: 63.6 us
  starting transfers between devices  28 us (44%)
  waiting for transfers between devices  26.5 us (42%)
  Pallas kernels  5.72 us (9%)
  local copies, waits for them, and re-layouts  2.55 us (4%)
  between operations  0.82 us (1%)
    ppermute x33, starting transfers between devices, partner(): return lax.ppermute(x, axis, [(i, i ^ mask) for i in range(n)])  28 us
    ppermute x33, waiting for transfers between devices, partner(): return lax.ppermute(x, axis, [(i, i ^ mask) for i in range(n)])  26.5 us
    pallas_call x13, Pallas kernels, call(): pl.pallas_call(kernel, name=name, out_shape=outs, in_specs=specs or [VMEM...  5.72 us
    unnamed x14, local copies, waits for them, and re-layouts  2.55 us
  transfers between devices with their start and end apart: 33, of which 12 were waited for; matrix products, arithmetic and copies ran while one was open for 0% of the time, Pallas kernels for 7%

profile of v3, /device:TPU:0, one launch (start us, length us, event | category | flops | bytes accessed | tf_op | source)
XLA Modules:
  0.0 63.6 jit_solution(3495205060094475274)
XLA Ops:
  0.6 3.1 %collective-permute-start = (bf16[128,256]{1,0:T(8,128)(2,1)}, bf16[128,256]{1,0:T(8,128)(2,1)S(1)}, u32[]{:S(2)}, u32[]{:S(2)}) collective-permute-start(bf16[128,256]{1,0:T(8,128)(2,1)} %refs_0_.1), channel_id=1, source_target_pairs={{0,8},{8,0},{16,24},{24,16},{1,9},{9,1},{17,25},{25,17},{2,10},{10... | collective-permute-start | bytes 196616 | tf_op jit(solution)/shard_map/ppermute | solution.py:21
  3.7 2.6 %collective-permute-start.1 = (bf16[128,256]{1,0:T(8,128)(2,1)}, bf16[128,256]{1,0:T(8,128)(2,1)S(1)}, u32[]{:S(2)}, u32[]{:S(2)}) collective-permute-start(bf16[128,256]{1,0:T(8,128)(2,1)} %refs_0_.1), channel_id=1, source_target_pairs={{0,16},{8,24},{16,0},{24,8},{1,17},{9,25},{17,1},{25,9},{2,18},{10... | collective-permute-start | bytes 196616 | tf_op jit(solution)/shard_map/ppermute | solution.py:21
  6.3 1.7 %collective-permute-start.7 = (bf16[128,256]{1,0:T(8,128)(2,1)}, bf16[128,256]{1,0:T(8,128)(2,1)S(1)}, u32[]{:S(2)}, u32[]{:S(2)}) collective-permute-start(bf16[128,256]{1,0:T(8,128)(2,1)} %refs_0_.1), channel_id=1, source_target_pairs={{0,4},{4,0},{1,5},{5,1},{2,6},{6,2},{3,7},{7,3},{8,12},{12,8},{9,1... | collective-permute-start | bytes 196616 | tf_op jit(solution)/shard_map/ppermute | solution.py:21
  8.3 3.0 %collective-permute-done.1.refs_2_ = bf16[128,256]{1,0:T(8,128)(2,1)S(1)} collective-permute-done((bf16[128,256]{1,0:T(8,128)(2,1)}, bf16[128,256]{1,0:T(8,128)(2,1)S(1)}, u32[]{:S(2)}, u32[]{:S(2)}) %collective-permute-start.1) | collective-permute-done | bytes 65568 | tf_op jit(solution)/shard_map/ppermute | solution.py:21
  11.2 1.4 %collective-permute-done.2.refs_3_ = bf16[128,256]{1,0:T(8,128)(2,1)S(1)} collective-permute-done((bf16[128,256]{1,0:T(8,128)(2,1)}, bf16[128,256]{1,0:T(8,128)(2,1)S(1)}, u32[]{:S(2)}, u32[]{:S(2)}) %collective-permute-start.2) | collective-permute-done | bytes 65568 | tf_op jit(solution)/shard_map/ppermute | solution.py:21
  12.6 1.5 %collective-permute-start.8 = (bf16[128,256]{1,0:T(8,128)(2,1)S(1)}, bf16[128,256]{1,0:T(8,128)(2,1)S(1)}, u32[]{:S(2)}, u32[]{:S(2)}) collective-permute-start(bf16[128,256]{1,0:T(8,128)(2,1)S(1)} %collective-permute-done.refs_1_), channel_id=1, source_target_pairs={{0,4},{4,0},{1,5},{5,1},{2,6},{6,2},{3,7},{7,3},{8,12},{12,8},{9,1... | collective-permute-start | bytes 196616 | tf_op jit(solution)/shard_map/ppermute | solution.py:21
  14.6 1.5 %collective-permute-start.10 = (bf16[128,256]{1,0:T(8,128)(2,1)S(1)}, bf16[128,256]{1,0:T(8,128)(2,1)S(1)}, u32[]{:S(2)}, u32[]{:S(2)}) collective-permute-start(bf16[128,256]{1,0:T(8,128)(2,1)S(1)} %collective-permute-done.2.refs_3_), channel_id=1, source_target_pairs={{0,4},{4,0},{1,5},{5,1},{2,6},{6,2},{3,7},{7,3},{8,12},{12,8},{9,1... | collective-permute-start | bytes 196616 | tf_op jit(solution)/shard_map/ppermute | solution.py:21
  16.7 0.9 %collective-permute-done.8.refs_1_ = bf16[128,256]{1,0:T(8,128)(2,1)S(1)} collective-permute-done((bf16[128,256]{1,0:T(8,128)(2,1)S(1)}, bf16[128,256]{1,0:T(8,128)(2,1)S(1)}, u32[]{:S(2)}, u32[]{:S(2)}) %collective-permute-start.8) | collective-permute-done | bytes 65568 | tf_op jit(solution)/shard_map/ppermute | solution.py:21
  17.5 0.8 %collective-permute-done.9.refs_2_ = bf16[128,256]{1,0:T(8,128)(2,1)S(1)} collective-permute-done((bf16[128,256]{1,0:T(8,128)(2,1)S(1)}, bf16[128,256]{1,0:T(8,128)(2,1)S(1)}, u32[]{:S(2)}, u32[]{:S(2)}) %collective-permute-start.9) | collective-permute-done | bytes 65568 | tf_op jit(solution)/shard_map/ppermute | solution.py:21
  18.4 0.7 %collective-permute-done.10.refs_3_ = bf16[128,256]{1,0:T(8,128)(2,1)S(1)} collective-permute-done((bf16[128,256]{1,0:T(8,128)(2,1)S(1)}, bf16[128,256]{1,0:T(8,128)(2,1)S(1)}, u32[]{:S(2)}, u32[]{:S(2)}) %collective-permute-start.10) | collective-permute-done | bytes 65568 | tf_op jit(solution)/shard_map/ppermute | solution.py:21
  19.1 1.2 %copy-done = bf16[32,128,128]{2,1,0:T(8,128)(2,1)S(1)} copy-done((bf16[32,128,128]{2,1,0:T(8,128)(2,1)S(1)}, bf16[32,128,128]{2,1,0:T(8,128)(2,1)}, u32[]{:S(2)}) %copy-start) | copy-done | bytes 1048600
  20.3 0.7 %copy-done.5 = s32[32]{0:T(128)S(1)} copy-done((s32[32]{0:T(128)S(1)}, s32[32]{0:T(128)}, u32[]{:S(2)}) %copy-start.5) | copy-done | bytes 152
  21.6 0.9 %expand.1.a_ref = bf16[256,2048]{1,0:T(8,128)(2,1)S(1)} custom-call(s32[32]{0:T(128)S(1)} %copy-done.5, s32[16]{0:T(128)S(1)} %copy-done.6, bf16[32,128,128]{2,1,0:T(8,128)(2,1)S(1)} %copy-done), custom_call_target="tpu_custom_call" | custom-call | bytes 2097344 | tf_op jit(solution)/shard_map/expand/pallas_call | solution.py:184
  23.2 1.6 %collective-permute-start.15 = (bf16[128,256]{1,0:T(8,128)(2,1)S(1)}, bf16[128,256]{1,0:T(8,128)(2,1)S(1)}, u32[]{:S(2)}, u32[]{:S(2)}) collective-permute-start(bf16[128,256]{1,0:T(8,128)(2,1)S(1)} %get-tuple-element.19), channel_id=1, source_target_pairs={{0,1},{1,0},{2,3},{3,2},{4,5},{5,4},{6,7},{7,6},{8,9},{9,8},{10,11... | collective-permute-start | bytes 196616 | tf_op jit(solution)/shard_map/ppermute | solution.py:21
  25.3 2.6 %collective-permute-done.15.refs_0_ = bf16[128,256]{1,0:T(8,128)(2,1)S(1)} collective-permute-done((bf16[128,256]{1,0:T(8,128)(2,1)S(1)}, bf16[128,256]{1,0:T(8,128)(2,1)S(1)}, u32[]{:S(2)}, u32[]{:S(2)}) %collective-permute-start.15) | collective-permute-done | bytes 65568 | tf_op jit(solution)/shard_map/ppermute | solution.py:21
  28.3 2.8 %collective-permute-start.20 = (bf16[128,256]{1,0:T(8,128)(2,1)S(1)}, bf16[128,256]{1,0:T(8,128)(2,1)S(1)}, u32[]{:S(2)}, u32[]{:S(2)}) collective-permute-start(bf16[128,256]{1,0:T(8,128)(2,1)S(1)} %copy-done.3), channel_id=1, source_target_pairs={{0,16},{8,24},{16,0},{24,8},{1,17},{9,25},{17,1},{25,9},{2,18},{10... | collective-permute-start | bytes 196616 | tf_op jit(solution)/shard_map/ppermute | solution.py:21
  31.1 1.2 %collective-permute-start.21 = (bf16[128,256]{1,0:T(8,128)(2,1)S(1)}, bf16[128,256]{1,0:T(8,128)(2,1)S(1)}, u32[]{:S(2)}, u32[]{:S(2)}) collective-permute-start(bf16[128,256]{1,0:T(8,128)(2,1)S(1)} %copy-done.3), channel_id=1, source_target_pairs={{0,24},{8,16},{16,8},{24,0},{1,25},{9,17},{17,9},{25,1},{2,26},{10... | collective-permute-start | bytes 196616 | tf_op jit(solution)/shard_map/ppermute | solution.py:21
  32.3 0.7 %collective-permute-start.18 = (bf16[128,256]{1,0:T(8,128)(2,1)S(1)}, bf16[128,256]{1,0:T(8,128)(2,1)S(1)}, u32[]{:S(2)}, u32[]{:S(2)}) collective-permute-start(bf16[128,256]{1,0:T(8,128)(2,1)S(1)} %forward_sum.1.refs_0_), channel_id=1, source_target_pairs={{0,16},{8,24},{16,0},{24,8},{1,17},{9,25},{17,1},{25,9},{2,18},{10... | collective-permute-start | bytes 196616 | tf_op jit(solution)/shard_map/ppermute | solution.py:21
  33.0 1.9 %collective-permute-start.19 = (bf16[128,256]{1,0:T(8,128)(2,1)S(1)}, bf16[128,256]{1,0:T(8,128)(2,1)S(1)}, u32[]{:S(2)}, u32[]{:S(2)}) collective-permute-start(bf16[128,256]{1,0:T(8,128)(2,1)S(1)} %forward_sum.1.refs_0_), channel_id=1, source_target_pairs={{0,24},{8,16},{16,8},{24,0},{1,25},{9,17},{17,9},{25,1},{2,26},{10... | collective-permute-start | bytes 196616 | tf_op jit(solution)/shard_map/ppermute | solution.py:21
  34.9 1.0 %first_chunk.1 = (bf16[256,256]{1,0:T(8,128)(2,1)S(1)}, bf16[128,256]{1,0:T(8,128)(2,1)}, f32[256,256]{1,0:T(8,128)S(1)}, f32[8,256]{1,0:T(8,128)S(1)}) custom-call(bf16[256,256]{1,0:T(8,128)(2,1)S(1)} %copy-done.1, f32[1,256]{1,0:T(1,128)S(1)} %bitcast.2, bf16[128,256]{1,0:T(8,128)(2,1)S(1)} %forward_sum.1.refs_0_, ...), custom_call_target="tpu_custom_call" | custom-call | flops 100663296 | bytes 861184 | tf_op jit(solution)/shard_map/first_chunk/pallas_call | solution.py:184
  36.0 3.5 %collective-permute-done.20.refs_2_ = bf16[128,256]{1,0:T(8,128)(2,1)S(1)} collective-permute-done((bf16[128,256]{1,0:T(8,128)(2,1)S(1)}, bf16[128,256]{1,0:T(8,128)(2,1)S(1)}, u32[]{:S(2)}, u32[]{:S(2)}) %collective-permute-start.20) | collective-permute-done | bytes 65568 | tf_op jit(solution)/shard_map/ppermute | solution.py:21
  39.5 2.8 %collective-permute-done.18.refs_0_ = bf16[128,256]{1,0:T(8,128)(2,1)S(1)} collective-permute-done((bf16[128,256]{1,0:T(8,128)(2,1)S(1)}, bf16[128,256]{1,0:T(8,128)(2,1)S(1)}, u32[]{:S(2)}, u32[]{:S(2)}) %collective-permute-start.18) | collective-permute-done | bytes 65568 | tf_op jit(solution)/shard_map/ppermute | solution.py:21
  42.9 1.4 %collective-permute-start.24 = (bf16[256,256]{1,0:T(8,128)(2,1)S(1)}, bf16[256,256]{1,0:T(8,128)(2,1)S(1)}, u32[]{:S(2)}, u32[]{:S(2)}) collective-permute-start(bf16[256,256]{1,0:T(8,128)(2,1)S(1)} %get-tuple-element.22.refs_0_), channel_id=1, source_target_pairs={{0,4},{4,0},{1,5},{5,1},{2,6},{6,2},{3,7},{7,3},{8,12},{12,8},{9,1... | collective-permute-start | bytes 393224 | tf_op jit(solution)/shard_map/ppermute | solution.py:21
  44.3 0.7 %collective-permute-start.25 = (bf16[256,256]{1,0:T(8,128)(2,1)S(1)}, bf16[256,256]{1,0:T(8,128)(2,1)S(1)}, u32[]{:S(2)}, u32[]{:S(2)}) collective-permute-start(bf16[256,256]{1,0:T(8,128)(2,1)S(1)} %get-tuple-element.25.refs_1_), channel_id=1, source_target_pairs={{0,4},{4,0},{1,5},{5,1},{2,6},{6,2},{3,7},{7,3},{8,12},{12,8},{9,1... | collective-permute-start | bytes 393224 | tf_op jit(solution)/shard_map/ppermute | solution.py:21
  45.0 1.6 %collective-permute-start.30 = (bf16[144,256]{1,0:T(8,128)(2,1)S(1)}, bf16[144,256]{1,0:T(8,128)(2,1)S(1)}, u32[]{:S(2)}, u32[]{:S(2)}) collective-permute-start(bf16[144,256]{1,0:T(8,128)(2,1)S(1)} %sum_core.1.own_ref), channel_id=1, source_target_pairs={{0,1},{1,0},{2,3},{3,2},{4,5},{5,4},{6,7},{7,6},{8,9},{9,8},{10,11... | collective-permute-start | bytes 221192 | tf_op jit(solution)/shard_map/ppermute | solution.py:21
  47.1 2.1 %collective-permute-done.24.refs_0_ = bf16[256,256]{1,0:T(8,128)(2,1)S(1)} collective-permute-done((bf16[256,256]{1,0:T(8,128)(2,1)S(1)}, bf16[256,256]{1,0:T(8,128)(2,1)S(1)}, u32[]{:S(2)}, u32[]{:S(2)}) %collective-permute-start.24) | collective-permute-done | bytes 131104 | tf_op jit(solution)/shard_map/ppermute | solution.py:21
  49.2 2.4 %collective-permute-done.25.refs_1_ = bf16[256,256]{1,0:T(8,128)(2,1)S(1)} collective-permute-done((bf16[256,256]{1,0:T(8,128)(2,1)S(1)}, bf16[256,256]{1,0:T(8,128)(2,1)S(1)}, u32[]{:S(2)}, u32[]{:S(2)}) %collective-permute-start.25) | collective-permute-done | bytes 131104 | tf_op jit(solution)/shard_map/ppermute | solution.py:21
  51.6 1.4 %collective-permute-start.31 = (bf16[144,256]{1,0:T(8,128)(2,1)S(1)}, bf16[144,256]{1,0:T(8,128)(2,1)S(1)}, u32[]{:S(2)}, u32[]{:S(2)}) collective-permute-start(bf16[144,256]{1,0:T(8,128)(2,1)S(1)} %sum_row.1.own_ref), channel_id=1, source_target_pairs={{0,4},{4,0},{1,5},{5,1},{2,6},{6,2},{3,7},{7,3},{8,12},{12,8},{9,1... | collective-permute-start | bytes 221192 | tf_op jit(solution)/shard_map/ppermute | solution.py:21
  53.1 3.3 %collective-permute-done.31.other_ref = bf16[144,256]{1,0:T(8,128)(2,1)S(1)} collective-permute-done((bf16[144,256]{1,0:T(8,128)(2,1)S(1)}, bf16[144,256]{1,0:T(8,128)(2,1)S(1)}, u32[]{:S(2)}, u32[]{:S(2)}) %collective-permute-start.31) | collective-permute-done | bytes 73760 | tf_op jit(solution)/shard_map/ppermute | solution.py:21
  57.6 1.6 %collective-permute-start.28 = (bf16[128,256]{1,0:T(8,128)(2,1)S(1)}, bf16[128,256]{1,0:T(8,128)(2,1)S(1)}, u32[]{:S(2)}, u32[]{:S(2)}) collective-permute-start(bf16[128,256]{1,0:T(8,128)(2,1)S(1)} %get-tuple-element.27), channel_id=1, source_target_pairs={{0,1},{1,0},{2,3},{3,2},{4,5},{5,4},{6,7},{7,6},{8,9},{9,8},{10,11... | collective-permute-start | bytes 196616 | tf_op jit(solution)/shard_map/ppermute | solution.py:21
  59.2 3.0 %collective-permute-done.28.refs_0_ = bf16[128,256]{1,0:T(8,128)(2,1)S(1)} collective-permute-done((bf16[128,256]{1,0:T(8,128)(2,1)S(1)}, bf16[128,256]{1,0:T(8,128)(2,1)S(1)}, u32[]{:S(2)}, u32[]{:S(2)}) %collective-permute-start.28) | collective-permute-done | bytes 65568 | tf_op jit(solution)/shard_map/ppermute | solution.py:21
  62.8 0.7 %halves.1 = f32[256,256]{1,0:T(8,128)} custom-call(f32[128,256]{1,0:T(8,128)S(1)} %get-tuple-element.30.own_ref, f32[128,256]{1,0:T(8,128)S(1)} %collective-permute-done.32.other_ref), custom_call_target="tpu_custom_call" | custom-call | bytes 524288 | tf_op jit(solution)/shard_map/halves/pallas_call | solution.py:184
  (61 shorter events, 6.5 us)
Async XLA Ops:
  0.6 7.4 %collective-permute-start = (bf16[128,256]{1,0:T(8,128)(2,1)}, bf16[128,256]{1,0:T(8,128)(2,1)S(1)}, u32[]{:S(2)}, u32[]{:S(2)}) collective-permute-start(bf16[128,256]{1,0:T(8,128)(2,1)} %refs_0_.1), channel_id=1, source_target_pairs={{0,8},{8,0},{16,24},{24,16},{1,9},{9,1},{17,25},{25,17},{2,10},{10... | collective-permute-start | bytes 196616 | tf_op jit(solution)/shard_map/ppermute | solution.py:21
  3.7 7.5 %collective-permute-start.1 = (bf16[128,256]{1,0:T(8,128)(2,1)}, bf16[128,256]{1,0:T(8,128)(2,1)S(1)}, u32[]{:S(2)}, u32[]{:S(2)}) collective-permute-start(bf16[128,256]{1,0:T(8,128)(2,1)} %refs_0_.1), channel_id=1, source_target_pairs={{0,16},{8,24},{16,0},{24,8},{1,17},{9,25},{17,1},{25,9},{2,18},{10... | collective-permute-start | bytes 196616 | tf_op jit(solution)/shard_map/ppermute | solution.py:21
  6.3 6.3 %collective-permute-start.2 = (bf16[128,256]{1,0:T(8,128)(2,1)}, bf16[128,256]{1,0:T(8,128)(2,1)S(1)}, u32[]{:S(2)}, u32[]{:S(2)}) collective-permute-start(bf16[128,256]{1,0:T(8,128)(2,1)} %refs_0_.1), channel_id=1, source_target_pairs={{0,24},{8,16},{16,8},{24,0},{1,25},{9,17},{17,9},{25,1},{2,26},{10... | collective-permute-start | bytes 196616 | tf_op jit(solution)/shard_map/ppermute | solution.py:21
  6.3 7.8 %collective-permute-start.3 = (bf16[128,256]{1,0:T(8,128)(2,1)}, bf16[128,256]{1,0:T(8,128)(2,1)S(1)}, u32[]{:S(2)}, u32[]{:S(2)}) collective-permute-start(bf16[128,256]{1,0:T(8,128)(2,1)} %refs_0_.1), channel_id=1, source_target_pairs={{0,2},{2,0},{1,3},{3,1},{4,6},{6,4},{5,7},{7,5},{8,10},{10,8},{9,1... | collective-permute-start | bytes 196616 | tf_op jit(solution)/shard_map/ppermute | solution.py:21
  6.3 8.3 %collective-permute-start.7 = (bf16[128,256]{1,0:T(8,128)(2,1)}, bf16[128,256]{1,0:T(8,128)(2,1)S(1)}, u32[]{:S(2)}, u32[]{:S(2)}) collective-permute-start(bf16[128,256]{1,0:T(8,128)(2,1)} %refs_0_.1), channel_id=1, source_target_pairs={{0,4},{4,0},{1,5},{5,1},{2,6},{6,2},{3,7},{7,3},{8,12},{12,8},{9,1... | collective-permute-start | bytes 196616 | tf_op jit(solution)/shard_map/ppermute | solution.py:21
  8.0 8.1 %collective-permute-start.4 = (bf16[128,256]{1,0:T(8,128)(2,1)S(1)}, bf16[128,256]{1,0:T(8,128)(2,1)S(1)}, u32[]{:S(2)}, u32[]{:S(2)}) collective-permute-start(bf16[128,256]{1,0:T(8,128)(2,1)S(1)} %collective-permute-done.refs_1_), channel_id=1, source_target_pairs={{0,2},{2,0},{1,3},{3,1},{4,6},{6,4},{5,7},{7,5},{8,10},{10,8},{9,1... | collective-permute-start | bytes 196616 | tf_op jit(solution)/shard_map/ppermute | solution.py:21
  11.2 4.9 %collective-permute-start.5 = (bf16[128,256]{1,0:T(8,128)(2,1)S(1)}, bf16[128,256]{1,0:T(8,128)(2,1)S(1)}, u32[]{:S(2)}, u32[]{:S(2)}) collective-permute-start(bf16[128,256]{1,0:T(8,128)(2,1)S(1)} %collective-permute-done.1.refs_2_), channel_id=1, source_target_pairs={{0,2},{2,0},{1,3},{3,1},{4,6},{6,4},{5,7},{7,5},{8,10},{10,8},{9,1... | collective-permute-start | bytes 196616 | tf_op jit(solution)/shard_map/ppermute | solution.py:21
  12.6 4.9 %collective-permute-start.8 = (bf16[128,256]{1,0:T(8,128)(2,1)S(1)}, bf16[128,256]{1,0:T(8,128)(2,1)S(1)}, u32[]{:S(2)}, u32[]{:S(2)}) collective-permute-start(bf16[128,256]{1,0:T(8,128)(2,1)S(1)} %collective-permute-done.refs_1_), channel_id=1, source_target_pairs={{0,4},{4,0},{1,5},{5,1},{2,6},{6,2},{3,7},{7,3},{8,12},{12,8},{9,1... | collective-permute-start | bytes 196616 | tf_op jit(solution)/shard_map/ppermute | solution.py:21
  14.1 4.3 %collective-permute-start.9 = (bf16[128,256]{1,0:T(8,128)(2,1)S(1)}, bf16[128,256]{1,0:T(8,128)(2,1)S(1)}, u32[]{:S(2)}, u32[]{:S(2)}) collective-permute-start(bf16[128,256]{1,0:T(8,128)(2,1)S(1)} %collective-permute-done.1.refs_2_), channel_id=1, source_target_pairs={{0,4},{4,0},{1,5},{5,1},{2,6},{6,2},{3,7},{7,3},{8,12},{12,8},{9,1... | collective-permute-start | bytes 196616 | tf_op jit(solution)/shard_map/ppermute | solution.py:21
  14.6 4.4 %collective-permute-start.10 = (bf16[128,256]{1,0:T(8,128)(2,1)S(1)}, bf16[128,256]{1,0:T(8,128)(2,1)S(1)}, u32[]{:S(2)}, u32[]{:S(2)}) collective-permute-start(bf16[128,256]{1,0:T(8,128)(2,1)S(1)} %collective-permute-done.2.refs_3_), channel_id=1, source_target_pairs={{0,4},{4,0},{1,5},{5,1},{2,6},{6,2},{3,7},{7,3},{8,12},{12,8},{9,1... | collective-permute-start | bytes 196616 | tf_op jit(solution)/shard_map/ppermute | solution.py:21
  16.1 6.4 %collective-permute-start.6 = (bf16[128,256]{1,0:T(8,128)(2,1)S(1)}, bf16[128,256]{1,0:T(8,128)(2,1)S(1)}, u32[]{:S(2)}, u32[]{:S(2)}) collective-permute-start(bf16[128,256]{1,0:T(8,128)(2,1)S(1)} %collective-permute-done.2.refs_3_), channel_id=1, source_target_pairs={{0,2},{2,0},{1,3},{3,1},{4,6},{6,4},{5,7},{7,5},{8,10},{10,8},{9,1... | collective-permute-start | bytes 196616 | tf_op jit(solution)/shard_map/ppermute | solution.py:21
  16.2 6.7 %collective-permute-start.11 = (bf16[128,256]{1,0:T(8,128)(2,1)S(1)}, bf16[128,256]{1,0:T(8,128)(2,1)S(1)}, u32[]{:S(2)}, u32[]{:S(2)}) collective-permute-start(bf16[128,256]{1,0:T(8,128)(2,1)S(1)} %collective-permute-done.7.refs_0_), channel_id=1, source_target_pairs={{0,2},{2,0},{1,3},{3,1},{4,6},{6,4},{5,7},{7,5},{8,10},{10,8},{9,1... | collective-permute-start | bytes 196616 | tf_op jit(solution)/shard_map/ppermute | solution.py:21
  17.5 5.4 %collective-permute-start.12 = (bf16[128,256]{1,0:T(8,128)(2,1)S(1)}, bf16[128,256]{1,0:T(8,128)(2,1)S(1)}, u32[]{:S(2)}, u32[]{:S(2)}) collective-permute-start(bf16[128,256]{1,0:T(8,128)(2,1)S(1)} %collective-permute-done.8.refs_1_), channel_id=1, source_target_pairs={{0,2},{2,0},{1,3},{3,1},{4,6},{6,4},{5,7},{7,5},{8,10},{10,8},{9,1... | collective-permute-start | bytes 196616 | tf_op jit(solution)/shard_map/ppermute | solution.py:21
  18.4 4.5 %collective-permute-start.13 = (bf16[128,256]{1,0:T(8,128)(2,1)S(1)}, bf16[128,256]{1,0:T(8,128)(2,1)S(1)}, u32[]{:S(2)}, u32[]{:S(2)}) collective-permute-start(bf16[128,256]{1,0:T(8,128)(2,1)S(1)} %collective-permute-done.9.refs_2_), channel_id=1, source_target_pairs={{0,2},{2,0},{1,3},{3,1},{4,6},{6,4},{5,7},{7,5},{8,10},{10,8},{9,1... | collective-permute-start | bytes 196616 | tf_op jit(solution)/shard_map/ppermute | solution.py:21
  19.1 3.9 %collective-permute-start.14 = (bf16[128,256]{1,0:T(8,128)(2,1)S(1)}, bf16[128,256]{1,0:T(8,128)(2,1)S(1)}, u32[]{:S(2)}, u32[]{:S(2)}) collective-permute-start(bf16[128,256]{1,0:T(8,128)(2,1)S(1)} %collective-permute-done.10.refs_3_), channel_id=1, source_target_pairs={{0,2},{2,0},{1,3},{3,1},{4,6},{6,4},{5,7},{7,5},{8,10},{10,8},{9,1... | collective-permute-start | bytes 196616 | tf_op jit(solution)/shard_map/ppermute | solution.py:21
  23.2 4.6 %collective-permute-start.15 = (bf16[128,256]{1,0:T(8,128)(2,1)S(1)}, bf16[128,256]{1,0:T(8,128)(2,1)S(1)}, u32[]{:S(2)}, u32[]{:S(2)}) collective-permute-start(bf16[128,256]{1,0:T(8,128)(2,1)S(1)} %get-tuple-element.19), channel_id=1, source_target_pairs={{0,1},{1,0},{2,3},{3,2},{4,5},{5,4},{6,7},{7,6},{8,9},{9,8},{10,11... | collective-permute-start | bytes 196616 | tf_op jit(solution)/shard_map/ppermute | solution.py:21
  24.8 8.1 %collective-permute-start.17 = (bf16[128,256]{1,0:T(8,128)(2,1)S(1)}, bf16[128,256]{1,0:T(8,128)(2,1)S(1)}, u32[]{:S(2)}, u32[]{:S(2)}) collective-permute-start(bf16[128,256]{1,0:T(8,128)(2,1)S(1)} %copy-done.3), channel_id=1, source_target_pairs={{0,8},{8,0},{16,24},{24,16},{1,9},{9,1},{17,25},{25,17},{2,10},{10... | collective-permute-start | bytes 196616 | tf_op jit(solution)/shard_map/ppermute | solution.py:21
  27.9 7.1 %collective-permute-start.16 = (bf16[128,256]{1,0:T(8,128)(2,1)S(1)}, bf16[128,256]{1,0:T(8,128)(2,1)S(1)}, u32[]{:S(2)}, u32[]{:S(2)}) collective-permute-start(bf16[128,256]{1,0:T(8,128)(2,1)S(1)} %forward_sum.1.refs_0_), channel_id=1, source_target_pairs={{0,8},{8,0},{16,24},{24,16},{1,9},{9,1},{17,25},{25,17},{2,10},{10... | collective-permute-start | bytes 196616 | tf_op jit(solution)/shard_map/ppermute | solution.py:21
  28.3 11.2 %collective-permute-start.20 = (bf16[128,256]{1,0:T(8,128)(2,1)S(1)}, bf16[128,256]{1,0:T(8,128)(2,1)S(1)}, u32[]{:S(2)}, u32[]{:S(2)}) collective-permute-start(bf16[128,256]{1,0:T(8,128)(2,1)S(1)} %copy-done.3), channel_id=1, source_target_pairs={{0,16},{8,24},{16,0},{24,8},{1,17},{9,25},{17,1},{25,9},{2,18},{10... | collective-permute-start | bytes 196616 | tf_op jit(solution)/shard_map/ppermute | solution.py:21
  31.1 8.4 %collective-permute-start.21 = (bf16[128,256]{1,0:T(8,128)(2,1)S(1)}, bf16[128,256]{1,0:T(8,128)(2,1)S(1)}, u32[]{:S(2)}, u32[]{:S(2)}) collective-permute-start(bf16[128,256]{1,0:T(8,128)(2,1)S(1)} %copy-done.3), channel_id=1, source_target_pairs={{0,24},{8,16},{16,8},{24,0},{1,25},{9,17},{17,9},{25,1},{2,26},{10... | collective-permute-start | bytes 196616 | tf_op jit(solution)/shard_map/ppermute | solution.py:21
  32.3 10.0 %collective-permute-start.18 = (bf16[128,256]{1,0:T(8,128)(2,1)S(1)}, bf16[128,256]{1,0:T(8,128)(2,1)S(1)}, u32[]{:S(2)}, u32[]{:S(2)}) collective-permute-start(bf16[128,256]{1,0:T(8,128)(2,1)S(1)} %forward_sum.1.refs_0_), channel_id=1, source_target_pairs={{0,16},{8,24},{16,0},{24,8},{1,17},{9,25},{17,1},{25,9},{2,18},{10... | collective-permute-start | bytes 196616 | tf_op jit(solution)/shard_map/ppermute | solution.py:21
  33.0 9.3 %collective-permute-start.19 = (bf16[128,256]{1,0:T(8,128)(2,1)S(1)}, bf16[128,256]{1,0:T(8,128)(2,1)S(1)}, u32[]{:S(2)}, u32[]{:S(2)}) collective-permute-start(bf16[128,256]{1,0:T(8,128)(2,1)S(1)} %forward_sum.1.refs_0_), channel_id=1, source_target_pairs={{0,24},{8,16},{16,8},{24,0},{1,25},{9,17},{17,9},{25,1},{2,26},{10... | collective-permute-start | bytes 196616 | tf_op jit(solution)/shard_map/ppermute | solution.py:21
  42.9 6.4 %collective-permute-start.24 = (bf16[256,256]{1,0:T(8,128)(2,1)S(1)}, bf16[256,256]{1,0:T(8,128)(2,1)S(1)}, u32[]{:S(2)}, u32[]{:S(2)}) collective-permute-start(bf16[256,256]{1,0:T(8,128)(2,1)S(1)} %get-tuple-element.22.refs_0_), channel_id=1, source_target_pairs={{0,4},{4,0},{1,5},{5,1},{2,6},{6,2},{3,7},{7,3},{8,12},{12,8},{9,1... | collective-permute-start | bytes 393224 | tf_op jit(solution)/shard_map/ppermute | solution.py:21
  44.3 7.3 %collective-permute-start.25 = (bf16[256,256]{1,0:T(8,128)(2,1)S(1)}, bf16[256,256]{1,0:T(8,128)(2,1)S(1)}, u32[]{:S(2)}, u32[]{:S(2)}) collective-permute-start(bf16[256,256]{1,0:T(8,128)(2,1)S(1)} %get-tuple-element.25.refs_1_), channel_id=1, source_target_pairs={{0,4},{4,0},{1,5},{5,1},{2,6},{6,2},{3,7},{7,3},{8,12},{12,8},{9,1... | collective-permute-start | bytes 393224 | tf_op jit(solution)/shard_map/ppermute | solution.py:21
  45.0 6.6 %collective-permute-start.30 = (bf16[144,256]{1,0:T(8,128)(2,1)S(1)}, bf16[144,256]{1,0:T(8,128)(2,1)S(1)}, u32[]{:S(2)}, u32[]{:S(2)}) collective-permute-start(bf16[144,256]{1,0:T(8,128)(2,1)S(1)} %sum_core.1.own_ref), channel_id=1, source_target_pairs={{0,1},{1,0},{2,3},{3,2},{4,5},{5,4},{6,7},{7,6},{8,9},{9,8},{10,11... | collective-permute-start | bytes 221192 | tf_op jit(solution)/shard_map/ppermute | solution.py:21
  46.6 10.4 %collective-permute-start.22 = (bf16[256,256]{1,0:T(8,128)(2,1)S(1)}, bf16[256,256]{1,0:T(8,128)(2,1)S(1)}, u32[]{:S(2)}, u32[]{:S(2)}) collective-permute-start(bf16[256,256]{1,0:T(8,128)(2,1)S(1)} %get-tuple-element.22.refs_0_), channel_id=1, source_target_pairs={{0,2},{2,0},{1,3},{3,1},{4,6},{6,4},{5,7},{7,5},{8,10},{10,8},{9,1... | collective-permute-start | bytes 393224 | tf_op jit(solution)/shard_map/ppermute | solution.py:21
  46.6 10.4 %collective-permute-start.23 = (bf16[256,256]{1,0:T(8,128)(2,1)S(1)}, bf16[256,256]{1,0:T(8,128)(2,1)S(1)}, u32[]{:S(2)}, u32[]{:S(2)}) collective-permute-start(bf16[256,256]{1,0:T(8,128)(2,1)S(1)} %get-tuple-element.25.refs_1_), channel_id=1, source_target_pairs={{0,2},{2,0},{1,3},{3,1},{4,6},{6,4},{5,7},{7,5},{8,10},{10,8},{9,1... | collective-permute-start | bytes 393224 | tf_op jit(solution)/shard_map/ppermute | solution.py:21
  49.2 8.0 %collective-permute-start.26 = (bf16[256,256]{1,0:T(8,128)(2,1)S(1)}, bf16[256,256]{1,0:T(8,128)(2,1)S(1)}, u32[]{:S(2)}, u32[]{:S(2)}) collective-permute-start(bf16[256,256]{1,0:T(8,128)(2,1)S(1)} %collective-permute-done.24.refs_0_), channel_id=1, source_target_pairs={{0,2},{2,0},{1,3},{3,1},{4,6},{6,4},{5,7},{7,5},{8,10},{10,8},{9,1... | collective-permute-start | bytes 393224 | tf_op jit(solution)/shard_map/ppermute | solution.py:21
  51.6 5.7 %collective-permute-start.27 = (bf16[256,256]{1,0:T(8,128)(2,1)S(1)}, bf16[256,256]{1,0:T(8,128)(2,1)S(1)}, u32[]{:S(2)}, u32[]{:S(2)}) collective-permute-start(bf16[256,256]{1,0:T(8,128)(2,1)S(1)} %collective-permute-done.25.refs_1_), channel_id=1, source_target_pairs={{0,2},{2,0},{1,3},{3,1},{4,6},{6,4},{5,7},{7,5},{8,10},{10,8},{9,1... | collective-permute-start | bytes 393224 | tf_op jit(solution)/shard_map/ppermute | solution.py:21
  51.6 4.7 %collective-permute-start.31 = (bf16[144,256]{1,0:T(8,128)(2,1)S(1)}, bf16[144,256]{1,0:T(8,128)(2,1)S(1)}, u32[]{:S(2)}, u32[]{:S(2)}) collective-permute-start(bf16[144,256]{1,0:T(8,128)(2,1)S(1)} %sum_row.1.own_ref), channel_id=1, source_target_pairs={{0,4},{4,0},{1,5},{5,1},{2,6},{6,2},{3,7},{7,3},{8,12},{12,8},{9,1... | collective-permute-start | bytes 221192 | tf_op jit(solution)/shard_map/ppermute | solution.py:21
  57.0 5.9 %collective-permute-start.32 = (f32[128,256]{1,0:T(8,128)S(1)}, f32[128,256]{1,0:T(8,128)S(1)}, u32[]{:S(2)}, u32[]{:S(2)}) collective-permute-start(f32[128,256]{1,0:T(8,128)S(1)} %get-tuple-element.30.own_ref), channel_id=1, source_target_pairs={{0,2},{2,0},{1,3},{3,1},{4,6},{6,4},{5,7},{7,5},{8,10},{10,8},{9,1... | collective-permute-start | bytes 393224 | tf_op jit(solution)/shard_map/ppermute | solution.py:21
  57.6 4.6 %collective-permute-start.28 = (bf16[128,256]{1,0:T(8,128)(2,1)S(1)}, bf16[128,256]{1,0:T(8,128)(2,1)S(1)}, u32[]{:S(2)}, u32[]{:S(2)}) collective-permute-start(bf16[128,256]{1,0:T(8,128)(2,1)S(1)} %get-tuple-element.27), channel_id=1, source_target_pairs={{0,1},{1,0},{2,3},{3,2},{4,5},{5,4},{6,7},{7,6},{8,9},{9,8},{10,11... | collective-permute-start | bytes 196616 | tf_op jit(solution)/shard_map/ppermute | solution.py:21
  (8 other events, 21.8 us)

commit v4 on v3

--- a/solution.py
+++ b/solution.py
@@ -47,6 +47,17 @@
     return parts[0]
 
 
+def far_masks(n_far):
+    return [1 << k for k in reversed(range(n_far.bit_length() - 1))]
+
+
+def far_place(mask, n_far):
+    place = 0
+    for k, step in enumerate(far_masks(n_far)):
+        place = place + jnp.where(jnp.bitwise_and(mask, step) > 0, 1 << k, 0)
+    return place
+
+
 def expand_kernel(n_loop, n_row, tile, rows_ref, counts_ref, tiles_ref, out_ref):
     n_far = n_loop // 4
     my_row, my_far = lax.axis_index("row"), lax.axis_index("far")
@@ -54,7 +65,7 @@
 
     def body(j, carry):
         near = jnp.bitwise_xor(lax.rem(j, 4), my_near)
-        column = near * n_far + jnp.bitwise_xor(lax.div(j, 4), my_far)
+        column = near * n_far + far_place(jnp.bitwise_xor(lax.div(j, 4), my_far), n_far)
         for s in range(n_row):
             slot = j * n_row + s
             place = jnp.bitwise_xor(rows_ref[slot], my_row)
@@ -72,6 +83,13 @@
 def product_rows(a_ref, first, block_refs, rows):
     x = jnp.concatenate([ref[...] for ref in block_refs], axis=0)
     return dot(a_ref[rows, first : first + x.shape[0]], x)
+
+
+def pack_kernel(*refs):
+    at = 0
+    for ref in refs[:-1]:
+        refs[-1][at : at + ref.shape[0], :] = ref[...]
+        at += ref.shape[0]
 
 
 def near_kernel(tile, n_row, a_ref, *refs):
@@ -105,27 +123,26 @@
     out_ref[...] = total.astype(BF16)
 
 
-def chunk_grads(w_ref, b_ref, h_refs, c_refs, gh_ref, out_ref=None):
-    tile, width = h_refs[0].shape
+def chunk_grads(w_ref, b_ref, h_ref, c_ref, gh_ref, out_ref=None):
+    tile, width = h_ref.shape[0] // 2, h_ref.shape[1]
     weight_sums, bias_sums = [], []
-    for k, (h_ref, c_ref) in enumerate(zip(h_refs, c_refs)):
-        hidden = h_ref[...]
+    for k in range(2):
+        rows = slice(k * tile, (k + 1) * tile)
+        hidden = h_ref[rows, :]
         preact = dot(hidden, w_ref[...]) + b_ref[...]
         sig = sigmoid(preact)
         if k == 0 and out_ref is not None:
             out_ref[...] = (preact * sig).astype(BF16)
-        grad_z = c_ref[...].astype(F32) * sig * (1.0 + preact * (1.0 - sig))
+        grad_z = c_ref[rows, :].astype(F32) * sig * (1.0 + preact * (1.0 - sig))
         half = grad_z.astype(BF16)
-        gh_ref[k * tile : (k + 1) * tile, :] = dot(half, w_ref[...], ((1,), (1,))).astype(BF16)
+        gh_ref[rows, :] = dot(half, w_ref[...], ((1,), (1,))).astype(BF16)
         bias_sums.append(jnp.sum(grad_z.reshape(tile // 8, 8, width), axis=0))
         weight_sums.append(dot(hidden, half, ((0,), (0,))))
     return tree_sum(weight_sums), tree_sum(bias_sums)
 
 
-def first_chunk_kernel(n, w_ref, b_ref, *refs):
-    h_refs, c_refs = refs[:n], refs[n : 2 * n]
-    gh_ref, out_ref, gw_ref, gb_ref = refs[2 * n :]
-    gw_ref[...], gb_ref[...] = chunk_grads(w_ref, b_ref, h_refs, c_refs, gh_ref, out_ref)
+def chunk_kernel(w_ref, b_ref, h_ref, c_ref, gh_ref, gw_ref, gb_ref, *out_refs):
+    gw_ref[...], gb_ref[...] = chunk_grads(w_ref, b_ref, h_ref, c_ref, gh_ref, *out_refs)
 
 
 def write_message(ref, grad_w, bias):
@@ -144,13 +161,14 @@
     return ref[:rows, :].astype(F32), tail[0:1, :] + tail[1:2, :]
 
 
-def last_chunk_kernel(n, w_ref, b_ref, *refs):
-    h_refs, c_refs = refs[:n], refs[n : 2 * n]
-    gw_ref, gb_ref, gh_ref, keep_ref, send_ref, sum_ref = refs[2 * n :]
+def last_chunk_kernel(n, w_ref, b_ref, h_ref, c_ref, *refs):
+    gw_refs, gb_refs = refs[:n], refs[n : 2 * n]
+    gh_ref, keep_ref, send_ref, sum_ref = refs[2 * n :]
     half = keep_ref.shape[0] - PAD
-    grad_w, grad_b = chunk_grads(w_ref, b_ref, h_refs, c_refs, gh_ref)
-    sum_ref[...] = gw_ref[...] + grad_w
-    bias = jnp.sum(gb_ref[...] + grad_b, axis=0, keepdims=True)
+    grad_w, grad_b = chunk_grads(w_ref, b_ref, h_ref, c_ref, gh_ref)
+    sum_ref[...] = tree_sum([ref[...] for ref in gw_refs] + [grad_w])
+    grad_b = tree_sum([ref[...] for ref in gb_refs] + [grad_b])
+    bias = jnp.sum(grad_b, axis=0, keepdims=True)
     core = lax.axis_index("core")
     kept = sum_ref[pl.ds(pl.multiple_of(core * half, half), half), :]
     sent = sum_ref[pl.ds(pl.multiple_of((1 - core) * half, half), half), :]
@@ -164,18 +182,19 @@
     write_message(out_ref, own_w + other_w, own_b + other_b)
 
 
-def scale_kernel(factor, own_ref, other_ref, half_ref, bias_ref):
-    own_w, own_b = read_message(own_ref)
-    other_w, other_b = read_message(other_ref)
-    half_ref[...] = (own_w + other_w) * factor
-    bias_ref[...] = (own_b + other_b) * factor
-
-
-def halves_kernel(own_ref, other_ref, out_ref):
-    half = own_ref.shape[0]
+def last_kernel(n_parts, factor, own_ref, *refs):
+    part_refs = refs[:n_parts]
+    m00_ref, m10_ref, m01_ref, m11_ref, features_ref, weight_ref, bias_ref = refs[n_parts:]
+    sum_kernel(own_ref, *part_refs, features_ref)
+    half = weight_ref.shape[0] // 2
     core = lax.axis_index("core")
-    out_ref[pl.ds(pl.multiple_of(core * half, half), half), :] = own_ref[...]
-    out_ref[pl.ds(pl.multiple_of((1 - core) * half, half), half), :] = other_ref[...]
+    for k, (near_ref, far_ref) in enumerate(((m00_ref, m10_ref), (m01_ref, m11_ref))):
+        near_w, near_b = read_message(near_ref)
+        far_w, far_b = read_message(far_ref)
+        at = jnp.bitwise_xor(core, k) * half
+        weight_ref[pl.ds(pl.multiple_of(at, half), half), :] = (near_w + far_w) * factor
+        if k == 0:
+            bias_ref[...] = (near_b + far_b) * factor
 
 
 def call(kernel, name, outs, operands, scratch=(), specs=None, flops=0):
@@ -200,73 +219,89 @@
     rows = n_row * tile
     flops = rows * n_loop * tile * width
 
-    def far_blocks(block):
-        return [block] + [partner(block, "far", m, n_far) for m in range(1, n_far)]
-
-    def product(near, rest, name):
-        (half,) = call(
+    steps = far_masks(n_far)
+
+    def far_pair(block):
+        blocks = [block, partner(block, "far", steps[0], n_far)]
+        return call(pack_kernel, "pack", [shape(2 * tile, width)], blocks)[0]
+
+    def far_chunks(pair):
+        chunks = [pair]
+        for step in steps[1:]:
+            chunks = chunks + [partner(chunk, "far", step, n_far) for chunk in chunks]
+        return chunks
+
+    def near_product(near, name):
+        return call(
             functools.partial(near_kernel, tile, n_row),
             name + "_near",
             [shape(rows, width, dtype=F32)],
             [adjacency] + near,
             flops=flops,
-        )
-        own, *parts = call(
+        )[0]
+
+    def rest_product(half, rest, name):
+        return call(
             functools.partial(rest_kernel, tile, n_row, len(rest)),
             name + "_rest",
             [shape(tile, width, dtype=F32)] + [shape(tile, width)] * (n_row - 1),
             [adjacency, half] + rest,
             flops=flops,
         )
-        others = [partner(part, "row", q + 1, n_row) for q, part in enumerate(parts)]
-        (total,) = call(sum_kernel, name + "_sum", [shape(tile, width)], [own] + others)
-        return total
-
+
+    def from_row(parts):
+        return [partner(part, "row", q + 1, n_row) for q, part in enumerate(parts)]
+
+    pair = far_pair(features)
     (adjacency,) = call(
         functools.partial(expand_kernel, n_loop, n_row, tile),
         "expand",
         [shape(rows, n_loop * tile)],
-        (tile_rows, counts, tile_values),
+        (after(tile_rows, pair), counts, tile_values),
         specs=[SMEM, SMEM, VMEM],
     )
-
-    f00 = far_blocks(features)
-    f10 = [swap(block, "mid") for block in f00]
-    f01 = [swap(block, "core") for block in f00]
-    f11 = [swap(block, "core") for block in f10]
-    cots = far_blocks(after(cotangent, *f00[1:]))
-    hidden = product(f00 + f01, f10 + f11, "forward")
-
-    hiddens = far_blocks(hidden)
+    f00 = far_chunks(pair)
+    cot_pair = far_pair(after(cotangent, adjacency))
+    f00 = f00[:1] + [after(chunk, adjacency) for chunk in f00[1:]]
+    f10 = [swap(chunk, "mid") for chunk in f00]
+    f01 = [swap(chunk, "core") for chunk in f00]
+    f11 = [swap(chunk, "core") for chunk in f10]
+    half = near_product(f00 + f01, "forward")
+    cots = far_chunks(after(cot_pair, half))
+    own, *parts = rest_product(half, f10 + f11, "forward")
+    (hidden,) = call(
+        sum_kernel, "hidden", [shape(tile, width)], [after(own, *cots)] + from_row(parts)
+    )
+
+    hiddens = far_chunks(far_pair(hidden))
     bias_row = bias_vector.reshape(1, width)
-    n = n_far // 2
-    chunk_flops = n * tile * 6 * width * width
-    gh_a, output, grad_w, grad_b = call(
-        functools.partial(first_chunk_kernel, n),
-        "first_chunk",
-        [
-            shape(n * tile, width),
-            shape(tile, width),
-            shape(width, width, dtype=F32),
-            shape(8, width, dtype=F32),
-        ],
-        [weight, bias_row] + hiddens[:n] + cots[:n],
-        flops=chunk_flops,
-    )
+    chunk_flops = 2 * tile * 6 * width * width
+    g00, weight_sums, bias_sums = [], [], []
+    sums = [shape(width, width, dtype=F32), shape(8, width, dtype=F32)]
+    for k, (chunk, cot) in enumerate(zip(hiddens[:-1], cots[:-1])):
+        outs = [shape(2 * tile, width)] + sums + [shape(tile, width)] * (k == 0)
+        gh, weight_sum, bias_sum, *rest = call(
+            chunk_kernel, "chunk", outs, [weight, bias_row, chunk, cot], flops=chunk_flops
+        )
+        g00.append(gh)
+        weight_sums.append(weight_sum)
+        bias_sums.append(bias_sum)
+        output = output if k else rest[0]
     half_rows = width // 2 + PAD
-    gh_b, keep, send = call(
-        functools.partial(last_chunk_kernel, n),
+    gh, keep, send = call(
+        functools.partial(last_chunk_kernel, len(g00)),
         "last_chunk",
-        [shape(n * tile, width), shape(half_rows, width), shape(half_rows, width)],
-        [weight, bias_row] + hiddens[n:] + cots[n:] + [grad_w, grad_b],
+        [shape(2 * tile, width), shape(half_rows, width), shape(half_rows, width)],
+        [weight, bias_row, hiddens[-1], cots[-1]] + weight_sums + bias_sums,
         scratch=[pltpu.VMEM((width, width), F32)],
         flops=chunk_flops,
     )
-    g00 = [gh_a, gh_b]
+    g00.append(gh)
     g10 = [swap(chunk, "mid") for chunk in g00]
     g01 = [swap(chunk, "core") for chunk in g00]
     g11 = [swap(chunk, "core") for chunk in g10]
-    grad_features = product(g00 + g01, g10 + g11, "backward")
+    half = near_product(g00 + g01, "backward")
+    own, *parts = rest_product(half, g10 + g11, "backward")
 
     (message,) = call(
         message_kernel, "sum_core", [shape(half_rows, width)], [keep, swap(send, "core")]
@@ -277,17 +312,21 @@
             message_kernel,
             "sum_row",
             [shape(half_rows, width)],
-            [message, partner(message, "row", bit, n_row)],
+            [after(message, own), partner(message, "row", bit, n_row)],
         )
         bit *= 2
-    half, bias_grad = call(
-        functools.partial(scale_kernel, 1.0 / nodes**0.5),
-        "sum_mid",
-        [shape(width // 2, width, dtype=F32), shape(1, width, dtype=F32)],
-        [message, swap(message, "mid")],
-    )
-    (weight_grad,) = call(
-        halves_kernel, "halves", [shape(width, width, dtype=F32)], [half, swap(half, "core")]
+    messages = [
+        message,
+        swap(message, "mid"),
+        swap(message, "core"),
+        lax.ppermute(message, ("mid", "core"), [(i, 3 - i) for i in range(4)]),
+    ]
+    others = from_row(parts)
+    grad_features, weight_grad, bias_grad = call(
+        functools.partial(last_kernel, len(others), 1.0 / nodes**0.5),
+        "last",
+        [shape(tile, width), shape(width, width, dtype=F32), shape(1, width, dtype=F32)],
+        [own] + others + messages,
     )
     return output, grad_features, weight_grad, bias_grad.reshape(width)
 

time: 63.7 us -> 56.9 us (0.89)
  starting transfers between devices: 28 us -> 25.3 us
  waiting for transfers between devices: 26.5 us -> 23.9 us
  Pallas kernels: 5.72 us -> 4.61 us
    ppermute x33 -> x24, starting transfers between devices: 28 us -> 24.6 us  [partner(): return lax.ppermute(x, axis, [(i, i ^ mask) for i in range(n)])]
    ppermute x33 -> x24, waiting for transfers between devices: 26.5 us -> 23.9 us  [partner(): return lax.ppermute(x, axis, [(i, i ^ mask) for i in range(n)])]
    pallas_call x13 -> x14, Pallas kernels: 5.72 us -> 4.61 us  [call(): pl.pallas_call(kernel, name=name, out_shape=outs, in_specs=specs or [VMEM...]
    ppermute x0 -> x1, starting transfers between devices: none -> 0.67 us  [shards(): lax.ppermute(message, ('mid', 'core'), [(i, 3 - i) for i in range(4)])]
  transfers between devices with their start and end apart: 33 -> 25, of which waited for: 12 -> 11; matrix products, arithmetic and copies ran while one was open for 0% -> 0% of each run, Pallas kernels for 7% -> 7%
where the time goes in v4:
time: 56.9 us; the launch traced here: 56.7 us
  starting transfers between devices  25.3 us (44%)
  waiting for transfers between devices  23.9 us (42%)
  Pallas kernels  4.61 us (8%)
  local copies, waits for them, and re-layouts  2.09 us (4%)
  between operations  0.78 us (1%)
    ppermute x24, starting transfers between devices, partner(): return lax.ppermute(x, axis, [(i, i ^ mask) for i in range(n)])  24.6 us
    ppermute x24, waiting for transfers between devices, partner(): return lax.ppermute(x, axis, [(i, i ^ mask) for i in range(n)])  23.9 us
    pallas_call x14, Pallas kernels, call(): pl.pallas_call(kernel, name=name, out_shape=outs, in_specs=specs or [VMEM...  4.61 us
    unnamed x14, local copies, waits for them, and re-layouts  2.09 us
  transfers between devices with their start and end apart: 25, of which 11 were waited for; matrix products, arithmetic and copies ran while one was open for 0% of the time, Pallas kernels for 7%

profile of v4, /device:TPU:0, one launch (start us, length us, event | category | flops | bytes accessed | tf_op | source)
XLA Modules:
  0.0 56.7 jit_solution(14208895144338504788)
XLA Ops:
  0.6 4.1 %collective-permute-start = (bf16[128,256]{1,0:T(8,128)(2,1)}, bf16[128,256]{1,0:T(8,128)(2,1)S(1)}, u32[]{:S(2)}, u32[]{:S(2)}) collective-permute-start(bf16[128,256]{1,0:T(8,128)(2,1)} %refs_0_.1), channel_id=1, source_target_pairs={{0,16},{8,24},{16,0},{24,8},{1,17},{9,25},{17,1},{25,9},{2,18},{10... | collective-permute-start | bytes 196616 | tf_op jit(solution)/shard_map/ppermute | solution.py:21
  4.7 3.9 %collective-permute-done.refs_1_ = bf16[128,256]{1,0:T(8,128)(2,1)S(1)} collective-permute-done((bf16[128,256]{1,0:T(8,128)(2,1)}, bf16[128,256]{1,0:T(8,128)(2,1)S(1)}, u32[]{:S(2)}, u32[]{:S(2)}) %collective-permute-start) | collective-permute-done | bytes 65568 | tf_op jit(solution)/shard_map/ppermute | solution.py:21
  8.6 0.8 %copy-done.2 = bf16[128,256]{1,0:T(8,128)(2,1)S(1)} copy-done((bf16[128,256]{1,0:T(8,128)(2,1)S(1)}, bf16[128,256]{1,0:T(8,128)(2,1)}, u32[]{:S(2)}) %copy-start.2) | copy-done | bytes 65560
  9.5 0.7 %collective-permute-start.1 = (bf16[256,256]{1,0:T(8,128)(2,1)S(1)}, bf16[256,256]{1,0:T(8,128)(2,1)S(1)}, u32[]{:S(2)}, u32[]{:S(2)}) collective-permute-start(bf16[256,256]{1,0:T(8,128)(2,1)S(1)} %pack.3.refs_0_), channel_id=1, source_target_pairs={{0,8},{8,0},{16,24},{24,16},{1,9},{9,1},{17,25},{25,17},{2,10},{10... | collective-permute-start | bytes 393224 | tf_op jit(solution)/shard_map/ppermute | solution.py:21
  10.2 1.5 %collective-permute-start.4 = (bf16[256,256]{1,0:T(8,128)(2,1)S(1)}, bf16[256,256]{1,0:T(8,128)(2,1)S(1)}, u32[]{:S(2)}, u32[]{:S(2)}) collective-permute-start(bf16[256,256]{1,0:T(8,128)(2,1)S(1)} %pack.3.refs_0_), channel_id=1, source_target_pairs={{0,4},{4,0},{1,5},{5,1},{2,6},{6,2},{3,7},{7,3},{8,12},{12,8},{9,1... | collective-permute-start | bytes 393224 | tf_op jit(solution)/shard_map/ppermute | solution.py:21
  11.7 1.2 %copy-done = bf16[32,128,128]{2,1,0:T(8,128)(2,1)S(1)} copy-done((bf16[32,128,128]{2,1,0:T(8,128)(2,1)S(1)}, bf16[32,128,128]{2,1,0:T(8,128)(2,1)}, u32[]{:S(2)}) %copy-start) | copy-done | bytes 1048600
  12.9 1.0 %expand.1.a_ref = bf16[256,2048]{1,0:T(8,128)(2,1)S(1)} custom-call(s32[32]{0:T(128)S(1)} %copy-done.5, s32[16]{0:T(128)S(1)} %copy-done.6, bf16[32,128,128]{2,1,0:T(8,128)(2,1)S(1)} %copy-done), custom_call_target="tpu_custom_call" | custom-call | bytes 2097344 | tf_op jit(solution)/shard_map/expand/pallas_call | solution.py:203
  13.9 0.6 %collective-permute-done.1.refs_1_ = bf16[256,256]{1,0:T(8,128)(2,1)S(1)} collective-permute-done((bf16[256,256]{1,0:T(8,128)(2,1)S(1)}, bf16[256,256]{1,0:T(8,128)(2,1)S(1)}, u32[]{:S(2)}, u32[]{:S(2)}) %collective-permute-start.1) | collective-permute-done | bytes 131104 | tf_op jit(solution)/shard_map/ppermute | solution.py:21
  14.5 1.7 %collective-permute-start.5 = (bf16[256,256]{1,0:T(8,128)(2,1)S(1)}, bf16[256,256]{1,0:T(8,128)(2,1)S(1)}, u32[]{:S(2)}, u32[]{:S(2)}) collective-permute-start(bf16[256,256]{1,0:T(8,128)(2,1)S(1)} %collective-permute-done.1.refs_1_), channel_id=1, source_target_pairs={{0,4},{4,0},{1,5},{5,1},{2,6},{6,2},{3,7},{7,3},{8,12},{12,8},{9,1... | collective-permute-start | bytes 393224 | tf_op jit(solution)/shard_map/ppermute | solution.py:21
  16.2 0.5 collective-permute-start.3
  16.7 2.1 %collective-permute-start.8 = (bf16[128,256]{1,0:T(8,128)(2,1)S(1)}, bf16[128,256]{1,0:T(8,128)(2,1)S(1)}, u32[]{:S(2)}, u32[]{:S(2)}) collective-permute-start(bf16[128,256]{1,0:T(8,128)(2,1)S(1)} %copy-done.3), channel_id=1, source_target_pairs={{0,16},{8,24},{16,0},{24,8},{1,17},{9,25},{17,1},{25,9},{2,18},{10... | collective-permute-start | bytes 196616 | tf_op jit(solution)/shard_map/ppermute | solution.py:21
  18.8 0.6 %collective-permute-done.5.refs_1_ = bf16[256,256]{1,0:T(8,128)(2,1)S(1)} collective-permute-done((bf16[256,256]{1,0:T(8,128)(2,1)S(1)}, bf16[256,256]{1,0:T(8,128)(2,1)S(1)}, u32[]{:S(2)}, u32[]{:S(2)}) %collective-permute-start.5) | collective-permute-done | bytes 131104 | tf_op jit(solution)/shard_map/ppermute | solution.py:21
  19.5 3.5 %collective-permute-done.8.refs_1_ = bf16[128,256]{1,0:T(8,128)(2,1)S(1)} collective-permute-done((bf16[128,256]{1,0:T(8,128)(2,1)S(1)}, bf16[128,256]{1,0:T(8,128)(2,1)S(1)}, u32[]{:S(2)}, u32[]{:S(2)}) %collective-permute-start.8) | collective-permute-done | bytes 65568 | tf_op jit(solution)/shard_map/ppermute | solution.py:21
  23.9 1.6 %collective-permute-start.10 = (bf16[128,256]{1,0:T(8,128)(2,1)S(1)}, bf16[128,256]{1,0:T(8,128)(2,1)S(1)}, u32[]{:S(2)}, u32[]{:S(2)}) collective-permute-start(bf16[128,256]{1,0:T(8,128)(2,1)S(1)} %get-tuple-element.30), channel_id=1, source_target_pairs={{0,1},{1,0},{2,3},{3,2},{4,5},{5,4},{6,7},{7,6},{8,9},{9,8},{10,11... | collective-permute-start | bytes 196616 | tf_op jit(solution)/shard_map/ppermute | solution.py:21
  25.5 2.9 %collective-permute-done.9.c_ref = bf16[256,256]{1,0:T(8,128)(2,1)S(1)} collective-permute-done((bf16[256,256]{1,0:T(8,128)(2,1)S(1)}, bf16[256,256]{1,0:T(8,128)(2,1)S(1)}, u32[]{:S(2)}, u32[]{:S(2)}) %collective-permute-start.9) | collective-permute-done | bytes 131104 | tf_op jit(solution)/shard_map/ppermute | solution.py:21
  28.4 3.3 %collective-permute-start.11 = (bf16[128,256]{1,0:T(8,128)(2,1)S(1)}, bf16[128,256]{1,0:T(8,128)(2,1)S(1)}, u32[]{:S(2)}, u32[]{:S(2)}) collective-permute-start(bf16[128,256]{1,0:T(8,128)(2,1)S(1)} %hidden.1.refs_0_), channel_id=1, source_target_pairs={{0,16},{8,24},{16,0},{24,8},{1,17},{9,25},{17,1},{25,9},{2,18},{10... | collective-permute-start | bytes 196616 | tf_op jit(solution)/shard_map/ppermute | solution.py:21
  31.7 2.3 %collective-permute-done.11.refs_1_ = bf16[128,256]{1,0:T(8,128)(2,1)S(1)} collective-permute-done((bf16[128,256]{1,0:T(8,128)(2,1)S(1)}, bf16[128,256]{1,0:T(8,128)(2,1)S(1)}, u32[]{:S(2)}, u32[]{:S(2)}) %collective-permute-start.11) | collective-permute-done | bytes 65568 | tf_op jit(solution)/shard_map/ppermute | solution.py:21
  34.0 1.4 %collective-permute-start.12 = (bf16[256,256]{1,0:T(8,128)(2,1)S(1)}, bf16[256,256]{1,0:T(8,128)(2,1)S(1)}, u32[]{:S(2)}, u32[]{:S(2)}) collective-permute-start(bf16[256,256]{1,0:T(8,128)(2,1)S(1)} %pack.5.h_ref), channel_id=1, source_target_pairs={{0,8},{8,0},{16,24},{24,16},{1,9},{9,1},{17,25},{25,17},{2,10},{10... | collective-permute-start | bytes 393224 | tf_op jit(solution)/shard_map/ppermute | solution.py:21
  35.5 1.0 %chunk.1 = (bf16[256,256]{1,0:T(8,128)(2,1)S(1)}, f32[256,256]{1,0:T(8,128)S(1)}, f32[8,256]{1,0:T(8,128)S(1)}, bf16[128,256]{1,0:T(8,128)(2,1)}) custom-call(bf16[256,256]{1,0:T(8,128)(2,1)S(1)} %copy-done.1, f32[1,256]{1,0:T(1,128)S(1)} %bitcast.2, bf16[256,256]{1,0:T(8,128)(2,1)S(1)} %pack.5.h_ref, bf16[256,256]{1,0:T(8,128)(2,1)S(1)} %pack.4.c_ref), custom_call_target="tpu_custom_call" | custom-call | flops 100663296 | bytes 861184 | tf_op jit(solution)/shard_map/chunk/pallas_call | solution.py:203
  36.5 0.7 %collective-permute-start.15 = (bf16[256,256]{1,0:T(8,128)(2,1)S(1)}, bf16[256,256]{1,0:T(8,128)(2,1)S(1)}, u32[]{:S(2)}, u32[]{:S(2)}) collective-permute-start(bf16[256,256]{1,0:T(8,128)(2,1)S(1)} %get-tuple-element.32.refs_0_), channel_id=1, source_target_pairs={{0,4},{4,0},{1,5},{5,1},{2,6},{6,2},{3,7},{7,3},{8,12},{12,8},{9,1... | collective-permute-start | bytes 393224 | tf_op jit(solution)/shard_map/ppermute | solution.py:21
  37.2 1.9 %collective-permute-done.12.h_ref = bf16[256,256]{1,0:T(8,128)(2,1)S(1)} collective-permute-done((bf16[256,256]{1,0:T(8,128)(2,1)S(1)}, bf16[256,256]{1,0:T(8,128)(2,1)S(1)}, u32[]{:S(2)}, u32[]{:S(2)}) %collective-permute-start.12) | collective-permute-done | bytes 131104 | tf_op jit(solution)/shard_map/ppermute | solution.py:21
  39.1 0.5 last_chunk.1
  39.6 1.5 %collective-permute-start.16 = (bf16[256,256]{1,0:T(8,128)(2,1)S(1)}, bf16[256,256]{1,0:T(8,128)(2,1)S(1)}, u32[]{:S(2)}, u32[]{:S(2)}) collective-permute-start(bf16[256,256]{1,0:T(8,128)(2,1)S(1)} %get-tuple-element.35.refs_1_), channel_id=1, source_target_pairs={{0,4},{4,0},{1,5},{5,1},{2,6},{6,2},{3,7},{7,3},{8,12},{12,8},{9,1... | collective-permute-start | bytes 393224 | tf_op jit(solution)/shard_map/ppermute | solution.py:21
  41.7 0.8 %collective-permute-done.15.refs_0_ = bf16[256,256]{1,0:T(8,128)(2,1)S(1)} collective-permute-done((bf16[256,256]{1,0:T(8,128)(2,1)S(1)}, bf16[256,256]{1,0:T(8,128)(2,1)S(1)}, u32[]{:S(2)}, u32[]{:S(2)}) %collective-permute-start.15) | collective-permute-done | bytes 131104 | tf_op jit(solution)/shard_map/ppermute | solution.py:21
  42.4 2.2 %collective-permute-done.16.refs_1_ = bf16[256,256]{1,0:T(8,128)(2,1)S(1)} collective-permute-done((bf16[256,256]{1,0:T(8,128)(2,1)S(1)}, bf16[256,256]{1,0:T(8,128)(2,1)S(1)}, u32[]{:S(2)}, u32[]{:S(2)}) %collective-permute-start.16) | collective-permute-done | bytes 131104 | tf_op jit(solution)/shard_map/ppermute | solution.py:21
  44.7 1.6 %collective-permute-start.21 = (bf16[144,256]{1,0:T(8,128)(2,1)S(1)}, bf16[144,256]{1,0:T(8,128)(2,1)S(1)}, u32[]{:S(2)}, u32[]{:S(2)}) collective-permute-start(bf16[144,256]{1,0:T(8,128)(2,1)S(1)} %sum_core.1.own_ref), channel_id=1, source_target_pairs={{0,1},{1,0},{2,3},{3,2},{4,5},{5,4},{6,7},{7,6},{8,9},{9,8},{10,11... | collective-permute-start | bytes 221192 | tf_op jit(solution)/shard_map/ppermute | solution.py:21
  46.9 2.5 %collective-permute-done.21.other_ref = bf16[144,256]{1,0:T(8,128)(2,1)S(1)} collective-permute-done((bf16[144,256]{1,0:T(8,128)(2,1)S(1)}, bf16[144,256]{1,0:T(8,128)(2,1)S(1)}, u32[]{:S(2)}, u32[]{:S(2)}) %collective-permute-start.21) | collective-permute-done | bytes 73760 | tf_op jit(solution)/shard_map/ppermute | solution.py:21
  49.5 1.5 %collective-permute-start.22 = (bf16[144,256]{1,0:T(8,128)(2,1)S(1)}, bf16[144,256]{1,0:T(8,128)(2,1)S(1)}, u32[]{:S(2)}, u32[]{:S(2)}) collective-permute-start(bf16[144,256]{1,0:T(8,128)(2,1)S(1)} %sum_row.1.refs_1_), channel_id=1, source_target_pairs={{0,4},{4,0},{1,5},{5,1},{2,6},{6,2},{3,7},{7,3},{8,12},{12,8},{9,1... | collective-permute-start | bytes 221192 | tf_op jit(solution)/shard_map/ppermute | solution.py:21
  51.0 0.7 %collective-permute-start.24 = (bf16[144,256]{1,0:T(8,128)(2,1)S(1)}, bf16[144,256]{1,0:T(8,128)(2,1)S(1)}, u32[]{:S(2)}, u32[]{:S(2)}) collective-permute-start(bf16[144,256]{1,0:T(8,128)(2,1)S(1)} %sum_row.1.refs_1_), channel_id=1, source_target_pairs={{0,6},{2,4},{4,2},{6,0},{1,7},{3,5},{5,3},{7,1},{8,14},{10,12},{12... | collective-permute-start | bytes 221192 | tf_op jit(solution)/shard_map/ppermute | solution.py:322
  51.7 1.5 %collective-permute-start.19 = (bf16[128,256]{1,0:T(8,128)(2,1)S(1)}, bf16[128,256]{1,0:T(8,128)(2,1)S(1)}, u32[]{:S(2)}, u32[]{:S(2)}) collective-permute-start(bf16[128,256]{1,0:T(8,128)(2,1)S(1)} %get-tuple-element.37), channel_id=1, source_target_pairs={{0,1},{1,0},{2,3},{3,2},{4,5},{5,4},{6,7},{7,6},{8,9},{9,8},{10,11... | collective-permute-start | bytes 196616 | tf_op jit(solution)/shard_map/ppermute | solution.py:21
  53.2 2.7 %collective-permute-done.19.refs_0_ = bf16[128,256]{1,0:T(8,128)(2,1)S(1)} collective-permute-done((bf16[128,256]{1,0:T(8,128)(2,1)S(1)}, bf16[128,256]{1,0:T(8,128)(2,1)S(1)}, u32[]{:S(2)}, u32[]{:S(2)}) %collective-permute-start.19) | collective-permute-done | bytes 65568 | tf_op jit(solution)/shard_map/ppermute | solution.py:21
  56.0 0.8 %last.1 = (bf16[128,256]{1,0:T(8,128)(2,1)}, f32[256,256]{1,0:T(8,128)}, f32[1,256]{1,0:T(1,128)}) custom-call(f32[128,256]{1,0:T(8,128)S(1)} %get-tuple-element.36.own_ref, bf16[128,256]{1,0:T(8,128)(2,1)S(1)} %collective-permute-done.19.refs_0_, bf16[144,256]{1,0:T(8,128)(2,1)S(1)} %sum_row.1.refs_1_, ...), custom_call_target="tpu_custom_call" | custom-call | bytes 820224 | tf_op jit(solution)/shard_map/last/pallas_call | solution.py:203
  (46 shorter events, 2.2 us)
Async XLA Ops:
  0.6 8.0 %collective-permute-start = (bf16[128,256]{1,0:T(8,128)(2,1)}, bf16[128,256]{1,0:T(8,128)(2,1)S(1)}, u32[]{:S(2)}, u32[]{:S(2)}) collective-permute-start(bf16[128,256]{1,0:T(8,128)(2,1)} %refs_0_.1), channel_id=1, source_target_pairs={{0,16},{8,24},{16,0},{24,8},{1,17},{9,25},{17,1},{25,9},{2,18},{10... | collective-permute-start | bytes 196616 | tf_op jit(solution)/shard_map/ppermute | solution.py:21
  8.6 0.8 %copy-start.2 = (bf16[128,256]{1,0:T(8,128)(2,1)S(1)}, bf16[128,256]{1,0:T(8,128)(2,1)}, u32[]{:S(2)}) copy-start(bf16[128,256]{1,0:T(8,128)(2,1)} %refs_0_.1) | copy-start | bytes 196612
  9.4 2.3 %copy-start.5 = (s32[32]{0:T(128)S(1)}, s32[32]{0:T(128)}, u32[]{:S(2)}) copy-start(s32[32]{0:T(128)} %rows_ref) | copy-start | bytes 388
  9.4 2.3 %copy-start.6 = (s32[16]{0:T(128)S(1)}, s32[16]{0:T(128)}, u32[]{:S(2)}) copy-start(s32[16]{0:T(128)} %counts_ref.1) | copy-start | bytes 196
  9.4 7.3 %copy-start.3 = (bf16[128,256]{1,0:T(8,128)(2,1)S(1)}, bf16[128,256]{1,0:T(8,128)(2,1)}, u32[]{:S(2)}) copy-start(bf16[128,256]{1,0:T(8,128)(2,1)} %refs_0_.2) | copy-start | bytes 196612
  9.5 5.0 %collective-permute-start.1 = (bf16[256,256]{1,0:T(8,128)(2,1)S(1)}, bf16[256,256]{1,0:T(8,128)(2,1)S(1)}, u32[]{:S(2)}, u32[]{:S(2)}) collective-permute-start(bf16[256,256]{1,0:T(8,128)(2,1)S(1)} %pack.3.refs_0_), channel_id=1, source_target_pairs={{0,8},{8,0},{16,24},{24,16},{1,9},{9,1},{17,25},{25,17},{2,10},{10... | collective-permute-start | bytes 393224 | tf_op jit(solution)/shard_map/ppermute | solution.py:21
  10.2 8.6 %collective-permute-start.4 = (bf16[256,256]{1,0:T(8,128)(2,1)S(1)}, bf16[256,256]{1,0:T(8,128)(2,1)S(1)}, u32[]{:S(2)}, u32[]{:S(2)}) collective-permute-start(bf16[256,256]{1,0:T(8,128)(2,1)S(1)} %pack.3.refs_0_), channel_id=1, source_target_pairs={{0,4},{4,0},{1,5},{5,1},{2,6},{6,2},{3,7},{7,3},{8,12},{12,8},{9,1... | collective-permute-start | bytes 393224 | tf_op jit(solution)/shard_map/ppermute | solution.py:21
  11.7 1.2 %copy-start = (bf16[32,128,128]{2,1,0:T(8,128)(2,1)S(1)}, bf16[32,128,128]{2,1,0:T(8,128)(2,1)}, u32[]{:S(2)}) copy-start(bf16[32,128,128]{2,1,0:T(8,128)(2,1)} %tiles_ref.1) | copy-start | bytes 3145732
  14.5 5.0 %collective-permute-start.5 = (bf16[256,256]{1,0:T(8,128)(2,1)S(1)}, bf16[256,256]{1,0:T(8,128)(2,1)S(1)}, u32[]{:S(2)}, u32[]{:S(2)}) collective-permute-start(bf16[256,256]{1,0:T(8,128)(2,1)S(1)} %collective-permute-done.1.refs_1_), channel_id=1, source_target_pairs={{0,4},{4,0},{1,5},{5,1},{2,6},{6,2},{3,7},{7,3},{8,12},{12,8},{9,1... | collective-permute-start | bytes 393224 | tf_op jit(solution)/shard_map/ppermute | solution.py:21
  16.2 6.8 %collective-permute-start.2 = (bf16[256,256]{1,0:T(8,128)(2,1)S(1)}, bf16[256,256]{1,0:T(8,128)(2,1)S(1)}, u32[]{:S(2)}, u32[]{:S(2)}) collective-permute-start(bf16[256,256]{1,0:T(8,128)(2,1)S(1)} %pack.3.refs_0_), channel_id=1, source_target_pairs={{0,2},{2,0},{1,3},{3,1},{4,6},{6,4},{5,7},{7,5},{8,10},{10,8},{9,1... | collective-permute-start | bytes 393224 | tf_op jit(solution)/shard_map/ppermute | solution.py:21
  16.2 6.8 %collective-permute-start.3 = (bf16[256,256]{1,0:T(8,128)(2,1)S(1)}, bf16[256,256]{1,0:T(8,128)(2,1)S(1)}, u32[]{:S(2)}, u32[]{:S(2)}) collective-permute-start(bf16[256,256]{1,0:T(8,128)(2,1)S(1)} %collective-permute-done.1.refs_1_), channel_id=1, source_target_pairs={{0,2},{2,0},{1,3},{3,1},{4,6},{6,4},{5,7},{7,5},{8,10},{10,8},{9,1... | collective-permute-start | bytes 393224 | tf_op jit(solution)/shard_map/ppermute | solution.py:21
  16.7 6.3 %collective-permute-start.8 = (bf16[128,256]{1,0:T(8,128)(2,1)S(1)}, bf16[128,256]{1,0:T(8,128)(2,1)S(1)}, u32[]{:S(2)}, u32[]{:S(2)}) collective-permute-start(bf16[128,256]{1,0:T(8,128)(2,1)S(1)} %copy-done.3), channel_id=1, source_target_pairs={{0,16},{8,24},{16,0},{24,8},{1,17},{9,25},{17,1},{25,9},{2,18},{10... | collective-permute-start | bytes 196616 | tf_op jit(solution)/shard_map/ppermute | solution.py:21
  18.8 4.8 %collective-permute-start.6 = (bf16[256,256]{1,0:T(8,128)(2,1)S(1)}, bf16[256,256]{1,0:T(8,128)(2,1)S(1)}, u32[]{:S(2)}, u32[]{:S(2)}) collective-permute-start(bf16[256,256]{1,0:T(8,128)(2,1)S(1)} %collective-permute-done.4.refs_0_), channel_id=1, source_target_pairs={{0,2},{2,0},{1,3},{3,1},{4,6},{6,4},{5,7},{7,5},{8,10},{10,8},{9,1... | collective-permute-start | bytes 393224 | tf_op jit(solution)/shard_map/ppermute | solution.py:21
  19.5 4.1 %collective-permute-start.7 = (bf16[256,256]{1,0:T(8,128)(2,1)S(1)}, bf16[256,256]{1,0:T(8,128)(2,1)S(1)}, u32[]{:S(2)}, u32[]{:S(2)}) collective-permute-start(bf16[256,256]{1,0:T(8,128)(2,1)S(1)} %collective-permute-done.5.refs_1_), channel_id=1, source_target_pairs={{0,2},{2,0},{1,3},{3,1},{4,6},{6,4},{5,7},{7,5},{8,10},{10,8},{9,1... | collective-permute-start | bytes 393224 | tf_op jit(solution)/shard_map/ppermute | solution.py:21
  23.4 5.0 %collective-permute-start.9 = (bf16[256,256]{1,0:T(8,128)(2,1)S(1)}, bf16[256,256]{1,0:T(8,128)(2,1)S(1)}, u32[]{:S(2)}, u32[]{:S(2)}) collective-permute-start(bf16[256,256]{1,0:T(8,128)(2,1)S(1)} %pack.4.c_ref), channel_id=1, source_target_pairs={{0,8},{8,0},{16,24},{24,16},{1,9},{9,1},{17,25},{25,17},{2,10},{10... | collective-permute-start | bytes 393224 | tf_op jit(solution)/shard_map/ppermute | solution.py:21
  23.9 4.5 %collective-permute-start.10 = (bf16[128,256]{1,0:T(8,128)(2,1)S(1)}, bf16[128,256]{1,0:T(8,128)(2,1)S(1)}, u32[]{:S(2)}, u32[]{:S(2)}) collective-permute-start(bf16[128,256]{1,0:T(8,128)(2,1)S(1)} %get-tuple-element.30), channel_id=1, source_target_pairs={{0,1},{1,0},{2,3},{3,2},{4,5},{5,4},{6,7},{7,6},{8,9},{9,8},{10,11... | collective-permute-start | bytes 196616 | tf_op jit(solution)/shard_map/ppermute | solution.py:21
  28.4 7.0 %copy-start.1 = (bf16[256,256]{1,0:T(8,128)(2,1)S(1)}, bf16[256,256]{1,0:T(8,128)(2,1)}, u32[]{:S(2)}) copy-start(bf16[256,256]{1,0:T(8,128)(2,1)} %w_ref.3) | copy-start | bytes 393220
  28.4 5.6 %collective-permute-start.11 = (bf16[128,256]{1,0:T(8,128)(2,1)S(1)}, bf16[128,256]{1,0:T(8,128)(2,1)S(1)}, u32[]{:S(2)}, u32[]{:S(2)}) collective-permute-start(bf16[128,256]{1,0:T(8,128)(2,1)S(1)} %hidden.1.refs_0_), channel_id=1, source_target_pairs={{0,16},{8,24},{16,0},{24,8},{1,17},{9,25},{17,1},{25,9},{2,18},{10... | collective-permute-start | bytes 196616 | tf_op jit(solution)/shard_map/ppermute | solution.py:21
  34.0 1.4 %copy-start.4 = (f32[256]{0:T(256)S(1)}, f32[256]{0:T(256)}, u32[]{:S(2)}) copy-start(f32[256]{0:T(256)} %param.9) | copy-start | bytes 3076
  34.0 5.0 %collective-permute-start.12 = (bf16[256,256]{1,0:T(8,128)(2,1)S(1)}, bf16[256,256]{1,0:T(8,128)(2,1)S(1)}, u32[]{:S(2)}, u32[]{:S(2)}) collective-permute-start(bf16[256,256]{1,0:T(8,128)(2,1)S(1)} %pack.5.h_ref), channel_id=1, source_target_pairs={{0,8},{8,0},{16,24},{24,16},{1,9},{9,1},{17,25},{25,17},{2,10},{10... | collective-permute-start | bytes 393224 | tf_op jit(solution)/shard_map/ppermute | solution.py:21
  36.5 6.0 %collective-permute-start.15 = (bf16[256,256]{1,0:T(8,128)(2,1)S(1)}, bf16[256,256]{1,0:T(8,128)(2,1)S(1)}, u32[]{:S(2)}, u32[]{:S(2)}) collective-permute-start(bf16[256,256]{1,0:T(8,128)(2,1)S(1)} %get-tuple-element.32.refs_0_), channel_id=1, source_target_pairs={{0,4},{4,0},{1,5},{5,1},{2,6},{6,2},{3,7},{7,3},{8,12},{12,8},{9,1... | collective-permute-start | bytes 393224 | tf_op jit(solution)/shard_map/ppermute | solution.py:21
  39.6 5.0 %collective-permute-start.16 = (bf16[256,256]{1,0:T(8,128)(2,1)S(1)}, bf16[256,256]{1,0:T(8,128)(2,1)S(1)}, u32[]{:S(2)}, u32[]{:S(2)}) collective-permute-start(bf16[256,256]{1,0:T(8,128)(2,1)S(1)} %get-tuple-element.35.refs_1_), channel_id=1, source_target_pairs={{0,4},{4,0},{1,5},{5,1},{2,6},{6,2},{3,7},{7,3},{8,12},{12,8},{9,1... | collective-permute-start | bytes 393224 | tf_op jit(solution)/shard_map/ppermute | solution.py:21
  41.2 5.1 %collective-permute-start.13 = (bf16[256,256]{1,0:T(8,128)(2,1)S(1)}, bf16[256,256]{1,0:T(8,128)(2,1)S(1)}, u32[]{:S(2)}, u32[]{:S(2)}) collective-permute-start(bf16[256,256]{1,0:T(8,128)(2,1)S(1)} %get-tuple-element.32.refs_0_), channel_id=1, source_target_pairs={{0,2},{2,0},{1,3},{3,1},{4,6},{6,4},{5,7},{7,5},{8,10},{10,8},{9,1... | collective-permute-start | bytes 393224 | tf_op jit(solution)/shard_map/ppermute | solution.py:21
  41.2 5.1 %collective-permute-start.14 = (bf16[256,256]{1,0:T(8,128)(2,1)S(1)}, bf16[256,256]{1,0:T(8,128)(2,1)S(1)}, u32[]{:S(2)}, u32[]{:S(2)}) collective-permute-start(bf16[256,256]{1,0:T(8,128)(2,1)S(1)} %get-tuple-element.35.refs_1_), channel_id=1, source_target_pairs={{0,2},{2,0},{1,3},{3,1},{4,6},{6,4},{5,7},{7,5},{8,10},{10,8},{9,1... | collective-permute-start | bytes 393224 | tf_op jit(solution)/shard_map/ppermute | solution.py:21
  41.7 3.0 %collective-permute-start.20 = (bf16[144,256]{1,0:T(8,128)(2,1)S(1)}, bf16[144,256]{1,0:T(8,128)(2,1)S(1)}, u32[]{:S(2)}, u32[]{:S(2)}) collective-permute-start(bf16[144,256]{1,0:T(8,128)(2,1)S(1)} %get-tuple-element.39), channel_id=1, source_target_pairs={{0,2},{2,0},{1,3},{3,1},{4,6},{6,4},{5,7},{7,5},{8,10},{10,8},{9,1... | collective-permute-start | bytes 221192 | tf_op jit(solution)/shard_map/ppermute | solution.py:21
  42.4 4.2 %collective-permute-start.17 = (bf16[256,256]{1,0:T(8,128)(2,1)S(1)}, bf16[256,256]{1,0:T(8,128)(2,1)S(1)}, u32[]{:S(2)}, u32[]{:S(2)}) collective-permute-start(bf16[256,256]{1,0:T(8,128)(2,1)S(1)} %collective-permute-done.15.refs_0_), channel_id=1, source_target_pairs={{0,2},{2,0},{1,3},{3,1},{4,6},{6,4},{5,7},{7,5},{8,10},{10,8},{9,1... | collective-permute-start | bytes 393224 | tf_op jit(solution)/shard_map/ppermute | solution.py:21
  44.7 2.0 %collective-permute-start.18 = (bf16[256,256]{1,0:T(8,128)(2,1)S(1)}, bf16[256,256]{1,0:T(8,128)(2,1)S(1)}, u32[]{:S(2)}, u32[]{:S(2)}) collective-permute-start(bf16[256,256]{1,0:T(8,128)(2,1)S(1)} %collective-permute-done.16.refs_1_), channel_id=1, source_target_pairs={{0,2},{2,0},{1,3},{3,1},{4,6},{6,4},{5,7},{7,5},{8,10},{10,8},{9,1... | collective-permute-start | bytes 393224 | tf_op jit(solution)/shard_map/ppermute | solution.py:21
  44.7 4.7 %collective-permute-start.21 = (bf16[144,256]{1,0:T(8,128)(2,1)S(1)}, bf16[144,256]{1,0:T(8,128)(2,1)S(1)}, u32[]{:S(2)}, u32[]{:S(2)}) collective-permute-start(bf16[144,256]{1,0:T(8,128)(2,1)S(1)} %sum_core.1.own_ref), channel_id=1, source_target_pairs={{0,1},{1,0},{2,3},{3,2},{4,5},{5,4},{6,7},{7,6},{8,9},{9,8},{10,11... | collective-permute-start | bytes 221192 | tf_op jit(solution)/shard_map/ppermute | solution.py:21
  49.5 6.5 %collective-permute-start.22 = (bf16[144,256]{1,0:T(8,128)(2,1)S(1)}, bf16[144,256]{1,0:T(8,128)(2,1)S(1)}, u32[]{:S(2)}, u32[]{:S(2)}) collective-permute-start(bf16[144,256]{1,0:T(8,128)(2,1)S(1)} %sum_row.1.refs_1_), channel_id=1, source_target_pairs={{0,4},{4,0},{1,5},{5,1},{2,6},{6,2},{3,7},{7,3},{8,12},{12,8},{9,1... | collective-permute-start | bytes 221192 | tf_op jit(solution)/shard_map/ppermute | solution.py:21
  51.0 4.9 %collective-permute-start.23 = (bf16[144,256]{1,0:T(8,128)(2,1)S(1)}, bf16[144,256]{1,0:T(8,128)(2,1)S(1)}, u32[]{:S(2)}, u32[]{:S(2)}) collective-permute-start(bf16[144,256]{1,0:T(8,128)(2,1)S(1)} %sum_row.1.refs_1_), channel_id=1, source_target_pairs={{0,2},{2,0},{1,3},{3,1},{4,6},{6,4},{5,7},{7,5},{8,10},{10,8},{9,1... | collective-permute-start | bytes 221192 | tf_op jit(solution)/shard_map/ppermute | solution.py:21
  51.0 4.9 %collective-permute-start.24 = (bf16[144,256]{1,0:T(8,128)(2,1)S(1)}, bf16[144,256]{1,0:T(8,128)(2,1)S(1)}, u32[]{:S(2)}, u32[]{:S(2)}) collective-permute-start(bf16[144,256]{1,0:T(8,128)(2,1)S(1)} %sum_row.1.refs_1_), channel_id=1, source_target_pairs={{0,6},{2,4},{4,2},{6,0},{1,7},{3,5},{5,3},{7,1},{8,14},{10,12},{12... | collective-permute-start | bytes 221192 | tf_op jit(solution)/shard_map/ppermute | solution.py:322
  51.7 4.3 %collective-permute-start.19 = (bf16[128,256]{1,0:T(8,128)(2,1)S(1)}, bf16[128,256]{1,0:T(8,128)(2,1)S(1)}, u32[]{:S(2)}, u32[]{:S(2)}) collective-permute-start(bf16[128,256]{1,0:T(8,128)(2,1)S(1)} %get-tuple-element.37), channel_id=1, source_target_pairs={{0,1},{1,0},{2,3},{3,2},{4,5},{5,4},{6,7},{7,6},{8,9},{9,8},{10,11... | collective-permute-start | bytes 196616 | tf_op jit(solution)/shard_map/ppermute | solution.py:21

commit v5 on v4

--- a/solution.py
+++ b/solution.py
@@ -58,7 +58,9 @@
     return place
 
 
-def expand_kernel(n_loop, n_row, tile, rows_ref, counts_ref, tiles_ref, out_ref):
+def expand_kernel(
+    n_loop, n_row, tile, rows_ref, counts_ref, tiles_ref, f_ref, c_ref, out_ref, f_out, c_out
+):
     n_far = n_loop // 4
     my_row, my_far = lax.axis_index("row"), lax.axis_index("far")
     my_near = 2 * lax.axis_index("mid") + lax.axis_index("core")
@@ -78,10 +80,13 @@
         return carry
 
     lax.fori_loop(0, n_loop, body, 0)
+    f_out[...] = f_ref[...]
+    c_out[...] = c_ref[...]
 
 
 def product_rows(a_ref, first, block_refs, rows):
-    x = jnp.concatenate([ref[...] for ref in block_refs], axis=0)
+    step = a_ref.shape[1] // (2 * len(block_refs))
+    x = jnp.concatenate([ref[:step, :] for ref in block_refs], axis=0)
     return dot(a_ref[rows, first : first + x.shape[0]], x)
 
 
@@ -98,6 +103,12 @@
     for at in range(0, n_row * tile, step):
         rows = slice(at, at + step)
         out_ref[rows, :] = product_rows(a_ref, 0, block_refs, rows)
+
+
+def output_near_kernel(tile, n_row, w_ref, b_ref, h_ref, a_ref, *refs):
+    preact = dot(h_ref[...], w_ref[...]) + b_ref[...]
+    refs[-2][...] = (preact * sigmoid(preact)).astype(BF16)
+    near_kernel(tile, n_row, a_ref, *refs[:-2], refs[-1])
 
 
 def rest_kernel(tile, n_row, n_blocks, a_ref, half_ref, *refs):
@@ -123,7 +134,7 @@
     out_ref[...] = total.astype(BF16)
 
 
-def chunk_grads(w_ref, b_ref, h_ref, c_ref, gh_ref, out_ref=None):
+def chunk_grads(w_ref, b_ref, h_ref, c_ref, gh_ref):
     tile, width = h_ref.shape[0] // 2, h_ref.shape[1]
     weight_sums, bias_sums = [], []
     for k in range(2):
@@ -131,8 +142,6 @@
         hidden = h_ref[rows, :]
         preact = dot(hidden, w_ref[...]) + b_ref[...]
         sig = sigmoid(preact)
-        if k == 0 and out_ref is not None:
-            out_ref[...] = (preact * sig).astype(BF16)
         grad_z = c_ref[rows, :].astype(F32) * sig * (1.0 + preact * (1.0 - sig))
         half = grad_z.astype(BF16)
         gh_ref[rows, :] = dot(half, w_ref[...], ((1,), (1,))).astype(BF16)
@@ -141,8 +150,8 @@
     return tree_sum(weight_sums), tree_sum(bias_sums)
 
 
-def chunk_kernel(w_ref, b_ref, h_ref, c_ref, gh_ref, gw_ref, gb_ref, *out_refs):
-    gw_ref[...], gb_ref[...] = chunk_grads(w_ref, b_ref, h_ref, c_ref, gh_ref, *out_refs)
+def chunk_kernel(w_ref, b_ref, h_ref, c_ref, gh_ref, gw_ref, gb_ref):
+    gw_ref[...], gb_ref[...] = chunk_grads(w_ref, b_ref, h_ref, c_ref, gh_ref)
 
 
 def write_message(ref, grad_w, bias):
@@ -163,7 +172,7 @@
 
 def last_chunk_kernel(n, w_ref, b_ref, h_ref, c_ref, *refs):
     gw_refs, gb_refs = refs[:n], refs[n : 2 * n]
-    gh_ref, keep_ref, send_ref, sum_ref = refs[2 * n :]
+    gh_ref, both_ref, keep_ref, sum_ref = refs[2 * n :]
     half = keep_ref.shape[0] - PAD
     grad_w, grad_b = chunk_grads(w_ref, b_ref, h_ref, c_ref, gh_ref)
     sum_ref[...] = tree_sum([ref[...] for ref in gw_refs] + [grad_w])
@@ -173,19 +182,18 @@
     kept = sum_ref[pl.ds(pl.multiple_of(core * half, half), half), :]
     sent = sum_ref[pl.ds(pl.multiple_of((1 - core) * half, half), half), :]
     write_message(keep_ref, kept, bias)
-    write_message(send_ref, sent, bias)
+    at = gh_ref.shape[0]
+    both_ref[:at, :] = gh_ref[...]
+    write_message(both_ref.at[at:, :], sent, bias)
 
 
 def message_kernel(own_ref, other_ref, out_ref):
     own_w, own_b = read_message(own_ref)
-    other_w, other_b = read_message(other_ref)
+    other_w, other_b = read_message(other_ref.at[other_ref.shape[0] - own_ref.shape[0] :, :])
     write_message(out_ref, own_w + other_w, own_b + other_b)
 
 
-def last_kernel(n_parts, factor, own_ref, *refs):
-    part_refs = refs[:n_parts]
-    m00_ref, m10_ref, m01_ref, m11_ref, features_ref, weight_ref, bias_ref = refs[n_parts:]
-    sum_kernel(own_ref, *part_refs, features_ref)
+def last_kernel(factor, m00_ref, m10_ref, m01_ref, m11_ref, weight_ref, bias_ref):
     half = weight_ref.shape[0] // 2
     core = lax.axis_index("core")
     for k, (near_ref, far_ref) in enumerate(((m00_ref, m10_ref), (m01_ref, m11_ref))):
@@ -221,9 +229,11 @@
 
     steps = far_masks(n_far)
 
-    def far_pair(block):
-        blocks = [block, partner(block, "far", steps[0], n_far)]
+    def pack(*blocks):
         return call(pack_kernel, "pack", [shape(2 * tile, width)], blocks)[0]
+
+    def far_partner(block):
+        return partner(block, "far", steps[0], n_far)
 
     def far_chunks(pair):
         chunks = [pair]
@@ -252,81 +262,89 @@
     def from_row(parts):
         return [partner(part, "row", q + 1, n_row) for q, part in enumerate(parts)]
 
-    pair = far_pair(features)
-    (adjacency,) = call(
+    other = far_partner(features)
+    adjacency, features, cotangent = call(
         functools.partial(expand_kernel, n_loop, n_row, tile),
         "expand",
-        [shape(rows, n_loop * tile)],
-        (after(tile_rows, pair), counts, tile_values),
-        specs=[SMEM, SMEM, VMEM],
-    )
-    f00 = far_chunks(pair)
-    cot_pair = far_pair(after(cotangent, adjacency))
-    f00 = f00[:1] + [after(chunk, adjacency) for chunk in f00[1:]]
+        [shape(rows, n_loop * tile), shape(tile, width), shape(tile, width)],
+        (tile_rows, counts, tile_values, features, cotangent),
+        specs=[SMEM, SMEM] + [VMEM] * 3,
+    )
+    f00 = far_chunks(pack(features, other))
     f10 = [swap(chunk, "mid") for chunk in f00]
+    other_cot = far_partner(after(cotangent, f00[-1]))
     f01 = [swap(chunk, "core") for chunk in f00]
     f11 = [swap(chunk, "core") for chunk in f10]
     half = near_product(f00 + f01, "forward")
-    cots = far_chunks(after(cot_pair, half))
     own, *parts = rest_product(half, f10 + f11, "forward")
-    (hidden,) = call(
-        sum_kernel, "hidden", [shape(tile, width)], [after(own, *cots)] + from_row(parts)
-    )
-
-    hiddens = far_chunks(far_pair(hidden))
+    others = from_row(parts)
+    cots = far_chunks(pack(after(cotangent, own), other_cot))
+    (hidden,) = call(sum_kernel, "hidden", [shape(tile, width)], [after(own, other_cot)] + others)
+
+    hiddens = far_chunks(pack(hidden, far_partner(hidden)))
     bias_row = bias_vector.reshape(1, width)
     chunk_flops = 2 * tile * 6 * width * width
     g00, weight_sums, bias_sums = [], [], []
     sums = [shape(width, width, dtype=F32), shape(8, width, dtype=F32)]
-    for k, (chunk, cot) in enumerate(zip(hiddens[:-1], cots[:-1])):
-        outs = [shape(2 * tile, width)] + sums + [shape(tile, width)] * (k == 0)
-        gh, weight_sum, bias_sum, *rest = call(
-            chunk_kernel, "chunk", outs, [weight, bias_row, chunk, cot], flops=chunk_flops
+    for chunk, cot in zip(hiddens[:-1], cots[:-1]):
+        gh, weight_sum, bias_sum = call(
+            chunk_kernel,
+            "chunk",
+            [shape(2 * tile, width)] + sums,
+            [weight, bias_row, chunk, after(cot, cots[-1])],
+            flops=chunk_flops,
         )
         g00.append(gh)
         weight_sums.append(weight_sum)
         bias_sums.append(bias_sum)
-        output = output if k else rest[0]
     half_rows = width // 2 + PAD
-    gh, keep, send = call(
+    g01 = [swap(chunk, "core") for chunk in g00]
+    g10 = [swap(chunk, "mid") for chunk in g00]
+    gh, both, keep = call(
         functools.partial(last_chunk_kernel, len(g00)),
         "last_chunk",
-        [shape(2 * tile, width), shape(half_rows, width), shape(half_rows, width)],
-        [weight, bias_row, hiddens[-1], cots[-1]] + weight_sums + bias_sums,
+        [shape(2 * tile, width), shape(2 * tile + half_rows, width), shape(half_rows, width)],
+        [weight, bias_row, after(hiddens[-1], *g10), cots[-1]] + weight_sums + bias_sums,
         scratch=[pltpu.VMEM((width, width), F32)],
         flops=chunk_flops,
     )
     g00.append(gh)
-    g10 = [swap(chunk, "mid") for chunk in g00]
-    g01 = [swap(chunk, "core") for chunk in g00]
-    g11 = [swap(chunk, "core") for chunk in g10]
-    half = near_product(g00 + g01, "backward")
-    own, *parts = rest_product(half, g10 + g11, "backward")
-
-    (message,) = call(
-        message_kernel, "sum_core", [shape(half_rows, width)], [keep, swap(send, "core")]
-    )
+    g01.append(swap(both, "core"))
+    g10.append(swap(gh, "mid"))
+
+    (message,) = call(message_kernel, "sum_core", [shape(half_rows, width)], [keep, g01[-1]])
     bit = 1
     while bit < n_row:
         (message,) = call(
             message_kernel,
             "sum_row",
             [shape(half_rows, width)],
-            [after(message, own), partner(message, "row", bit, n_row)],
+            [message, partner(message, "row", bit, n_row)],
         )
         bit *= 2
+    g11 = [swap(chunk, "core") for chunk in g10[:-1] + [after(g10[-1], message)]]
+    output, half = call(
+        functools.partial(output_near_kernel, tile, n_row),
+        "backward_near",
+        [shape(tile, width), shape(rows, width, dtype=F32)],
+        [weight, bias_row, hidden, adjacency] + g00 + g01,
+        flops=flops,
+    )
+    own, *parts = rest_product(half, g10 + g11, "backward")
+    others = from_row(parts)
+    (grad_features,) = call(sum_kernel, "features_sum", [shape(tile, width)], [own] + others)
+    message = after(message, own)
     messages = [
         message,
         swap(message, "mid"),
         swap(message, "core"),
         lax.ppermute(message, ("mid", "core"), [(i, 3 - i) for i in range(4)]),
     ]
-    others = from_row(parts)
-    grad_features, weight_grad, bias_grad = call(
-        functools.partial(last_kernel, len(others), 1.0 / nodes**0.5),
+    weight_grad, bias_grad = call(
+        functools.partial(last_kernel, 1.0 / nodes**0.5),
         "last",
-        [shape(tile, width), shape(width, width, dtype=F32), shape(1, width, dtype=F32)],
-        [own] + others + messages,
+        [shape(width, width, dtype=F32), shape(1, width, dtype=F32)],
+        messages,
     )
     return output, grad_features, weight_grad, bias_grad.reshape(width)
 

time: 56.9 us -> 56.6 us (level)
  waiting for transfers between devices: 23.9 us -> 21.1 us
  local copies, waits for them, and re-layouts: 2.09 us -> 4.22 us
  Pallas kernels: 4.61 us -> 5.26 us
    ppermute x24 -> x23, waiting for transfers between devices: 23.9 us -> 21.1 us  [partner(): return lax.ppermute(x, axis, [(i, i ^ mask) for i in range(n)])]
    unnamed x14, local copies, waits for them, and re-layouts: 2.09 us -> 4.22 us
    pallas_call x14 -> x15, Pallas kernels: 4.61 us -> 5.26 us  [call(): pl.pallas_call(kernel, name=name, out_shape=outs, in_specs=specs or [VMEM...]
    ppermute x24 -> x23, starting transfers between devices: 24.6 us -> 24.2 us  [partner(): return lax.ppermute(x, axis, [(i, i ^ mask) for i in range(n)])]
  transfers between devices with their start and end apart: 25 -> 24, of which waited for: 11 -> 11; matrix products, arithmetic and copies ran while one was open for 0% -> 0% of each run, Pallas kernels for 7% -> 7%
where the time goes in v5:
time: 56.6 us; the launch traced here: 56.3 us
  starting transfers between devices  25 us (44%)
  waiting for transfers between devices  21.1 us (37%)
  Pallas kernels  5.26 us (9%)
  local copies, waits for them, and re-layouts  4.22 us (7%)
  between operations  0.79 us (1%)
    ppermute x23, starting transfers between devices, partner(): return lax.ppermute(x, axis, [(i, i ^ mask) for i in range(n)])  24.2 us
    ppermute x23, waiting for transfers between devices, partner(): return lax.ppermute(x, axis, [(i, i ^ mask) for i in range(n)])  21.1 us
    pallas_call x15, Pallas kernels, call(): pl.pallas_call(kernel, name=name, out_shape=outs, in_specs=specs or [VMEM...  5.26 us
    unnamed x14, local copies, waits for them, and re-layouts  4.22 us
  transfers between devices with their start and end apart: 24, of which 11 were waited for; matrix products, arithmetic and copies ran while one was open for 0% of the time, Pallas kernels for 7%

profile of v5, /device:TPU:0, one launch (start us, length us, event | category | flops | bytes accessed | tf_op | source)
XLA Modules:
  0.0 56.3 jit_solution(7430422342242059715)
XLA Ops:
  0.6 4.1 %collective-permute-start = (bf16[128,256]{1,0:T(8,128)(2,1)}, bf16[128,256]{1,0:T(8,128)(2,1)S(1)}, u32[]{:S(2)}, u32[]{:S(2)}) collective-permute-start(bf16[128,256]{1,0:T(8,128)(2,1)} %f_ref.1), channel_id=1, source_target_pairs={{0,16},{8,24},{16,0},{24,8},{1,17},{9,25},{17,1},{25,9},{2,18},{10... | collective-permute-start | bytes 196616 | tf_op jit(solution)/shard_map/ppermute | solution.py:21
  4.7 1.2 %copy-done.1 = bf16[32,128,128]{2,1,0:T(8,128)(2,1)S(1)} copy-done((bf16[32,128,128]{2,1,0:T(8,128)(2,1)S(1)}, bf16[32,128,128]{2,1,0:T(8,128)(2,1)}, u32[]{:S(2)}) %copy-start.1) | copy-done | bytes 1048600
  6.0 0.8 %copy-done.2 = bf16[128,256]{1,0:T(8,128)(2,1)S(1)} copy-done((bf16[128,256]{1,0:T(8,128)(2,1)S(1)}, bf16[128,256]{1,0:T(8,128)(2,1)}, u32[]{:S(2)}) %copy-start.2) | copy-done | bytes 65560
  6.8 0.8 %copy-done.3 = bf16[128,256]{1,0:T(8,128)(2,1)S(1)} copy-done((bf16[128,256]{1,0:T(8,128)(2,1)S(1)}, bf16[128,256]{1,0:T(8,128)(2,1)}, u32[]{:S(2)}) %copy-start.3) | copy-done | bytes 65560
  7.6 0.7 %copy-done.5 = s32[32]{0:T(128)S(1)} copy-done((s32[32]{0:T(128)S(1)}, s32[32]{0:T(128)}, u32[]{:S(2)}) %copy-start.5) | copy-done | bytes 152
  8.3 0.7 %copy-done.6 = s32[16]{0:T(128)S(1)} copy-done((s32[16]{0:T(128)S(1)}, s32[16]{0:T(128)}, u32[]{:S(2)}) %copy-start.6) | copy-done | bytes 88
  9.0 1.0 %expand.1 = (bf16[256,2048]{1,0:T(8,128)(2,1)S(1)}, bf16[128,256]{1,0:T(8,128)(2,1)S(1)}, bf16[128,256]{1,0:T(8,128)(2,1)S(1)}) custom-call(s32[32]{0:T(128)S(1)} %copy-done.5, s32[16]{0:T(128)S(1)} %copy-done.6, bf16[32,128,128]{2,1,0:T(8,128)(2,1)S(1)} %copy-done.1, bf16[128,256]{1,0:T(8,128)(2,1)S(1)} %copy-done.3, bf16[128,256]{1,0:T(8,128)(2,1)S(1)} %copy-done.2), custom_call_target="tpu_custom_call" | custom-call | bytes 2359488 | tf_op jit(solution)/shard_map/expand/pallas_call | solution.py:211
  10.0 1.6 %collective-permute-start.1 = (bf16[256,256]{1,0:T(8,128)(2,1)S(1)}, bf16[256,256]{1,0:T(8,128)(2,1)S(1)}, u32[]{:S(2)}, u32[]{:S(2)}) collective-permute-start(bf16[256,256]{1,0:T(8,128)(2,1)S(1)} %pack.3.refs_0_), channel_id=1, source_target_pairs={{0,8},{8,0},{16,24},{24,16},{1,9},{9,1},{17,25},{25,17},{2,10},{10... | collective-permute-start | bytes 393224 | tf_op jit(solution)/shard_map/ppermute | solution.py:21
  11.6 1.5 %collective-permute-start.4 = (bf16[256,256]{1,0:T(8,128)(2,1)S(1)}, bf16[256,256]{1,0:T(8,128)(2,1)S(1)}, u32[]{:S(2)}, u32[]{:S(2)}) collective-permute-start(bf16[256,256]{1,0:T(8,128)(2,1)S(1)} %pack.3.refs_0_), channel_id=1, source_target_pairs={{0,4},{4,0},{1,5},{5,1},{2,6},{6,2},{3,7},{7,3},{8,12},{12,8},{9,1... | collective-permute-start | bytes 393224 | tf_op jit(solution)/shard_map/ppermute | solution.py:21
  13.1 1.9 %collective-permute-done.1.refs_1_ = bf16[256,256]{1,0:T(8,128)(2,1)S(1)} collective-permute-done((bf16[256,256]{1,0:T(8,128)(2,1)S(1)}, bf16[256,256]{1,0:T(8,128)(2,1)S(1)}, u32[]{:S(2)}, u32[]{:S(2)}) %collective-permute-start.1) | collective-permute-done | bytes 131104 | tf_op jit(solution)/shard_map/ppermute | solution.py:21
  15.0 1.5 %collective-permute-start.5 = (bf16[256,256]{1,0:T(8,128)(2,1)S(1)}, bf16[256,256]{1,0:T(8,128)(2,1)S(1)}, u32[]{:S(2)}, u32[]{:S(2)}) collective-permute-start(bf16[256,256]{1,0:T(8,128)(2,1)S(1)} %collective-permute-done.1.refs_1_), channel_id=1, source_target_pairs={{0,4},{4,0},{1,5},{5,1},{2,6},{6,2},{3,7},{7,3},{8,12},{12,8},{9,1... | collective-permute-start | bytes 393224 | tf_op jit(solution)/shard_map/ppermute | solution.py:21
  17.2 2.8 %collective-permute-done.5.refs_1_ = bf16[256,256]{1,0:T(8,128)(2,1)S(1)} collective-permute-done((bf16[256,256]{1,0:T(8,128)(2,1)S(1)}, bf16[256,256]{1,0:T(8,128)(2,1)S(1)}, u32[]{:S(2)}, u32[]{:S(2)}) %collective-permute-start.5) | collective-permute-done | bytes 131104 | tf_op jit(solution)/shard_map/ppermute | solution.py:21
  20.0 1.0 %collective-permute-start.8 = (bf16[128,256]{1,0:T(8,128)(2,1)S(1)}, bf16[128,256]{1,0:T(8,128)(2,1)S(1)}, u32[]{:S(2)}, u32[]{:S(2)}) collective-permute-start(bf16[128,256]{1,0:T(8,128)(2,1)S(1)} %get-tuple-element.35.refs_0_), channel_id=1, source_target_pairs={{0,16},{8,24},{16,0},{24,8},{1,17},{9,25},{17,1},{25,9},{2,18},{10... | collective-permute-start | bytes 196616 | tf_op jit(solution)/shard_map/ppermute | solution.py:21
  21.6 1.6 %collective-permute-start.9 = (bf16[128,256]{1,0:T(8,128)(2,1)S(1)}, bf16[128,256]{1,0:T(8,128)(2,1)S(1)}, u32[]{:S(2)}, u32[]{:S(2)}) collective-permute-start(bf16[128,256]{1,0:T(8,128)(2,1)S(1)} %get-tuple-element.34), channel_id=1, source_target_pairs={{0,1},{1,0},{2,3},{3,2},{4,5},{5,4},{6,7},{7,6},{8,9},{9,8},{10,11... | collective-permute-start | bytes 196616 | tf_op jit(solution)/shard_map/ppermute | solution.py:21
  23.2 3.6 %collective-permute-done.8.refs_1_ = bf16[128,256]{1,0:T(8,128)(2,1)S(1)} collective-permute-done((bf16[128,256]{1,0:T(8,128)(2,1)S(1)}, bf16[128,256]{1,0:T(8,128)(2,1)S(1)}, u32[]{:S(2)}, u32[]{:S(2)}) %collective-permute-start.8) | collective-permute-done | bytes 65568 | tf_op jit(solution)/shard_map/ppermute | solution.py:21
  27.2 2.2 %collective-permute-start.10 = (bf16[128,256]{1,0:T(8,128)(2,1)S(1)}, bf16[128,256]{1,0:T(8,128)(2,1)S(1)}, u32[]{:S(2)}, u32[]{:S(2)}) collective-permute-start(bf16[128,256]{1,0:T(8,128)(2,1)S(1)} %hidden.1.refs_0_.h_ref), channel_id=1, source_target_pairs={{0,16},{8,24},{16,0},{24,8},{1,17},{9,25},{17,1},{25,9},{2,18},{10... | collective-permute-start | bytes 196616 | tf_op jit(solution)/shard_map/ppermute | solution.py:21
  29.4 3.5 %collective-permute-done.10.refs_1_ = bf16[128,256]{1,0:T(8,128)(2,1)S(1)} collective-permute-done((bf16[128,256]{1,0:T(8,128)(2,1)S(1)}, bf16[128,256]{1,0:T(8,128)(2,1)S(1)}, u32[]{:S(2)}, u32[]{:S(2)}) %collective-permute-start.10) | collective-permute-done | bytes 65568 | tf_op jit(solution)/shard_map/ppermute | solution.py:21
  32.9 1.6 %collective-permute-start.12 = (bf16[256,256]{1,0:T(8,128)(2,1)S(1)}, bf16[256,256]{1,0:T(8,128)(2,1)S(1)}, u32[]{:S(2)}, u32[]{:S(2)}) collective-permute-start(bf16[256,256]{1,0:T(8,128)(2,1)S(1)} %pack.4.h_ref), channel_id=1, source_target_pairs={{0,8},{8,0},{16,24},{24,16},{1,9},{9,1},{17,25},{25,17},{2,10},{10... | collective-permute-start | bytes 393224 | tf_op jit(solution)/shard_map/ppermute | solution.py:21
  35.0 1.6 %collective-permute-start.13 = (bf16[256,256]{1,0:T(8,128)(2,1)S(1)}, bf16[256,256]{1,0:T(8,128)(2,1)S(1)}, u32[]{:S(2)}, u32[]{:S(2)}) collective-permute-start(bf16[256,256]{1,0:T(8,128)(2,1)S(1)} %get-tuple-element.37.refs_0_), channel_id=1, source_target_pairs={{0,4},{4,0},{1,5},{5,1},{2,6},{6,2},{3,7},{7,3},{8,12},{12,8},{9,1... | collective-permute-start | bytes 393224 | tf_op jit(solution)/shard_map/ppermute | solution.py:21
  36.6 1.4 %collective-permute-done.12.h_ref = bf16[256,256]{1,0:T(8,128)(2,1)S(1)} collective-permute-done((bf16[256,256]{1,0:T(8,128)(2,1)S(1)}, bf16[256,256]{1,0:T(8,128)(2,1)S(1)}, u32[]{:S(2)}, u32[]{:S(2)}) %collective-permute-start.12) | collective-permute-done | bytes 131104 | tf_op jit(solution)/shard_map/ppermute | solution.py:21
  38.0 2.1 %collective-permute-done.13.refs_0_ = bf16[256,256]{1,0:T(8,128)(2,1)S(1)} collective-permute-done((bf16[256,256]{1,0:T(8,128)(2,1)S(1)}, bf16[256,256]{1,0:T(8,128)(2,1)S(1)}, u32[]{:S(2)}, u32[]{:S(2)}) %collective-permute-start.13) | collective-permute-done | bytes 131104 | tf_op jit(solution)/shard_map/ppermute | solution.py:21
  40.0 0.5 last_chunk.1
  40.7 1.6 %collective-permute-start.16 = (bf16[256,256]{1,0:T(8,128)(2,1)S(1)}, bf16[256,256]{1,0:T(8,128)(2,1)S(1)}, u32[]{:S(2)}, u32[]{:S(2)}) collective-permute-start(bf16[256,256]{1,0:T(8,128)(2,1)S(1)} %get-tuple-element.41.refs_1_), channel_id=1, source_target_pairs={{0,4},{4,0},{1,5},{5,1},{2,6},{6,2},{3,7},{7,3},{8,12},{12,8},{9,1... | collective-permute-start | bytes 393224 | tf_op jit(solution)/shard_map/ppermute | solution.py:21
  42.2 1.6 %collective-permute-start.18 = (bf16[144,256]{1,0:T(8,128)(2,1)S(1)}, bf16[144,256]{1,0:T(8,128)(2,1)S(1)}, u32[]{:S(2)}, u32[]{:S(2)}) collective-permute-start(bf16[144,256]{1,0:T(8,128)(2,1)S(1)} %sum_core.1.own_ref), channel_id=1, source_target_pairs={{0,1},{1,0},{2,3},{3,2},{4,5},{5,4},{6,7},{7,6},{8,9},{9,8},{10,11... | collective-permute-start | bytes 221192 | tf_op jit(solution)/shard_map/ppermute | solution.py:21
  44.3 2.3 %collective-permute-done.18.other_ref = bf16[144,256]{1,0:T(8,128)(2,1)S(1)} collective-permute-done((bf16[144,256]{1,0:T(8,128)(2,1)S(1)}, bf16[144,256]{1,0:T(8,128)(2,1)S(1)}, u32[]{:S(2)}, u32[]{:S(2)}) %collective-permute-start.18) | collective-permute-done | bytes 73760 | tf_op jit(solution)/shard_map/ppermute | solution.py:21
  46.8 0.9 %backward_near.1 = (bf16[128,256]{1,0:T(8,128)(2,1)}, f32[256,256]{1,0:T(8,128)S(1)}) custom-call(bf16[256,256]{1,0:T(8,128)(2,1)S(1)} %copy-done, f32[1,256]{1,0:T(1,128)S(1)} %bitcast.4, bf16[128,256]{1,0:T(8,128)(2,1)S(1)} %hidden.1.refs_0_.h_ref, bf16[256,2048]{1,0:T(8,128)(2,1)S(1)} %get-tuple-element.28.a_ref, ...), custom_call_target="tpu_custom_call" | custom-call | flops 134217728 | bytes 2171904 | tf_op jit(solution)/shard_map/backward_near/pallas_call | solution.py:211
  48.4 1.4 %collective-permute-start.21 = (bf16[144,256]{1,0:T(8,128)(2,1)S(1)}, bf16[144,256]{1,0:T(8,128)(2,1)S(1)}, u32[]{:S(2)}, u32[]{:S(2)}) collective-permute-start(bf16[144,256]{1,0:T(8,128)(2,1)S(1)} %sum_row.1.m00_ref), channel_id=1, source_target_pairs={{0,4},{4,0},{1,5},{5,1},{2,6},{6,2},{3,7},{7,3},{8,12},{12,8},{9,1... | collective-permute-start | bytes 221192 | tf_op jit(solution)/shard_map/ppermute | solution.py:21
  49.9 0.8 %collective-permute-start.23 = (bf16[144,256]{1,0:T(8,128)(2,1)S(1)}, bf16[144,256]{1,0:T(8,128)(2,1)S(1)}, u32[]{:S(2)}, u32[]{:S(2)}) collective-permute-start(bf16[144,256]{1,0:T(8,128)(2,1)S(1)} %sum_row.1.m00_ref), channel_id=1, source_target_pairs={{0,6},{2,4},{4,2},{6,0},{1,7},{3,5},{5,3},{7,1},{8,14},{10,12},{12... | collective-permute-start | bytes 221192 | tf_op jit(solution)/shard_map/ppermute | solution.py:341
  50.6 1.5 %collective-permute-start.20 = (bf16[128,256]{1,0:T(8,128)(2,1)S(1)}, bf16[128,256]{1,0:T(8,128)(2,1)S(1)}, u32[]{:S(2)}, u32[]{:S(2)}) collective-permute-start(bf16[128,256]{1,0:T(8,128)(2,1)S(1)} %get-tuple-element.48), channel_id=1, source_target_pairs={{0,1},{1,0},{2,3},{3,2},{4,5},{5,4},{6,7},{7,6},{8,9},{9,8},{10,11... | collective-permute-start | bytes 196616 | tf_op jit(solution)/shard_map/ppermute | solution.py:21
  52.2 2.7 %collective-permute-done.20.refs_0_ = bf16[128,256]{1,0:T(8,128)(2,1)S(1)} collective-permute-done((bf16[128,256]{1,0:T(8,128)(2,1)S(1)}, bf16[128,256]{1,0:T(8,128)(2,1)S(1)}, u32[]{:S(2)}, u32[]{:S(2)}) %collective-permute-start.20) | collective-permute-done | bytes 65568 | tf_op jit(solution)/shard_map/ppermute | solution.py:21
  54.9 0.6 %features_sum.1 = bf16[128,256]{1,0:T(8,128)(2,1)} custom-call(f32[128,256]{1,0:T(8,128)S(1)} %get-tuple-element.47.own_ref, bf16[128,256]{1,0:T(8,128)(2,1)S(1)} %collective-permute-done.20.refs_0_), custom_call_target="tpu_custom_call" | custom-call | bytes 262144 | tf_op jit(solution)/shard_map/features_sum/pallas_call | solution.py:211
  55.6 0.7 %last.1 = (f32[256,256]{1,0:T(8,128)}, f32[1,256]{1,0:T(1,128)}) custom-call(bf16[144,256]{1,0:T(8,128)(2,1)S(1)} %sum_row.1.m00_ref, bf16[144,256]{1,0:T(8,128)(2,1)S(1)} %collective-permute-done.21.m10_ref, bf16[144,256]{1,0:T(8,128)(2,1)S(1)} %collective-permute-done.22.m01_ref, bf16[144,256]{1,0:T(8,128)(2,1)S(1)} %collective-permute-done.23.m11_ref), custom_call_target="tpu_custom_call" | custom-call | bytes 558080 | tf_op jit(solution)/shard_map/last/pallas_call | solution.py:211
  (45 shorter events, 3.8 us)
Async XLA Ops:
  0.6 9.3 %collective-permute-start = (bf16[128,256]{1,0:T(8,128)(2,1)}, bf16[128,256]{1,0:T(8,128)(2,1)S(1)}, u32[]{:S(2)}, u32[]{:S(2)}) collective-permute-start(bf16[128,256]{1,0:T(8,128)(2,1)} %f_ref.1), channel_id=1, source_target_pairs={{0,16},{8,24},{16,0},{24,8},{1,17},{9,25},{17,1},{25,9},{2,18},{10... | collective-permute-start | bytes 196616 | tf_op jit(solution)/shard_map/ppermute | solution.py:21
  4.7 1.2 %copy-start.1 = (bf16[32,128,128]{2,1,0:T(8,128)(2,1)S(1)}, bf16[32,128,128]{2,1,0:T(8,128)(2,1)}, u32[]{:S(2)}) copy-start(bf16[32,128,128]{2,1,0:T(8,128)(2,1)} %tiles_ref.1) | copy-start | bytes 3145732
  6.0 0.8 %copy-start.2 = (bf16[128,256]{1,0:T(8,128)(2,1)S(1)}, bf16[128,256]{1,0:T(8,128)(2,1)}, u32[]{:S(2)}) copy-start(bf16[128,256]{1,0:T(8,128)(2,1)} %c_ref.1) | copy-start | bytes 196612
  6.8 0.8 %copy-start.3 = (bf16[128,256]{1,0:T(8,128)(2,1)S(1)}, bf16[128,256]{1,0:T(8,128)(2,1)}, u32[]{:S(2)}) copy-start(bf16[128,256]{1,0:T(8,128)(2,1)} %f_ref.1) | copy-start | bytes 196612
  7.6 0.7 %copy-start.5 = (s32[32]{0:T(128)S(1)}, s32[32]{0:T(128)}, u32[]{:S(2)}) copy-start(s32[32]{0:T(128)} %rows_ref.1) | copy-start | bytes 388
  8.3 0.7 %copy-start.6 = (s32[16]{0:T(128)S(1)}, s32[16]{0:T(128)}, u32[]{:S(2)}) copy-start(s32[16]{0:T(128)} %counts_ref.1) | copy-start | bytes 196
  10.0 5.0 %collective-permute-start.1 = (bf16[256,256]{1,0:T(8,128)(2,1)S(1)}, bf16[256,256]{1,0:T(8,128)(2,1)S(1)}, u32[]{:S(2)}, u32[]{:S(2)}) collective-permute-start(bf16[256,256]{1,0:T(8,128)(2,1)S(1)} %pack.3.refs_0_), channel_id=1, source_target_pairs={{0,8},{8,0},{16,24},{24,16},{1,9},{9,1},{17,25},{25,17},{2,10},{10... | collective-permute-start | bytes 393224 | tf_op jit(solution)/shard_map/ppermute | solution.py:21
  11.6 5.6 %collective-permute-start.4 = (bf16[256,256]{1,0:T(8,128)(2,1)S(1)}, bf16[256,256]{1,0:T(8,128)(2,1)S(1)}, u32[]{:S(2)}, u32[]{:S(2)}) collective-permute-start(bf16[256,256]{1,0:T(8,128)(2,1)S(1)} %pack.3.refs_0_), channel_id=1, source_target_pairs={{0,4},{4,0},{1,5},{5,1},{2,6},{6,2},{3,7},{7,3},{8,12},{12,8},{9,1... | collective-permute-start | bytes 393224 | tf_op jit(solution)/shard_map/ppermute | solution.py:21
  15.0 5.0 %collective-permute-start.5 = (bf16[256,256]{1,0:T(8,128)(2,1)S(1)}, bf16[256,256]{1,0:T(8,128)(2,1)S(1)}, u32[]{:S(2)}, u32[]{:S(2)}) collective-permute-start(bf16[256,256]{1,0:T(8,128)(2,1)S(1)} %collective-permute-done.1.refs_1_), channel_id=1, source_target_pairs={{0,4},{4,0},{1,5},{5,1},{2,6},{6,2},{3,7},{7,3},{8,12},{12,8},{9,1... | collective-permute-start | bytes 393224 | tf_op jit(solution)/shard_map/ppermute | solution.py:21
  16.5 4.4 %collective-permute-start.2 = (bf16[256,256]{1,0:T(8,128)(2,1)S(1)}, bf16[256,256]{1,0:T(8,128)(2,1)S(1)}, u32[]{:S(2)}, u32[]{:S(2)}) collective-permute-start(bf16[256,256]{1,0:T(8,128)(2,1)S(1)} %pack.3.refs_0_), channel_id=1, source_target_pairs={{0,2},{2,0},{1,3},{3,1},{4,6},{6,4},{5,7},{7,5},{8,10},{10,8},{9,1... | collective-permute-start | bytes 393224 | tf_op jit(solution)/shard_map/ppermute | solution.py:21
  16.5 4.4 %collective-permute-start.3 = (bf16[256,256]{1,0:T(8,128)(2,1)S(1)}, bf16[256,256]{1,0:T(8,128)(2,1)S(1)}, u32[]{:S(2)}, u32[]{:S(2)}) collective-permute-start(bf16[256,256]{1,0:T(8,128)(2,1)S(1)} %collective-permute-done.1.refs_1_), channel_id=1, source_target_pairs={{0,2},{2,0},{1,3},{3,1},{4,6},{6,4},{5,7},{7,5},{8,10},{10,8},{9,1... | collective-permute-start | bytes 393224 | tf_op jit(solution)/shard_map/ppermute | solution.py:21
  17.2 4.1 %collective-permute-start.6 = (bf16[256,256]{1,0:T(8,128)(2,1)S(1)}, bf16[256,256]{1,0:T(8,128)(2,1)S(1)}, u32[]{:S(2)}, u32[]{:S(2)}) collective-permute-start(bf16[256,256]{1,0:T(8,128)(2,1)S(1)} %collective-permute-done.4.refs_0_), channel_id=1, source_target_pairs={{0,2},{2,0},{1,3},{3,1},{4,6},{6,4},{5,7},{7,5},{8,10},{10,8},{9,1... | collective-permute-start | bytes 393224 | tf_op jit(solution)/shard_map/ppermute | solution.py:21
  20.0 1.3 %collective-permute-start.7 = (bf16[256,256]{1,0:T(8,128)(2,1)S(1)}, bf16[256,256]{1,0:T(8,128)(2,1)S(1)}, u32[]{:S(2)}, u32[]{:S(2)}) collective-permute-start(bf16[256,256]{1,0:T(8,128)(2,1)S(1)} %collective-permute-done.5.refs_1_), channel_id=1, source_target_pairs={{0,2},{2,0},{1,3},{3,1},{4,6},{6,4},{5,7},{7,5},{8,10},{10,8},{9,1... | collective-permute-start | bytes 393224 | tf_op jit(solution)/shard_map/ppermute | solution.py:21
  20.0 6.8 %collective-permute-start.8 = (bf16[128,256]{1,0:T(8,128)(2,1)S(1)}, bf16[128,256]{1,0:T(8,128)(2,1)S(1)}, u32[]{:S(2)}, u32[]{:S(2)}) collective-permute-start(bf16[128,256]{1,0:T(8,128)(2,1)S(1)} %get-tuple-element.35.refs_0_), channel_id=1, source_target_pairs={{0,16},{8,24},{16,0},{24,8},{1,17},{9,25},{17,1},{25,9},{2,18},{10... | collective-permute-start | bytes 196616 | tf_op jit(solution)/shard_map/ppermute | solution.py:21
  21.6 5.5 %collective-permute-start.9 = (bf16[128,256]{1,0:T(8,128)(2,1)S(1)}, bf16[128,256]{1,0:T(8,128)(2,1)S(1)}, u32[]{:S(2)}, u32[]{:S(2)}) collective-permute-start(bf16[128,256]{1,0:T(8,128)(2,1)S(1)} %get-tuple-element.34), channel_id=1, source_target_pairs={{0,1},{1,0},{2,3},{3,2},{4,5},{5,4},{6,7},{7,6},{8,9},{9,8},{10,11... | collective-permute-start | bytes 196616 | tf_op jit(solution)/shard_map/ppermute | solution.py:21
  26.8 7.7 %collective-permute-start.11 = (bf16[256,256]{1,0:T(8,128)(2,1)S(1)}, bf16[256,256]{1,0:T(8,128)(2,1)S(1)}, u32[]{:S(2)}, u32[]{:S(2)}) collective-permute-start(bf16[256,256]{1,0:T(8,128)(2,1)S(1)} %pack.5.c_ref), channel_id=1, source_target_pairs={{0,8},{8,0},{16,24},{24,16},{1,9},{9,1},{17,25},{25,17},{2,10},{10... | collective-permute-start | bytes 393224 | tf_op jit(solution)/shard_map/ppermute | solution.py:21
  27.2 7.4 %copy-start = (bf16[256,256]{1,0:T(8,128)(2,1)S(1)}, bf16[256,256]{1,0:T(8,128)(2,1)}, u32[]{:S(2)}) copy-start(bf16[256,256]{1,0:T(8,128)(2,1)} %w_ref.5) | copy-start | bytes 393220
  27.2 5.7 %collective-permute-start.10 = (bf16[128,256]{1,0:T(8,128)(2,1)S(1)}, bf16[128,256]{1,0:T(8,128)(2,1)S(1)}, u32[]{:S(2)}, u32[]{:S(2)}) collective-permute-start(bf16[128,256]{1,0:T(8,128)(2,1)S(1)} %hidden.1.refs_0_.h_ref), channel_id=1, source_target_pairs={{0,16},{8,24},{16,0},{24,8},{1,17},{9,25},{17,1},{25,9},{2,18},{10... | collective-permute-start | bytes 196616 | tf_op jit(solution)/shard_map/ppermute | solution.py:21
  32.9 1.6 %copy-start.4 = (f32[256]{0:T(256)S(1)}, f32[256]{0:T(256)}, u32[]{:S(2)}) copy-start(f32[256]{0:T(256)} %param.9) | copy-start | bytes 3076
  32.9 5.0 %collective-permute-start.12 = (bf16[256,256]{1,0:T(8,128)(2,1)S(1)}, bf16[256,256]{1,0:T(8,128)(2,1)S(1)}, u32[]{:S(2)}, u32[]{:S(2)}) collective-permute-start(bf16[256,256]{1,0:T(8,128)(2,1)S(1)} %pack.4.h_ref), channel_id=1, source_target_pairs={{0,8},{8,0},{16,24},{24,16},{1,9},{9,1},{17,25},{25,17},{2,10},{10... | collective-permute-start | bytes 393224 | tf_op jit(solution)/shard_map/ppermute | solution.py:21
  35.0 5.0 %collective-permute-start.13 = (bf16[256,256]{1,0:T(8,128)(2,1)S(1)}, bf16[256,256]{1,0:T(8,128)(2,1)S(1)}, u32[]{:S(2)}, u32[]{:S(2)}) collective-permute-start(bf16[256,256]{1,0:T(8,128)(2,1)S(1)} %get-tuple-element.37.refs_0_), channel_id=1, source_target_pairs={{0,4},{4,0},{1,5},{5,1},{2,6},{6,2},{3,7},{7,3},{8,12},{12,8},{9,1... | collective-permute-start | bytes 393224 | tf_op jit(solution)/shard_map/ppermute | solution.py:21
  40.6 1.6 %collective-permute-start.15 = (bf16[400,256]{1,0:T(8,128)(2,1)S(1)}, bf16[400,256]{1,0:T(8,128)(2,1)S(1)}, u32[]{:S(2)}, u32[]{:S(2)}) collective-permute-start(bf16[400,256]{1,0:T(8,128)(2,1)S(1)} %get-tuple-element.42), channel_id=1, source_target_pairs={{0,2},{2,0},{1,3},{3,1},{4,6},{6,4},{5,7},{7,5},{8,10},{10,8},{9,1... | collective-permute-start | bytes 614408 | tf_op jit(solution)/shard_map/ppermute | solution.py:21
  40.7 6.0 %collective-permute-start.16 = (bf16[256,256]{1,0:T(8,128)(2,1)S(1)}, bf16[256,256]{1,0:T(8,128)(2,1)S(1)}, u32[]{:S(2)}, u32[]{:S(2)}) collective-permute-start(bf16[256,256]{1,0:T(8,128)(2,1)S(1)} %get-tuple-element.41.refs_1_), channel_id=1, source_target_pairs={{0,4},{4,0},{1,5},{5,1},{2,6},{6,2},{3,7},{7,3},{8,12},{12,8},{9,1... | collective-permute-start | bytes 393224 | tf_op jit(solution)/shard_map/ppermute | solution.py:21
  42.2 4.4 %collective-permute-start.18 = (bf16[144,256]{1,0:T(8,128)(2,1)S(1)}, bf16[144,256]{1,0:T(8,128)(2,1)S(1)}, u32[]{:S(2)}, u32[]{:S(2)}) collective-permute-start(bf16[144,256]{1,0:T(8,128)(2,1)S(1)} %sum_core.1.own_ref), channel_id=1, source_target_pairs={{0,1},{1,0},{2,3},{3,2},{4,5},{5,4},{6,7},{7,6},{8,9},{9,8},{10,11... | collective-permute-start | bytes 221192 | tf_op jit(solution)/shard_map/ppermute | solution.py:21
  43.8 3.0 %collective-permute-start.14 = (bf16[256,256]{1,0:T(8,128)(2,1)S(1)}, bf16[256,256]{1,0:T(8,128)(2,1)S(1)}, u32[]{:S(2)}, u32[]{:S(2)}) collective-permute-start(bf16[256,256]{1,0:T(8,128)(2,1)S(1)} %get-tuple-element.37.refs_0_), channel_id=1, source_target_pairs={{0,2},{2,0},{1,3},{3,1},{4,6},{6,4},{5,7},{7,5},{8,10},{10,8},{9,1... | collective-permute-start | bytes 393224 | tf_op jit(solution)/shard_map/ppermute | solution.py:21
  43.8 3.8 %collective-permute-start.17 = (bf16[256,256]{1,0:T(8,128)(2,1)S(1)}, bf16[256,256]{1,0:T(8,128)(2,1)S(1)}, u32[]{:S(2)}, u32[]{:S(2)}) collective-permute-start(bf16[256,256]{1,0:T(8,128)(2,1)S(1)} %collective-permute-done.13.refs_0_), channel_id=1, source_target_pairs={{0,2},{2,0},{1,3},{3,1},{4,6},{6,4},{5,7},{7,5},{8,10},{10,8},{9,1... | collective-permute-start | bytes 393224 | tf_op jit(solution)/shard_map/ppermute | solution.py:21
  46.7 1.4 %collective-permute-start.19 = (bf16[256,256]{1,0:T(8,128)(2,1)S(1)}, bf16[256,256]{1,0:T(8,128)(2,1)S(1)}, u32[]{:S(2)}, u32[]{:S(2)}) collective-permute-start(bf16[256,256]{1,0:T(8,128)(2,1)S(1)} %collective-permute-done.16.refs_1_), channel_id=1, source_target_pairs={{0,2},{2,0},{1,3},{3,1},{4,6},{6,4},{5,7},{7,5},{8,10},{10,8},{9,1... | collective-permute-start | bytes 393224 | tf_op jit(solution)/shard_map/ppermute | solution.py:21
  48.4 7.1 %collective-permute-start.21 = (bf16[144,256]{1,0:T(8,128)(2,1)S(1)}, bf16[144,256]{1,0:T(8,128)(2,1)S(1)}, u32[]{:S(2)}, u32[]{:S(2)}) collective-permute-start(bf16[144,256]{1,0:T(8,128)(2,1)S(1)} %sum_row.1.m00_ref), channel_id=1, source_target_pairs={{0,4},{4,0},{1,5},{5,1},{2,6},{6,2},{3,7},{7,3},{8,12},{12,8},{9,1... | collective-permute-start | bytes 221192 | tf_op jit(solution)/shard_map/ppermute | solution.py:21
  49.9 5.7 %collective-permute-start.22 = (bf16[144,256]{1,0:T(8,128)(2,1)S(1)}, bf16[144,256]{1,0:T(8,128)(2,1)S(1)}, u32[]{:S(2)}, u32[]{:S(2)}) collective-permute-start(bf16[144,256]{1,0:T(8,128)(2,1)S(1)} %sum_row.1.m00_ref), channel_id=1, source_target_pairs={{0,2},{2,0},{1,3},{3,1},{4,6},{6,4},{5,7},{7,5},{8,10},{10,8},{9,1... | collective-permute-start | bytes 221192 | tf_op jit(solution)/shard_map/ppermute | solution.py:21
  49.9 5.7 %collective-permute-start.23 = (bf16[144,256]{1,0:T(8,128)(2,1)S(1)}, bf16[144,256]{1,0:T(8,128)(2,1)S(1)}, u32[]{:S(2)}, u32[]{:S(2)}) collective-permute-start(bf16[144,256]{1,0:T(8,128)(2,1)S(1)} %sum_row.1.m00_ref), channel_id=1, source_target_pairs={{0,6},{2,4},{4,2},{6,0},{1,7},{3,5},{5,3},{7,1},{8,14},{10,12},{12... | collective-permute-start | bytes 221192 | tf_op jit(solution)/shard_map/ppermute | solution.py:341
  50.6 4.3 %collective-permute-start.20 = (bf16[128,256]{1,0:T(8,128)(2,1)S(1)}, bf16[128,256]{1,0:T(8,128)(2,1)S(1)}, u32[]{:S(2)}, u32[]{:S(2)}) collective-permute-start(bf16[128,256]{1,0:T(8,128)(2,1)S(1)} %get-tuple-element.48), channel_id=1, source_target_pairs={{0,1},{1,0},{2,3},{3,2},{4,5},{5,4},{6,7},{7,6},{8,9},{9,8},{10,11... | collective-permute-start | bytes 196616 | tf_op jit(solution)/shard_map/ppermute | solution.py:21

commit v6 on v5

--- a/solution.py
+++ b/solution.py
@@ -59,11 +59,28 @@
 
 
 def expand_kernel(
-    n_loop, n_row, tile, rows_ref, counts_ref, tiles_ref, f_ref, c_ref, out_ref, f_out, c_out
+    n_loop, n_row, tile, rows_hbm, counts_hbm, tiles_hbm, f_hbm, c_hbm, out_ref, f_out, c_out,
+    rows_ref, counts_ref, tiles_ref, sems,
 ):
+    copies = [
+        pltpu.make_async_copy(source, target, sems.at[k])
+        for k, (source, target) in enumerate(
+            (
+                (rows_hbm, rows_ref),
+                (counts_hbm, counts_ref),
+                (tiles_hbm, tiles_ref),
+                (f_hbm, f_out),
+                (c_hbm, c_out),
+            )
+        )
+    ]
+    for copy in copies:
+        copy.start()
     n_far = n_loop // 4
     my_row, my_far = lax.axis_index("row"), lax.axis_index("far")
     my_near = 2 * lax.axis_index("mid") + lax.axis_index("core")
+    for copy in copies:
+        copy.wait()
 
     def body(j, carry):
         near = jnp.bitwise_xor(lax.rem(j, 4), my_near)
@@ -80,8 +97,6 @@
         return carry
 
     lax.fori_loop(0, n_loop, body, 0)
-    f_out[...] = f_ref[...]
-    c_out[...] = c_ref[...]
 
 
 def product_rows(a_ref, first, block_refs, rows):
@@ -105,10 +120,9 @@
         out_ref[rows, :] = product_rows(a_ref, 0, block_refs, rows)
 
 
-def output_near_kernel(tile, n_row, w_ref, b_ref, h_ref, a_ref, *refs):
+def output_kernel(w_ref, b_ref, h_ref, out_ref):
     preact = dot(h_ref[...], w_ref[...]) + b_ref[...]
-    refs[-2][...] = (preact * sigmoid(preact)).astype(BF16)
-    near_kernel(tile, n_row, a_ref, *refs[:-2], refs[-1])
+    out_ref[...] = (preact * sigmoid(preact)).astype(BF16)
 
 
 def rest_kernel(tile, n_row, n_blocks, a_ref, half_ref, *refs):
@@ -193,7 +207,9 @@
     write_message(out_ref, own_w + other_w, own_b + other_b)
 
 
-def last_kernel(factor, m00_ref, m10_ref, m01_ref, m11_ref, weight_ref, bias_ref):
+def last_kernel(factor, m00_ref, m10_ref, m01_ref, m11_ref, *refs):
+    weight_ref, bias_ref, features_ref = refs[-3:]
+    sum_kernel(*refs[:-3], features_ref)
     half = weight_ref.shape[0] // 2
     core = lax.axis_index("core")
     for k, (near_ref, far_ref) in enumerate(((m00_ref, m10_ref), (m01_ref, m11_ref))):
@@ -207,7 +223,9 @@
 
 def call(kernel, name, outs, operands, scratch=(), specs=None, flops=0):
     size = sum(o.size * o.dtype.itemsize for o in list(operands) + list(outs))
-    held = size + sum(math.prod(s.shape) * jnp.dtype(s.dtype).itemsize for s in scratch)
+    held = size + sum(
+        math.prod(s.shape) * s.dtype.itemsize for s in scratch if hasattr(s.dtype, "itemsize")
+    )
     return pl.pallas_call(
         kernel,
         name=name,
@@ -267,8 +285,17 @@
         functools.partial(expand_kernel, n_loop, n_row, tile),
         "expand",
         [shape(rows, n_loop * tile), shape(tile, width), shape(tile, width)],
-        (tile_rows, counts, tile_values, features, cotangent),
-        specs=[SMEM, SMEM] + [VMEM] * 3,
+        [
+            pltpu.with_memory_space_constraint(x, pltpu.HBM)
+            for x in (tile_rows, counts, tile_values, features, cotangent)
+        ],
+        scratch=[
+            pltpu.SMEM(tile_rows.shape, jnp.int32),
+            pltpu.SMEM(counts.shape, jnp.int32),
+            pltpu.VMEM(tile_values.shape, BF16),
+            pltpu.SemaphoreType.DMA((5,)),
+        ],
+        specs=[pl.BlockSpec(memory_space=pltpu.HBM)] * 5,
     )
     f00 = far_chunks(pack(features, other))
     f10 = [swap(chunk, "mid") for chunk in f00]
@@ -281,8 +308,12 @@
     cots = far_chunks(pack(after(cotangent, own), other_cot))
     (hidden,) = call(sum_kernel, "hidden", [shape(tile, width)], [after(own, other_cot)] + others)
 
-    hiddens = far_chunks(pack(hidden, far_partner(hidden)))
     bias_row = bias_vector.reshape(1, width)
+    (output,) = call(
+        output_kernel, "output", [shape(tile, width)], [weight, bias_row, hidden]
+    )
+    other, hidden = far_partner(hidden), after(hidden, output)
+    hiddens = far_chunks(pack(hidden, other))
     chunk_flops = 2 * tile * 6 * width * width
     g00, weight_sums, bias_sums = [], [], []
     sums = [shape(width, width, dtype=F32), shape(8, width, dtype=F32)]
@@ -304,12 +335,12 @@
         functools.partial(last_chunk_kernel, len(g00)),
         "last_chunk",
         [shape(2 * tile, width), shape(2 * tile + half_rows, width), shape(half_rows, width)],
-        [weight, bias_row, after(hiddens[-1], *g10), cots[-1]] + weight_sums + bias_sums,
+        [weight, bias_row, hiddens[-1], cots[-1]] + weight_sums + bias_sums,
         scratch=[pltpu.VMEM((width, width), F32)],
         flops=chunk_flops,
     )
     g00.append(gh)
-    g01.append(swap(both, "core"))
+    g01.append(swap(after(both, *g10), "core"))
     g10.append(swap(gh, "mid"))
 
     (message,) = call(message_kernel, "sum_core", [shape(half_rows, width)], [keep, g01[-1]])
@@ -323,16 +354,9 @@
         )
         bit *= 2
     g11 = [swap(chunk, "core") for chunk in g10[:-1] + [after(g10[-1], message)]]
-    output, half = call(
-        functools.partial(output_near_kernel, tile, n_row),
-        "backward_near",
-        [shape(tile, width), shape(rows, width, dtype=F32)],
-        [weight, bias_row, hidden, adjacency] + g00 + g01,
-        flops=flops,
-    )
+    half = near_product(g00 + g01, "backward")
     own, *parts = rest_product(half, g10 + g11, "backward")
     others = from_row(parts)
-    (grad_features,) = call(sum_kernel, "features_sum", [shape(tile, width)], [own] + others)
     message = after(message, own)
     messages = [
         message,
@@ -340,11 +364,11 @@
         swap(message, "core"),
         lax.ppermute(message, ("mid", "core"), [(i, 3 - i) for i in range(4)]),
     ]
-    weight_grad, bias_grad = call(
+    weight_grad, bias_grad, grad_features = call(
         functools.partial(last_kernel, 1.0 / nodes**0.5),
         "last",
-        [shape(width, width, dtype=F32), shape(1, width, dtype=F32)],
-        messages,
+        [shape(width, width, dtype=F32), shape(1, width, dtype=F32), shape(tile, width)],
+        messages + [own] + others,
     )
     return output, grad_features, weight_grad, bias_grad.reshape(width)
 

time: 56.6 us -> 55.2 us (0.975)
  local copies, waits for them, and re-layouts: 4.22 us -> 0.01 us
  starting transfers between devices: 25 us -> 28.1 us
    unnamed x14 -> x4, local copies, waits for them, and re-layouts: 4.22 us -> 0.01 us
    ppermute x23, starting transfers between devices: 24.2 us -> 27.3 us  [partner(): return lax.ppermute(x, axis, [(i, i ^ mask) for i in range(n)])]
  transfers between devices with their start and end apart: 24 -> 24, of which waited for: 11 -> 10; matrix products, arithmetic and copies ran while one was open for 0% -> 0% of each run, Pallas kernels for 7% -> 8%
where the time goes in v6:
time: 55.2 us; the launch traced here: 55 us
  starting transfers between devices  28.1 us (51%)
  waiting for transfers between devices  20.6 us (37%)
  Pallas kernels  5.6 us (10%)
  between operations  0.79 us (1%)
    ppermute x23, starting transfers between devices, partner(): return lax.ppermute(x, axis, [(i, i ^ mask) for i in range(n)])  27.3 us
    ppermute x23, waiting for transfers between devices, partner(): return lax.ppermute(x, axis, [(i, i ^ mask) for i in range(n)])  20.6 us
    pallas_call x15, Pallas kernels, call(): pl.pallas_call(kernel, name=name, out_shape=outs, in_specs=specs or [VMEM...  5.6 us
  transfers between devices with their start and end apart: 24, of which 10 were waited for; matrix products, arithmetic and copies ran while one was open for 0% of the time, Pallas kernels for 8%

profile of v6, /device:TPU:0, one launch (start us, length us, event | category | flops | bytes accessed | tf_op | source)
XLA Modules:
  0.0 55.0 jit_solution(11744441681346690649)
XLA Ops:
  0.6 4.1 %collective-permute-start = (bf16[128,256]{1,0:T(8,128)(2,1)}, bf16[128,256]{1,0:T(8,128)(2,1)S(1)}, u32[]{:S(2)}, u32[]{:S(2)}) collective-permute-start(bf16[128,256]{1,0:T(8,128)(2,1)} %f_hbm.1), channel_id=1, source_target_pairs={{0,16},{8,24},{16,0},{24,8},{1,17},{9,25},{17,1},{25,9},{2,18},{10... | collective-permute-start | bytes 196616 | tf_op jit(solution)/shard_map/ppermute | solution.py:21
  4.7 1.7 %expand.1 = (bf16[256,2048]{1,0:T(8,128)(2,1)S(1)}, bf16[128,256]{1,0:T(8,128)(2,1)S(1)}, bf16[128,256]{1,0:T(8,128)(2,1)S(1)}) custom-call(s32[32]{0:T(128)} %rows_hbm.1, s32[16]{0:T(128)} %counts_hbm.1, bf16[32,128,128]{2,1,0:T(8,128)(2,1)} %tiles_hbm.1, bf16[128,256]{1,0:T(8,128)(2,1)} %f_hbm.1, bf16[128,256]{1,0:T(8,128)(2,1)} %c_hbm.1), custom_call_target="tpu_custom_call" | custom-call | bytes 2359488 | tf_op jit(solution)/shard_map/expand/pallas_call | solution.py:229
  6.4 2.2 %collective-permute-done.refs_1_ = bf16[128,256]{1,0:T(8,128)(2,1)S(1)} collective-permute-done((bf16[128,256]{1,0:T(8,128)(2,1)}, bf16[128,256]{1,0:T(8,128)(2,1)S(1)}, u32[]{:S(2)}, u32[]{:S(2)}) %collective-permute-start) | collective-permute-done | bytes 65568 | tf_op jit(solution)/shard_map/ppermute | solution.py:21
  8.6 0.7 %collective-permute-start.1 = (bf16[256,256]{1,0:T(8,128)(2,1)S(1)}, bf16[256,256]{1,0:T(8,128)(2,1)S(1)}, u32[]{:S(2)}, u32[]{:S(2)}) collective-permute-start(bf16[256,256]{1,0:T(8,128)(2,1)S(1)} %pack.3.refs_0_), channel_id=1, source_target_pairs={{0,8},{8,0},{16,24},{24,16},{1,9},{9,1},{17,25},{25,17},{2,10},{10... | collective-permute-start | bytes 393224 | tf_op jit(solution)/shard_map/ppermute | solution.py:21
  9.3 1.5 %collective-permute-start.4 = (bf16[256,256]{1,0:T(8,128)(2,1)S(1)}, bf16[256,256]{1,0:T(8,128)(2,1)S(1)}, u32[]{:S(2)}, u32[]{:S(2)}) collective-permute-start(bf16[256,256]{1,0:T(8,128)(2,1)S(1)} %pack.3.refs_0_), channel_id=1, source_target_pairs={{0,4},{4,0},{1,5},{5,1},{2,6},{6,2},{3,7},{7,3},{8,12},{12,8},{9,1... | collective-permute-start | bytes 393224 | tf_op jit(solution)/shard_map/ppermute | solution.py:21
  10.8 2.8 %collective-permute-done.1.refs_1_ = bf16[256,256]{1,0:T(8,128)(2,1)S(1)} collective-permute-done((bf16[256,256]{1,0:T(8,128)(2,1)S(1)}, bf16[256,256]{1,0:T(8,128)(2,1)S(1)}, u32[]{:S(2)}, u32[]{:S(2)}) %collective-permute-start.1) | collective-permute-done | bytes 131104 | tf_op jit(solution)/shard_map/ppermute | solution.py:21
  13.6 1.7 %collective-permute-start.5 = (bf16[256,256]{1,0:T(8,128)(2,1)S(1)}, bf16[256,256]{1,0:T(8,128)(2,1)S(1)}, u32[]{:S(2)}, u32[]{:S(2)}) collective-permute-start(bf16[256,256]{1,0:T(8,128)(2,1)S(1)} %collective-permute-done.1.refs_1_), channel_id=1, source_target_pairs={{0,4},{4,0},{1,5},{5,1},{2,6},{6,2},{3,7},{7,3},{8,12},{12,8},{9,1... | collective-permute-start | bytes 393224 | tf_op jit(solution)/shard_map/ppermute | solution.py:21
  15.3 0.5 collective-permute-start.3
  15.9 2.8 %collective-permute-done.5.refs_1_ = bf16[256,256]{1,0:T(8,128)(2,1)S(1)} collective-permute-done((bf16[256,256]{1,0:T(8,128)(2,1)S(1)}, bf16[256,256]{1,0:T(8,128)(2,1)S(1)}, u32[]{:S(2)}, u32[]{:S(2)}) %collective-permute-start.5) | collective-permute-done | bytes 131104 | tf_op jit(solution)/shard_map/ppermute | solution.py:21
  18.6 2.3 %collective-permute-start.8 = (bf16[128,256]{1,0:T(8,128)(2,1)S(1)}, bf16[128,256]{1,0:T(8,128)(2,1)S(1)}, u32[]{:S(2)}, u32[]{:S(2)}) collective-permute-start(bf16[128,256]{1,0:T(8,128)(2,1)S(1)} %get-tuple-element.36.refs_0_), channel_id=1, source_target_pairs={{0,16},{8,24},{16,0},{24,8},{1,17},{9,25},{17,1},{25,9},{2,18},{10... | collective-permute-start | bytes 196616 | tf_op jit(solution)/shard_map/ppermute | solution.py:21
  21.6 1.6 %collective-permute-start.9 = (bf16[128,256]{1,0:T(8,128)(2,1)S(1)}, bf16[128,256]{1,0:T(8,128)(2,1)S(1)}, u32[]{:S(2)}, u32[]{:S(2)}) collective-permute-start(bf16[128,256]{1,0:T(8,128)(2,1)S(1)} %get-tuple-element.34), channel_id=1, source_target_pairs={{0,1},{1,0},{2,3},{3,2},{4,5},{5,4},{6,7},{7,6},{8,9},{9,8},{10,11... | collective-permute-start | bytes 196616 | tf_op jit(solution)/shard_map/ppermute | solution.py:21
  23.2 2.3 %collective-permute-done.8.refs_1_ = bf16[128,256]{1,0:T(8,128)(2,1)S(1)} collective-permute-done((bf16[128,256]{1,0:T(8,128)(2,1)S(1)}, bf16[128,256]{1,0:T(8,128)(2,1)S(1)}, u32[]{:S(2)}, u32[]{:S(2)}) %collective-permute-start.8) | collective-permute-done | bytes 65568 | tf_op jit(solution)/shard_map/ppermute | solution.py:21
  25.4 0.5 collective-permute-start.12
  26.0 3.4 %collective-permute-start.10 = (bf16[128,256]{1,0:T(8,128)(2,1)S(1)}, bf16[128,256]{1,0:T(8,128)(2,1)S(1)}, u32[]{:S(2)}, u32[]{:S(2)}) collective-permute-start(bf16[128,256]{1,0:T(8,128)(2,1)S(1)} %hidden.1.h_ref.refs_0_), channel_id=1, source_target_pairs={{0,16},{8,24},{16,0},{24,8},{1,17},{9,25},{17,1},{25,9},{2,18},{10... | collective-permute-start | bytes 196616 | tf_op jit(solution)/shard_map/ppermute | solution.py:21
  29.4 0.8 %output.1 = bf16[128,256]{1,0:T(8,128)(2,1)} custom-call(bf16[256,256]{1,0:T(8,128)(2,1)S(1)} %copy-done, f32[1,256]{1,0:T(1,128)S(1)} %bitcast.2, bf16[128,256]{1,0:T(8,128)(2,1)S(1)} %hidden.1.h_ref.refs_0_), custom_call_target="tpu_custom_call" | custom-call | bytes 263168 | tf_op jit(solution)/shard_map/output/pallas_call | solution.py:229
  30.2 1.5 %collective-permute-done.10.refs_1_ = bf16[128,256]{1,0:T(8,128)(2,1)S(1)} collective-permute-done((bf16[128,256]{1,0:T(8,128)(2,1)S(1)}, bf16[128,256]{1,0:T(8,128)(2,1)S(1)}, u32[]{:S(2)}, u32[]{:S(2)}) %collective-permute-start.10) | collective-permute-done | bytes 65568 | tf_op jit(solution)/shard_map/ppermute | solution.py:21
  31.7 2.8 %collective-permute-start.11 = (bf16[256,256]{1,0:T(8,128)(2,1)S(1)}, bf16[256,256]{1,0:T(8,128)(2,1)S(1)}, u32[]{:S(2)}, u32[]{:S(2)}) collective-permute-start(bf16[256,256]{1,0:T(8,128)(2,1)S(1)} %pack.4.h_ref), channel_id=1, source_target_pairs={{0,8},{8,0},{16,24},{24,16},{1,9},{9,1},{17,25},{25,17},{2,10},{10... | collective-permute-start | bytes 393224 | tf_op jit(solution)/shard_map/ppermute | solution.py:21
  34.5 0.5 chunk.1
  35.0 1.6 %collective-permute-start.13 = (bf16[256,256]{1,0:T(8,128)(2,1)S(1)}, bf16[256,256]{1,0:T(8,128)(2,1)S(1)}, u32[]{:S(2)}, u32[]{:S(2)}) collective-permute-start(bf16[256,256]{1,0:T(8,128)(2,1)S(1)} %get-tuple-element.42.refs_0_), channel_id=1, source_target_pairs={{0,4},{4,0},{1,5},{5,1},{2,6},{6,2},{3,7},{7,3},{8,12},{12,8},{9,1... | collective-permute-start | bytes 393224 | tf_op jit(solution)/shard_map/ppermute | solution.py:21
  36.5 1.2 %collective-permute-done.11.h_ref = bf16[256,256]{1,0:T(8,128)(2,1)S(1)} collective-permute-done((bf16[256,256]{1,0:T(8,128)(2,1)S(1)}, bf16[256,256]{1,0:T(8,128)(2,1)S(1)}, u32[]{:S(2)}, u32[]{:S(2)}) %collective-permute-start.11) | collective-permute-done | bytes 131104 | tf_op jit(solution)/shard_map/ppermute | solution.py:21
  37.7 0.5 last_chunk.1
  38.3 1.8 %collective-permute-done.13.refs_0_ = bf16[256,256]{1,0:T(8,128)(2,1)S(1)} collective-permute-done((bf16[256,256]{1,0:T(8,128)(2,1)S(1)}, bf16[256,256]{1,0:T(8,128)(2,1)S(1)}, u32[]{:S(2)}, u32[]{:S(2)}) %collective-permute-start.13) | collective-permute-done | bytes 131104 | tf_op jit(solution)/shard_map/ppermute | solution.py:21
  40.0 1.5 %collective-permute-start.17 = (bf16[256,256]{1,0:T(8,128)(2,1)S(1)}, bf16[256,256]{1,0:T(8,128)(2,1)S(1)}, u32[]{:S(2)}, u32[]{:S(2)}) collective-permute-start(bf16[256,256]{1,0:T(8,128)(2,1)S(1)} %get-tuple-element.44.refs_1_), channel_id=1, source_target_pairs={{0,4},{4,0},{1,5},{5,1},{2,6},{6,2},{3,7},{7,3},{8,12},{12,8},{9,1... | collective-permute-start | bytes 393224 | tf_op jit(solution)/shard_map/ppermute | solution.py:21
  41.6 1.6 %collective-permute-start.15 = (bf16[144,256]{1,0:T(8,128)(2,1)S(1)}, bf16[144,256]{1,0:T(8,128)(2,1)S(1)}, u32[]{:S(2)}, u32[]{:S(2)}) collective-permute-start(bf16[144,256]{1,0:T(8,128)(2,1)S(1)} %sum_core.1.own_ref), channel_id=1, source_target_pairs={{0,1},{1,0},{2,3},{3,2},{4,5},{5,4},{6,7},{7,6},{8,9},{9,8},{10,11... | collective-permute-start | bytes 221192 | tf_op jit(solution)/shard_map/ppermute | solution.py:21
  43.1 0.5 collective-permute-start.18
  43.6 2.4 %collective-permute-done.15.other_ref = bf16[144,256]{1,0:T(8,128)(2,1)S(1)} collective-permute-done((bf16[144,256]{1,0:T(8,128)(2,1)S(1)}, bf16[144,256]{1,0:T(8,128)(2,1)S(1)}, u32[]{:S(2)}, u32[]{:S(2)}) %collective-permute-start.15) | collective-permute-done | bytes 73760 | tf_op jit(solution)/shard_map/ppermute | solution.py:21
  46.5 1.0 %collective-permute-done.19.refs_3_ = bf16[256,256]{1,0:T(8,128)(2,1)S(1)} collective-permute-done((bf16[256,256]{1,0:T(8,128)(2,1)S(1)}, bf16[256,256]{1,0:T(8,128)(2,1)S(1)}, u32[]{:S(2)}, u32[]{:S(2)}) %collective-permute-start.19) | collective-permute-done | bytes 131104 | tf_op jit(solution)/shard_map/ppermute | solution.py:21
  47.8 1.5 %collective-permute-start.20 = (bf16[144,256]{1,0:T(8,128)(2,1)S(1)}, bf16[144,256]{1,0:T(8,128)(2,1)S(1)}, u32[]{:S(2)}, u32[]{:S(2)}) collective-permute-start(bf16[144,256]{1,0:T(8,128)(2,1)S(1)} %sum_row.1.m00_ref), channel_id=1, source_target_pairs={{0,4},{4,0},{1,5},{5,1},{2,6},{6,2},{3,7},{7,3},{8,12},{12,8},{9,1... | collective-permute-start | bytes 221192 | tf_op jit(solution)/shard_map/ppermute | solution.py:21
  49.3 0.7 %collective-permute-start.22 = (bf16[144,256]{1,0:T(8,128)(2,1)S(1)}, bf16[144,256]{1,0:T(8,128)(2,1)S(1)}, u32[]{:S(2)}, u32[]{:S(2)}) collective-permute-start(bf16[144,256]{1,0:T(8,128)(2,1)S(1)} %sum_row.1.m00_ref), channel_id=1, source_target_pairs={{0,6},{2,4},{4,2},{6,0},{1,7},{3,5},{5,3},{7,1},{8,14},{10,12},{12... | collective-permute-start | bytes 221192 | tf_op jit(solution)/shard_map/ppermute | solution.py:365
  50.0 1.5 %collective-permute-start.23 = (bf16[128,256]{1,0:T(8,128)(2,1)S(1)}, bf16[128,256]{1,0:T(8,128)(2,1)S(1)}, u32[]{:S(2)}, u32[]{:S(2)}) collective-permute-start(bf16[128,256]{1,0:T(8,128)(2,1)S(1)} %get-tuple-element.48), channel_id=1, source_target_pairs={{0,1},{1,0},{2,3},{3,2},{4,5},{5,4},{6,7},{7,6},{8,9},{9,8},{10,11... | collective-permute-start | bytes 196616 | tf_op jit(solution)/shard_map/ppermute | solution.py:21
  51.5 2.7 %collective-permute-done.23.refs_1_ = bf16[128,256]{1,0:T(8,128)(2,1)S(1)} collective-permute-done((bf16[128,256]{1,0:T(8,128)(2,1)S(1)}, bf16[128,256]{1,0:T(8,128)(2,1)S(1)}, u32[]{:S(2)}, u32[]{:S(2)}) %collective-permute-start.23) | collective-permute-done | bytes 65568 | tf_op jit(solution)/shard_map/ppermute | solution.py:21
  54.3 0.8 %last.1 = (f32[256,256]{1,0:T(8,128)}, f32[1,256]{1,0:T(1,128)}, bf16[128,256]{1,0:T(8,128)(2,1)}) custom-call(bf16[144,256]{1,0:T(8,128)(2,1)S(1)} %sum_row.1.m00_ref, bf16[144,256]{1,0:T(8,128)(2,1)S(1)} %collective-permute-done.20.m10_ref, bf16[144,256]{1,0:T(8,128)(2,1)S(1)} %collective-permute-done.21.m01_ref, ...), custom_call_target="tpu_custom_call" | custom-call | bytes 820224 | tf_op jit(solution)/shard_map/last/pallas_call | solution.py:229
  (35 shorter events, 1.5 us)
Async XLA Ops:
  0.6 8.0 %collective-permute-start = (bf16[128,256]{1,0:T(8,128)(2,1)}, bf16[128,256]{1,0:T(8,128)(2,1)S(1)}, u32[]{:S(2)}, u32[]{:S(2)}) collective-permute-start(bf16[128,256]{1,0:T(8,128)(2,1)} %f_hbm.1), channel_id=1, source_target_pairs={{0,16},{8,24},{16,0},{24,8},{1,17},{9,25},{17,1},{25,9},{2,18},{10... | collective-permute-start | bytes 196616 | tf_op jit(solution)/shard_map/ppermute | solution.py:21
  8.6 5.0 %collective-permute-start.1 = (bf16[256,256]{1,0:T(8,128)(2,1)S(1)}, bf16[256,256]{1,0:T(8,128)(2,1)S(1)}, u32[]{:S(2)}, u32[]{:S(2)}) collective-permute-start(bf16[256,256]{1,0:T(8,128)(2,1)S(1)} %pack.3.refs_0_), channel_id=1, source_target_pairs={{0,8},{8,0},{16,24},{24,16},{1,9},{9,1},{17,25},{25,17},{2,10},{10... | collective-permute-start | bytes 393224 | tf_op jit(solution)/shard_map/ppermute | solution.py:21
  9.3 6.5 %collective-permute-start.4 = (bf16[256,256]{1,0:T(8,128)(2,1)S(1)}, bf16[256,256]{1,0:T(8,128)(2,1)S(1)}, u32[]{:S(2)}, u32[]{:S(2)}) collective-permute-start(bf16[256,256]{1,0:T(8,128)(2,1)S(1)} %pack.3.refs_0_), channel_id=1, source_target_pairs={{0,4},{4,0},{1,5},{5,1},{2,6},{6,2},{3,7},{7,3},{8,12},{12,8},{9,1... | collective-permute-start | bytes 393224 | tf_op jit(solution)/shard_map/ppermute | solution.py:21
  13.6 5.0 %collective-permute-start.5 = (bf16[256,256]{1,0:T(8,128)(2,1)S(1)}, bf16[256,256]{1,0:T(8,128)(2,1)S(1)}, u32[]{:S(2)}, u32[]{:S(2)}) collective-permute-start(bf16[256,256]{1,0:T(8,128)(2,1)S(1)} %collective-permute-done.1.refs_1_), channel_id=1, source_target_pairs={{0,4},{4,0},{1,5},{5,1},{2,6},{6,2},{3,7},{7,3},{8,12},{12,8},{9,1... | collective-permute-start | bytes 393224 | tf_op jit(solution)/shard_map/ppermute | solution.py:21
  15.3 5.6 %collective-permute-start.2 = (bf16[256,256]{1,0:T(8,128)(2,1)S(1)}, bf16[256,256]{1,0:T(8,128)(2,1)S(1)}, u32[]{:S(2)}, u32[]{:S(2)}) collective-permute-start(bf16[256,256]{1,0:T(8,128)(2,1)S(1)} %pack.3.refs_0_), channel_id=1, source_target_pairs={{0,2},{2,0},{1,3},{3,1},{4,6},{6,4},{5,7},{7,5},{8,10},{10,8},{9,1... | collective-permute-start | bytes 393224 | tf_op jit(solution)/shard_map/ppermute | solution.py:21
  15.3 5.6 %collective-permute-start.3 = (bf16[256,256]{1,0:T(8,128)(2,1)S(1)}, bf16[256,256]{1,0:T(8,128)(2,1)S(1)}, u32[]{:S(2)}, u32[]{:S(2)}) collective-permute-start(bf16[256,256]{1,0:T(8,128)(2,1)S(1)} %collective-permute-done.1.refs_1_), channel_id=1, source_target_pairs={{0,2},{2,0},{1,3},{3,1},{4,6},{6,4},{5,7},{7,5},{8,10},{10,8},{9,1... | collective-permute-start | bytes 393224 | tf_op jit(solution)/shard_map/ppermute | solution.py:21
  15.9 5.4 %collective-permute-start.6 = (bf16[256,256]{1,0:T(8,128)(2,1)S(1)}, bf16[256,256]{1,0:T(8,128)(2,1)S(1)}, u32[]{:S(2)}, u32[]{:S(2)}) collective-permute-start(bf16[256,256]{1,0:T(8,128)(2,1)S(1)} %collective-permute-done.4.refs_0_), channel_id=1, source_target_pairs={{0,2},{2,0},{1,3},{3,1},{4,6},{6,4},{5,7},{7,5},{8,10},{10,8},{9,1... | collective-permute-start | bytes 393224 | tf_op jit(solution)/shard_map/ppermute | solution.py:21
  18.6 2.6 %collective-permute-start.7 = (bf16[256,256]{1,0:T(8,128)(2,1)S(1)}, bf16[256,256]{1,0:T(8,128)(2,1)S(1)}, u32[]{:S(2)}, u32[]{:S(2)}) collective-permute-start(bf16[256,256]{1,0:T(8,128)(2,1)S(1)} %collective-permute-done.5.refs_1_), channel_id=1, source_target_pairs={{0,2},{2,0},{1,3},{3,1},{4,6},{6,4},{5,7},{7,5},{8,10},{10,8},{9,1... | collective-permute-start | bytes 393224 | tf_op jit(solution)/shard_map/ppermute | solution.py:21
  18.6 6.8 %collective-permute-start.8 = (bf16[128,256]{1,0:T(8,128)(2,1)S(1)}, bf16[128,256]{1,0:T(8,128)(2,1)S(1)}, u32[]{:S(2)}, u32[]{:S(2)}) collective-permute-start(bf16[128,256]{1,0:T(8,128)(2,1)S(1)} %get-tuple-element.36.refs_0_), channel_id=1, source_target_pairs={{0,16},{8,24},{16,0},{24,8},{1,17},{9,25},{17,1},{25,9},{2,18},{10... | collective-permute-start | bytes 196616 | tf_op jit(solution)/shard_map/ppermute | solution.py:21
  21.6 4.4 %collective-permute-start.9 = (bf16[128,256]{1,0:T(8,128)(2,1)S(1)}, bf16[128,256]{1,0:T(8,128)(2,1)S(1)}, u32[]{:S(2)}, u32[]{:S(2)}) collective-permute-start(bf16[128,256]{1,0:T(8,128)(2,1)S(1)} %get-tuple-element.34), channel_id=1, source_target_pairs={{0,1},{1,0},{2,3},{3,2},{4,5},{5,4},{6,7},{7,6},{8,9},{9,8},{10,11... | collective-permute-start | bytes 196616 | tf_op jit(solution)/shard_map/ppermute | solution.py:21
  25.4 4.0 %copy-start = (bf16[256,256]{1,0:T(8,128)(2,1)S(1)}, bf16[256,256]{1,0:T(8,128)(2,1)}, u32[]{:S(2)}) copy-start(bf16[256,256]{1,0:T(8,128)(2,1)} %w_ref.5) | copy-start | bytes 393220
  25.4 9.1 %collective-permute-start.12 = (bf16[256,256]{1,0:T(8,128)(2,1)S(1)}, bf16[256,256]{1,0:T(8,128)(2,1)S(1)}, u32[]{:S(2)}, u32[]{:S(2)}) collective-permute-start(bf16[256,256]{1,0:T(8,128)(2,1)S(1)} %pack.5.c_ref), channel_id=1, source_target_pairs={{0,8},{8,0},{16,24},{24,16},{1,9},{9,1},{17,25},{25,17},{2,10},{10... | collective-permute-start | bytes 393224 | tf_op jit(solution)/shard_map/ppermute | solution.py:21
  26.0 3.4 %copy-start.1 = (f32[256]{0:T(256)S(1)}, f32[256]{0:T(256)}, u32[]{:S(2)}) copy-start(f32[256]{0:T(256)} %param.9) | copy-start | bytes 3076
  26.0 5.7 %collective-permute-start.10 = (bf16[128,256]{1,0:T(8,128)(2,1)S(1)}, bf16[128,256]{1,0:T(8,128)(2,1)S(1)}, u32[]{:S(2)}, u32[]{:S(2)}) collective-permute-start(bf16[128,256]{1,0:T(8,128)(2,1)S(1)} %hidden.1.h_ref.refs_0_), channel_id=1, source_target_pairs={{0,16},{8,24},{16,0},{24,8},{1,17},{9,25},{17,1},{25,9},{2,18},{10... | collective-permute-start | bytes 196616 | tf_op jit(solution)/shard_map/ppermute | solution.py:21
  31.7 6.0 %collective-permute-start.11 = (bf16[256,256]{1,0:T(8,128)(2,1)S(1)}, bf16[256,256]{1,0:T(8,128)(2,1)S(1)}, u32[]{:S(2)}, u32[]{:S(2)}) collective-permute-start(bf16[256,256]{1,0:T(8,128)(2,1)S(1)} %pack.4.h_ref), channel_id=1, source_target_pairs={{0,8},{8,0},{16,24},{24,16},{1,9},{9,1},{17,25},{25,17},{2,10},{10... | collective-permute-start | bytes 393224 | tf_op jit(solution)/shard_map/ppermute | solution.py:21
  35.0 5.0 %collective-permute-start.13 = (bf16[256,256]{1,0:T(8,128)(2,1)S(1)}, bf16[256,256]{1,0:T(8,128)(2,1)S(1)}, u32[]{:S(2)}, u32[]{:S(2)}) collective-permute-start(bf16[256,256]{1,0:T(8,128)(2,1)S(1)} %get-tuple-element.42.refs_0_), channel_id=1, source_target_pairs={{0,4},{4,0},{1,5},{5,1},{2,6},{6,2},{3,7},{7,3},{8,12},{12,8},{9,1... | collective-permute-start | bytes 393224 | tf_op jit(solution)/shard_map/ppermute | solution.py:21
  40.0 1.5 %collective-permute-start.14 = (bf16[400,256]{1,0:T(8,128)(2,1)S(1)}, bf16[400,256]{1,0:T(8,128)(2,1)S(1)}, u32[]{:S(2)}, u32[]{:S(2)}) collective-permute-start(bf16[400,256]{1,0:T(8,128)(2,1)S(1)} %get-tuple-element.43), channel_id=1, source_target_pairs={{0,2},{2,0},{1,3},{3,1},{4,6},{6,4},{5,7},{7,5},{8,10},{10,8},{9,1... | collective-permute-start | bytes 614408 | tf_op jit(solution)/shard_map/ppermute | solution.py:21
  40.0 6.0 %collective-permute-start.17 = (bf16[256,256]{1,0:T(8,128)(2,1)S(1)}, bf16[256,256]{1,0:T(8,128)(2,1)S(1)}, u32[]{:S(2)}, u32[]{:S(2)}) collective-permute-start(bf16[256,256]{1,0:T(8,128)(2,1)S(1)} %get-tuple-element.44.refs_1_), channel_id=1, source_target_pairs={{0,4},{4,0},{1,5},{5,1},{2,6},{6,2},{3,7},{7,3},{8,12},{12,8},{9,1... | collective-permute-start | bytes 393224 | tf_op jit(solution)/shard_map/ppermute | solution.py:21
  41.6 4.5 %collective-permute-start.15 = (bf16[144,256]{1,0:T(8,128)(2,1)S(1)}, bf16[144,256]{1,0:T(8,128)(2,1)S(1)}, u32[]{:S(2)}, u32[]{:S(2)}) collective-permute-start(bf16[144,256]{1,0:T(8,128)(2,1)S(1)} %sum_core.1.own_ref), channel_id=1, source_target_pairs={{0,1},{1,0},{2,3},{3,2},{4,5},{5,4},{6,7},{7,6},{8,9},{9,8},{10,11... | collective-permute-start | bytes 221192 | tf_op jit(solution)/shard_map/ppermute | solution.py:21
  43.1 3.0 %collective-permute-start.16 = (bf16[256,256]{1,0:T(8,128)(2,1)S(1)}, bf16[256,256]{1,0:T(8,128)(2,1)S(1)}, u32[]{:S(2)}, u32[]{:S(2)}) collective-permute-start(bf16[256,256]{1,0:T(8,128)(2,1)S(1)} %get-tuple-element.42.refs_0_), channel_id=1, source_target_pairs={{0,2},{2,0},{1,3},{3,1},{4,6},{6,4},{5,7},{7,5},{8,10},{10,8},{9,1... | collective-permute-start | bytes 393224 | tf_op jit(solution)/shard_map/ppermute | solution.py:21
  43.1 3.3 %collective-permute-start.18 = (bf16[256,256]{1,0:T(8,128)(2,1)S(1)}, bf16[256,256]{1,0:T(8,128)(2,1)S(1)}, u32[]{:S(2)}, u32[]{:S(2)}) collective-permute-start(bf16[256,256]{1,0:T(8,128)(2,1)S(1)} %collective-permute-done.13.refs_0_), channel_id=1, source_target_pairs={{0,2},{2,0},{1,3},{3,1},{4,6},{6,4},{5,7},{7,5},{8,10},{10,8},{9,1... | collective-permute-start | bytes 393224 | tf_op jit(solution)/shard_map/ppermute | solution.py:21
  46.1 1.4 %collective-permute-start.19 = (bf16[256,256]{1,0:T(8,128)(2,1)S(1)}, bf16[256,256]{1,0:T(8,128)(2,1)S(1)}, u32[]{:S(2)}, u32[]{:S(2)}) collective-permute-start(bf16[256,256]{1,0:T(8,128)(2,1)S(1)} %collective-permute-done.17.refs_1_), channel_id=1, source_target_pairs={{0,2},{2,0},{1,3},{3,1},{4,6},{6,4},{5,7},{7,5},{8,10},{10,8},{9,1... | collective-permute-start | bytes 393224 | tf_op jit(solution)/shard_map/ppermute | solution.py:21
  47.8 6.5 %collective-permute-start.20 = (bf16[144,256]{1,0:T(8,128)(2,1)S(1)}, bf16[144,256]{1,0:T(8,128)(2,1)S(1)}, u32[]{:S(2)}, u32[]{:S(2)}) collective-permute-start(bf16[144,256]{1,0:T(8,128)(2,1)S(1)} %sum_row.1.m00_ref), channel_id=1, source_target_pairs={{0,4},{4,0},{1,5},{5,1},{2,6},{6,2},{3,7},{7,3},{8,12},{12,8},{9,1... | collective-permute-start | bytes 221192 | tf_op jit(solution)/shard_map/ppermute | solution.py:21
  49.3 5.0 %collective-permute-start.21 = (bf16[144,256]{1,0:T(8,128)(2,1)S(1)}, bf16[144,256]{1,0:T(8,128)(2,1)S(1)}, u32[]{:S(2)}, u32[]{:S(2)}) collective-permute-start(bf16[144,256]{1,0:T(8,128)(2,1)S(1)} %sum_row.1.m00_ref), channel_id=1, source_target_pairs={{0,2},{2,0},{1,3},{3,1},{4,6},{6,4},{5,7},{7,5},{8,10},{10,8},{9,1... | collective-permute-start | bytes 221192 | tf_op jit(solution)/shard_map/ppermute | solution.py:21
  49.3 5.0 %collective-permute-start.22 = (bf16[144,256]{1,0:T(8,128)(2,1)S(1)}, bf16[144,256]{1,0:T(8,128)(2,1)S(1)}, u32[]{:S(2)}, u32[]{:S(2)}) collective-permute-start(bf16[144,256]{1,0:T(8,128)(2,1)S(1)} %sum_row.1.m00_ref), channel_id=1, source_target_pairs={{0,6},{2,4},{4,2},{6,0},{1,7},{3,5},{5,3},{7,1},{8,14},{10,12},{12... | collective-permute-start | bytes 221192 | tf_op jit(solution)/shard_map/ppermute | solution.py:365
  50.0 4.3 %collective-permute-start.23 = (bf16[128,256]{1,0:T(8,128)(2,1)S(1)}, bf16[128,256]{1,0:T(8,128)(2,1)S(1)}, u32[]{:S(2)}, u32[]{:S(2)}) collective-permute-start(bf16[128,256]{1,0:T(8,128)(2,1)S(1)} %get-tuple-element.48), channel_id=1, source_target_pairs={{0,1},{1,0},{2,3},{3,2},{4,5},{5,4},{6,7},{7,6},{8,9},{9,8},{10,11... | collective-permute-start | bytes 196616 | tf_op jit(solution)/shard_map/ppermute | solution.py:21

commit v7 on v6

--- a/solution.py
+++ b/solution.py
@@ -207,18 +207,21 @@
     write_message(out_ref, own_w + other_w, own_b + other_b)
 
 
-def last_kernel(factor, m00_ref, m10_ref, m01_ref, m11_ref, *refs):
+def halves_kernel(own_ref, other_ref, out_ref):
+    half = own_ref.shape[0] - PAD
+    core = lax.axis_index("core")
+    out_ref[pl.ds(pl.multiple_of(core * half, half), half), :] = own_ref[:half, :]
+    out_ref[pl.ds(pl.multiple_of((1 - core) * half, half), half), :] = other_ref[:half, :]
+    out_ref[2 * half :, :] = own_ref[half:, :]
+
+
+def last_kernel(factor, near_ref, far_ref, *refs):
     weight_ref, bias_ref, features_ref = refs[-3:]
     sum_kernel(*refs[:-3], features_ref)
-    half = weight_ref.shape[0] // 2
-    core = lax.axis_index("core")
-    for k, (near_ref, far_ref) in enumerate(((m00_ref, m10_ref), (m01_ref, m11_ref))):
-        near_w, near_b = read_message(near_ref)
-        far_w, far_b = read_message(far_ref)
-        at = jnp.bitwise_xor(core, k) * half
-        weight_ref[pl.ds(pl.multiple_of(at, half), half), :] = (near_w + far_w) * factor
-        if k == 0:
-            bias_ref[...] = (near_b + far_b) * factor
+    near_w, near_b = read_message(near_ref)
+    far_w, far_b = read_message(far_ref)
+    weight_ref[...] = (near_w + far_w) * factor
+    bias_ref[...] = (near_b + far_b) * factor
 
 
 def call(kernel, name, outs, operands, scratch=(), specs=None, flops=0):
@@ -280,7 +283,7 @@
     def from_row(parts):
         return [partner(part, "row", q + 1, n_row) for q, part in enumerate(parts)]
 
-    other = far_partner(features)
+    other, other_cot = far_partner(features), far_partner(cotangent)
     adjacency, features, cotangent = call(
         functools.partial(expand_kernel, n_loop, n_row, tile),
         "expand",
@@ -297,16 +300,15 @@
         ],
         specs=[pl.BlockSpec(memory_space=pltpu.HBM)] * 5,
     )
-    f00 = far_chunks(pack(features, other))
+    f00 = far_chunks(pack(features, after(other, other_cot)))
     f10 = [swap(chunk, "mid") for chunk in f00]
-    other_cot = far_partner(after(cotangent, f00[-1]))
+    cots = far_chunks(pack(cotangent, other_cot))
     f01 = [swap(chunk, "core") for chunk in f00]
-    f11 = [swap(chunk, "core") for chunk in f10]
+    f11 = [swap(chunk, "core") for chunk in f10[:-1] + [after(f10[-1], *cots)]]
     half = near_product(f00 + f01, "forward")
     own, *parts = rest_product(half, f10 + f11, "forward")
     others = from_row(parts)
-    cots = far_chunks(pack(after(cotangent, own), other_cot))
-    (hidden,) = call(sum_kernel, "hidden", [shape(tile, width)], [after(own, other_cot)] + others)
+    (hidden,) = call(sum_kernel, "hidden", [shape(tile, width)], [own] + others)
 
     bias_row = bias_vector.reshape(1, width)
     (output,) = call(
@@ -322,7 +324,7 @@
             chunk_kernel,
             "chunk",
             [shape(2 * tile, width)] + sums,
-            [weight, bias_row, chunk, after(cot, cots[-1])],
+            [weight, bias_row, chunk, cot],
             flops=chunk_flops,
         )
         g00.append(gh)
@@ -357,13 +359,14 @@
     half = near_product(g00 + g01, "backward")
     own, *parts = rest_product(half, g10 + g11, "backward")
     others = from_row(parts)
+    (message,) = call(
+        halves_kernel,
+        "halves",
+        [shape(width + PAD, width)],
+        [message, swap(message, "core")],
+    )
     message = after(message, own)
-    messages = [
-        message,
-        swap(message, "mid"),
-        swap(message, "core"),
-        lax.ppermute(message, ("mid", "core"), [(i, 3 - i) for i in range(4)]),
-    ]
+    messages = [message, swap(message, "mid")]
     weight_grad, bias_grad, grad_features = call(
         functools.partial(last_kernel, 1.0 / nodes**0.5),
         "last",

time: 55.2 us -> 55.6 us (level)
  waiting for transfers between devices: 20.6 us -> 25 us
  starting transfers between devices: 28.1 us -> 24 us
    ppermute x23, waiting for transfers between devices: 20.6 us -> 25 us  [partner(): return lax.ppermute(x, axis, [(i, i ^ mask) for i in range(n)])]
    ppermute x23, starting transfers between devices: 27.3 us -> 24 us  [partner(): return lax.ppermute(x, axis, [(i, i ^ mask) for i in range(n)])]
    ppermute x1 -> x0, starting transfers between devices: 0.74 us -> none  [shards(): lax.ppermute(message, ('mid', 'core'), [(i, 3 - i) for i in range(4)])]
    pallas_call x15 -> x16, Pallas kernels: 5.6 us -> 5.6 us  [call(): pl.pallas_call(kernel, name=name, out_shape=outs, in_specs=specs or [VMEM...]
  transfers between devices with their start and end apart: 24 -> 23, of which waited for: 10 -> 13; matrix products, arithmetic and copies ran while one was open for 0% -> 0% of each run, Pallas kernels for 8% -> 8%
where the time goes in v7:
time: 55.6 us; the launch traced here: 55.4 us
  waiting for transfers between devices  25 us (45%)
  starting transfers between devices  24 us (43%)
  Pallas kernels  5.6 us (10%)
  between operations  0.78 us (1%)
    ppermute x23, waiting for transfers between devices, partner(): return lax.ppermute(x, axis, [(i, i ^ mask) for i in range(n)])  25 us
    ppermute x23, starting transfers between devices, partner(): return lax.ppermute(x, axis, [(i, i ^ mask) for i in range(n)])  24 us
    pallas_call x16, Pallas kernels, call(): pl.pallas_call(kernel, name=name, out_shape=outs, in_specs=specs or [VMEM...  5.6 us
  transfers between devices with their start and end apart: 23, of which 13 were waited for; matrix products, arithmetic and copies ran while one was open for 0% of the time, Pallas kernels for 8%

profile of v7, /device:TPU:0, one launch (start us, length us, event | category | flops | bytes accessed | tf_op | source)
XLA Modules:
  0.0 55.4 jit_solution(12344411750529276825)
XLA Ops:
  0.6 4.1 %collective-permute-start = (bf16[128,256]{1,0:T(8,128)(2,1)}, bf16[128,256]{1,0:T(8,128)(2,1)S(1)}, u32[]{:S(2)}, u32[]{:S(2)}) collective-permute-start(bf16[128,256]{1,0:T(8,128)(2,1)} %f_hbm.1), channel_id=1, source_target_pairs={{0,16},{8,24},{16,0},{24,8},{1,17},{9,25},{17,1},{25,9},{2,18},{10... | collective-permute-start | bytes 196616 | tf_op jit(solution)/shard_map/ppermute | solution.py:21
  4.8 1.7 %expand.1 = (bf16[256,2048]{1,0:T(8,128)(2,1)S(1)}, bf16[128,256]{1,0:T(8,128)(2,1)S(1)}, bf16[128,256]{1,0:T(8,128)(2,1)S(1)}) custom-call(s32[32]{0:T(128)} %rows_hbm.1, s32[16]{0:T(128)} %counts_hbm.1, bf16[32,128,128]{2,1,0:T(8,128)(2,1)} %tiles_hbm.1, bf16[128,256]{1,0:T(8,128)(2,1)} %f_hbm.1, bf16[128,256]{1,0:T(8,128)(2,1)} %c_hbm.1), custom_call_target="tpu_custom_call" | custom-call | bytes 2359488 | tf_op jit(solution)/shard_map/expand/pallas_call | solution.py:232
  6.5 2.1 %collective-permute-done.refs_1_ = bf16[128,256]{1,0:T(8,128)(2,1)S(1)} collective-permute-done((bf16[128,256]{1,0:T(8,128)(2,1)}, bf16[128,256]{1,0:T(8,128)(2,1)S(1)}, u32[]{:S(2)}, u32[]{:S(2)}) %collective-permute-start) | collective-permute-done | bytes 65568 | tf_op jit(solution)/shard_map/ppermute | solution.py:21
  8.6 2.8 %collective-permute-done.1.refs_1_ = bf16[128,256]{1,0:T(8,128)(2,1)S(1)} collective-permute-done((bf16[128,256]{1,0:T(8,128)(2,1)}, bf16[128,256]{1,0:T(8,128)(2,1)S(1)}, u32[]{:S(2)}, u32[]{:S(2)}) %collective-permute-start.1) | collective-permute-done | bytes 65568 | tf_op jit(solution)/shard_map/ppermute | solution.py:21
  11.4 0.7 %collective-permute-start.2 = (bf16[256,256]{1,0:T(8,128)(2,1)S(1)}, bf16[256,256]{1,0:T(8,128)(2,1)S(1)}, u32[]{:S(2)}, u32[]{:S(2)}) collective-permute-start(bf16[256,256]{1,0:T(8,128)(2,1)S(1)} %pack.3.refs_0_), channel_id=1, source_target_pairs={{0,8},{8,0},{16,24},{24,16},{1,9},{9,1},{17,25},{25,17},{2,10},{10... | collective-permute-start | bytes 393224 | tf_op jit(solution)/shard_map/ppermute | solution.py:21
  12.2 1.5 %collective-permute-start.5 = (bf16[256,256]{1,0:T(8,128)(2,1)S(1)}, bf16[256,256]{1,0:T(8,128)(2,1)S(1)}, u32[]{:S(2)}, u32[]{:S(2)}) collective-permute-start(bf16[256,256]{1,0:T(8,128)(2,1)S(1)} %pack.3.refs_0_), channel_id=1, source_target_pairs={{0,4},{4,0},{1,5},{5,1},{2,6},{6,2},{3,7},{7,3},{8,12},{12,8},{9,1... | collective-permute-start | bytes 393224 | tf_op jit(solution)/shard_map/ppermute | solution.py:21
  13.7 1.6 %collective-permute-start.8 = (bf16[256,256]{1,0:T(8,128)(2,1)S(1)}, bf16[256,256]{1,0:T(8,128)(2,1)S(1)}, u32[]{:S(2)}, u32[]{:S(2)}) collective-permute-start(bf16[256,256]{1,0:T(8,128)(2,1)S(1)} %pack.4.c_ref), channel_id=1, source_target_pairs={{0,8},{8,0},{16,24},{24,16},{1,9},{9,1},{17,25},{25,17},{2,10},{10... | collective-permute-start | bytes 393224 | tf_op jit(solution)/shard_map/ppermute | solution.py:21
  15.3 1.9 %collective-permute-done.2.refs_1_ = bf16[256,256]{1,0:T(8,128)(2,1)S(1)} collective-permute-done((bf16[256,256]{1,0:T(8,128)(2,1)S(1)}, bf16[256,256]{1,0:T(8,128)(2,1)S(1)}, u32[]{:S(2)}, u32[]{:S(2)}) %collective-permute-start.2) | collective-permute-done | bytes 131104 | tf_op jit(solution)/shard_map/ppermute | solution.py:21
  17.2 2.4 %collective-permute-start.6 = (bf16[256,256]{1,0:T(8,128)(2,1)S(1)}, bf16[256,256]{1,0:T(8,128)(2,1)S(1)}, u32[]{:S(2)}, u32[]{:S(2)}) collective-permute-start(bf16[256,256]{1,0:T(8,128)(2,1)S(1)} %collective-permute-done.2.refs_1_), channel_id=1, source_target_pairs={{0,4},{4,0},{1,5},{5,1},{2,6},{6,2},{3,7},{7,3},{8,12},{12,8},{9,1... | collective-permute-start | bytes 393224 | tf_op jit(solution)/shard_map/ppermute | solution.py:21
  19.6 0.5 collective-permute-start.4
  20.1 2.4 %collective-permute-done.6.refs_1_ = bf16[256,256]{1,0:T(8,128)(2,1)S(1)} collective-permute-done((bf16[256,256]{1,0:T(8,128)(2,1)S(1)}, bf16[256,256]{1,0:T(8,128)(2,1)S(1)}, u32[]{:S(2)}, u32[]{:S(2)}) %collective-permute-start.6) | collective-permute-done | bytes 131104 | tf_op jit(solution)/shard_map/ppermute | solution.py:21
  22.9 1.0 %collective-permute-done.9.refs_3_ = bf16[256,256]{1,0:T(8,128)(2,1)S(1)} collective-permute-done((bf16[256,256]{1,0:T(8,128)(2,1)S(1)}, bf16[256,256]{1,0:T(8,128)(2,1)S(1)}, u32[]{:S(2)}, u32[]{:S(2)}) %collective-permute-start.9) | collective-permute-done | bytes 131104 | tf_op jit(solution)/shard_map/ppermute | solution.py:21
  24.2 2.1 %collective-permute-start.10 = (bf16[128,256]{1,0:T(8,128)(2,1)S(1)}, bf16[128,256]{1,0:T(8,128)(2,1)S(1)}, u32[]{:S(2)}, u32[]{:S(2)}) collective-permute-start(bf16[128,256]{1,0:T(8,128)(2,1)S(1)} %get-tuple-element.32), channel_id=1, source_target_pairs={{0,1},{1,0},{2,3},{3,2},{4,5},{5,4},{6,7},{7,6},{8,9},{9,8},{10,11... | collective-permute-start | bytes 196616 | tf_op jit(solution)/shard_map/ppermute | solution.py:21
  26.2 2.4 %collective-permute-done.10.refs_0_ = bf16[128,256]{1,0:T(8,128)(2,1)S(1)} collective-permute-done((bf16[128,256]{1,0:T(8,128)(2,1)S(1)}, bf16[128,256]{1,0:T(8,128)(2,1)S(1)}, u32[]{:S(2)}, u32[]{:S(2)}) %collective-permute-start.10) | collective-permute-done | bytes 65568 | tf_op jit(solution)/shard_map/ppermute | solution.py:21
  28.7 1.7 %collective-permute-start.11 = (bf16[128,256]{1,0:T(8,128)(2,1)S(1)}, bf16[128,256]{1,0:T(8,128)(2,1)S(1)}, u32[]{:S(2)}, u32[]{:S(2)}) collective-permute-start(bf16[128,256]{1,0:T(8,128)(2,1)S(1)} %hidden.1.h_ref.refs_0_), channel_id=1, source_target_pairs={{0,16},{8,24},{16,0},{24,8},{1,17},{9,25},{17,1},{25,9},{2,18},{10... | collective-permute-start | bytes 196616 | tf_op jit(solution)/shard_map/ppermute | solution.py:21
  30.4 0.8 %output.1 = bf16[128,256]{1,0:T(8,128)(2,1)} custom-call(bf16[256,256]{1,0:T(8,128)(2,1)S(1)} %copy-done, f32[1,256]{1,0:T(1,128)S(1)} %bitcast.2, bf16[128,256]{1,0:T(8,128)(2,1)S(1)} %hidden.1.h_ref.refs_0_), custom_call_target="tpu_custom_call" | custom-call | bytes 263168 | tf_op jit(solution)/shard_map/output/pallas_call | solution.py:232
  31.2 3.5 %collective-permute-done.11.refs_1_ = bf16[128,256]{1,0:T(8,128)(2,1)S(1)} collective-permute-done((bf16[128,256]{1,0:T(8,128)(2,1)S(1)}, bf16[128,256]{1,0:T(8,128)(2,1)S(1)}, u32[]{:S(2)}, u32[]{:S(2)}) %collective-permute-start.11) | collective-permute-done | bytes 65568 | tf_op jit(solution)/shard_map/ppermute | solution.py:21
  34.7 0.6 %collective-permute-start.12 = (bf16[256,256]{1,0:T(8,128)(2,1)S(1)}, bf16[256,256]{1,0:T(8,128)(2,1)S(1)}, u32[]{:S(2)}, u32[]{:S(2)}) collective-permute-start(bf16[256,256]{1,0:T(8,128)(2,1)S(1)} %pack.5.h_ref), channel_id=1, source_target_pairs={{0,8},{8,0},{16,24},{24,16},{1,9},{9,1},{17,25},{25,17},{2,10},{10... | collective-permute-start | bytes 393224 | tf_op jit(solution)/shard_map/ppermute | solution.py:21
  35.8 1.6 %collective-permute-start.13 = (bf16[256,256]{1,0:T(8,128)(2,1)S(1)}, bf16[256,256]{1,0:T(8,128)(2,1)S(1)}, u32[]{:S(2)}, u32[]{:S(2)}) collective-permute-start(bf16[256,256]{1,0:T(8,128)(2,1)S(1)} %get-tuple-element.38.refs_0_), channel_id=1, source_target_pairs={{0,4},{4,0},{1,5},{5,1},{2,6},{6,2},{3,7},{7,3},{8,12},{12,8},{9,1... | collective-permute-start | bytes 393224 | tf_op jit(solution)/shard_map/ppermute | solution.py:21
  37.3 2.4 %collective-permute-done.12.h_ref = bf16[256,256]{1,0:T(8,128)(2,1)S(1)} collective-permute-done((bf16[256,256]{1,0:T(8,128)(2,1)S(1)}, bf16[256,256]{1,0:T(8,128)(2,1)S(1)}, u32[]{:S(2)}, u32[]{:S(2)}) %collective-permute-start.12) | collective-permute-done | bytes 131104 | tf_op jit(solution)/shard_map/ppermute | solution.py:21
  39.7 0.5 last_chunk.1
  40.3 0.5 collective-permute-done.13.refs_0_
  40.8 1.5 %collective-permute-start.18 = (bf16[256,256]{1,0:T(8,128)(2,1)S(1)}, bf16[256,256]{1,0:T(8,128)(2,1)S(1)}, u32[]{:S(2)}, u32[]{:S(2)}) collective-permute-start(bf16[256,256]{1,0:T(8,128)(2,1)S(1)} %get-tuple-element.40.refs_1_), channel_id=1, source_target_pairs={{0,4},{4,0},{1,5},{5,1},{2,6},{6,2},{3,7},{7,3},{8,12},{12,8},{9,1... | collective-permute-start | bytes 393224 | tf_op jit(solution)/shard_map/ppermute | solution.py:21
  42.3 1.6 %collective-permute-start.15 = (bf16[144,256]{1,0:T(8,128)(2,1)S(1)}, bf16[144,256]{1,0:T(8,128)(2,1)S(1)}, u32[]{:S(2)}, u32[]{:S(2)}) collective-permute-start(bf16[144,256]{1,0:T(8,128)(2,1)S(1)} %sum_core.1.own_ref), channel_id=1, source_target_pairs={{0,1},{1,0},{2,3},{3,2},{4,5},{5,4},{6,7},{7,6},{8,9},{9,8},{10,11... | collective-permute-start | bytes 221192 | tf_op jit(solution)/shard_map/ppermute | solution.py:21
  43.9 0.5 collective-permute-start.19
  44.4 2.4 %collective-permute-done.15.other_ref = bf16[144,256]{1,0:T(8,128)(2,1)S(1)} collective-permute-done((bf16[144,256]{1,0:T(8,128)(2,1)S(1)}, bf16[144,256]{1,0:T(8,128)(2,1)S(1)}, u32[]{:S(2)}, u32[]{:S(2)}) %collective-permute-start.15) | collective-permute-done | bytes 73760 | tf_op jit(solution)/shard_map/ppermute | solution.py:21
  46.9 0.5 collective-permute-start.16
  47.7 0.6 %collective-permute-done.16.other_ref = bf16[144,256]{1,0:T(8,128)(2,1)S(1)} collective-permute-done((bf16[144,256]{1,0:T(8,128)(2,1)S(1)}, bf16[144,256]{1,0:T(8,128)(2,1)S(1)}, u32[]{:S(2)}, u32[]{:S(2)}) %collective-permute-start.16) | collective-permute-done | bytes 73760 | tf_op jit(solution)/shard_map/ppermute | solution.py:21
  48.7 1.5 %collective-permute-start.21 = (bf16[272,256]{1,0:T(8,128)(2,1)S(1)}, bf16[272,256]{1,0:T(8,128)(2,1)S(1)}, u32[]{:S(2)}, u32[]{:S(2)}) collective-permute-start(bf16[272,256]{1,0:T(8,128)(2,1)S(1)} %halves.1.near_ref), channel_id=1, source_target_pairs={{0,4},{4,0},{1,5},{5,1},{2,6},{6,2},{3,7},{7,3},{8,12},{12,8},{9,1... | collective-permute-start | bytes 417800 | tf_op jit(solution)/shard_map/ppermute | solution.py:21
  50.2 1.5 %collective-permute-start.22 = (bf16[128,256]{1,0:T(8,128)(2,1)S(1)}, bf16[128,256]{1,0:T(8,128)(2,1)S(1)}, u32[]{:S(2)}, u32[]{:S(2)}) collective-permute-start(bf16[128,256]{1,0:T(8,128)(2,1)S(1)} %get-tuple-element.44), channel_id=1, source_target_pairs={{0,1},{1,0},{2,3},{3,2},{4,5},{5,4},{6,7},{7,6},{8,9},{9,8},{10,11... | collective-permute-start | bytes 196616 | tf_op jit(solution)/shard_map/ppermute | solution.py:21
  51.7 2.7 %collective-permute-done.22.refs_1_ = bf16[128,256]{1,0:T(8,128)(2,1)S(1)} collective-permute-done((bf16[128,256]{1,0:T(8,128)(2,1)S(1)}, bf16[128,256]{1,0:T(8,128)(2,1)S(1)}, u32[]{:S(2)}, u32[]{:S(2)}) %collective-permute-start.22) | collective-permute-done | bytes 65568 | tf_op jit(solution)/shard_map/ppermute | solution.py:21
  54.7 0.8 %last.1 = (f32[256,256]{1,0:T(8,128)}, f32[1,256]{1,0:T(1,128)}, bf16[128,256]{1,0:T(8,128)(2,1)}) custom-call(bf16[272,256]{1,0:T(8,128)(2,1)S(1)} %halves.1.near_ref, bf16[272,256]{1,0:T(8,128)(2,1)S(1)} %collective-permute-done.21.far_ref, f32[128,256]{1,0:T(8,128)S(1)} %get-tuple-element.42.refs_0_, bf16[128,256]{1,0:T(8,128)(2,1)S(1)} %collective-permute-done.22.refs_1_), custom_call_target="tpu_custom_call" | custom-call | bytes 803840 | tf_op jit(solution)/shard_map/last/pallas_call | solution.py:232
  (34 shorter events, 2.2 us)
Async XLA Ops:
  0.6 8.0 %collective-permute-start = (bf16[128,256]{1,0:T(8,128)(2,1)}, bf16[128,256]{1,0:T(8,128)(2,1)S(1)}, u32[]{:S(2)}, u32[]{:S(2)}) collective-permute-start(bf16[128,256]{1,0:T(8,128)(2,1)} %f_hbm.1), channel_id=1, source_target_pairs={{0,16},{8,24},{16,0},{24,8},{1,17},{9,25},{17,1},{25,9},{2,18},{10... | collective-permute-start | bytes 196616 | tf_op jit(solution)/shard_map/ppermute | solution.py:21
  4.7 6.7 %collective-permute-start.1 = (bf16[128,256]{1,0:T(8,128)(2,1)}, bf16[128,256]{1,0:T(8,128)(2,1)S(1)}, u32[]{:S(2)}, u32[]{:S(2)}) collective-permute-start(bf16[128,256]{1,0:T(8,128)(2,1)} %c_hbm.1), channel_id=1, source_target_pairs={{0,16},{8,24},{16,0},{24,8},{1,17},{9,25},{17,1},{25,9},{2,18},{10... | collective-permute-start | bytes 196616 | tf_op jit(solution)/shard_map/ppermute | solution.py:21
  11.4 5.7 %collective-permute-start.2 = (bf16[256,256]{1,0:T(8,128)(2,1)S(1)}, bf16[256,256]{1,0:T(8,128)(2,1)S(1)}, u32[]{:S(2)}, u32[]{:S(2)}) collective-permute-start(bf16[256,256]{1,0:T(8,128)(2,1)S(1)} %pack.3.refs_0_), channel_id=1, source_target_pairs={{0,8},{8,0},{16,24},{24,16},{1,9},{9,1},{17,25},{25,17},{2,10},{10... | collective-permute-start | bytes 393224 | tf_op jit(solution)/shard_map/ppermute | solution.py:21
  12.2 7.9 %collective-permute-start.5 = (bf16[256,256]{1,0:T(8,128)(2,1)S(1)}, bf16[256,256]{1,0:T(8,128)(2,1)S(1)}, u32[]{:S(2)}, u32[]{:S(2)}) collective-permute-start(bf16[256,256]{1,0:T(8,128)(2,1)S(1)} %pack.3.refs_0_), channel_id=1, source_target_pairs={{0,4},{4,0},{1,5},{5,1},{2,6},{6,2},{3,7},{7,3},{8,12},{12,8},{9,1... | collective-permute-start | bytes 393224 | tf_op jit(solution)/shard_map/ppermute | solution.py:21
  13.7 6.4 %collective-permute-start.8 = (bf16[256,256]{1,0:T(8,128)(2,1)S(1)}, bf16[256,256]{1,0:T(8,128)(2,1)S(1)}, u32[]{:S(2)}, u32[]{:S(2)}) collective-permute-start(bf16[256,256]{1,0:T(8,128)(2,1)S(1)} %pack.4.c_ref), channel_id=1, source_target_pairs={{0,8},{8,0},{16,24},{24,16},{1,9},{9,1},{17,25},{25,17},{2,10},{10... | collective-permute-start | bytes 393224 | tf_op jit(solution)/shard_map/ppermute | solution.py:21
  17.2 5.4 %collective-permute-start.6 = (bf16[256,256]{1,0:T(8,128)(2,1)S(1)}, bf16[256,256]{1,0:T(8,128)(2,1)S(1)}, u32[]{:S(2)}, u32[]{:S(2)}) collective-permute-start(bf16[256,256]{1,0:T(8,128)(2,1)S(1)} %collective-permute-done.2.refs_1_), channel_id=1, source_target_pairs={{0,4},{4,0},{1,5},{5,1},{2,6},{6,2},{3,7},{7,3},{8,12},{12,8},{9,1... | collective-permute-start | bytes 393224 | tf_op jit(solution)/shard_map/ppermute | solution.py:21
  19.6 3.0 %collective-permute-start.3 = (bf16[256,256]{1,0:T(8,128)(2,1)S(1)}, bf16[256,256]{1,0:T(8,128)(2,1)S(1)}, u32[]{:S(2)}, u32[]{:S(2)}) collective-permute-start(bf16[256,256]{1,0:T(8,128)(2,1)S(1)} %pack.3.refs_0_), channel_id=1, source_target_pairs={{0,2},{2,0},{1,3},{3,1},{4,6},{6,4},{5,7},{7,5},{8,10},{10,8},{9,1... | collective-permute-start | bytes 393224 | tf_op jit(solution)/shard_map/ppermute | solution.py:21
  19.6 3.0 %collective-permute-start.4 = (bf16[256,256]{1,0:T(8,128)(2,1)S(1)}, bf16[256,256]{1,0:T(8,128)(2,1)S(1)}, u32[]{:S(2)}, u32[]{:S(2)}) collective-permute-start(bf16[256,256]{1,0:T(8,128)(2,1)S(1)} %collective-permute-done.2.refs_1_), channel_id=1, source_target_pairs={{0,2},{2,0},{1,3},{3,1},{4,6},{6,4},{5,7},{7,5},{8,10},{10,8},{9,1... | collective-permute-start | bytes 393224 | tf_op jit(solution)/shard_map/ppermute | solution.py:21
  20.1 2.8 %collective-permute-start.7 = (bf16[256,256]{1,0:T(8,128)(2,1)S(1)}, bf16[256,256]{1,0:T(8,128)(2,1)S(1)}, u32[]{:S(2)}, u32[]{:S(2)}) collective-permute-start(bf16[256,256]{1,0:T(8,128)(2,1)S(1)} %collective-permute-done.5.refs_0_), channel_id=1, source_target_pairs={{0,2},{2,0},{1,3},{3,1},{4,6},{6,4},{5,7},{7,5},{8,10},{10,8},{9,1... | collective-permute-start | bytes 393224 | tf_op jit(solution)/shard_map/ppermute | solution.py:21
  22.5 1.3 %collective-permute-start.9 = (bf16[256,256]{1,0:T(8,128)(2,1)S(1)}, bf16[256,256]{1,0:T(8,128)(2,1)S(1)}, u32[]{:S(2)}, u32[]{:S(2)}) collective-permute-start(bf16[256,256]{1,0:T(8,128)(2,1)S(1)} %collective-permute-done.6.refs_1_), channel_id=1, source_target_pairs={{0,2},{2,0},{1,3},{3,1},{4,6},{6,4},{5,7},{7,5},{8,10},{10,8},{9,1... | collective-permute-start | bytes 393224 | tf_op jit(solution)/shard_map/ppermute | solution.py:21
  24.2 4.5 %collective-permute-start.10 = (bf16[128,256]{1,0:T(8,128)(2,1)S(1)}, bf16[128,256]{1,0:T(8,128)(2,1)S(1)}, u32[]{:S(2)}, u32[]{:S(2)}) collective-permute-start(bf16[128,256]{1,0:T(8,128)(2,1)S(1)} %get-tuple-element.32), channel_id=1, source_target_pairs={{0,1},{1,0},{2,3},{3,2},{4,5},{5,4},{6,7},{7,6},{8,9},{9,8},{10,11... | collective-permute-start | bytes 196616 | tf_op jit(solution)/shard_map/ppermute | solution.py:21
  28.6 1.7 %copy-start = (bf16[256,256]{1,0:T(8,128)(2,1)S(1)}, bf16[256,256]{1,0:T(8,128)(2,1)}, u32[]{:S(2)}) copy-start(bf16[256,256]{1,0:T(8,128)(2,1)} %w_ref.5) | copy-start | bytes 393220
  28.7 1.7 %copy-start.1 = (f32[256]{0:T(256)S(1)}, f32[256]{0:T(256)}, u32[]{:S(2)}) copy-start(f32[256]{0:T(256)} %param.9) | copy-start | bytes 3076
  28.7 6.0 %collective-permute-start.11 = (bf16[128,256]{1,0:T(8,128)(2,1)S(1)}, bf16[128,256]{1,0:T(8,128)(2,1)S(1)}, u32[]{:S(2)}, u32[]{:S(2)}) collective-permute-start(bf16[128,256]{1,0:T(8,128)(2,1)S(1)} %hidden.1.h_ref.refs_0_), channel_id=1, source_target_pairs={{0,16},{8,24},{16,0},{24,8},{1,17},{9,25},{17,1},{25,9},{2,18},{10... | collective-permute-start | bytes 196616 | tf_op jit(solution)/shard_map/ppermute | solution.py:21
  34.7 5.0 %collective-permute-start.12 = (bf16[256,256]{1,0:T(8,128)(2,1)S(1)}, bf16[256,256]{1,0:T(8,128)(2,1)S(1)}, u32[]{:S(2)}, u32[]{:S(2)}) collective-permute-start(bf16[256,256]{1,0:T(8,128)(2,1)S(1)} %pack.5.h_ref), channel_id=1, source_target_pairs={{0,8},{8,0},{16,24},{24,16},{1,9},{9,1},{17,25},{25,17},{2,10},{10... | collective-permute-start | bytes 393224 | tf_op jit(solution)/shard_map/ppermute | solution.py:21
  35.8 5.0 %collective-permute-start.13 = (bf16[256,256]{1,0:T(8,128)(2,1)S(1)}, bf16[256,256]{1,0:T(8,128)(2,1)S(1)}, u32[]{:S(2)}, u32[]{:S(2)}) collective-permute-start(bf16[256,256]{1,0:T(8,128)(2,1)S(1)} %get-tuple-element.38.refs_0_), channel_id=1, source_target_pairs={{0,4},{4,0},{1,5},{5,1},{2,6},{6,2},{3,7},{7,3},{8,12},{12,8},{9,1... | collective-permute-start | bytes 393224 | tf_op jit(solution)/shard_map/ppermute | solution.py:21
  40.8 1.5 %collective-permute-start.14 = (bf16[400,256]{1,0:T(8,128)(2,1)S(1)}, bf16[400,256]{1,0:T(8,128)(2,1)S(1)}, u32[]{:S(2)}, u32[]{:S(2)}) collective-permute-start(bf16[400,256]{1,0:T(8,128)(2,1)S(1)} %get-tuple-element.39), channel_id=1, source_target_pairs={{0,2},{2,0},{1,3},{3,1},{4,6},{6,4},{5,7},{7,5},{8,10},{10,8},{9,1... | collective-permute-start | bytes 614408 | tf_op jit(solution)/shard_map/ppermute | solution.py:21
  40.8 6.0 %collective-permute-start.18 = (bf16[256,256]{1,0:T(8,128)(2,1)S(1)}, bf16[256,256]{1,0:T(8,128)(2,1)S(1)}, u32[]{:S(2)}, u32[]{:S(2)}) collective-permute-start(bf16[256,256]{1,0:T(8,128)(2,1)S(1)} %get-tuple-element.40.refs_1_), channel_id=1, source_target_pairs={{0,4},{4,0},{1,5},{5,1},{2,6},{6,2},{3,7},{7,3},{8,12},{12,8},{9,1... | collective-permute-start | bytes 393224 | tf_op jit(solution)/shard_map/ppermute | solution.py:21
  42.3 4.5 %collective-permute-start.15 = (bf16[144,256]{1,0:T(8,128)(2,1)S(1)}, bf16[144,256]{1,0:T(8,128)(2,1)S(1)}, u32[]{:S(2)}, u32[]{:S(2)}) collective-permute-start(bf16[144,256]{1,0:T(8,128)(2,1)S(1)} %sum_core.1.own_ref), channel_id=1, source_target_pairs={{0,1},{1,0},{2,3},{3,2},{4,5},{5,4},{6,7},{7,6},{8,9},{9,8},{10,11... | collective-permute-start | bytes 221192 | tf_op jit(solution)/shard_map/ppermute | solution.py:21
  43.9 3.5 %collective-permute-start.17 = (bf16[256,256]{1,0:T(8,128)(2,1)S(1)}, bf16[256,256]{1,0:T(8,128)(2,1)S(1)}, u32[]{:S(2)}, u32[]{:S(2)}) collective-permute-start(bf16[256,256]{1,0:T(8,128)(2,1)S(1)} %get-tuple-element.38.refs_0_), channel_id=1, source_target_pairs={{0,2},{2,0},{1,3},{3,1},{4,6},{6,4},{5,7},{7,5},{8,10},{10,8},{9,1... | collective-permute-start | bytes 393224 | tf_op jit(solution)/shard_map/ppermute | solution.py:21
  43.9 4.5 %collective-permute-start.19 = (bf16[256,256]{1,0:T(8,128)(2,1)S(1)}, bf16[256,256]{1,0:T(8,128)(2,1)S(1)}, u32[]{:S(2)}, u32[]{:S(2)}) collective-permute-start(bf16[256,256]{1,0:T(8,128)(2,1)S(1)} %collective-permute-done.13.refs_0_), channel_id=1, source_target_pairs={{0,2},{2,0},{1,3},{3,1},{4,6},{6,4},{5,7},{7,5},{8,10},{10,8},{9,1... | collective-permute-start | bytes 393224 | tf_op jit(solution)/shard_map/ppermute | solution.py:21
  46.8 1.6 %collective-permute-start.20 = (bf16[256,256]{1,0:T(8,128)(2,1)S(1)}, bf16[256,256]{1,0:T(8,128)(2,1)S(1)}, u32[]{:S(2)}, u32[]{:S(2)}) collective-permute-start(bf16[256,256]{1,0:T(8,128)(2,1)S(1)} %collective-permute-done.18.refs_1_), channel_id=1, source_target_pairs={{0,2},{2,0},{1,3},{3,1},{4,6},{6,4},{5,7},{7,5},{8,10},{10,8},{9,1... | collective-permute-start | bytes 393224 | tf_op jit(solution)/shard_map/ppermute | solution.py:21
  46.9 1.4 %collective-permute-start.16 = (bf16[144,256]{1,0:T(8,128)(2,1)S(1)}, bf16[144,256]{1,0:T(8,128)(2,1)S(1)}, u32[]{:S(2)}, u32[]{:S(2)}) collective-permute-start(bf16[144,256]{1,0:T(8,128)(2,1)S(1)} %sum_row.1.own_ref), channel_id=1, source_target_pairs={{0,2},{2,0},{1,3},{3,1},{4,6},{6,4},{5,7},{7,5},{8,10},{10,8},{9,1... | collective-permute-start | bytes 221192 | tf_op jit(solution)/shard_map/ppermute | solution.py:21
  48.7 6.0 %collective-permute-start.21 = (bf16[272,256]{1,0:T(8,128)(2,1)S(1)}, bf16[272,256]{1,0:T(8,128)(2,1)S(1)}, u32[]{:S(2)}, u32[]{:S(2)}) collective-permute-start(bf16[272,256]{1,0:T(8,128)(2,1)S(1)} %halves.1.near_ref), channel_id=1, source_target_pairs={{0,4},{4,0},{1,5},{5,1},{2,6},{6,2},{3,7},{7,3},{8,12},{12,8},{9,1... | collective-permute-start | bytes 417800 | tf_op jit(solution)/shard_map/ppermute | solution.py:21
  50.2 4.3 %collective-permute-start.22 = (bf16[128,256]{1,0:T(8,128)(2,1)S(1)}, bf16[128,256]{1,0:T(8,128)(2,1)S(1)}, u32[]{:S(2)}, u32[]{:S(2)}) collective-permute-start(bf16[128,256]{1,0:T(8,128)(2,1)S(1)} %get-tuple-element.44), channel_id=1, source_target_pairs={{0,1},{1,0},{2,3},{3,2},{4,5},{5,4},{6,7},{7,6},{8,9},{9,8},{10,11... | collective-permute-start | bytes 196616 | tf_op jit(solution)/shard_map/ppermute | solution.py:21

commit v8 on v7

--- a/solution.py
+++ b/solution.py
@@ -148,15 +148,16 @@
     out_ref[...] = total.astype(BF16)
 
 
-def chunk_grads(w_ref, b_ref, h_ref, c_ref, gh_ref):
+def chunk_grads(w_ref, b_ref, h_ref, c_refs, gh_ref):
     tile, width = h_ref.shape[0] // 2, h_ref.shape[1]
     weight_sums, bias_sums = [], []
-    for k in range(2):
+    for k, (c_ref, half) in enumerate(c_refs):
         rows = slice(k * tile, (k + 1) * tile)
         hidden = h_ref[rows, :]
         preact = dot(hidden, w_ref[...]) + b_ref[...]
         sig = sigmoid(preact)
-        grad_z = c_ref[rows, :].astype(F32) * sig * (1.0 + preact * (1.0 - sig))
+        cot = c_ref[half * tile : (half + 1) * tile, :].astype(F32)
+        grad_z = cot * sig * (1.0 + preact * (1.0 - sig))
         half = grad_z.astype(BF16)
         gh_ref[rows, :] = dot(half, w_ref[...], ((1,), (1,))).astype(BF16)
         bias_sums.append(jnp.sum(grad_z.reshape(tile // 8, 8, width), axis=0))
@@ -164,8 +165,9 @@
     return tree_sum(weight_sums), tree_sum(bias_sums)
 
 
-def chunk_kernel(w_ref, b_ref, h_ref, c_ref, gh_ref, gw_ref, gb_ref):
-    gw_ref[...], gb_ref[...] = chunk_grads(w_ref, b_ref, h_ref, c_ref, gh_ref)
+def chunk_kernel(halves, w_ref, b_ref, h_ref, c0_ref, c1_ref, gh_ref, gw_ref, gb_ref):
+    c_refs = list(zip((c0_ref, c1_ref), halves))
+    gw_ref[...], gb_ref[...] = chunk_grads(w_ref, b_ref, h_ref, c_refs, gh_ref)
 
 
 def write_message(ref, grad_w, bias):
@@ -184,11 +186,12 @@
     return ref[:rows, :].astype(F32), tail[0:1, :] + tail[1:2, :]
 
 
-def last_chunk_kernel(n, w_ref, b_ref, h_ref, c_ref, *refs):
+def last_chunk_kernel(halves, n, w_ref, b_ref, h_ref, c0_ref, c1_ref, *refs):
     gw_refs, gb_refs = refs[:n], refs[n : 2 * n]
     gh_ref, both_ref, keep_ref, sum_ref = refs[2 * n :]
     half = keep_ref.shape[0] - PAD
-    grad_w, grad_b = chunk_grads(w_ref, b_ref, h_ref, c_ref, gh_ref)
+    c_refs = list(zip((c0_ref, c1_ref), halves))
+    grad_w, grad_b = chunk_grads(w_ref, b_ref, h_ref, c_refs, gh_ref)
     sum_ref[...] = tree_sum([ref[...] for ref in gw_refs] + [grad_w])
     grad_b = tree_sum([ref[...] for ref in gb_refs] + [grad_b])
     bias = jnp.sum(grad_b, axis=0, keepdims=True)
@@ -253,10 +256,10 @@
     def pack(*blocks):
         return call(pack_kernel, "pack", [shape(2 * tile, width)], blocks)[0]
 
-    def far_partner(block):
-        return partner(block, "far", steps[0], n_far)
-
-    def far_chunks(pair):
+    def far_partner(block, step):
+        return partner(block, "far", step, n_far)
+
+    def far_chunks(pair, steps):
         chunks = [pair]
         for step in steps[1:]:
             chunks = chunks + [partner(chunk, "far", step, n_far) for chunk in chunks]
@@ -283,7 +286,8 @@
     def from_row(parts):
         return [partner(part, "row", q + 1, n_row) for q, part in enumerate(parts)]
 
-    other, other_cot = far_partner(features), far_partner(cotangent)
+    cot_steps = steps[::-1]
+    other, other_cot = far_partner(features, steps[0]), far_partner(cotangent, cot_steps[0])
     adjacency, features, cotangent = call(
         functools.partial(expand_kernel, n_loop, n_row, tile),
         "expand",
@@ -300,9 +304,9 @@
         ],
         specs=[pl.BlockSpec(memory_space=pltpu.HBM)] * 5,
     )
-    f00 = far_chunks(pack(features, after(other, other_cot)))
+    f00 = far_chunks(pack(features, after(other, other_cot)), steps)
     f10 = [swap(chunk, "mid") for chunk in f00]
-    cots = far_chunks(pack(cotangent, other_cot))
+    cots = far_chunks(pack(cotangent, other_cot), cot_steps)
     f01 = [swap(chunk, "core") for chunk in f00]
     f11 = [swap(chunk, "core") for chunk in f10[:-1] + [after(f10[-1], *cots)]]
     half = near_product(f00 + f01, "forward")
@@ -314,17 +318,24 @@
     (output,) = call(
         output_kernel, "output", [shape(tile, width)], [weight, bias_row, hidden]
     )
-    other, hidden = far_partner(hidden), after(hidden, output)
-    hiddens = far_chunks(pack(hidden, other))
+    other, hidden = far_partner(hidden, steps[0]), after(hidden, output)
+    hiddens = far_chunks(pack(hidden, other), steps)
+
+    def chunk_cots(k):
+        bits = len(steps)
+        places = [int(f"{2 * k + b:0{bits}b}"[::-1], 2) for b in range(2)]
+        return [cots[p // 2] for p in places], [p % 2 for p in places]
+
     chunk_flops = 2 * tile * 6 * width * width
     g00, weight_sums, bias_sums = [], [], []
     sums = [shape(width, width, dtype=F32), shape(8, width, dtype=F32)]
-    for chunk, cot in zip(hiddens[:-1], cots[:-1]):
+    for k, chunk in enumerate(hiddens[:-1]):
+        chunk_cot, halves = chunk_cots(k)
         gh, weight_sum, bias_sum = call(
-            chunk_kernel,
+            functools.partial(chunk_kernel, halves),
             "chunk",
             [shape(2 * tile, width)] + sums,
-            [weight, bias_row, chunk, cot],
+            [weight, bias_row, chunk] + chunk_cot,
             flops=chunk_flops,
         )
         g00.append(gh)
@@ -333,11 +344,12 @@
     half_rows = width // 2 + PAD
     g01 = [swap(chunk, "core") for chunk in g00]
     g10 = [swap(chunk, "mid") for chunk in g00]
+    chunk_cot, halves = chunk_cots(len(g00))
     gh, both, keep = call(
-        functools.partial(last_chunk_kernel, len(g00)),
+        functools.partial(last_chunk_kernel, halves, len(g00)),
         "last_chunk",
         [shape(2 * tile, width), shape(2 * tile + half_rows, width), shape(half_rows, width)],
-        [weight, bias_row, hiddens[-1], cots[-1]] + weight_sums + bias_sums,
+        [weight, bias_row, hiddens[-1]] + chunk_cot + weight_sums + bias_sums,
         scratch=[pltpu.VMEM((width, width), F32)],
         flops=chunk_flops,
     )
@@ -355,8 +367,8 @@
             [message, partner(message, "row", bit, n_row)],
         )
         bit *= 2
-    g11 = [swap(chunk, "core") for chunk in g10[:-1] + [after(g10[-1], message)]]
-    half = near_product(g00 + g01, "backward")
+    g11 = [swap(chunk, "core") for chunk in g10]
+    half = near_product([after(g00[0], message)] + g00[1:] + g01, "backward")
     own, *parts = rest_product(half, g10 + g11, "backward")
     others = from_row(parts)
     (message,) = call(

time: 55.6 us -> 52.9 us (0.951)
  starting transfers between devices: 24 us -> 21.3 us
    ppermute x23, starting transfers between devices: 24 us -> 21.3 us  [partner(): return lax.ppermute(x, axis, [(i, i ^ mask) for i in range(n)])]
  transfers between devices with their start and end apart: 23 -> 23, of which waited for: 13 -> 13; matrix products, arithmetic and copies ran while one was open for 0% -> 0% of each run, Pallas kernels for 8% -> 9%
where the time goes in v8:
time: 52.9 us; the launch traced here: 52.7 us
  waiting for transfers between devices  25 us (47%)
  starting transfers between devices  21.3 us (40%)
  Pallas kernels  5.61 us (11%)
  between operations  0.79 us (1%)
    ppermute x23, waiting for transfers between devices, partner(): return lax.ppermute(x, axis, [(i, i ^ mask) for i in range(n)])  25 us
    ppermute x23, starting transfers between devices, partner(): return lax.ppermute(x, axis, [(i, i ^ mask) for i in range(n)])  21.3 us
    pallas_call x16, Pallas kernels, call(): pl.pallas_call(kernel, name=name, out_shape=outs, in_specs=specs or [VMEM...  5.61 us
  transfers between devices with their start and end apart: 23, of which 13 were waited for; matrix products, arithmetic and copies ran while one was open for 0% of the time, Pallas kernels for 9%

profile of v8, /device:TPU:0, one launch (start us, length us, event | category | flops | bytes accessed | tf_op | source)
XLA Modules:
  0.0 52.7 jit_solution(13471334219601906977)
XLA Ops:
  0.6 3.1 %collective-permute-start.1 = (bf16[128,256]{1,0:T(8,128)(2,1)}, bf16[128,256]{1,0:T(8,128)(2,1)S(1)}, u32[]{:S(2)}, u32[]{:S(2)}) collective-permute-start(bf16[128,256]{1,0:T(8,128)(2,1)} %c_hbm.1), channel_id=1, source_target_pairs={{0,8},{8,0},{16,24},{24,16},{1,9},{9,1},{17,25},{25,17},{2,10},{10... | collective-permute-start | bytes 196616 | tf_op jit(solution)/shard_map/ppermute | solution.py:21
  3.7 2.6 %collective-permute-start = (bf16[128,256]{1,0:T(8,128)(2,1)}, bf16[128,256]{1,0:T(8,128)(2,1)S(1)}, u32[]{:S(2)}, u32[]{:S(2)}) collective-permute-start(bf16[128,256]{1,0:T(8,128)(2,1)} %f_hbm.1), channel_id=1, source_target_pairs={{0,16},{8,24},{16,0},{24,8},{1,17},{9,25},{17,1},{25,9},{2,18},{10... | collective-permute-start | bytes 196616 | tf_op jit(solution)/shard_map/ppermute | solution.py:21
  6.3 1.7 %expand.1 = (bf16[256,2048]{1,0:T(8,128)(2,1)S(1)}, bf16[128,256]{1,0:T(8,128)(2,1)S(1)}, bf16[128,256]{1,0:T(8,128)(2,1)S(1)}) custom-call(s32[32]{0:T(128)} %rows_hbm.1, s32[16]{0:T(128)} %counts_hbm.1, bf16[32,128,128]{2,1,0:T(8,128)(2,1)} %tiles_hbm.1, bf16[128,256]{1,0:T(8,128)(2,1)} %f_hbm.1, bf16[128,256]{1,0:T(8,128)(2,1)} %c_hbm.1), custom_call_target="tpu_custom_call" | custom-call | bytes 2359488 | tf_op jit(solution)/shard_map/expand/pallas_call | solution.py:235
  8.0 1.8 %collective-permute-done.refs_1_ = bf16[128,256]{1,0:T(8,128)(2,1)S(1)} collective-permute-done((bf16[128,256]{1,0:T(8,128)(2,1)}, bf16[128,256]{1,0:T(8,128)(2,1)S(1)}, u32[]{:S(2)}, u32[]{:S(2)}) %collective-permute-start) | collective-permute-done | bytes 65568 | tf_op jit(solution)/shard_map/ppermute | solution.py:21
  9.9 0.5 collective-permute-start.2
  10.4 1.5 %collective-permute-start.5 = (bf16[256,256]{1,0:T(8,128)(2,1)S(1)}, bf16[256,256]{1,0:T(8,128)(2,1)S(1)}, u32[]{:S(2)}, u32[]{:S(2)}) collective-permute-start(bf16[256,256]{1,0:T(8,128)(2,1)S(1)} %pack.3.refs_0_), channel_id=1, source_target_pairs={{0,4},{4,0},{1,5},{5,1},{2,6},{6,2},{3,7},{7,3},{8,12},{12,8},{9,1... | collective-permute-start | bytes 393224 | tf_op jit(solution)/shard_map/ppermute | solution.py:21
  11.9 2.2 %collective-permute-start.8 = (bf16[256,256]{1,0:T(8,128)(2,1)S(1)}, bf16[256,256]{1,0:T(8,128)(2,1)S(1)}, u32[]{:S(2)}, u32[]{:S(2)}) collective-permute-start(bf16[256,256]{1,0:T(8,128)(2,1)S(1)} %pack.4.c0_ref), channel_id=1, source_target_pairs={{0,16},{8,24},{16,0},{24,8},{1,17},{9,25},{17,1},{25,9},{2,18},{10... | collective-permute-start | bytes 393224 | tf_op jit(solution)/shard_map/ppermute | solution.py:21
  14.1 2.2 %collective-permute-done.2.refs_1_ = bf16[256,256]{1,0:T(8,128)(2,1)S(1)} collective-permute-done((bf16[256,256]{1,0:T(8,128)(2,1)S(1)}, bf16[256,256]{1,0:T(8,128)(2,1)S(1)}, u32[]{:S(2)}, u32[]{:S(2)}) %collective-permute-start.2) | collective-permute-done | bytes 131104 | tf_op jit(solution)/shard_map/ppermute | solution.py:21
  16.2 0.5 %collective-permute-start.6 = (bf16[256,256]{1,0:T(8,128)(2,1)S(1)}, bf16[256,256]{1,0:T(8,128)(2,1)S(1)}, u32[]{:S(2)}, u32[]{:S(2)}) collective-permute-start(bf16[256,256]{1,0:T(8,128)(2,1)S(1)} %collective-permute-done.2.refs_1_), channel_id=1, source_target_pairs={{0,4},{4,0},{1,5},{5,1},{2,6},{6,2},{3,7},{7,3},{8,12},{12,8},{9,1... | collective-permute-start | bytes 393224 | tf_op jit(solution)/shard_map/ppermute | solution.py:21
  16.8 0.5 collective-permute-start.4
  17.3 1.9 %collective-permute-done.8.c1_ref = bf16[256,256]{1,0:T(8,128)(2,1)S(1)} collective-permute-done((bf16[256,256]{1,0:T(8,128)(2,1)S(1)}, bf16[256,256]{1,0:T(8,128)(2,1)S(1)}, u32[]{:S(2)}, u32[]{:S(2)}) %collective-permute-start.8) | collective-permute-done | bytes 131104 | tf_op jit(solution)/shard_map/ppermute | solution.py:21
  19.2 2.0 %collective-permute-done.6.refs_1_ = bf16[256,256]{1,0:T(8,128)(2,1)S(1)} collective-permute-done((bf16[256,256]{1,0:T(8,128)(2,1)S(1)}, bf16[256,256]{1,0:T(8,128)(2,1)S(1)}, u32[]{:S(2)}, u32[]{:S(2)}) %collective-permute-start.6) | collective-permute-done | bytes 131104 | tf_op jit(solution)/shard_map/ppermute | solution.py:21
  21.5 1.0 %collective-permute-done.9.refs_3_ = bf16[256,256]{1,0:T(8,128)(2,1)S(1)} collective-permute-done((bf16[256,256]{1,0:T(8,128)(2,1)S(1)}, bf16[256,256]{1,0:T(8,128)(2,1)S(1)}, u32[]{:S(2)}, u32[]{:S(2)}) %collective-permute-start.9) | collective-permute-done | bytes 131104 | tf_op jit(solution)/shard_map/ppermute | solution.py:21
  22.9 1.6 %collective-permute-start.10 = (bf16[128,256]{1,0:T(8,128)(2,1)S(1)}, bf16[128,256]{1,0:T(8,128)(2,1)S(1)}, u32[]{:S(2)}, u32[]{:S(2)}) collective-permute-start(bf16[128,256]{1,0:T(8,128)(2,1)S(1)} %get-tuple-element.32), channel_id=1, source_target_pairs={{0,1},{1,0},{2,3},{3,2},{4,5},{5,4},{6,7},{7,6},{8,9},{9,8},{10,11... | collective-permute-start | bytes 196616 | tf_op jit(solution)/shard_map/ppermute | solution.py:21
  24.5 2.7 %collective-permute-done.10.refs_0_ = bf16[128,256]{1,0:T(8,128)(2,1)S(1)} collective-permute-done((bf16[128,256]{1,0:T(8,128)(2,1)S(1)}, bf16[128,256]{1,0:T(8,128)(2,1)S(1)}, u32[]{:S(2)}, u32[]{:S(2)}) %collective-permute-start.10) | collective-permute-done | bytes 65568 | tf_op jit(solution)/shard_map/ppermute | solution.py:21
  27.2 1.4 %collective-permute-start.11 = (bf16[128,256]{1,0:T(8,128)(2,1)S(1)}, bf16[128,256]{1,0:T(8,128)(2,1)S(1)}, u32[]{:S(2)}, u32[]{:S(2)}) collective-permute-start(bf16[128,256]{1,0:T(8,128)(2,1)S(1)} %hidden.1.h_ref.refs_0_), channel_id=1, source_target_pairs={{0,16},{8,24},{16,0},{24,8},{1,17},{9,25},{17,1},{25,9},{2,18},{10... | collective-permute-start | bytes 196616 | tf_op jit(solution)/shard_map/ppermute | solution.py:21
  28.6 0.8 %output.1 = bf16[128,256]{1,0:T(8,128)(2,1)} custom-call(bf16[256,256]{1,0:T(8,128)(2,1)S(1)} %copy-done, f32[1,256]{1,0:T(1,128)S(1)} %bitcast.2, bf16[128,256]{1,0:T(8,128)(2,1)S(1)} %hidden.1.h_ref.refs_0_), custom_call_target="tpu_custom_call" | custom-call | bytes 263168 | tf_op jit(solution)/shard_map/output/pallas_call | solution.py:235
  29.4 3.4 %collective-permute-done.11.refs_1_ = bf16[128,256]{1,0:T(8,128)(2,1)S(1)} collective-permute-done((bf16[128,256]{1,0:T(8,128)(2,1)S(1)}, bf16[128,256]{1,0:T(8,128)(2,1)S(1)}, u32[]{:S(2)}, u32[]{:S(2)}) %collective-permute-start.11) | collective-permute-done | bytes 65568 | tf_op jit(solution)/shard_map/ppermute | solution.py:21
  32.9 0.5 chunk.1
  33.4 1.2 %collective-permute-start.13 = (bf16[256,256]{1,0:T(8,128)(2,1)S(1)}, bf16[256,256]{1,0:T(8,128)(2,1)S(1)}, u32[]{:S(2)}, u32[]{:S(2)}) collective-permute-start(bf16[256,256]{1,0:T(8,128)(2,1)S(1)} %get-tuple-element.40.refs_0_), channel_id=1, source_target_pairs={{0,4},{4,0},{1,5},{5,1},{2,6},{6,2},{3,7},{7,3},{8,12},{12,8},{9,1... | collective-permute-start | bytes 393224 | tf_op jit(solution)/shard_map/ppermute | solution.py:21
  34.6 3.3 %collective-permute-done.12.h_ref = bf16[256,256]{1,0:T(8,128)(2,1)S(1)} collective-permute-done((bf16[256,256]{1,0:T(8,128)(2,1)S(1)}, bf16[256,256]{1,0:T(8,128)(2,1)S(1)}, u32[]{:S(2)}, u32[]{:S(2)}) %collective-permute-start.12) | collective-permute-done | bytes 131104 | tf_op jit(solution)/shard_map/ppermute | solution.py:21
  37.9 0.5 %last_chunk.1 = (bf16[256,256]{1,0:T(8,128)(2,1)S(1)}, bf16[400,256]{1,0:T(8,128)(2,1)S(1)}, bf16[144,256]{1,0:T(8,128)(2,1)S(1)}) custom-call(bf16[256,256]{1,0:T(8,128)(2,1)S(1)} %copy-done, f32[1,256]{1,0:T(1,128)S(1)} %bitcast.4, bf16[256,256]{1,0:T(8,128)(2,1)S(1)} %collective-permute-done.12.h_ref, bf16[256,256]{1,0:T(8,128)(2,1)S(1)} %pack.4.c0_ref, ...), custom_call_target="tpu_custom_call" | custom-call | flops 100663296 | bytes 1205248 | tf_op jit(solution)/shard_map/last_chunk/pallas_call | solution.py:235
  38.5 1.1 %collective-permute-start.18 = (bf16[256,256]{1,0:T(8,128)(2,1)S(1)}, bf16[256,256]{1,0:T(8,128)(2,1)S(1)}, u32[]{:S(2)}, u32[]{:S(2)}) collective-permute-start(bf16[256,256]{1,0:T(8,128)(2,1)S(1)} %get-tuple-element.41.refs_1_), channel_id=1, source_target_pairs={{0,4},{4,0},{1,5},{5,1},{2,6},{6,2},{3,7},{7,3},{8,12},{12,8},{9,1... | collective-permute-start | bytes 393224 | tf_op jit(solution)/shard_map/ppermute | solution.py:21
  40.0 1.6 %collective-permute-start.15 = (bf16[144,256]{1,0:T(8,128)(2,1)S(1)}, bf16[144,256]{1,0:T(8,128)(2,1)S(1)}, u32[]{:S(2)}, u32[]{:S(2)}) collective-permute-start(bf16[144,256]{1,0:T(8,128)(2,1)S(1)} %sum_core.1.own_ref), channel_id=1, source_target_pairs={{0,1},{1,0},{2,3},{3,2},{4,5},{5,4},{6,7},{7,6},{8,9},{9,8},{10,11... | collective-permute-start | bytes 221192 | tf_op jit(solution)/shard_map/ppermute | solution.py:21
  41.6 2.9 %collective-permute-done.18.refs_1_ = bf16[256,256]{1,0:T(8,128)(2,1)S(1)} collective-permute-done((bf16[256,256]{1,0:T(8,128)(2,1)S(1)}, bf16[256,256]{1,0:T(8,128)(2,1)S(1)}, u32[]{:S(2)}, u32[]{:S(2)}) %collective-permute-start.18) | collective-permute-done | bytes 131104 | tf_op jit(solution)/shard_map/ppermute | solution.py:21
  44.4 0.6 %collective-permute-start.16 = (bf16[144,256]{1,0:T(8,128)(2,1)S(1)}, bf16[144,256]{1,0:T(8,128)(2,1)S(1)}, u32[]{:S(2)}, u32[]{:S(2)}) collective-permute-start(bf16[144,256]{1,0:T(8,128)(2,1)S(1)} %sum_row.1.own_ref), channel_id=1, source_target_pairs={{0,2},{2,0},{1,3},{3,1},{4,6},{6,4},{5,7},{7,5},{8,10},{10,8},{9,1... | collective-permute-start | bytes 221192 | tf_op jit(solution)/shard_map/ppermute | solution.py:21
  45.3 0.4 collective-permute-done.20.refs_3_
  46.1 1.1 %collective-permute-start.21 = (bf16[272,256]{1,0:T(8,128)(2,1)S(1)}, bf16[272,256]{1,0:T(8,128)(2,1)S(1)}, u32[]{:S(2)}, u32[]{:S(2)}) collective-permute-start(bf16[272,256]{1,0:T(8,128)(2,1)S(1)} %halves.1.near_ref), channel_id=1, source_target_pairs={{0,4},{4,0},{1,5},{5,1},{2,6},{6,2},{3,7},{7,3},{8,12},{12,8},{9,1... | collective-permute-start | bytes 417800 | tf_op jit(solution)/shard_map/ppermute | solution.py:21
  47.2 1.5 %collective-permute-start.22 = (bf16[128,256]{1,0:T(8,128)(2,1)S(1)}, bf16[128,256]{1,0:T(8,128)(2,1)S(1)}, u32[]{:S(2)}, u32[]{:S(2)}) collective-permute-start(bf16[128,256]{1,0:T(8,128)(2,1)S(1)} %get-tuple-element.44), channel_id=1, source_target_pairs={{0,1},{1,0},{2,3},{3,2},{4,5},{5,4},{6,7},{7,6},{8,9},{9,8},{10,11... | collective-permute-start | bytes 196616 | tf_op jit(solution)/shard_map/ppermute | solution.py:21
  48.8 2.7 %collective-permute-done.22.refs_1_ = bf16[128,256]{1,0:T(8,128)(2,1)S(1)} collective-permute-done((bf16[128,256]{1,0:T(8,128)(2,1)S(1)}, bf16[128,256]{1,0:T(8,128)(2,1)S(1)}, u32[]{:S(2)}, u32[]{:S(2)}) %collective-permute-start.22) | collective-permute-done | bytes 65568 | tf_op jit(solution)/shard_map/ppermute | solution.py:21
  51.5 0.5 collective-permute-done.21.far_ref
  52.0 0.8 %last.1 = (f32[256,256]{1,0:T(8,128)}, f32[1,256]{1,0:T(1,128)}, bf16[128,256]{1,0:T(8,128)(2,1)}) custom-call(bf16[272,256]{1,0:T(8,128)(2,1)S(1)} %halves.1.near_ref, bf16[272,256]{1,0:T(8,128)(2,1)S(1)} %collective-permute-done.21.far_ref, f32[128,256]{1,0:T(8,128)S(1)} %get-tuple-element.42.refs_0_, bf16[128,256]{1,0:T(8,128)(2,1)S(1)} %collective-permute-done.22.refs_1_), custom_call_target="tpu_custom_call" | custom-call | bytes 803840 | tf_op jit(solution)/shard_map/last/pallas_call | solution.py:235
  (34 shorter events, 1.9 us)
Async XLA Ops:
  0.6 7.4 %collective-permute-start.1 = (bf16[128,256]{1,0:T(8,128)(2,1)}, bf16[128,256]{1,0:T(8,128)(2,1)S(1)}, u32[]{:S(2)}, u32[]{:S(2)}) collective-permute-start(bf16[128,256]{1,0:T(8,128)(2,1)} %c_hbm.1), channel_id=1, source_target_pairs={{0,8},{8,0},{16,24},{24,16},{1,9},{9,1},{17,25},{25,17},{2,10},{10... | collective-permute-start | bytes 196616 | tf_op jit(solution)/shard_map/ppermute | solution.py:21
  3.7 6.1 %collective-permute-start = (bf16[128,256]{1,0:T(8,128)(2,1)}, bf16[128,256]{1,0:T(8,128)(2,1)S(1)}, u32[]{:S(2)}, u32[]{:S(2)}) collective-permute-start(bf16[128,256]{1,0:T(8,128)(2,1)} %f_hbm.1), channel_id=1, source_target_pairs={{0,16},{8,24},{16,0},{24,8},{1,17},{9,25},{17,1},{25,9},{2,18},{10... | collective-permute-start | bytes 196616 | tf_op jit(solution)/shard_map/ppermute | solution.py:21
  9.9 6.4 %collective-permute-start.2 = (bf16[256,256]{1,0:T(8,128)(2,1)S(1)}, bf16[256,256]{1,0:T(8,128)(2,1)S(1)}, u32[]{:S(2)}, u32[]{:S(2)}) collective-permute-start(bf16[256,256]{1,0:T(8,128)(2,1)S(1)} %pack.3.refs_0_), channel_id=1, source_target_pairs={{0,8},{8,0},{16,24},{24,16},{1,9},{9,1},{17,25},{25,17},{2,10},{10... | collective-permute-start | bytes 393224 | tf_op jit(solution)/shard_map/ppermute | solution.py:21
  10.4 6.9 %collective-permute-start.5 = (bf16[256,256]{1,0:T(8,128)(2,1)S(1)}, bf16[256,256]{1,0:T(8,128)(2,1)S(1)}, u32[]{:S(2)}, u32[]{:S(2)}) collective-permute-start(bf16[256,256]{1,0:T(8,128)(2,1)S(1)} %pack.3.refs_0_), channel_id=1, source_target_pairs={{0,4},{4,0},{1,5},{5,1},{2,6},{6,2},{3,7},{7,3},{8,12},{12,8},{9,1... | collective-permute-start | bytes 393224 | tf_op jit(solution)/shard_map/ppermute | solution.py:21
  11.9 7.4 %collective-permute-start.8 = (bf16[256,256]{1,0:T(8,128)(2,1)S(1)}, bf16[256,256]{1,0:T(8,128)(2,1)S(1)}, u32[]{:S(2)}, u32[]{:S(2)}) collective-permute-start(bf16[256,256]{1,0:T(8,128)(2,1)S(1)} %pack.4.c0_ref), channel_id=1, source_target_pairs={{0,16},{8,24},{16,0},{24,8},{1,17},{9,25},{17,1},{25,9},{2,18},{10... | collective-permute-start | bytes 393224 | tf_op jit(solution)/shard_map/ppermute | solution.py:21
  16.2 5.0 %collective-permute-start.6 = (bf16[256,256]{1,0:T(8,128)(2,1)S(1)}, bf16[256,256]{1,0:T(8,128)(2,1)S(1)}, u32[]{:S(2)}, u32[]{:S(2)}) collective-permute-start(bf16[256,256]{1,0:T(8,128)(2,1)S(1)} %collective-permute-done.2.refs_1_), channel_id=1, source_target_pairs={{0,4},{4,0},{1,5},{5,1},{2,6},{6,2},{3,7},{7,3},{8,12},{12,8},{9,1... | collective-permute-start | bytes 393224 | tf_op jit(solution)/shard_map/ppermute | solution.py:21
  16.8 4.4 %collective-permute-start.3 = (bf16[256,256]{1,0:T(8,128)(2,1)S(1)}, bf16[256,256]{1,0:T(8,128)(2,1)S(1)}, u32[]{:S(2)}, u32[]{:S(2)}) collective-permute-start(bf16[256,256]{1,0:T(8,128)(2,1)S(1)} %pack.3.refs_0_), channel_id=1, source_target_pairs={{0,2},{2,0},{1,3},{3,1},{4,6},{6,4},{5,7},{7,5},{8,10},{10,8},{9,1... | collective-permute-start | bytes 393224 | tf_op jit(solution)/shard_map/ppermute | solution.py:21
  16.8 4.4 %collective-permute-start.4 = (bf16[256,256]{1,0:T(8,128)(2,1)S(1)}, bf16[256,256]{1,0:T(8,128)(2,1)S(1)}, u32[]{:S(2)}, u32[]{:S(2)}) collective-permute-start(bf16[256,256]{1,0:T(8,128)(2,1)S(1)} %collective-permute-done.2.refs_1_), channel_id=1, source_target_pairs={{0,2},{2,0},{1,3},{3,1},{4,6},{6,4},{5,7},{7,5},{8,10},{10,8},{9,1... | collective-permute-start | bytes 393224 | tf_op jit(solution)/shard_map/ppermute | solution.py:21
  17.3 4.2 %collective-permute-start.7 = (bf16[256,256]{1,0:T(8,128)(2,1)S(1)}, bf16[256,256]{1,0:T(8,128)(2,1)S(1)}, u32[]{:S(2)}, u32[]{:S(2)}) collective-permute-start(bf16[256,256]{1,0:T(8,128)(2,1)S(1)} %collective-permute-done.5.refs_0_), channel_id=1, source_target_pairs={{0,2},{2,0},{1,3},{3,1},{4,6},{6,4},{5,7},{7,5},{8,10},{10,8},{9,1... | collective-permute-start | bytes 393224 | tf_op jit(solution)/shard_map/ppermute | solution.py:21
  21.2 1.3 %collective-permute-start.9 = (bf16[256,256]{1,0:T(8,128)(2,1)S(1)}, bf16[256,256]{1,0:T(8,128)(2,1)S(1)}, u32[]{:S(2)}, u32[]{:S(2)}) collective-permute-start(bf16[256,256]{1,0:T(8,128)(2,1)S(1)} %collective-permute-done.6.refs_1_), channel_id=1, source_target_pairs={{0,2},{2,0},{1,3},{3,1},{4,6},{6,4},{5,7},{7,5},{8,10},{10,8},{9,1... | collective-permute-start | bytes 393224 | tf_op jit(solution)/shard_map/ppermute | solution.py:21
  22.9 4.3 %collective-permute-start.10 = (bf16[128,256]{1,0:T(8,128)(2,1)S(1)}, bf16[128,256]{1,0:T(8,128)(2,1)S(1)}, u32[]{:S(2)}, u32[]{:S(2)}) collective-permute-start(bf16[128,256]{1,0:T(8,128)(2,1)S(1)} %get-tuple-element.32), channel_id=1, source_target_pairs={{0,1},{1,0},{2,3},{3,2},{4,5},{5,4},{6,7},{7,6},{8,9},{9,8},{10,11... | collective-permute-start | bytes 196616 | tf_op jit(solution)/shard_map/ppermute | solution.py:21
  27.2 1.4 %copy-start = (bf16[256,256]{1,0:T(8,128)(2,1)S(1)}, bf16[256,256]{1,0:T(8,128)(2,1)}, u32[]{:S(2)}) copy-start(bf16[256,256]{1,0:T(8,128)(2,1)} %w_ref.5) | copy-start | bytes 393220
  27.2 1.4 %copy-start.1 = (f32[256]{0:T(256)S(1)}, f32[256]{0:T(256)}, u32[]{:S(2)}) copy-start(f32[256]{0:T(256)} %param.9) | copy-start | bytes 3076
  27.2 5.6 %collective-permute-start.11 = (bf16[128,256]{1,0:T(8,128)(2,1)S(1)}, bf16[128,256]{1,0:T(8,128)(2,1)S(1)}, u32[]{:S(2)}, u32[]{:S(2)}) collective-permute-start(bf16[128,256]{1,0:T(8,128)(2,1)S(1)} %hidden.1.h_ref.refs_0_), channel_id=1, source_target_pairs={{0,16},{8,24},{16,0},{24,8},{1,17},{9,25},{17,1},{25,9},{2,18},{10... | collective-permute-start | bytes 196616 | tf_op jit(solution)/shard_map/ppermute | solution.py:21
  32.8 5.0 %collective-permute-start.12 = (bf16[256,256]{1,0:T(8,128)(2,1)S(1)}, bf16[256,256]{1,0:T(8,128)(2,1)S(1)}, u32[]{:S(2)}, u32[]{:S(2)}) collective-permute-start(bf16[256,256]{1,0:T(8,128)(2,1)S(1)} %pack.5.h_ref), channel_id=1, source_target_pairs={{0,8},{8,0},{16,24},{24,16},{1,9},{9,1},{17,25},{25,17},{2,10},{10... | collective-permute-start | bytes 393224 | tf_op jit(solution)/shard_map/ppermute | solution.py:21
  33.4 5.0 %collective-permute-start.13 = (bf16[256,256]{1,0:T(8,128)(2,1)S(1)}, bf16[256,256]{1,0:T(8,128)(2,1)S(1)}, u32[]{:S(2)}, u32[]{:S(2)}) collective-permute-start(bf16[256,256]{1,0:T(8,128)(2,1)S(1)} %get-tuple-element.40.refs_0_), channel_id=1, source_target_pairs={{0,4},{4,0},{1,5},{5,1},{2,6},{6,2},{3,7},{7,3},{8,12},{12,8},{9,1... | collective-permute-start | bytes 393224 | tf_op jit(solution)/shard_map/ppermute | solution.py:21
  38.4 1.5 %collective-permute-start.14 = (bf16[400,256]{1,0:T(8,128)(2,1)S(1)}, bf16[400,256]{1,0:T(8,128)(2,1)S(1)}, u32[]{:S(2)}, u32[]{:S(2)}) collective-permute-start(bf16[400,256]{1,0:T(8,128)(2,1)S(1)} %get-tuple-element.39), channel_id=1, source_target_pairs={{0,2},{2,0},{1,3},{3,1},{4,6},{6,4},{5,7},{7,5},{8,10},{10,8},{9,1... | collective-permute-start | bytes 614408 | tf_op jit(solution)/shard_map/ppermute | solution.py:21
  38.5 5.9 %collective-permute-start.18 = (bf16[256,256]{1,0:T(8,128)(2,1)S(1)}, bf16[256,256]{1,0:T(8,128)(2,1)S(1)}, u32[]{:S(2)}, u32[]{:S(2)}) collective-permute-start(bf16[256,256]{1,0:T(8,128)(2,1)S(1)} %get-tuple-element.41.refs_1_), channel_id=1, source_target_pairs={{0,4},{4,0},{1,5},{5,1},{2,6},{6,2},{3,7},{7,3},{8,12},{12,8},{9,1... | collective-permute-start | bytes 393224 | tf_op jit(solution)/shard_map/ppermute | solution.py:21
  39.6 5.5 %collective-permute-start.17 = (bf16[256,256]{1,0:T(8,128)(2,1)S(1)}, bf16[256,256]{1,0:T(8,128)(2,1)S(1)}, u32[]{:S(2)}, u32[]{:S(2)}) collective-permute-start(bf16[256,256]{1,0:T(8,128)(2,1)S(1)} %get-tuple-element.40.refs_0_), channel_id=1, source_target_pairs={{0,2},{2,0},{1,3},{3,1},{4,6},{6,4},{5,7},{7,5},{8,10},{10,8},{9,1... | collective-permute-start | bytes 393224 | tf_op jit(solution)/shard_map/ppermute | solution.py:21
  40.0 4.4 %collective-permute-start.15 = (bf16[144,256]{1,0:T(8,128)(2,1)S(1)}, bf16[144,256]{1,0:T(8,128)(2,1)S(1)}, u32[]{:S(2)}, u32[]{:S(2)}) collective-permute-start(bf16[144,256]{1,0:T(8,128)(2,1)S(1)} %sum_core.1.own_ref), channel_id=1, source_target_pairs={{0,1},{1,0},{2,3},{3,2},{4,5},{5,4},{6,7},{7,6},{8,9},{9,8},{10,11... | collective-permute-start | bytes 221192 | tf_op jit(solution)/shard_map/ppermute | solution.py:21
  41.6 3.8 %collective-permute-start.19 = (bf16[256,256]{1,0:T(8,128)(2,1)S(1)}, bf16[256,256]{1,0:T(8,128)(2,1)S(1)}, u32[]{:S(2)}, u32[]{:S(2)}) collective-permute-start(bf16[256,256]{1,0:T(8,128)(2,1)S(1)} %collective-permute-done.13.refs_0_), channel_id=1, source_target_pairs={{0,2},{2,0},{1,3},{3,1},{4,6},{6,4},{5,7},{7,5},{8,10},{10,8},{9,1... | collective-permute-start | bytes 393224 | tf_op jit(solution)/shard_map/ppermute | solution.py:21
  44.4 1.3 %collective-permute-start.20 = (bf16[256,256]{1,0:T(8,128)(2,1)S(1)}, bf16[256,256]{1,0:T(8,128)(2,1)S(1)}, u32[]{:S(2)}, u32[]{:S(2)}) collective-permute-start(bf16[256,256]{1,0:T(8,128)(2,1)S(1)} %collective-permute-done.18.refs_1_), channel_id=1, source_target_pairs={{0,2},{2,0},{1,3},{3,1},{4,6},{6,4},{5,7},{7,5},{8,10},{10,8},{9,1... | collective-permute-start | bytes 393224 | tf_op jit(solution)/shard_map/ppermute | solution.py:21
  44.4 1.6 %collective-permute-start.16 = (bf16[144,256]{1,0:T(8,128)(2,1)S(1)}, bf16[144,256]{1,0:T(8,128)(2,1)S(1)}, u32[]{:S(2)}, u32[]{:S(2)}) collective-permute-start(bf16[144,256]{1,0:T(8,128)(2,1)S(1)} %sum_row.1.own_ref), channel_id=1, source_target_pairs={{0,2},{2,0},{1,3},{3,1},{4,6},{6,4},{5,7},{7,5},{8,10},{10,8},{9,1... | collective-permute-start | bytes 221192 | tf_op jit(solution)/shard_map/ppermute | solution.py:21
  46.1 5.8 %collective-permute-start.21 = (bf16[272,256]{1,0:T(8,128)(2,1)S(1)}, bf16[272,256]{1,0:T(8,128)(2,1)S(1)}, u32[]{:S(2)}, u32[]{:S(2)}) collective-permute-start(bf16[272,256]{1,0:T(8,128)(2,1)S(1)} %halves.1.near_ref), channel_id=1, source_target_pairs={{0,4},{4,0},{1,5},{5,1},{2,6},{6,2},{3,7},{7,3},{8,12},{12,8},{9,1... | collective-permute-start | bytes 417800 | tf_op jit(solution)/shard_map/ppermute | solution.py:21
  47.2 4.3 %collective-permute-start.22 = (bf16[128,256]{1,0:T(8,128)(2,1)S(1)}, bf16[128,256]{1,0:T(8,128)(2,1)S(1)}, u32[]{:S(2)}, u32[]{:S(2)}) collective-permute-start(bf16[128,256]{1,0:T(8,128)(2,1)S(1)} %get-tuple-element.44), channel_id=1, source_target_pairs={{0,1},{1,0},{2,3},{3,2},{4,5},{5,4},{6,7},{7,6},{8,9},{9,8},{10,11... | collective-permute-start | bytes 196616 | tf_op jit(solution)/shard_map/ppermute | solution.py:21

commit v9 on v6

--- a/solution.py
+++ b/solution.py
@@ -39,12 +39,6 @@
 
 def sigmoid(x):
     return 0.5 * jnp.tanh(0.5 * x) + 0.5
-
-
-def tree_sum(parts):
-    while len(parts) > 1:
-        parts = [parts[i] + parts[i + 1] for i in range(0, len(parts), 2)]
-    return parts[0]
 
 
 def far_masks(n_far):
@@ -106,10 +100,9 @@
 
 
 def pack_kernel(*refs):
-    at = 0
-    for ref in refs[:-1]:
-        refs[-1][at : at + ref.shape[0], :] = ref[...]
-        at += ref.shape[0]
+    tile = refs[-1].shape[0] // (len(refs) - 1)
+    for k, ref in enumerate(refs[:-1]):
+        refs[-1][k * tile : (k + 1) * tile, :] = ref[:tile, :]
 
 
 def near_kernel(tile, n_row, a_ref, *refs):
@@ -148,26 +141,6 @@
     out_ref[...] = total.astype(BF16)
 
 
-def chunk_grads(w_ref, b_ref, h_ref, c_ref, gh_ref):
-    tile, width = h_ref.shape[0] // 2, h_ref.shape[1]
-    weight_sums, bias_sums = [], []
-    for k in range(2):
-        rows = slice(k * tile, (k + 1) * tile)
-        hidden = h_ref[rows, :]
-        preact = dot(hidden, w_ref[...]) + b_ref[...]
-        sig = sigmoid(preact)
-        grad_z = c_ref[rows, :].astype(F32) * sig * (1.0 + preact * (1.0 - sig))
-        half = grad_z.astype(BF16)
-        gh_ref[rows, :] = dot(half, w_ref[...], ((1,), (1,))).astype(BF16)
-        bias_sums.append(jnp.sum(grad_z.reshape(tile // 8, 8, width), axis=0))
-        weight_sums.append(dot(hidden, half, ((0,), (0,))))
-    return tree_sum(weight_sums), tree_sum(bias_sums)
-
-
-def chunk_kernel(w_ref, b_ref, h_ref, c_ref, gh_ref, gw_ref, gb_ref):
-    gw_ref[...], gb_ref[...] = chunk_grads(w_ref, b_ref, h_ref, c_ref, gh_ref)
-
-
 def write_message(ref, grad_w, bias):
     rows, width = grad_w.shape
     ref[:rows, :] = grad_w.astype(BF16)
@@ -184,41 +157,39 @@
     return ref[:rows, :].astype(F32), tail[0:1, :] + tail[1:2, :]
 
 
-def last_chunk_kernel(n, w_ref, b_ref, h_ref, c_ref, *refs):
-    gw_refs, gb_refs = refs[:n], refs[n : 2 * n]
-    gh_ref, both_ref, keep_ref, sum_ref = refs[2 * n :]
-    half = keep_ref.shape[0] - PAD
-    grad_w, grad_b = chunk_grads(w_ref, b_ref, h_ref, c_ref, gh_ref)
-    sum_ref[...] = tree_sum([ref[...] for ref in gw_refs] + [grad_w])
-    grad_b = tree_sum([ref[...] for ref in gb_refs] + [grad_b])
-    bias = jnp.sum(grad_b, axis=0, keepdims=True)
+def grads_kernel(w_ref, b_ref, h_ref, c_ref, gh_ref, keep_ref, send_ref, sum_ref):
+    half_rows = keep_ref.shape[0] - PAD
+    hidden = h_ref[...]
+    preact = dot(hidden, w_ref[...]) + b_ref[...]
+    sig = sigmoid(preact)
+    grad_z = c_ref[...].astype(F32) * sig * (1.0 + preact * (1.0 - sig))
+    half = grad_z.astype(BF16)
+    tile, width = h_ref.shape
+    gh_ref[:tile, :] = dot(half, w_ref[...], ((1,), (1,))).astype(BF16)
+    gh_ref[tile:, :] = jnp.zeros((gh_ref.shape[0] - tile, width), BF16)
+    sum_ref[...] = dot(hidden, half, ((0,), (0,)))
+    bias = jnp.sum(grad_z, axis=0, keepdims=True)
     core = lax.axis_index("core")
-    kept = sum_ref[pl.ds(pl.multiple_of(core * half, half), half), :]
-    sent = sum_ref[pl.ds(pl.multiple_of((1 - core) * half, half), half), :]
-    write_message(keep_ref, kept, bias)
-    at = gh_ref.shape[0]
-    both_ref[:at, :] = gh_ref[...]
-    write_message(both_ref.at[at:, :], sent, bias)
+    for at, ref in ((core, keep_ref), (1 - core, send_ref)):
+        rows = pl.ds(pl.multiple_of(at * half_rows, half_rows), half_rows)
+        write_message(ref, sum_ref[rows, :], bias)
 
 
 def message_kernel(own_ref, other_ref, out_ref):
     own_w, own_b = read_message(own_ref)
-    other_w, other_b = read_message(other_ref.at[other_ref.shape[0] - own_ref.shape[0] :, :])
+    other_w, other_b = read_message(other_ref)
     write_message(out_ref, own_w + other_w, own_b + other_b)
 
 
-def last_kernel(factor, m00_ref, m10_ref, m01_ref, m11_ref, *refs):
+def last_kernel(factor, half_ref, other_ref, *refs):
     weight_ref, bias_ref, features_ref = refs[-3:]
     sum_kernel(*refs[:-3], features_ref)
     half = weight_ref.shape[0] // 2
     core = lax.axis_index("core")
-    for k, (near_ref, far_ref) in enumerate(((m00_ref, m10_ref), (m01_ref, m11_ref))):
-        near_w, near_b = read_message(near_ref)
-        far_w, far_b = read_message(far_ref)
-        at = jnp.bitwise_xor(core, k) * half
-        weight_ref[pl.ds(pl.multiple_of(at, half), half), :] = (near_w + far_w) * factor
-        if k == 0:
-            bias_ref[...] = (near_b + far_b) * factor
+    for at, ref in ((core, half_ref), (1 - core, other_ref)):
+        weight, bias = read_message(ref)
+        weight_ref[pl.ds(pl.multiple_of(at * half, half), half), :] = weight * factor
+    bias_ref[...] = bias * factor
 
 
 def call(kernel, name, outs, operands, scratch=(), specs=None, flops=0):
@@ -250,9 +221,6 @@
     def pack(*blocks):
         return call(pack_kernel, "pack", [shape(2 * tile, width)], blocks)[0]
 
-    def far_partner(block):
-        return partner(block, "far", steps[0], n_far)
-
     def far_chunks(pair):
         chunks = [pair]
         for step in steps[1:]:
@@ -280,7 +248,7 @@
     def from_row(parts):
         return [partner(part, "row", q + 1, n_row) for q, part in enumerate(parts)]
 
-    other = far_partner(features)
+    other = partner(features, "far", steps[0], n_far)
     adjacency, features, cotangent = call(
         functools.partial(expand_kernel, n_loop, n_row, tile),
         "expand",
@@ -299,76 +267,51 @@
     )
     f00 = far_chunks(pack(features, other))
     f10 = [swap(chunk, "mid") for chunk in f00]
-    other_cot = far_partner(after(cotangent, f00[-1]))
     f01 = [swap(chunk, "core") for chunk in f00]
     f11 = [swap(chunk, "core") for chunk in f10]
     half = near_product(f00 + f01, "forward")
     own, *parts = rest_product(half, f10 + f11, "forward")
-    others = from_row(parts)
-    cots = far_chunks(pack(after(cotangent, own), other_cot))
-    (hidden,) = call(sum_kernel, "hidden", [shape(tile, width)], [after(own, other_cot)] + others)
+    (hidden,) = call(sum_kernel, "hidden", [shape(tile, width)], [own] + from_row(parts))
 
     bias_row = bias_vector.reshape(1, width)
+    message_shape = shape(width // 2 + PAD, width)
+    grad_hidden, message, send = call(
+        grads_kernel,
+        "grads",
+        [shape(tile + 2 * PAD, width), message_shape, message_shape],
+        [weight, bias_row, hidden, cotangent],
+        scratch=[pltpu.VMEM((width, width), F32)],
+        flops=6 * tile * width * width,
+    )
     (output,) = call(
         output_kernel, "output", [shape(tile, width)], [weight, bias_row, hidden]
     )
-    other, hidden = far_partner(hidden), after(hidden, output)
-    hiddens = far_chunks(pack(hidden, other))
-    chunk_flops = 2 * tile * 6 * width * width
-    g00, weight_sums, bias_sums = [], [], []
-    sums = [shape(width, width, dtype=F32), shape(8, width, dtype=F32)]
-    for chunk, cot in zip(hiddens[:-1], cots[:-1]):
-        gh, weight_sum, bias_sum = call(
-            chunk_kernel,
-            "chunk",
-            [shape(2 * tile, width)] + sums,
-            [weight, bias_row, chunk, after(cot, cots[-1])],
-            flops=chunk_flops,
-        )
-        g00.append(gh)
-        weight_sums.append(weight_sum)
-        bias_sums.append(bias_sum)
-    half_rows = width // 2 + PAD
-    g01 = [swap(chunk, "core") for chunk in g00]
-    g10 = [swap(chunk, "mid") for chunk in g00]
-    gh, both, keep = call(
-        functools.partial(last_chunk_kernel, len(g00)),
-        "last_chunk",
-        [shape(2 * tile, width), shape(2 * tile + half_rows, width), shape(half_rows, width)],
-        [weight, bias_row, hiddens[-1], cots[-1]] + weight_sums + bias_sums,
-        scratch=[pltpu.VMEM((width, width), F32)],
-        flops=chunk_flops,
-    )
-    g00.append(gh)
-    g01.append(swap(after(both, *g10), "core"))
-    g10.append(swap(gh, "mid"))
-
-    (message,) = call(message_kernel, "sum_core", [shape(half_rows, width)], [keep, g01[-1]])
+
+    def add(message, other, name):
+        return call(message_kernel, name, [message_shape], [message, other])[0]
+
+    message = add(message, swap(send, "core"), "sum_core")
     bit = 1
     while bit < n_row:
-        (message,) = call(
-            message_kernel,
-            "sum_row",
-            [shape(half_rows, width)],
-            [message, partner(message, "row", bit, n_row)],
-        )
+        message = add(message, partner(message, "row", bit, n_row), "sum_row")
         bit *= 2
-    g11 = [swap(chunk, "core") for chunk in g10[:-1] + [after(g10[-1], message)]]
-    half = near_product(g00 + g01, "backward")
+    other = after(partner(grad_hidden, "far", steps[0], n_far), message, output)
+    g00 = far_chunks(pack(grad_hidden, other))
+    g10 = [swap(chunk, "mid") for chunk in g00]
+    g01 = [swap(chunk, "core") for chunk in g00]
+    g11 = [swap(chunk, "core") for chunk in g10]
+    message = add(message, partner(message, "far", steps[0], n_far), "sum_far")
+    half = near_product([after(g00[0], message)] + g00[1:] + g01, "backward")
     own, *parts = rest_product(half, g10 + g11, "backward")
     others = from_row(parts)
-    message = after(message, own)
-    messages = [
-        message,
-        swap(message, "mid"),
-        swap(message, "core"),
-        lax.ppermute(message, ("mid", "core"), [(i, 3 - i) for i in range(4)]),
-    ]
+    for step in steps[1:]:
+        message = add(after(message, own), partner(message, "far", step, n_far), "sum_far")
+    message = add(after(message, *others), swap(message, "mid"), "sum_mid")
     weight_grad, bias_grad, grad_features = call(
         functools.partial(last_kernel, 1.0 / nodes**0.5),
         "last",
         [shape(width, width, dtype=F32), shape(1, width, dtype=F32), shape(tile, width)],
-        messages + [own] + others,
+        [message, swap(message, "core"), own] + others,
     )
     return output, grad_features, weight_grad, bias_grad.reshape(width)
 

time: 55.2 us -> 59.1 us (1.071)
  waiting for transfers between devices: 20.6 us -> 28.2 us
  starting transfers between devices: 28.1 us -> 24 us
  local copies, waits for them, and re-layouts: 0.01 us -> 0.88 us
    ppermute x23 -> x24, waiting for transfers between devices: 20.6 us -> 28.2 us  [partner(): return lax.ppermute(x, axis, [(i, i ^ mask) for i in range(n)])]
    ppermute x23 -> x24, starting transfers between devices: 27.3 us -> 24 us  [partner(): return lax.ppermute(x, axis, [(i, i ^ mask) for i in range(n)])]
    unnamed x4, local copies, waits for them, and re-layouts: 0.01 us -> 0.88 us
    ppermute x1 -> x0, starting transfers between devices: 0.74 us -> none  [shards(): lax.ppermute(message, ('mid', 'core'), [(i, 3 - i) for i in range(4)])]
    pallas_call x15 -> x16, Pallas kernels: 5.6 us -> 5.05 us  [call(): pl.pallas_call(kernel, name=name, out_shape=outs, in_specs=specs or [VMEM...]
  transfers between devices with their start and end apart: 24 -> 24, of which waited for: 10 -> 13; matrix products, arithmetic and copies ran while one was open for 0% -> 0% of each run, Pallas kernels for 8% -> 6%
where the time goes in v9:
time: 59.1 us; the launch traced here: 59 us
  waiting for transfers between devices  28.2 us (48%)
  starting transfers between devices  24 us (41%)
  Pallas kernels  5.05 us (9%)
  local copies, waits for them, and re-layouts  0.88 us (1%)
  between operations  0.78 us (1%)
    ppermute x24, waiting for transfers between devices, partner(): return lax.ppermute(x, axis, [(i, i ^ mask) for i in range(n)])  28.2 us
    ppermute x24, starting transfers between devices, partner(): return lax.ppermute(x, axis, [(i, i ^ mask) for i in range(n)])  24 us
    pallas_call x16, Pallas kernels, call(): pl.pallas_call(kernel, name=name, out_shape=outs, in_specs=specs or [VMEM...  5.05 us
  transfers between devices with their start and end apart: 24, of which 13 were waited for; matrix products, arithmetic and copies ran while one was open for 0% of the time, Pallas kernels for 6%

profile of v9, /device:TPU:0, one launch (start us, length us, event | category | flops | bytes accessed | tf_op | source)
XLA Modules:
  0.0 59.0 jit_solution(13028018023073830979)
XLA Ops:
  0.6 4.1 %collective-permute-start = (bf16[128,256]{1,0:T(8,128)(2,1)}, bf16[128,256]{1,0:T(8,128)(2,1)S(1)}, u32[]{:S(2)}, u32[]{:S(2)}) collective-permute-start(bf16[128,256]{1,0:T(8,128)(2,1)} %f_hbm.1), channel_id=1, source_target_pairs={{0,16},{8,24},{16,0},{24,8},{1,17},{9,25},{17,1},{25,9},{2,18},{10... | collective-permute-start | bytes 196616 | tf_op jit(solution)/shard_map/ppermute | solution.py:21
  4.7 1.7 %expand.1 = (bf16[256,2048]{1,0:T(8,128)(2,1)S(1)}, bf16[128,256]{1,0:T(8,128)(2,1)S(1)}, bf16[128,256]{1,0:T(8,128)(2,1)S(1)}) custom-call(s32[32]{0:T(128)} %rows_hbm.1, s32[16]{0:T(128)} %counts_hbm.1, bf16[32,128,128]{2,1,0:T(8,128)(2,1)} %tiles_hbm.1, bf16[128,256]{1,0:T(8,128)(2,1)} %f_hbm.1, bf16[128,256]{1,0:T(8,128)(2,1)} %c_hbm.1), custom_call_target="tpu_custom_call" | custom-call | bytes 2359488 | tf_op jit(solution)/shard_map/expand/pallas_call | solution.py:200
  6.4 2.2 %collective-permute-done.refs_1_ = bf16[128,256]{1,0:T(8,128)(2,1)S(1)} collective-permute-done((bf16[128,256]{1,0:T(8,128)(2,1)}, bf16[128,256]{1,0:T(8,128)(2,1)S(1)}, u32[]{:S(2)}, u32[]{:S(2)}) %collective-permute-start) | collective-permute-done | bytes 65568 | tf_op jit(solution)/shard_map/ppermute | solution.py:21
  8.6 0.7 %collective-permute-start.1 = (bf16[256,256]{1,0:T(8,128)(2,1)S(1)}, bf16[256,256]{1,0:T(8,128)(2,1)S(1)}, u32[]{:S(2)}, u32[]{:S(2)}) collective-permute-start(bf16[256,256]{1,0:T(8,128)(2,1)S(1)} %pack.2.refs_0_), channel_id=1, source_target_pairs={{0,8},{8,0},{16,24},{24,16},{1,9},{9,1},{17,25},{25,17},{2,10},{10... | collective-permute-start | bytes 393224 | tf_op jit(solution)/shard_map/ppermute | solution.py:21
  9.3 1.5 %collective-permute-start.4 = (bf16[256,256]{1,0:T(8,128)(2,1)S(1)}, bf16[256,256]{1,0:T(8,128)(2,1)S(1)}, u32[]{:S(2)}, u32[]{:S(2)}) collective-permute-start(bf16[256,256]{1,0:T(8,128)(2,1)S(1)} %pack.2.refs_0_), channel_id=1, source_target_pairs={{0,4},{4,0},{1,5},{5,1},{2,6},{6,2},{3,7},{7,3},{8,12},{12,8},{9,1... | collective-permute-start | bytes 393224 | tf_op jit(solution)/shard_map/ppermute | solution.py:21
  10.8 2.8 %collective-permute-done.1.refs_1_ = bf16[256,256]{1,0:T(8,128)(2,1)S(1)} collective-permute-done((bf16[256,256]{1,0:T(8,128)(2,1)S(1)}, bf16[256,256]{1,0:T(8,128)(2,1)S(1)}, u32[]{:S(2)}, u32[]{:S(2)}) %collective-permute-start.1) | collective-permute-done | bytes 131104 | tf_op jit(solution)/shard_map/ppermute | solution.py:21
  13.6 1.7 %collective-permute-start.5 = (bf16[256,256]{1,0:T(8,128)(2,1)S(1)}, bf16[256,256]{1,0:T(8,128)(2,1)S(1)}, u32[]{:S(2)}, u32[]{:S(2)}) collective-permute-start(bf16[256,256]{1,0:T(8,128)(2,1)S(1)} %collective-permute-done.1.refs_1_), channel_id=1, source_target_pairs={{0,4},{4,0},{1,5},{5,1},{2,6},{6,2},{3,7},{7,3},{8,12},{12,8},{9,1... | collective-permute-start | bytes 393224 | tf_op jit(solution)/shard_map/ppermute | solution.py:21
  15.3 0.5 collective-permute-start.3
  15.9 2.8 %collective-permute-done.5.refs_1_ = bf16[256,256]{1,0:T(8,128)(2,1)S(1)} collective-permute-done((bf16[256,256]{1,0:T(8,128)(2,1)S(1)}, bf16[256,256]{1,0:T(8,128)(2,1)S(1)}, u32[]{:S(2)}, u32[]{:S(2)}) %collective-permute-start.5) | collective-permute-done | bytes 131104 | tf_op jit(solution)/shard_map/ppermute | solution.py:21
  18.9 1.0 %collective-permute-done.7.refs_3_ = bf16[256,256]{1,0:T(8,128)(2,1)S(1)} collective-permute-done((bf16[256,256]{1,0:T(8,128)(2,1)S(1)}, bf16[256,256]{1,0:T(8,128)(2,1)S(1)}, u32[]{:S(2)}, u32[]{:S(2)}) %collective-permute-start.7) | collective-permute-done | bytes 131104 | tf_op jit(solution)/shard_map/ppermute | solution.py:21
  20.3 1.8 %collective-permute-start.8 = (bf16[128,256]{1,0:T(8,128)(2,1)S(1)}, bf16[128,256]{1,0:T(8,128)(2,1)S(1)}, u32[]{:S(2)}, u32[]{:S(2)}) collective-permute-start(bf16[128,256]{1,0:T(8,128)(2,1)S(1)} %get-tuple-element.24), channel_id=1, source_target_pairs={{0,1},{1,0},{2,3},{3,2},{4,5},{5,4},{6,7},{7,6},{8,9},{9,8},{10,11... | collective-permute-start | bytes 196616 | tf_op jit(solution)/shard_map/ppermute | solution.py:21
  22.1 2.5 %collective-permute-done.8.refs_0_ = bf16[128,256]{1,0:T(8,128)(2,1)S(1)} collective-permute-done((bf16[128,256]{1,0:T(8,128)(2,1)S(1)}, bf16[128,256]{1,0:T(8,128)(2,1)S(1)}, u32[]{:S(2)}, u32[]{:S(2)}) %collective-permute-start.8) | collective-permute-done | bytes 65568 | tf_op jit(solution)/shard_map/ppermute | solution.py:21
  24.6 0.9 %copy-done = bf16[256,256]{1,0:T(8,128)(2,1)S(1)} copy-done((bf16[256,256]{1,0:T(8,128)(2,1)S(1)}, bf16[256,256]{1,0:T(8,128)(2,1)}, u32[]{:S(2)}) %copy-start) | copy-done | bytes 131096
  26.0 2.4 %collective-permute-start.12 = (bf16[160,256]{1,0:T(8,128)(2,1)S(1)}, bf16[160,256]{1,0:T(8,128)(2,1)S(1)}, u32[]{:S(2)}, u32[]{:S(2)}) collective-permute-start(bf16[160,256]{1,0:T(8,128)(2,1)S(1)} %get-tuple-element.28.refs_0_), channel_id=1, source_target_pairs={{0,16},{8,24},{16,0},{24,8},{1,17},{9,25},{17,1},{25,9},{2,18},{10... | collective-permute-start | bytes 245768 | tf_op jit(solution)/shard_map/ppermute | solution.py:21
  28.4 1.6 %collective-permute-start.10 = (bf16[144,256]{1,0:T(8,128)(2,1)S(1)}, bf16[144,256]{1,0:T(8,128)(2,1)S(1)}, u32[]{:S(2)}, u32[]{:S(2)}) collective-permute-start(bf16[144,256]{1,0:T(8,128)(2,1)S(1)} %sum_core.1.own_ref), channel_id=1, source_target_pairs={{0,1},{1,0},{2,3},{3,2},{4,5},{5,4},{6,7},{7,6},{8,9},{9,8},{10,11... | collective-permute-start | bytes 221192 | tf_op jit(solution)/shard_map/ppermute | solution.py:21
  30.0 0.8 %output.1 = bf16[128,256]{1,0:T(8,128)(2,1)} custom-call(bf16[256,256]{1,0:T(8,128)(2,1)S(1)} %copy-done, f32[1,256]{1,0:T(1,128)S(1)} %bitcast.3, bf16[128,256]{1,0:T(8,128)(2,1)S(1)} %hidden.1.h_ref), custom_call_target="tpu_custom_call" | custom-call | bytes 263168 | tf_op jit(solution)/shard_map/output/pallas_call | solution.py:200
  30.8 2.0 %collective-permute-done.10.other_ref = bf16[144,256]{1,0:T(8,128)(2,1)S(1)} collective-permute-done((bf16[144,256]{1,0:T(8,128)(2,1)S(1)}, bf16[144,256]{1,0:T(8,128)(2,1)S(1)}, u32[]{:S(2)}, u32[]{:S(2)}) %collective-permute-start.10) | collective-permute-done | bytes 73760 | tf_op jit(solution)/shard_map/ppermute | solution.py:21
  32.9 0.7 %collective-permute-done.12.refs_1_ = bf16[160,256]{1,0:T(8,128)(2,1)S(1)} collective-permute-done((bf16[160,256]{1,0:T(8,128)(2,1)S(1)}, bf16[160,256]{1,0:T(8,128)(2,1)S(1)}, u32[]{:S(2)}, u32[]{:S(2)}) %collective-permute-start.12) | collective-permute-done | bytes 81952 | tf_op jit(solution)/shard_map/ppermute | solution.py:21
  33.5 1.2 %collective-permute-start.13 = (bf16[256,256]{1,0:T(8,128)(2,1)S(1)}, bf16[256,256]{1,0:T(8,128)(2,1)S(1)}, u32[]{:S(2)}, u32[]{:S(2)}) collective-permute-start(bf16[256,256]{1,0:T(8,128)(2,1)S(1)} %pack.3.refs_0_), channel_id=1, source_target_pairs={{0,8},{8,0},{16,24},{24,16},{1,9},{9,1},{17,25},{25,17},{2,10},{10... | collective-permute-start | bytes 393224 | tf_op jit(solution)/shard_map/ppermute | solution.py:21
  34.7 1.5 %collective-permute-start.16 = (bf16[256,256]{1,0:T(8,128)(2,1)S(1)}, bf16[256,256]{1,0:T(8,128)(2,1)S(1)}, u32[]{:S(2)}, u32[]{:S(2)}) collective-permute-start(bf16[256,256]{1,0:T(8,128)(2,1)S(1)} %pack.3.refs_0_), channel_id=1, source_target_pairs={{0,4},{4,0},{1,5},{5,1},{2,6},{6,2},{3,7},{7,3},{8,12},{12,8},{9,1... | collective-permute-start | bytes 393224 | tf_op jit(solution)/shard_map/ppermute | solution.py:21
  36.2 2.5 %collective-permute-done.13.refs_1_ = bf16[256,256]{1,0:T(8,128)(2,1)S(1)} collective-permute-done((bf16[256,256]{1,0:T(8,128)(2,1)S(1)}, bf16[256,256]{1,0:T(8,128)(2,1)S(1)}, u32[]{:S(2)}, u32[]{:S(2)}) %collective-permute-start.13) | collective-permute-done | bytes 131104 | tf_op jit(solution)/shard_map/ppermute | solution.py:21
  38.7 1.7 %collective-permute-start.17 = (bf16[256,256]{1,0:T(8,128)(2,1)S(1)}, bf16[256,256]{1,0:T(8,128)(2,1)S(1)}, u32[]{:S(2)}, u32[]{:S(2)}) collective-permute-start(bf16[256,256]{1,0:T(8,128)(2,1)S(1)} %collective-permute-done.13.refs_1_), channel_id=1, source_target_pairs={{0,4},{4,0},{1,5},{5,1},{2,6},{6,2},{3,7},{7,3},{8,12},{12,8},{9,1... | collective-permute-start | bytes 393224 | tf_op jit(solution)/shard_map/ppermute | solution.py:21
  40.4 0.5 collective-permute-start.15
  40.9 2.2 %collective-permute-start.11 = (bf16[144,256]{1,0:T(8,128)(2,1)S(1)}, bf16[144,256]{1,0:T(8,128)(2,1)S(1)}, u32[]{:S(2)}, u32[]{:S(2)}) collective-permute-start(bf16[144,256]{1,0:T(8,128)(2,1)S(1)} %sum_row.1.own_ref), channel_id=1, source_target_pairs={{0,16},{8,24},{16,0},{24,8},{1,17},{9,25},{17,1},{25,9},{2,18},{10... | collective-permute-start | bytes 221192 | tf_op jit(solution)/shard_map/ppermute | solution.py:21
  43.1 0.5 collective-permute-done.17.refs_1_
  43.6 3.9 %collective-permute-done.11.other_ref = bf16[144,256]{1,0:T(8,128)(2,1)S(1)} collective-permute-done((bf16[144,256]{1,0:T(8,128)(2,1)S(1)}, bf16[144,256]{1,0:T(8,128)(2,1)S(1)}, u32[]{:S(2)}, u32[]{:S(2)}) %collective-permute-start.11) | collective-permute-done | bytes 73760 | tf_op jit(solution)/shard_map/ppermute | solution.py:21
  48.6 3.4 %collective-permute-done.20.other_ref = bf16[144,256]{1,0:T(8,128)(2,1)S(1)} collective-permute-done((bf16[144,256]{1,0:T(8,128)(2,1)S(1)}, bf16[144,256]{1,0:T(8,128)(2,1)S(1)}, u32[]{:S(2)}, u32[]{:S(2)}) %collective-permute-start.20) | collective-permute-done | bytes 73760 | tf_op jit(solution)/shard_map/ppermute | solution.py:21
  52.0 0.6 collective-permute-start.22
  52.6 1.6 %collective-permute-start.21 = (bf16[128,256]{1,0:T(8,128)(2,1)S(1)}, bf16[128,256]{1,0:T(8,128)(2,1)S(1)}, u32[]{:S(2)}, u32[]{:S(2)}) collective-permute-start(bf16[128,256]{1,0:T(8,128)(2,1)S(1)} %get-tuple-element.33), channel_id=1, source_target_pairs={{0,1},{1,0},{2,3},{3,2},{4,5},{5,4},{6,7},{7,6},{8,9},{9,8},{10,11... | collective-permute-start | bytes 196616 | tf_op jit(solution)/shard_map/ppermute | solution.py:21
  54.1 2.7 %collective-permute-done.21.refs_1_ = bf16[128,256]{1,0:T(8,128)(2,1)S(1)} collective-permute-done((bf16[128,256]{1,0:T(8,128)(2,1)S(1)}, bf16[128,256]{1,0:T(8,128)(2,1)S(1)}, u32[]{:S(2)}, u32[]{:S(2)}) %collective-permute-start.21) | collective-permute-done | bytes 65568 | tf_op jit(solution)/shard_map/ppermute | solution.py:21
  57.0 1.3 %collective-permute-done.23.other_ref = bf16[144,256]{1,0:T(8,128)(2,1)S(1)} collective-permute-done((bf16[144,256]{1,0:T(8,128)(2,1)S(1)}, bf16[144,256]{1,0:T(8,128)(2,1)S(1)}, u32[]{:S(2)}, u32[]{:S(2)}) %collective-permute-start.23) | collective-permute-done | bytes 73760 | tf_op jit(solution)/shard_map/ppermute | solution.py:21
  58.2 0.8 %last.1 = (f32[256,256]{1,0:T(8,128)}, f32[1,256]{1,0:T(1,128)}, bf16[128,256]{1,0:T(8,128)(2,1)}) custom-call(bf16[144,256]{1,0:T(8,128)(2,1)S(1)} %sum_mid.1.half_ref, bf16[144,256]{1,0:T(8,128)(2,1)S(1)} %collective-permute-done.23.other_ref, f32[128,256]{1,0:T(8,128)S(1)} %get-tuple-element.31.refs_0_, bf16[128,256]{1,0:T(8,128)(2,1)S(1)} %collective-permute-done.21.refs_1_), custom_call_target="tpu_custom_call" | custom-call | bytes 672768 | tf_op jit(solution)/shard_map/last/pallas_call | solution.py:200
  (36 shorter events, 2.4 us)
Async XLA Ops:
  0.6 8.0 %collective-permute-start = (bf16[128,256]{1,0:T(8,128)(2,1)}, bf16[128,256]{1,0:T(8,128)(2,1)S(1)}, u32[]{:S(2)}, u32[]{:S(2)}) collective-permute-start(bf16[128,256]{1,0:T(8,128)(2,1)} %f_hbm.1), channel_id=1, source_target_pairs={{0,16},{8,24},{16,0},{24,8},{1,17},{9,25},{17,1},{25,9},{2,18},{10... | collective-permute-start | bytes 196616 | tf_op jit(solution)/shard_map/ppermute | solution.py:21
  8.6 5.0 %collective-permute-start.1 = (bf16[256,256]{1,0:T(8,128)(2,1)S(1)}, bf16[256,256]{1,0:T(8,128)(2,1)S(1)}, u32[]{:S(2)}, u32[]{:S(2)}) collective-permute-start(bf16[256,256]{1,0:T(8,128)(2,1)S(1)} %pack.2.refs_0_), channel_id=1, source_target_pairs={{0,8},{8,0},{16,24},{24,16},{1,9},{9,1},{17,25},{25,17},{2,10},{10... | collective-permute-start | bytes 393224 | tf_op jit(solution)/shard_map/ppermute | solution.py:21
  9.3 6.5 %collective-permute-start.4 = (bf16[256,256]{1,0:T(8,128)(2,1)S(1)}, bf16[256,256]{1,0:T(8,128)(2,1)S(1)}, u32[]{:S(2)}, u32[]{:S(2)}) collective-permute-start(bf16[256,256]{1,0:T(8,128)(2,1)S(1)} %pack.2.refs_0_), channel_id=1, source_target_pairs={{0,4},{4,0},{1,5},{5,1},{2,6},{6,2},{3,7},{7,3},{8,12},{12,8},{9,1... | collective-permute-start | bytes 393224 | tf_op jit(solution)/shard_map/ppermute | solution.py:21
  13.6 5.0 %collective-permute-start.5 = (bf16[256,256]{1,0:T(8,128)(2,1)S(1)}, bf16[256,256]{1,0:T(8,128)(2,1)S(1)}, u32[]{:S(2)}, u32[]{:S(2)}) collective-permute-start(bf16[256,256]{1,0:T(8,128)(2,1)S(1)} %collective-permute-done.1.refs_1_), channel_id=1, source_target_pairs={{0,4},{4,0},{1,5},{5,1},{2,6},{6,2},{3,7},{7,3},{8,12},{12,8},{9,1... | collective-permute-start | bytes 393224 | tf_op jit(solution)/shard_map/ppermute | solution.py:21
  15.3 3.3 %collective-permute-start.2 = (bf16[256,256]{1,0:T(8,128)(2,1)S(1)}, bf16[256,256]{1,0:T(8,128)(2,1)S(1)}, u32[]{:S(2)}, u32[]{:S(2)}) collective-permute-start(bf16[256,256]{1,0:T(8,128)(2,1)S(1)} %pack.2.refs_0_), channel_id=1, source_target_pairs={{0,2},{2,0},{1,3},{3,1},{4,6},{6,4},{5,7},{7,5},{8,10},{10,8},{9,1... | collective-permute-start | bytes 393224 | tf_op jit(solution)/shard_map/ppermute | solution.py:21
  15.3 3.3 %collective-permute-start.3 = (bf16[256,256]{1,0:T(8,128)(2,1)S(1)}, bf16[256,256]{1,0:T(8,128)(2,1)S(1)}, u32[]{:S(2)}, u32[]{:S(2)}) collective-permute-start(bf16[256,256]{1,0:T(8,128)(2,1)S(1)} %collective-permute-done.1.refs_1_), channel_id=1, source_target_pairs={{0,2},{2,0},{1,3},{3,1},{4,6},{6,4},{5,7},{7,5},{8,10},{10,8},{9,1... | collective-permute-start | bytes 393224 | tf_op jit(solution)/shard_map/ppermute | solution.py:21
  15.9 3.1 %collective-permute-start.6 = (bf16[256,256]{1,0:T(8,128)(2,1)S(1)}, bf16[256,256]{1,0:T(8,128)(2,1)S(1)}, u32[]{:S(2)}, u32[]{:S(2)}) collective-permute-start(bf16[256,256]{1,0:T(8,128)(2,1)S(1)} %collective-permute-done.4.refs_0_), channel_id=1, source_target_pairs={{0,2},{2,0},{1,3},{3,1},{4,6},{6,4},{5,7},{7,5},{8,10},{10,8},{9,1... | collective-permute-start | bytes 393224 | tf_op jit(solution)/shard_map/ppermute | solution.py:21
  18.6 1.3 %collective-permute-start.7 = (bf16[256,256]{1,0:T(8,128)(2,1)S(1)}, bf16[256,256]{1,0:T(8,128)(2,1)S(1)}, u32[]{:S(2)}, u32[]{:S(2)}) collective-permute-start(bf16[256,256]{1,0:T(8,128)(2,1)S(1)} %collective-permute-done.5.refs_1_), channel_id=1, source_target_pairs={{0,2},{2,0},{1,3},{3,1},{4,6},{6,4},{5,7},{7,5},{8,10},{10,8},{9,1... | collective-permute-start | bytes 393224 | tf_op jit(solution)/shard_map/ppermute | solution.py:21
  20.3 4.3 %collective-permute-start.8 = (bf16[128,256]{1,0:T(8,128)(2,1)S(1)}, bf16[128,256]{1,0:T(8,128)(2,1)S(1)}, u32[]{:S(2)}, u32[]{:S(2)}) collective-permute-start(bf16[128,256]{1,0:T(8,128)(2,1)S(1)} %get-tuple-element.24), channel_id=1, source_target_pairs={{0,1},{1,0},{2,3},{3,2},{4,5},{5,4},{6,7},{7,6},{8,9},{9,8},{10,11... | collective-permute-start | bytes 196616 | tf_op jit(solution)/shard_map/ppermute | solution.py:21
  24.6 0.9 %copy-start = (bf16[256,256]{1,0:T(8,128)(2,1)S(1)}, bf16[256,256]{1,0:T(8,128)(2,1)}, u32[]{:S(2)}) copy-start(bf16[256,256]{1,0:T(8,128)(2,1)} %w_ref.3) | copy-start | bytes 393220
  24.6 0.9 %copy-start.1 = (f32[256]{0:T(256)S(1)}, f32[256]{0:T(256)}, u32[]{:S(2)}) copy-start(f32[256]{0:T(256)} %param.9) | copy-start | bytes 3076
  25.9 2.5 %collective-permute-start.9 = (bf16[144,256]{1,0:T(8,128)(2,1)S(1)}, bf16[144,256]{1,0:T(8,128)(2,1)S(1)}, u32[]{:S(2)}, u32[]{:S(2)}) collective-permute-start(bf16[144,256]{1,0:T(8,128)(2,1)S(1)} %get-tuple-element.27), channel_id=1, source_target_pairs={{0,2},{2,0},{1,3},{3,1},{4,6},{6,4},{5,7},{7,5},{8,10},{10,8},{9,1... | collective-permute-start | bytes 221192 | tf_op jit(solution)/shard_map/ppermute | solution.py:21
  26.0 7.5 %collective-permute-start.12 = (bf16[160,256]{1,0:T(8,128)(2,1)S(1)}, bf16[160,256]{1,0:T(8,128)(2,1)S(1)}, u32[]{:S(2)}, u32[]{:S(2)}) collective-permute-start(bf16[160,256]{1,0:T(8,128)(2,1)S(1)} %get-tuple-element.28.refs_0_), channel_id=1, source_target_pairs={{0,16},{8,24},{16,0},{24,8},{1,17},{9,25},{17,1},{25,9},{2,18},{10... | collective-permute-start | bytes 245768 | tf_op jit(solution)/shard_map/ppermute | solution.py:21
  28.4 4.4 %collective-permute-start.10 = (bf16[144,256]{1,0:T(8,128)(2,1)S(1)}, bf16[144,256]{1,0:T(8,128)(2,1)S(1)}, u32[]{:S(2)}, u32[]{:S(2)}) collective-permute-start(bf16[144,256]{1,0:T(8,128)(2,1)S(1)} %sum_core.1.own_ref), channel_id=1, source_target_pairs={{0,1},{1,0},{2,3},{3,2},{4,5},{5,4},{6,7},{7,6},{8,9},{9,8},{10,11... | collective-permute-start | bytes 221192 | tf_op jit(solution)/shard_map/ppermute | solution.py:21
  33.5 5.1 %collective-permute-start.13 = (bf16[256,256]{1,0:T(8,128)(2,1)S(1)}, bf16[256,256]{1,0:T(8,128)(2,1)S(1)}, u32[]{:S(2)}, u32[]{:S(2)}) collective-permute-start(bf16[256,256]{1,0:T(8,128)(2,1)S(1)} %pack.3.refs_0_), channel_id=1, source_target_pairs={{0,8},{8,0},{16,24},{24,16},{1,9},{9,1},{17,25},{25,17},{2,10},{10... | collective-permute-start | bytes 393224 | tf_op jit(solution)/shard_map/ppermute | solution.py:21
  34.7 8.4 %collective-permute-start.16 = (bf16[256,256]{1,0:T(8,128)(2,1)S(1)}, bf16[256,256]{1,0:T(8,128)(2,1)S(1)}, u32[]{:S(2)}, u32[]{:S(2)}) collective-permute-start(bf16[256,256]{1,0:T(8,128)(2,1)S(1)} %pack.3.refs_0_), channel_id=1, source_target_pairs={{0,4},{4,0},{1,5},{5,1},{2,6},{6,2},{3,7},{7,3},{8,12},{12,8},{9,1... | collective-permute-start | bytes 393224 | tf_op jit(solution)/shard_map/ppermute | solution.py:21
  38.7 5.0 %collective-permute-start.17 = (bf16[256,256]{1,0:T(8,128)(2,1)S(1)}, bf16[256,256]{1,0:T(8,128)(2,1)S(1)}, u32[]{:S(2)}, u32[]{:S(2)}) collective-permute-start(bf16[256,256]{1,0:T(8,128)(2,1)S(1)} %collective-permute-done.13.refs_1_), channel_id=1, source_target_pairs={{0,4},{4,0},{1,5},{5,1},{2,6},{6,2},{3,7},{7,3},{8,12},{12,8},{9,1... | collective-permute-start | bytes 393224 | tf_op jit(solution)/shard_map/ppermute | solution.py:21
  40.4 7.6 %collective-permute-start.14 = (bf16[256,256]{1,0:T(8,128)(2,1)S(1)}, bf16[256,256]{1,0:T(8,128)(2,1)S(1)}, u32[]{:S(2)}, u32[]{:S(2)}) collective-permute-start(bf16[256,256]{1,0:T(8,128)(2,1)S(1)} %pack.3.refs_0_), channel_id=1, source_target_pairs={{0,2},{2,0},{1,3},{3,1},{4,6},{6,4},{5,7},{7,5},{8,10},{10,8},{9,1... | collective-permute-start | bytes 393224 | tf_op jit(solution)/shard_map/ppermute | solution.py:21
  40.4 7.6 %collective-permute-start.15 = (bf16[256,256]{1,0:T(8,128)(2,1)S(1)}, bf16[256,256]{1,0:T(8,128)(2,1)S(1)}, u32[]{:S(2)}, u32[]{:S(2)}) collective-permute-start(bf16[256,256]{1,0:T(8,128)(2,1)S(1)} %collective-permute-done.13.refs_1_), channel_id=1, source_target_pairs={{0,2},{2,0},{1,3},{3,1},{4,6},{6,4},{5,7},{7,5},{8,10},{10,8},{9,1... | collective-permute-start | bytes 393224 | tf_op jit(solution)/shard_map/ppermute | solution.py:21
  40.9 6.7 %collective-permute-start.11 = (bf16[144,256]{1,0:T(8,128)(2,1)S(1)}, bf16[144,256]{1,0:T(8,128)(2,1)S(1)}, u32[]{:S(2)}, u32[]{:S(2)}) collective-permute-start(bf16[144,256]{1,0:T(8,128)(2,1)S(1)} %sum_row.1.own_ref), channel_id=1, source_target_pairs={{0,16},{8,24},{16,0},{24,8},{1,17},{9,25},{17,1},{25,9},{2,18},{10... | collective-permute-start | bytes 221192 | tf_op jit(solution)/shard_map/ppermute | solution.py:21
  43.1 5.1 %collective-permute-start.18 = (bf16[256,256]{1,0:T(8,128)(2,1)S(1)}, bf16[256,256]{1,0:T(8,128)(2,1)S(1)}, u32[]{:S(2)}, u32[]{:S(2)}) collective-permute-start(bf16[256,256]{1,0:T(8,128)(2,1)S(1)} %collective-permute-done.16.refs_0_), channel_id=1, source_target_pairs={{0,2},{2,0},{1,3},{3,1},{4,6},{6,4},{5,7},{7,5},{8,10},{10,8},{9,1... | collective-permute-start | bytes 393224 | tf_op jit(solution)/shard_map/ppermute | solution.py:21
  43.6 4.6 %collective-permute-start.19 = (bf16[256,256]{1,0:T(8,128)(2,1)S(1)}, bf16[256,256]{1,0:T(8,128)(2,1)S(1)}, u32[]{:S(2)}, u32[]{:S(2)}) collective-permute-start(bf16[256,256]{1,0:T(8,128)(2,1)S(1)} %collective-permute-done.17.refs_1_), channel_id=1, source_target_pairs={{0,2},{2,0},{1,3},{3,1},{4,6},{6,4},{5,7},{7,5},{8,10},{10,8},{9,1... | collective-permute-start | bytes 393224 | tf_op jit(solution)/shard_map/ppermute | solution.py:21
  47.6 4.4 %collective-permute-start.20 = (bf16[144,256]{1,0:T(8,128)(2,1)S(1)}, bf16[144,256]{1,0:T(8,128)(2,1)S(1)}, u32[]{:S(2)}, u32[]{:S(2)}) collective-permute-start(bf16[144,256]{1,0:T(8,128)(2,1)S(1)} %sum_far.2.own_ref), channel_id=1, source_target_pairs={{0,8},{8,0},{16,24},{24,16},{1,9},{9,1},{17,25},{25,17},{2,10},{10... | collective-permute-start | bytes 221192 | tf_op jit(solution)/shard_map/ppermute | solution.py:21
  52.0 4.8 %collective-permute-start.22 = (bf16[144,256]{1,0:T(8,128)(2,1)S(1)}, bf16[144,256]{1,0:T(8,128)(2,1)S(1)}, u32[]{:S(2)}, u32[]{:S(2)}) collective-permute-start(bf16[144,256]{1,0:T(8,128)(2,1)S(1)} %sum_far.3.own_ref), channel_id=1, source_target_pairs={{0,4},{4,0},{1,5},{5,1},{2,6},{6,2},{3,7},{7,3},{8,12},{12,8},{9,1... | collective-permute-start | bytes 221192 | tf_op jit(solution)/shard_map/ppermute | solution.py:21
  52.6 4.3 %collective-permute-start.21 = (bf16[128,256]{1,0:T(8,128)(2,1)S(1)}, bf16[128,256]{1,0:T(8,128)(2,1)S(1)}, u32[]{:S(2)}, u32[]{:S(2)}) collective-permute-start(bf16[128,256]{1,0:T(8,128)(2,1)S(1)} %get-tuple-element.33), channel_id=1, source_target_pairs={{0,1},{1,0},{2,3},{3,2},{4,5},{5,4},{6,7},{7,6},{8,9},{9,8},{10,11... | collective-permute-start | bytes 196616 | tf_op jit(solution)/shard_map/ppermute | solution.py:21
  56.9 1.3 %collective-permute-start.23 = (bf16[144,256]{1,0:T(8,128)(2,1)S(1)}, bf16[144,256]{1,0:T(8,128)(2,1)S(1)}, u32[]{:S(2)}, u32[]{:S(2)}) collective-permute-start(bf16[144,256]{1,0:T(8,128)(2,1)S(1)} %sum_mid.1.half_ref), channel_id=1, source_target_pairs={{0,2},{2,0},{1,3},{3,1},{4,6},{6,4},{5,7},{7,5},{8,10},{10,8},{9,1... | collective-permute-start | bytes 221192 | tf_op jit(solution)/shard_map/ppermute | solution.py:21

commit v10 on v9

--- a/solution.py
+++ b/solution.py
@@ -53,8 +53,8 @@
 
 
 def expand_kernel(
-    n_loop, n_row, tile, rows_hbm, counts_hbm, tiles_hbm, f_hbm, c_hbm, out_ref, f_out, c_out,
-    rows_ref, counts_ref, tiles_ref, sems,
+    n_loop, n_row, tile, rows_hbm, counts_hbm, tiles_hbm, f_hbm, c_hbm, w_hbm, b_hbm,
+    out_ref, f_out, c_out, w_out, b_out, rows_ref, counts_ref, tiles_ref, sems,
 ):
     copies = [
         pltpu.make_async_copy(source, target, sems.at[k])
@@ -65,6 +65,8 @@
                 (tiles_hbm, tiles_ref),
                 (f_hbm, f_out),
                 (c_hbm, c_out),
+                (w_hbm, w_out),
+                (b_hbm, b_out),
             )
         )
     ]
@@ -181,15 +183,21 @@
     write_message(out_ref, own_w + other_w, own_b + other_b)
 
 
-def last_kernel(factor, half_ref, other_ref, *refs):
+def halves_kernel(own_ref, other_ref, out_ref):
+    half = own_ref.shape[0] - PAD
+    core = lax.axis_index("core")
+    out_ref[pl.ds(pl.multiple_of(core * half, half), half), :] = own_ref[:half, :]
+    out_ref[pl.ds(pl.multiple_of((1 - core) * half, half), half), :] = other_ref[:half, :]
+    out_ref[2 * half :, :] = own_ref[half:, :]
+
+
+def last_kernel(factor, near_ref, far_ref, *refs):
     weight_ref, bias_ref, features_ref = refs[-3:]
     sum_kernel(*refs[:-3], features_ref)
-    half = weight_ref.shape[0] // 2
-    core = lax.axis_index("core")
-    for at, ref in ((core, half_ref), (1 - core, other_ref)):
-        weight, bias = read_message(ref)
-        weight_ref[pl.ds(pl.multiple_of(at * half, half), half), :] = weight * factor
-    bias_ref[...] = bias * factor
+    near_w, near_b = read_message(near_ref)
+    far_w, far_b = read_message(far_ref)
+    weight_ref[...] = (near_w + far_w) * factor
+    bias_ref[...] = (near_b + far_b) * factor
 
 
 def call(kernel, name, outs, operands, scratch=(), specs=None, flops=0):
@@ -249,21 +257,30 @@
         return [partner(part, "row", q + 1, n_row) for q, part in enumerate(parts)]
 
     other = partner(features, "far", steps[0], n_far)
-    adjacency, features, cotangent = call(
+    adjacency, features, cotangent, weight, bias_row = call(
         functools.partial(expand_kernel, n_loop, n_row, tile),
         "expand",
-        [shape(rows, n_loop * tile), shape(tile, width), shape(tile, width)],
+        [
+            shape(rows, n_loop * tile),
+            shape(tile, width),
+            shape(tile, width),
+            shape(width, width),
+            shape(1, width, dtype=F32),
+        ],
         [
             pltpu.with_memory_space_constraint(x, pltpu.HBM)
-            for x in (tile_rows, counts, tile_values, features, cotangent)
+            for x in (
+                tile_rows, counts, tile_values, features, cotangent, weight,
+                bias_vector.reshape(1, width),
+            )
         ],
         scratch=[
             pltpu.SMEM(tile_rows.shape, jnp.int32),
             pltpu.SMEM(counts.shape, jnp.int32),
             pltpu.VMEM(tile_values.shape, BF16),
-            pltpu.SemaphoreType.DMA((5,)),
+            pltpu.SemaphoreType.DMA((7,)),
         ],
-        specs=[pl.BlockSpec(memory_space=pltpu.HBM)] * 5,
+        specs=[pl.BlockSpec(memory_space=pltpu.HBM)] * 7,
     )
     f00 = far_chunks(pack(features, other))
     f10 = [swap(chunk, "mid") for chunk in f00]
@@ -273,7 +290,6 @@
     own, *parts = rest_product(half, f10 + f11, "forward")
     (hidden,) = call(sum_kernel, "hidden", [shape(tile, width)], [own] + from_row(parts))
 
-    bias_row = bias_vector.reshape(1, width)
     message_shape = shape(width // 2 + PAD, width)
     grad_hidden, message, send = call(
         grads_kernel,
@@ -297,21 +313,27 @@
         bit *= 2
     other = after(partner(grad_hidden, "far", steps[0], n_far), message, output)
     g00 = far_chunks(pack(grad_hidden, other))
-    g10 = [swap(chunk, "mid") for chunk in g00]
+    message = add(message, partner(message, "far", steps[0], n_far), "sum_far")
+    g10 = [swap(chunk, "mid") for chunk in g00[:1] + [after(c, message) for c in g00[1:]]]
     g01 = [swap(chunk, "core") for chunk in g00]
-    g11 = [swap(chunk, "core") for chunk in g10]
-    message = add(message, partner(message, "far", steps[0], n_far), "sum_far")
-    half = near_product([after(g00[0], message)] + g00[1:] + g01, "backward")
+    for step in steps[1:]:
+        message = add(message, partner(message, "far", step, n_far), "sum_far")
+    g11 = [swap(chunk, "core") for chunk in g10[:-1] + [after(g10[-1], message)]]
+    half = near_product(g00 + g01, "backward")
     own, *parts = rest_product(half, g10 + g11, "backward")
     others = from_row(parts)
-    for step in steps[1:]:
-        message = add(after(message, own), partner(message, "far", step, n_far), "sum_far")
-    message = add(after(message, *others), swap(message, "mid"), "sum_mid")
+    (message,) = call(
+        halves_kernel,
+        "halves",
+        [shape(width + PAD, width)],
+        [message, swap(message, "core")],
+    )
+    message = after(message, own)
     weight_grad, bias_grad, grad_features = call(
         functools.partial(last_kernel, 1.0 / nodes**0.5),
         "last",
         [shape(width, width, dtype=F32), shape(1, width, dtype=F32), shape(tile, width)],
-        [message, swap(message, "core"), own] + others,
+        [message, swap(message, "mid"), own] + others,
     )
     return output, grad_features, weight_grad, bias_grad.reshape(width)
 

time: 59.1 us -> 54.9 us (0.929)
  waiting for transfers between devices: 28.2 us -> 21.9 us
  starting transfers between devices: 24 us -> 26.9 us
  local copies, waits for them, and re-layouts: 0.88 us -> 0 us
    ppermute x24, waiting for transfers between devices: 28.2 us -> 21.9 us  [partner(): return lax.ppermute(x, axis, [(i, i ^ mask) for i in range(n)])]
    ppermute x24, starting transfers between devices: 24 us -> 26.9 us  [partner(): return lax.ppermute(x, axis, [(i, i ^ mask) for i in range(n)])]
    unnamed x4 -> x0, local copies, waits for them, and re-layouts: 0.88 us -> none
where the time goes in v10:
time: 54.9 us; the launch traced here: 54.7 us
  starting transfers between devices  26.9 us (49%)
  waiting for transfers between devices  21.9 us (40%)
  Pallas kernels  5.12 us (9%)
  between operations  0.79 us (1%)
    ppermute x24, starting transfers between devices, partner(): return lax.ppermute(x, axis, [(i, i ^ mask) for i in range(n)])  26.9 us
    ppermute x24, waiting for transfers between devices, partner(): return lax.ppermute(x, axis, [(i, i ^ mask) for i in range(n)])  21.9 us
    pallas_call x16, Pallas kernels, call(): pl.pallas_call(kernel, name=name, out_shape=outs, in_specs=specs or [VMEM...  5.12 us
  transfers between devices with their start and end apart: 24, of which 13 were waited for; matrix products, arithmetic and copies ran while one was open for 0% of the time, Pallas kernels for 6%

profile of v10, /device:TPU:0, one launch (start us, length us, event | category | flops | bytes accessed | tf_op | source)
XLA Modules:
  0.0 54.7 jit_solution(7980576129912392790)
XLA Ops:
  0.6 4.1 %collective-permute-start = (bf16[128,256]{1,0:T(8,128)(2,1)}, bf16[128,256]{1,0:T(8,128)(2,1)S(1)}, u32[]{:S(2)}, u32[]{:S(2)}) collective-permute-start(bf16[128,256]{1,0:T(8,128)(2,1)} %f_hbm.1), channel_id=1, source_target_pairs={{0,16},{8,24},{16,0},{24,8},{1,17},{9,25},{17,1},{25,9},{2,18},{10... | collective-permute-start | bytes 196616 | tf_op jit(solution)/shard_map/ppermute | solution.py:21
  4.7 1.7 %expand.1 = (bf16[256,2048]{1,0:T(8,128)(2,1)S(1)}, bf16[128,256]{1,0:T(8,128)(2,1)S(1)}, bf16[128,256]{1,0:T(8,128)(2,1)S(1)}, bf16[256,256]{1,0:T(8,128)(2,1)S(1)}, f32[1,256]{1,0:T(1,128)S(1)}) custom-call(s32[32]{0:T(128)} %rows_hbm.1, s32[16]{0:T(128)} %counts_hbm.1, bf16[32,128,128]{2,1,0:T(8,128)(2,1)} %tiles_hbm.1, bf16[128,256]{1,0:T(8,128)(2,1)} %f_hbm.1, ...), custom_call_target="tpu_custom_call" | custom-call | bytes 2623680 | tf_op jit(solution)/shard_map/expand/pallas_call | solution.py:208
  6.5 2.1 %collective-permute-done.refs_1_ = bf16[128,256]{1,0:T(8,128)(2,1)S(1)} collective-permute-done((bf16[128,256]{1,0:T(8,128)(2,1)}, bf16[128,256]{1,0:T(8,128)(2,1)S(1)}, u32[]{:S(2)}, u32[]{:S(2)}) %collective-permute-start) | collective-permute-done | bytes 65568 | tf_op jit(solution)/shard_map/ppermute | solution.py:21
  8.6 0.7 %collective-permute-start.1 = (bf16[256,256]{1,0:T(8,128)(2,1)S(1)}, bf16[256,256]{1,0:T(8,128)(2,1)S(1)}, u32[]{:S(2)}, u32[]{:S(2)}) collective-permute-start(bf16[256,256]{1,0:T(8,128)(2,1)S(1)} %pack.2.refs_0_), channel_id=1, source_target_pairs={{0,8},{8,0},{16,24},{24,16},{1,9},{9,1},{17,25},{25,17},{2,10},{10... | collective-permute-start | bytes 393224 | tf_op jit(solution)/shard_map/ppermute | solution.py:21
  9.3 1.5 %collective-permute-start.4 = (bf16[256,256]{1,0:T(8,128)(2,1)S(1)}, bf16[256,256]{1,0:T(8,128)(2,1)S(1)}, u32[]{:S(2)}, u32[]{:S(2)}) collective-permute-start(bf16[256,256]{1,0:T(8,128)(2,1)S(1)} %pack.2.refs_0_), channel_id=1, source_target_pairs={{0,4},{4,0},{1,5},{5,1},{2,6},{6,2},{3,7},{7,3},{8,12},{12,8},{9,1... | collective-permute-start | bytes 393224 | tf_op jit(solution)/shard_map/ppermute | solution.py:21
  10.8 2.8 %collective-permute-done.1.refs_1_ = bf16[256,256]{1,0:T(8,128)(2,1)S(1)} collective-permute-done((bf16[256,256]{1,0:T(8,128)(2,1)S(1)}, bf16[256,256]{1,0:T(8,128)(2,1)S(1)}, u32[]{:S(2)}, u32[]{:S(2)}) %collective-permute-start.1) | collective-permute-done | bytes 131104 | tf_op jit(solution)/shard_map/ppermute | solution.py:21
  13.6 1.7 %collective-permute-start.5 = (bf16[256,256]{1,0:T(8,128)(2,1)S(1)}, bf16[256,256]{1,0:T(8,128)(2,1)S(1)}, u32[]{:S(2)}, u32[]{:S(2)}) collective-permute-start(bf16[256,256]{1,0:T(8,128)(2,1)S(1)} %collective-permute-done.1.refs_1_), channel_id=1, source_target_pairs={{0,4},{4,0},{1,5},{5,1},{2,6},{6,2},{3,7},{7,3},{8,12},{12,8},{9,1... | collective-permute-start | bytes 393224 | tf_op jit(solution)/shard_map/ppermute | solution.py:21
  15.3 0.5 collective-permute-start.3
  15.9 2.8 %collective-permute-done.5.refs_1_ = bf16[256,256]{1,0:T(8,128)(2,1)S(1)} collective-permute-done((bf16[256,256]{1,0:T(8,128)(2,1)S(1)}, bf16[256,256]{1,0:T(8,128)(2,1)S(1)}, u32[]{:S(2)}, u32[]{:S(2)}) %collective-permute-start.5) | collective-permute-done | bytes 131104 | tf_op jit(solution)/shard_map/ppermute | solution.py:21
  18.9 1.0 %collective-permute-done.7.refs_3_ = bf16[256,256]{1,0:T(8,128)(2,1)S(1)} collective-permute-done((bf16[256,256]{1,0:T(8,128)(2,1)S(1)}, bf16[256,256]{1,0:T(8,128)(2,1)S(1)}, u32[]{:S(2)}, u32[]{:S(2)}) %collective-permute-start.7) | collective-permute-done | bytes 131104 | tf_op jit(solution)/shard_map/ppermute | solution.py:21
  20.3 1.8 %collective-permute-start.8 = (bf16[128,256]{1,0:T(8,128)(2,1)S(1)}, bf16[128,256]{1,0:T(8,128)(2,1)S(1)}, u32[]{:S(2)}, u32[]{:S(2)}) collective-permute-start(bf16[128,256]{1,0:T(8,128)(2,1)S(1)} %get-tuple-element.28), channel_id=1, source_target_pairs={{0,1},{1,0},{2,3},{3,2},{4,5},{5,4},{6,7},{7,6},{8,9},{9,8},{10,11... | collective-permute-start | bytes 196616 | tf_op jit(solution)/shard_map/ppermute | solution.py:21
  22.1 2.5 %collective-permute-done.8.refs_0_ = bf16[128,256]{1,0:T(8,128)(2,1)S(1)} collective-permute-done((bf16[128,256]{1,0:T(8,128)(2,1)S(1)}, bf16[128,256]{1,0:T(8,128)(2,1)S(1)}, u32[]{:S(2)}, u32[]{:S(2)}) %collective-permute-start.8) | collective-permute-done | bytes 65568 | tf_op jit(solution)/shard_map/ppermute | solution.py:21
  25.1 2.4 %collective-permute-start.14 = (bf16[160,256]{1,0:T(8,128)(2,1)S(1)}, bf16[160,256]{1,0:T(8,128)(2,1)S(1)}, u32[]{:S(2)}, u32[]{:S(2)}) collective-permute-start(bf16[160,256]{1,0:T(8,128)(2,1)S(1)} %get-tuple-element.32.refs_0_), channel_id=1, source_target_pairs={{0,16},{8,24},{16,0},{24,8},{1,17},{9,25},{17,1},{25,9},{2,18},{10... | collective-permute-start | bytes 245768 | tf_op jit(solution)/shard_map/ppermute | solution.py:21
  27.5 1.6 %collective-permute-start.10 = (bf16[144,256]{1,0:T(8,128)(2,1)S(1)}, bf16[144,256]{1,0:T(8,128)(2,1)S(1)}, u32[]{:S(2)}, u32[]{:S(2)}) collective-permute-start(bf16[144,256]{1,0:T(8,128)(2,1)S(1)} %sum_core.1.own_ref), channel_id=1, source_target_pairs={{0,1},{1,0},{2,3},{3,2},{4,5},{5,4},{6,7},{7,6},{8,9},{9,8},{10,11... | collective-permute-start | bytes 221192 | tf_op jit(solution)/shard_map/ppermute | solution.py:21
  29.1 0.8 %output.1 = bf16[128,256]{1,0:T(8,128)(2,1)} custom-call(bf16[256,256]{1,0:T(8,128)(2,1)S(1)} %get-tuple-element.23.w_ref, f32[1,256]{1,0:T(1,128)S(1)} %get-tuple-element.24.b_ref, bf16[128,256]{1,0:T(8,128)(2,1)S(1)} %hidden.1.h_ref), custom_call_target="tpu_custom_call" | custom-call | bytes 263168 | tf_op jit(solution)/shard_map/output/pallas_call | solution.py:208
  29.9 2.0 %collective-permute-done.10.other_ref = bf16[144,256]{1,0:T(8,128)(2,1)S(1)} collective-permute-done((bf16[144,256]{1,0:T(8,128)(2,1)S(1)}, bf16[144,256]{1,0:T(8,128)(2,1)S(1)}, u32[]{:S(2)}, u32[]{:S(2)}) %collective-permute-start.10) | collective-permute-done | bytes 73760 | tf_op jit(solution)/shard_map/ppermute | solution.py:21
  32.0 0.7 %collective-permute-done.14.refs_1_ = bf16[160,256]{1,0:T(8,128)(2,1)S(1)} collective-permute-done((bf16[160,256]{1,0:T(8,128)(2,1)S(1)}, bf16[160,256]{1,0:T(8,128)(2,1)S(1)}, u32[]{:S(2)}, u32[]{:S(2)}) %collective-permute-start.14) | collective-permute-done | bytes 81952 | tf_op jit(solution)/shard_map/ppermute | solution.py:21
  32.7 1.2 %collective-permute-start.15 = (bf16[256,256]{1,0:T(8,128)(2,1)S(1)}, bf16[256,256]{1,0:T(8,128)(2,1)S(1)}, u32[]{:S(2)}, u32[]{:S(2)}) collective-permute-start(bf16[256,256]{1,0:T(8,128)(2,1)S(1)} %pack.3.refs_0_), channel_id=1, source_target_pairs={{0,8},{8,0},{16,24},{24,16},{1,9},{9,1},{17,25},{25,17},{2,10},{10... | collective-permute-start | bytes 393224 | tf_op jit(solution)/shard_map/ppermute | solution.py:21
  33.8 2.7 %collective-permute-start.11 = (bf16[144,256]{1,0:T(8,128)(2,1)S(1)}, bf16[144,256]{1,0:T(8,128)(2,1)S(1)}, u32[]{:S(2)}, u32[]{:S(2)}) collective-permute-start(bf16[144,256]{1,0:T(8,128)(2,1)S(1)} %sum_row.1.own_ref), channel_id=1, source_target_pairs={{0,16},{8,24},{16,0},{24,8},{1,17},{9,25},{17,1},{25,9},{2,18},{10... | collective-permute-start | bytes 221192 | tf_op jit(solution)/shard_map/ppermute | solution.py:21
  36.5 1.5 %collective-permute-start.18 = (bf16[256,256]{1,0:T(8,128)(2,1)S(1)}, bf16[256,256]{1,0:T(8,128)(2,1)S(1)}, u32[]{:S(2)}, u32[]{:S(2)}) collective-permute-start(bf16[256,256]{1,0:T(8,128)(2,1)S(1)} %pack.3.refs_0_), channel_id=1, source_target_pairs={{0,4},{4,0},{1,5},{5,1},{2,6},{6,2},{3,7},{7,3},{8,12},{12,8},{9,1... | collective-permute-start | bytes 393224 | tf_op jit(solution)/shard_map/ppermute | solution.py:21
  38.0 1.1 %collective-permute-done.11.other_ref = bf16[144,256]{1,0:T(8,128)(2,1)S(1)} collective-permute-done((bf16[144,256]{1,0:T(8,128)(2,1)S(1)}, bf16[144,256]{1,0:T(8,128)(2,1)S(1)}, u32[]{:S(2)}, u32[]{:S(2)}) %collective-permute-start.11) | collective-permute-done | bytes 73760 | tf_op jit(solution)/shard_map/ppermute | solution.py:21
  39.4 1.7 %collective-permute-start.19 = (bf16[256,256]{1,0:T(8,128)(2,1)S(1)}, bf16[256,256]{1,0:T(8,128)(2,1)S(1)}, u32[]{:S(2)}, u32[]{:S(2)}) collective-permute-start(bf16[256,256]{1,0:T(8,128)(2,1)S(1)} %collective-permute-done.15.refs_1_), channel_id=1, source_target_pairs={{0,4},{4,0},{1,5},{5,1},{2,6},{6,2},{3,7},{7,3},{8,12},{12,8},{9,1... | collective-permute-start | bytes 393224 | tf_op jit(solution)/shard_map/ppermute | solution.py:21
  41.1 2.3 %collective-permute-start.12 = (bf16[144,256]{1,0:T(8,128)(2,1)S(1)}, bf16[144,256]{1,0:T(8,128)(2,1)S(1)}, u32[]{:S(2)}, u32[]{:S(2)}) collective-permute-start(bf16[144,256]{1,0:T(8,128)(2,1)S(1)} %sum_far.2.own_ref), channel_id=1, source_target_pairs={{0,8},{8,0},{16,24},{24,16},{1,9},{9,1},{17,25},{25,17},{2,10},{10... | collective-permute-start | bytes 221192 | tf_op jit(solution)/shard_map/ppermute | solution.py:21
  43.4 0.5 collective-permute-start.17
  43.9 1.8 %collective-permute-done.12.other_ref = bf16[144,256]{1,0:T(8,128)(2,1)S(1)} collective-permute-done((bf16[144,256]{1,0:T(8,128)(2,1)S(1)}, bf16[144,256]{1,0:T(8,128)(2,1)S(1)}, u32[]{:S(2)}, u32[]{:S(2)}) %collective-permute-start.12) | collective-permute-done | bytes 73760 | tf_op jit(solution)/shard_map/ppermute | solution.py:21
  45.9 0.5 collective-permute-start.13
  46.3 0.9 %collective-permute-done.13.other_ref = bf16[144,256]{1,0:T(8,128)(2,1)S(1)} collective-permute-done((bf16[144,256]{1,0:T(8,128)(2,1)S(1)}, bf16[144,256]{1,0:T(8,128)(2,1)S(1)}, u32[]{:S(2)}, u32[]{:S(2)}) %collective-permute-start.13) | collective-permute-done | bytes 73760 | tf_op jit(solution)/shard_map/ppermute | solution.py:21
  48.0 0.6 %collective-permute-start.22 = (bf16[272,256]{1,0:T(8,128)(2,1)S(1)}, bf16[272,256]{1,0:T(8,128)(2,1)S(1)}, u32[]{:S(2)}, u32[]{:S(2)}) collective-permute-start(bf16[272,256]{1,0:T(8,128)(2,1)S(1)} %halves.1.near_ref), channel_id=1, source_target_pairs={{0,4},{4,0},{1,5},{5,1},{2,6},{6,2},{3,7},{7,3},{8,12},{12,8},{9,1... | collective-permute-start | bytes 417800 | tf_op jit(solution)/shard_map/ppermute | solution.py:21
  48.6 1.5 %collective-permute-start.23 = (bf16[128,256]{1,0:T(8,128)(2,1)S(1)}, bf16[128,256]{1,0:T(8,128)(2,1)S(1)}, u32[]{:S(2)}, u32[]{:S(2)}) collective-permute-start(bf16[128,256]{1,0:T(8,128)(2,1)S(1)} %get-tuple-element.38), channel_id=1, source_target_pairs={{0,1},{1,0},{2,3},{3,2},{4,5},{5,4},{6,7},{7,6},{8,9},{9,8},{10,11... | collective-permute-start | bytes 196616 | tf_op jit(solution)/shard_map/ppermute | solution.py:21
  50.1 2.7 %collective-permute-done.23.refs_1_ = bf16[128,256]{1,0:T(8,128)(2,1)S(1)} collective-permute-done((bf16[128,256]{1,0:T(8,128)(2,1)S(1)}, bf16[128,256]{1,0:T(8,128)(2,1)S(1)}, u32[]{:S(2)}, u32[]{:S(2)}) %collective-permute-start.23) | collective-permute-done | bytes 65568 | tf_op jit(solution)/shard_map/ppermute | solution.py:21
  52.9 1.1 %collective-permute-done.22.far_ref = bf16[272,256]{1,0:T(8,128)(2,1)S(1)} collective-permute-done((bf16[272,256]{1,0:T(8,128)(2,1)S(1)}, bf16[272,256]{1,0:T(8,128)(2,1)S(1)}, u32[]{:S(2)}, u32[]{:S(2)}) %collective-permute-start.22) | collective-permute-done | bytes 139296 | tf_op jit(solution)/shard_map/ppermute | solution.py:21
  54.0 0.8 %last.1 = (f32[256,256]{1,0:T(8,128)}, f32[1,256]{1,0:T(1,128)}, bf16[128,256]{1,0:T(8,128)(2,1)}) custom-call(bf16[272,256]{1,0:T(8,128)(2,1)S(1)} %halves.1.near_ref, bf16[272,256]{1,0:T(8,128)(2,1)S(1)} %collective-permute-done.22.far_ref, f32[128,256]{1,0:T(8,128)S(1)} %get-tuple-element.36.refs_0_, bf16[128,256]{1,0:T(8,128)(2,1)S(1)} %collective-permute-done.23.refs_1_), custom_call_target="tpu_custom_call" | custom-call | bytes 803840 | tf_op jit(solution)/shard_map/last/pallas_call | solution.py:208
  (32 shorter events, 2.2 us)
Async XLA Ops:
  0.6 8.0 %collective-permute-start = (bf16[128,256]{1,0:T(8,128)(2,1)}, bf16[128,256]{1,0:T(8,128)(2,1)S(1)}, u32[]{:S(2)}, u32[]{:S(2)}) collective-permute-start(bf16[128,256]{1,0:T(8,128)(2,1)} %f_hbm.1), channel_id=1, source_target_pairs={{0,16},{8,24},{16,0},{24,8},{1,17},{9,25},{17,1},{25,9},{2,18},{10... | collective-permute-start | bytes 196616 | tf_op jit(solution)/shard_map/ppermute | solution.py:21
  8.6 5.0 %collective-permute-start.1 = (bf16[256,256]{1,0:T(8,128)(2,1)S(1)}, bf16[256,256]{1,0:T(8,128)(2,1)S(1)}, u32[]{:S(2)}, u32[]{:S(2)}) collective-permute-start(bf16[256,256]{1,0:T(8,128)(2,1)S(1)} %pack.2.refs_0_), channel_id=1, source_target_pairs={{0,8},{8,0},{16,24},{24,16},{1,9},{9,1},{17,25},{25,17},{2,10},{10... | collective-permute-start | bytes 393224 | tf_op jit(solution)/shard_map/ppermute | solution.py:21
  9.3 6.5 %collective-permute-start.4 = (bf16[256,256]{1,0:T(8,128)(2,1)S(1)}, bf16[256,256]{1,0:T(8,128)(2,1)S(1)}, u32[]{:S(2)}, u32[]{:S(2)}) collective-permute-start(bf16[256,256]{1,0:T(8,128)(2,1)S(1)} %pack.2.refs_0_), channel_id=1, source_target_pairs={{0,4},{4,0},{1,5},{5,1},{2,6},{6,2},{3,7},{7,3},{8,12},{12,8},{9,1... | collective-permute-start | bytes 393224 | tf_op jit(solution)/shard_map/ppermute | solution.py:21
  13.6 5.0 %collective-permute-start.5 = (bf16[256,256]{1,0:T(8,128)(2,1)S(1)}, bf16[256,256]{1,0:T(8,128)(2,1)S(1)}, u32[]{:S(2)}, u32[]{:S(2)}) collective-permute-start(bf16[256,256]{1,0:T(8,128)(2,1)S(1)} %collective-permute-done.1.refs_1_), channel_id=1, source_target_pairs={{0,4},{4,0},{1,5},{5,1},{2,6},{6,2},{3,7},{7,3},{8,12},{12,8},{9,1... | collective-permute-start | bytes 393224 | tf_op jit(solution)/shard_map/ppermute | solution.py:21
  15.3 3.3 %collective-permute-start.2 = (bf16[256,256]{1,0:T(8,128)(2,1)S(1)}, bf16[256,256]{1,0:T(8,128)(2,1)S(1)}, u32[]{:S(2)}, u32[]{:S(2)}) collective-permute-start(bf16[256,256]{1,0:T(8,128)(2,1)S(1)} %pack.2.refs_0_), channel_id=1, source_target_pairs={{0,2},{2,0},{1,3},{3,1},{4,6},{6,4},{5,7},{7,5},{8,10},{10,8},{9,1... | collective-permute-start | bytes 393224 | tf_op jit(solution)/shard_map/ppermute | solution.py:21
  15.3 3.3 %collective-permute-start.3 = (bf16[256,256]{1,0:T(8,128)(2,1)S(1)}, bf16[256,256]{1,0:T(8,128)(2,1)S(1)}, u32[]{:S(2)}, u32[]{:S(2)}) collective-permute-start(bf16[256,256]{1,0:T(8,128)(2,1)S(1)} %collective-permute-done.1.refs_1_), channel_id=1, source_target_pairs={{0,2},{2,0},{1,3},{3,1},{4,6},{6,4},{5,7},{7,5},{8,10},{10,8},{9,1... | collective-permute-start | bytes 393224 | tf_op jit(solution)/shard_map/ppermute | solution.py:21
  15.9 3.1 %collective-permute-start.6 = (bf16[256,256]{1,0:T(8,128)(2,1)S(1)}, bf16[256,256]{1,0:T(8,128)(2,1)S(1)}, u32[]{:S(2)}, u32[]{:S(2)}) collective-permute-start(bf16[256,256]{1,0:T(8,128)(2,1)S(1)} %collective-permute-done.4.refs_0_), channel_id=1, source_target_pairs={{0,2},{2,0},{1,3},{3,1},{4,6},{6,4},{5,7},{7,5},{8,10},{10,8},{9,1... | collective-permute-start | bytes 393224 | tf_op jit(solution)/shard_map/ppermute | solution.py:21
  18.6 1.3 %collective-permute-start.7 = (bf16[256,256]{1,0:T(8,128)(2,1)S(1)}, bf16[256,256]{1,0:T(8,128)(2,1)S(1)}, u32[]{:S(2)}, u32[]{:S(2)}) collective-permute-start(bf16[256,256]{1,0:T(8,128)(2,1)S(1)} %collective-permute-done.5.refs_1_), channel_id=1, source_target_pairs={{0,2},{2,0},{1,3},{3,1},{4,6},{6,4},{5,7},{7,5},{8,10},{10,8},{9,1... | collective-permute-start | bytes 393224 | tf_op jit(solution)/shard_map/ppermute | solution.py:21
  20.3 4.3 %collective-permute-start.8 = (bf16[128,256]{1,0:T(8,128)(2,1)S(1)}, bf16[128,256]{1,0:T(8,128)(2,1)S(1)}, u32[]{:S(2)}, u32[]{:S(2)}) collective-permute-start(bf16[128,256]{1,0:T(8,128)(2,1)S(1)} %get-tuple-element.28), channel_id=1, source_target_pairs={{0,1},{1,0},{2,3},{3,2},{4,5},{5,4},{6,7},{7,6},{8,9},{9,8},{10,11... | collective-permute-start | bytes 196616 | tf_op jit(solution)/shard_map/ppermute | solution.py:21
  25.0 2.5 %collective-permute-start.9 = (bf16[144,256]{1,0:T(8,128)(2,1)S(1)}, bf16[144,256]{1,0:T(8,128)(2,1)S(1)}, u32[]{:S(2)}, u32[]{:S(2)}) collective-permute-start(bf16[144,256]{1,0:T(8,128)(2,1)S(1)} %get-tuple-element.31), channel_id=1, source_target_pairs={{0,2},{2,0},{1,3},{3,1},{4,6},{6,4},{5,7},{7,5},{8,10},{10,8},{9,1... | collective-permute-start | bytes 221192 | tf_op jit(solution)/shard_map/ppermute | solution.py:21
  25.1 7.5 %collective-permute-start.14 = (bf16[160,256]{1,0:T(8,128)(2,1)S(1)}, bf16[160,256]{1,0:T(8,128)(2,1)S(1)}, u32[]{:S(2)}, u32[]{:S(2)}) collective-permute-start(bf16[160,256]{1,0:T(8,128)(2,1)S(1)} %get-tuple-element.32.refs_0_), channel_id=1, source_target_pairs={{0,16},{8,24},{16,0},{24,8},{1,17},{9,25},{17,1},{25,9},{2,18},{10... | collective-permute-start | bytes 245768 | tf_op jit(solution)/shard_map/ppermute | solution.py:21
  27.5 4.4 %collective-permute-start.10 = (bf16[144,256]{1,0:T(8,128)(2,1)S(1)}, bf16[144,256]{1,0:T(8,128)(2,1)S(1)}, u32[]{:S(2)}, u32[]{:S(2)}) collective-permute-start(bf16[144,256]{1,0:T(8,128)(2,1)S(1)} %sum_core.1.own_ref), channel_id=1, source_target_pairs={{0,1},{1,0},{2,3},{3,2},{4,5},{5,4},{6,7},{7,6},{8,9},{9,8},{10,11... | collective-permute-start | bytes 221192 | tf_op jit(solution)/shard_map/ppermute | solution.py:21
  32.7 6.7 %collective-permute-start.15 = (bf16[256,256]{1,0:T(8,128)(2,1)S(1)}, bf16[256,256]{1,0:T(8,128)(2,1)S(1)}, u32[]{:S(2)}, u32[]{:S(2)}) collective-permute-start(bf16[256,256]{1,0:T(8,128)(2,1)S(1)} %pack.3.refs_0_), channel_id=1, source_target_pairs={{0,8},{8,0},{16,24},{24,16},{1,9},{9,1},{17,25},{25,17},{2,10},{10... | collective-permute-start | bytes 393224 | tf_op jit(solution)/shard_map/ppermute | solution.py:21
  33.8 5.3 %collective-permute-start.11 = (bf16[144,256]{1,0:T(8,128)(2,1)S(1)}, bf16[144,256]{1,0:T(8,128)(2,1)S(1)}, u32[]{:S(2)}, u32[]{:S(2)}) collective-permute-start(bf16[144,256]{1,0:T(8,128)(2,1)S(1)} %sum_row.1.own_ref), channel_id=1, source_target_pairs={{0,16},{8,24},{16,0},{24,8},{1,17},{9,25},{17,1},{25,9},{2,18},{10... | collective-permute-start | bytes 221192 | tf_op jit(solution)/shard_map/ppermute | solution.py:21
  36.5 7.4 %collective-permute-start.18 = (bf16[256,256]{1,0:T(8,128)(2,1)S(1)}, bf16[256,256]{1,0:T(8,128)(2,1)S(1)}, u32[]{:S(2)}, u32[]{:S(2)}) collective-permute-start(bf16[256,256]{1,0:T(8,128)(2,1)S(1)} %pack.3.refs_0_), channel_id=1, source_target_pairs={{0,4},{4,0},{1,5},{5,1},{2,6},{6,2},{3,7},{7,3},{8,12},{12,8},{9,1... | collective-permute-start | bytes 393224 | tf_op jit(solution)/shard_map/ppermute | solution.py:21
  39.4 6.4 %collective-permute-start.19 = (bf16[256,256]{1,0:T(8,128)(2,1)S(1)}, bf16[256,256]{1,0:T(8,128)(2,1)S(1)}, u32[]{:S(2)}, u32[]{:S(2)}) collective-permute-start(bf16[256,256]{1,0:T(8,128)(2,1)S(1)} %collective-permute-done.15.refs_1_), channel_id=1, source_target_pairs={{0,4},{4,0},{1,5},{5,1},{2,6},{6,2},{3,7},{7,3},{8,12},{12,8},{9,1... | collective-permute-start | bytes 393224 | tf_op jit(solution)/shard_map/ppermute | solution.py:21
  41.1 4.7 %collective-permute-start.12 = (bf16[144,256]{1,0:T(8,128)(2,1)S(1)}, bf16[144,256]{1,0:T(8,128)(2,1)S(1)}, u32[]{:S(2)}, u32[]{:S(2)}) collective-permute-start(bf16[144,256]{1,0:T(8,128)(2,1)S(1)} %sum_far.2.own_ref), channel_id=1, source_target_pairs={{0,8},{8,0},{16,24},{24,16},{1,9},{9,1},{17,25},{25,17},{2,10},{10... | collective-permute-start | bytes 221192 | tf_op jit(solution)/shard_map/ppermute | solution.py:21
  43.4 3.9 %collective-permute-start.16 = (bf16[256,256]{1,0:T(8,128)(2,1)S(1)}, bf16[256,256]{1,0:T(8,128)(2,1)S(1)}, u32[]{:S(2)}, u32[]{:S(2)}) collective-permute-start(bf16[256,256]{1,0:T(8,128)(2,1)S(1)} %pack.3.refs_0_), channel_id=1, source_target_pairs={{0,2},{2,0},{1,3},{3,1},{4,6},{6,4},{5,7},{7,5},{8,10},{10,8},{9,1... | collective-permute-start | bytes 393224 | tf_op jit(solution)/shard_map/ppermute | solution.py:21
  43.4 3.9 %collective-permute-start.17 = (bf16[256,256]{1,0:T(8,128)(2,1)S(1)}, bf16[256,256]{1,0:T(8,128)(2,1)S(1)}, u32[]{:S(2)}, u32[]{:S(2)}) collective-permute-start(bf16[256,256]{1,0:T(8,128)(2,1)S(1)} %collective-permute-done.15.refs_1_), channel_id=1, source_target_pairs={{0,2},{2,0},{1,3},{3,1},{4,6},{6,4},{5,7},{7,5},{8,10},{10,8},{9,1... | collective-permute-start | bytes 393224 | tf_op jit(solution)/shard_map/ppermute | solution.py:21
  43.9 3.7 %collective-permute-start.20 = (bf16[256,256]{1,0:T(8,128)(2,1)S(1)}, bf16[256,256]{1,0:T(8,128)(2,1)S(1)}, u32[]{:S(2)}, u32[]{:S(2)}) collective-permute-start(bf16[256,256]{1,0:T(8,128)(2,1)S(1)} %collective-permute-done.18.refs_0_), channel_id=1, source_target_pairs={{0,2},{2,0},{1,3},{3,1},{4,6},{6,4},{5,7},{7,5},{8,10},{10,8},{9,1... | collective-permute-start | bytes 393224 | tf_op jit(solution)/shard_map/ppermute | solution.py:21
  45.8 1.9 %collective-permute-start.21 = (bf16[256,256]{1,0:T(8,128)(2,1)S(1)}, bf16[256,256]{1,0:T(8,128)(2,1)S(1)}, u32[]{:S(2)}, u32[]{:S(2)}) collective-permute-start(bf16[256,256]{1,0:T(8,128)(2,1)S(1)} %collective-permute-done.19.refs_1_), channel_id=1, source_target_pairs={{0,2},{2,0},{1,3},{3,1},{4,6},{6,4},{5,7},{7,5},{8,10},{10,8},{9,1... | collective-permute-start | bytes 393224 | tf_op jit(solution)/shard_map/ppermute | solution.py:21
  45.9 1.4 %collective-permute-start.13 = (bf16[144,256]{1,0:T(8,128)(2,1)S(1)}, bf16[144,256]{1,0:T(8,128)(2,1)S(1)}, u32[]{:S(2)}, u32[]{:S(2)}) collective-permute-start(bf16[144,256]{1,0:T(8,128)(2,1)S(1)} %sum_far.3.own_ref), channel_id=1, source_target_pairs={{0,2},{2,0},{1,3},{3,1},{4,6},{6,4},{5,7},{7,5},{8,10},{10,8},{9,1... | collective-permute-start | bytes 221192 | tf_op jit(solution)/shard_map/ppermute | solution.py:21
  48.0 6.0 %collective-permute-start.22 = (bf16[272,256]{1,0:T(8,128)(2,1)S(1)}, bf16[272,256]{1,0:T(8,128)(2,1)S(1)}, u32[]{:S(2)}, u32[]{:S(2)}) collective-permute-start(bf16[272,256]{1,0:T(8,128)(2,1)S(1)} %halves.1.near_ref), channel_id=1, source_target_pairs={{0,4},{4,0},{1,5},{5,1},{2,6},{6,2},{3,7},{7,3},{8,12},{12,8},{9,1... | collective-permute-start | bytes 417800 | tf_op jit(solution)/shard_map/ppermute | solution.py:21
  48.6 4.3 %collective-permute-start.23 = (bf16[128,256]{1,0:T(8,128)(2,1)S(1)}, bf16[128,256]{1,0:T(8,128)(2,1)S(1)}, u32[]{:S(2)}, u32[]{:S(2)}) collective-permute-start(bf16[128,256]{1,0:T(8,128)(2,1)S(1)} %get-tuple-element.38), channel_id=1, source_target_pairs={{0,1},{1,0},{2,3},{3,2},{4,5},{5,4},{6,7},{7,6},{8,9},{9,8},{10,11... | collective-permute-start | bytes 196616 | tf_op jit(solution)/shard_map/ppermute | solution.py:21

commit v11 on v10

--- a/solution.py
+++ b/solution.py
@@ -95,6 +95,19 @@
     lax.fori_loop(0, n_loop, body, 0)
 
 
+def pack_message_kernel(a_ref, b_ref, message_ref, pair_ref, packed_ref):
+    rows = pair_ref.shape[0]
+    pack_kernel(a_ref, b_ref, pair_ref)
+    packed_ref[:rows, :] = pair_ref[...]
+    packed_ref[rows:, :] = message_ref[...]
+
+
+def unpack_message_kernel(message_ref, packed_ref, pair_ref, sum_ref):
+    rows = pair_ref.shape[0]
+    pair_ref[...] = packed_ref[:rows, :]
+    message_kernel(message_ref, packed_ref.at[rows:, :], sum_ref)
+
+
 def product_rows(a_ref, first, block_refs, rows):
     step = a_ref.shape[1] // (2 * len(block_refs))
     x = jnp.concatenate([ref[:step, :] for ref in block_refs], axis=0)
@@ -312,14 +325,28 @@
         message = add(message, partner(message, "row", bit, n_row), "sum_row")
         bit *= 2
     other = after(partner(grad_hidden, "far", steps[0], n_far), message, output)
-    g00 = far_chunks(pack(grad_hidden, other))
-    message = add(message, partner(message, "far", steps[0], n_far), "sum_far")
-    g10 = [swap(chunk, "mid") for chunk in g00[:1] + [after(c, message) for c in g00[1:]]]
+    pair_shape = shape(2 * tile, width)
+    pair, packed = call(
+        pack_message_kernel,
+        "pack_message",
+        [pair_shape, shape(2 * tile + message_shape.shape[0], width)],
+        [grad_hidden, other, message],
+    )
+    chunk, message = call(
+        unpack_message_kernel,
+        "unpack_message",
+        [pair_shape, message_shape],
+        [message, partner(packed, "far", steps[1], n_far)],
+    )
+    g00 = [pair, chunk]
+    for step in steps[2:]:
+        g00 = g00 + [partner(chunk, "far", step, n_far) for chunk in g00]
+    g10 = [swap(chunk, "mid") for chunk in g00]
     g01 = [swap(chunk, "core") for chunk in g00]
-    for step in steps[1:]:
+    g11 = [swap(chunk, "core") for chunk in g10]
+    for step in steps[:1] + steps[2:]:
         message = add(message, partner(message, "far", step, n_far), "sum_far")
-    g11 = [swap(chunk, "core") for chunk in g10[:-1] + [after(g10[-1], message)]]
-    half = near_product(g00 + g01, "backward")
+    half = near_product([after(g00[0], message)] + g00[1:] + g01, "backward")
     own, *parts = rest_product(half, g10 + g11, "backward")
     others = from_row(parts)
     (message,) = call(

time: 54.9 us -> 55.7 us (1.015)
  waiting for transfers between devices: 21.9 us -> 25.9 us
  starting transfers between devices: 26.9 us -> 23.7 us
    ppermute x24 -> x23, waiting for transfers between devices: 21.9 us -> 25.9 us  [partner(): return lax.ppermute(x, axis, [(i, i ^ mask) for i in range(n)])]
    ppermute x24 -> x23, starting transfers between devices: 26.9 us -> 23.7 us  [partner(): return lax.ppermute(x, axis, [(i, i ^ mask) for i in range(n)])]
  transfers between devices with their start and end apart: 24 -> 23, of which waited for: 13 -> 13; matrix products, arithmetic and copies ran while one was open for 0% -> 0% of each run, Pallas kernels for 6% -> 6%
where the time goes in v11:
time: 55.7 us; the launch traced here: 55.5 us
  waiting for transfers between devices  25.9 us (46%)
  starting transfers between devices  23.7 us (43%)
  Pallas kernels  5.14 us (9%)
  between operations  0.79 us (1%)
    ppermute x23, waiting for transfers between devices, partner(): return lax.ppermute(x, axis, [(i, i ^ mask) for i in range(n)])  25.9 us
    ppermute x23, starting transfers between devices, partner(): return lax.ppermute(x, axis, [(i, i ^ mask) for i in range(n)])  23.7 us
    pallas_call x16, Pallas kernels, call(): pl.pallas_call(kernel, name=name, out_shape=outs, in_specs=specs or [VMEM...  5.14 us
  transfers between devices with their start and end apart: 23, of which 13 were waited for; matrix products, arithmetic and copies ran while one was open for 0% of the time, Pallas kernels for 6%

profile of v11, /device:TPU:0, one launch (start us, length us, event | category | flops | bytes accessed | tf_op | source)
XLA Modules:
  0.0 55.5 jit_solution(11346219475340798225)
XLA Ops:
  0.6 4.1 %collective-permute-start = (bf16[128,256]{1,0:T(8,128)(2,1)}, bf16[128,256]{1,0:T(8,128)(2,1)S(1)}, u32[]{:S(2)}, u32[]{:S(2)}) collective-permute-start(bf16[128,256]{1,0:T(8,128)(2,1)} %f_hbm.1), channel_id=1, source_target_pairs={{0,16},{8,24},{16,0},{24,8},{1,17},{9,25},{17,1},{25,9},{2,18},{10... | collective-permute-start | bytes 196616 | tf_op jit(solution)/shard_map/ppermute | solution.py:21
  4.7 1.7 %expand.1 = (bf16[256,2048]{1,0:T(8,128)(2,1)S(1)}, bf16[128,256]{1,0:T(8,128)(2,1)S(1)}, bf16[128,256]{1,0:T(8,128)(2,1)S(1)}, bf16[256,256]{1,0:T(8,128)(2,1)S(1)}, f32[1,256]{1,0:T(1,128)S(1)}) custom-call(s32[32]{0:T(128)} %rows_hbm.1, s32[16]{0:T(128)} %counts_hbm.1, bf16[32,128,128]{2,1,0:T(8,128)(2,1)} %tiles_hbm.1, bf16[128,256]{1,0:T(8,128)(2,1)} %f_hbm.1, ...), custom_call_target="tpu_custom_call" | custom-call | bytes 2623680 | tf_op jit(solution)/shard_map/expand/pallas_call | solution.py:221
  6.5 2.1 %collective-permute-done.refs_1_ = bf16[128,256]{1,0:T(8,128)(2,1)S(1)} collective-permute-done((bf16[128,256]{1,0:T(8,128)(2,1)}, bf16[128,256]{1,0:T(8,128)(2,1)S(1)}, u32[]{:S(2)}, u32[]{:S(2)}) %collective-permute-start) | collective-permute-done | bytes 65568 | tf_op jit(solution)/shard_map/ppermute | solution.py:21
  8.6 0.7 %collective-permute-start.1 = (bf16[256,256]{1,0:T(8,128)(2,1)S(1)}, bf16[256,256]{1,0:T(8,128)(2,1)S(1)}, u32[]{:S(2)}, u32[]{:S(2)}) collective-permute-start(bf16[256,256]{1,0:T(8,128)(2,1)S(1)} %pack.1.refs_0_), channel_id=1, source_target_pairs={{0,8},{8,0},{16,24},{24,16},{1,9},{9,1},{17,25},{25,17},{2,10},{10... | collective-permute-start | bytes 393224 | tf_op jit(solution)/shard_map/ppermute | solution.py:21
  9.3 1.5 %collective-permute-start.4 = (bf16[256,256]{1,0:T(8,128)(2,1)S(1)}, bf16[256,256]{1,0:T(8,128)(2,1)S(1)}, u32[]{:S(2)}, u32[]{:S(2)}) collective-permute-start(bf16[256,256]{1,0:T(8,128)(2,1)S(1)} %pack.1.refs_0_), channel_id=1, source_target_pairs={{0,4},{4,0},{1,5},{5,1},{2,6},{6,2},{3,7},{7,3},{8,12},{12,8},{9,1... | collective-permute-start | bytes 393224 | tf_op jit(solution)/shard_map/ppermute | solution.py:21
  10.8 2.8 %collective-permute-done.1.refs_1_ = bf16[256,256]{1,0:T(8,128)(2,1)S(1)} collective-permute-done((bf16[256,256]{1,0:T(8,128)(2,1)S(1)}, bf16[256,256]{1,0:T(8,128)(2,1)S(1)}, u32[]{:S(2)}, u32[]{:S(2)}) %collective-permute-start.1) | collective-permute-done | bytes 131104 | tf_op jit(solution)/shard_map/ppermute | solution.py:21
  13.6 1.7 %collective-permute-start.5 = (bf16[256,256]{1,0:T(8,128)(2,1)S(1)}, bf16[256,256]{1,0:T(8,128)(2,1)S(1)}, u32[]{:S(2)}, u32[]{:S(2)}) collective-permute-start(bf16[256,256]{1,0:T(8,128)(2,1)S(1)} %collective-permute-done.1.refs_1_), channel_id=1, source_target_pairs={{0,4},{4,0},{1,5},{5,1},{2,6},{6,2},{3,7},{7,3},{8,12},{12,8},{9,1... | collective-permute-start | bytes 393224 | tf_op jit(solution)/shard_map/ppermute | solution.py:21
  15.3 0.5 collective-permute-start.3
  15.9 2.8 %collective-permute-done.5.refs_1_ = bf16[256,256]{1,0:T(8,128)(2,1)S(1)} collective-permute-done((bf16[256,256]{1,0:T(8,128)(2,1)S(1)}, bf16[256,256]{1,0:T(8,128)(2,1)S(1)}, u32[]{:S(2)}, u32[]{:S(2)}) %collective-permute-start.5) | collective-permute-done | bytes 131104 | tf_op jit(solution)/shard_map/ppermute | solution.py:21
  18.9 1.0 %collective-permute-done.7.refs_3_ = bf16[256,256]{1,0:T(8,128)(2,1)S(1)} collective-permute-done((bf16[256,256]{1,0:T(8,128)(2,1)S(1)}, bf16[256,256]{1,0:T(8,128)(2,1)S(1)}, u32[]{:S(2)}, u32[]{:S(2)}) %collective-permute-start.7) | collective-permute-done | bytes 131104 | tf_op jit(solution)/shard_map/ppermute | solution.py:21
  20.3 1.8 %collective-permute-start.8 = (bf16[128,256]{1,0:T(8,128)(2,1)S(1)}, bf16[128,256]{1,0:T(8,128)(2,1)S(1)}, u32[]{:S(2)}, u32[]{:S(2)}) collective-permute-start(bf16[128,256]{1,0:T(8,128)(2,1)S(1)} %get-tuple-element.31), channel_id=1, source_target_pairs={{0,1},{1,0},{2,3},{3,2},{4,5},{5,4},{6,7},{7,6},{8,9},{9,8},{10,11... | collective-permute-start | bytes 196616 | tf_op jit(solution)/shard_map/ppermute | solution.py:21
  22.1 2.5 %collective-permute-done.8.refs_0_ = bf16[128,256]{1,0:T(8,128)(2,1)S(1)} collective-permute-done((bf16[128,256]{1,0:T(8,128)(2,1)S(1)}, bf16[128,256]{1,0:T(8,128)(2,1)S(1)}, u32[]{:S(2)}, u32[]{:S(2)}) %collective-permute-start.8) | collective-permute-done | bytes 65568 | tf_op jit(solution)/shard_map/ppermute | solution.py:21
  24.6 0.4 grads.1
  25.1 2.4 %collective-permute-start.11 = (bf16[160,256]{1,0:T(8,128)(2,1)S(1)}, bf16[160,256]{1,0:T(8,128)(2,1)S(1)}, u32[]{:S(2)}, u32[]{:S(2)}) collective-permute-start(bf16[160,256]{1,0:T(8,128)(2,1)S(1)} %get-tuple-element.35.a_ref), channel_id=1, source_target_pairs={{0,16},{8,24},{16,0},{24,8},{1,17},{9,25},{17,1},{25,9},{2,18},{10... | collective-permute-start | bytes 245768 | tf_op jit(solution)/shard_map/ppermute | solution.py:21
  27.5 1.6 %collective-permute-start.10 = (bf16[144,256]{1,0:T(8,128)(2,1)S(1)}, bf16[144,256]{1,0:T(8,128)(2,1)S(1)}, u32[]{:S(2)}, u32[]{:S(2)}) collective-permute-start(bf16[144,256]{1,0:T(8,128)(2,1)S(1)} %sum_core.1.own_ref), channel_id=1, source_target_pairs={{0,1},{1,0},{2,3},{3,2},{4,5},{5,4},{6,7},{7,6},{8,9},{9,8},{10,11... | collective-permute-start | bytes 221192 | tf_op jit(solution)/shard_map/ppermute | solution.py:21
  29.1 0.8 %output.1 = bf16[128,256]{1,0:T(8,128)(2,1)} custom-call(bf16[256,256]{1,0:T(8,128)(2,1)S(1)} %get-tuple-element.26.w_ref, f32[1,256]{1,0:T(1,128)S(1)} %get-tuple-element.27.b_ref, bf16[128,256]{1,0:T(8,128)(2,1)S(1)} %hidden.1.h_ref), custom_call_target="tpu_custom_call" | custom-call | bytes 263168 | tf_op jit(solution)/shard_map/output/pallas_call | solution.py:221
  29.9 2.0 %collective-permute-done.10.other_ref = bf16[144,256]{1,0:T(8,128)(2,1)S(1)} collective-permute-done((bf16[144,256]{1,0:T(8,128)(2,1)S(1)}, bf16[144,256]{1,0:T(8,128)(2,1)S(1)}, u32[]{:S(2)}, u32[]{:S(2)}) %collective-permute-start.10) | collective-permute-done | bytes 73760 | tf_op jit(solution)/shard_map/ppermute | solution.py:21
  32.0 0.7 %collective-permute-done.11.b_ref = bf16[160,256]{1,0:T(8,128)(2,1)S(1)} collective-permute-done((bf16[160,256]{1,0:T(8,128)(2,1)S(1)}, bf16[160,256]{1,0:T(8,128)(2,1)S(1)}, u32[]{:S(2)}, u32[]{:S(2)}) %collective-permute-start.11) | collective-permute-done | bytes 81952 | tf_op jit(solution)/shard_map/ppermute | solution.py:21
  32.7 1.2 %collective-permute-start.12 = (bf16[400,256]{1,0:T(8,128)(2,1)S(1)}, bf16[400,256]{1,0:T(8,128)(2,1)S(1)}, u32[]{:S(2)}, u32[]{:S(2)}) collective-permute-start(bf16[400,256]{1,0:T(8,128)(2,1)S(1)} %get-tuple-element.37), channel_id=1, source_target_pairs={{0,8},{8,0},{16,24},{24,16},{1,9},{9,1},{17,25},{25,17},{2,10},{10... | collective-permute-start | bytes 614408 | tf_op jit(solution)/shard_map/ppermute | solution.py:21
  33.8 1.5 %collective-permute-start.17 = (bf16[256,256]{1,0:T(8,128)(2,1)S(1)}, bf16[256,256]{1,0:T(8,128)(2,1)S(1)}, u32[]{:S(2)}, u32[]{:S(2)}) collective-permute-start(bf16[256,256]{1,0:T(8,128)(2,1)S(1)} %get-tuple-element.40.refs_0_), channel_id=1, source_target_pairs={{0,4},{4,0},{1,5},{5,1},{2,6},{6,2},{3,7},{7,3},{8,12},{12,8},{9,1... | collective-permute-start | bytes 393224 | tf_op jit(solution)/shard_map/ppermute | solution.py:21
  35.3 4.0 %collective-permute-done.12.packed_ref = bf16[400,256]{1,0:T(8,128)(2,1)S(1)} collective-permute-done((bf16[400,256]{1,0:T(8,128)(2,1)S(1)}, bf16[400,256]{1,0:T(8,128)(2,1)S(1)}, u32[]{:S(2)}, u32[]{:S(2)}) %collective-permute-start.12) | collective-permute-done | bytes 204832 | tf_op jit(solution)/shard_map/ppermute | solution.py:21
  39.4 1.8 %collective-permute-start.18 = (bf16[256,256]{1,0:T(8,128)(2,1)S(1)}, bf16[256,256]{1,0:T(8,128)(2,1)S(1)}, u32[]{:S(2)}, u32[]{:S(2)}) collective-permute-start(bf16[256,256]{1,0:T(8,128)(2,1)S(1)} %get-tuple-element.41.refs_1_), channel_id=1, source_target_pairs={{0,4},{4,0},{1,5},{5,1},{2,6},{6,2},{3,7},{7,3},{8,12},{12,8},{9,1... | collective-permute-start | bytes 393224 | tf_op jit(solution)/shard_map/ppermute | solution.py:21
  41.2 2.2 %collective-permute-start.13 = (bf16[144,256]{1,0:T(8,128)(2,1)S(1)}, bf16[144,256]{1,0:T(8,128)(2,1)S(1)}, u32[]{:S(2)}, u32[]{:S(2)}) collective-permute-start(bf16[144,256]{1,0:T(8,128)(2,1)S(1)} %get-tuple-element.38.own_ref), channel_id=1, source_target_pairs={{0,16},{8,24},{16,0},{24,8},{1,17},{9,25},{17,1},{25,9},{2,18},{10... | collective-permute-start | bytes 221192 | tf_op jit(solution)/shard_map/ppermute | solution.py:21
  43.4 0.5 collective-permute-start.16
  43.9 0.5 collective-permute-done.18.refs_1_
  44.5 2.8 %collective-permute-done.13.other_ref = bf16[144,256]{1,0:T(8,128)(2,1)S(1)} collective-permute-done((bf16[144,256]{1,0:T(8,128)(2,1)S(1)}, bf16[144,256]{1,0:T(8,128)(2,1)S(1)}, u32[]{:S(2)}, u32[]{:S(2)}) %collective-permute-start.13) | collective-permute-done | bytes 73760 | tf_op jit(solution)/shard_map/ppermute | solution.py:21
  47.7 0.9 %collective-permute-done.14.other_ref = bf16[144,256]{1,0:T(8,128)(2,1)S(1)} collective-permute-done((bf16[144,256]{1,0:T(8,128)(2,1)S(1)}, bf16[144,256]{1,0:T(8,128)(2,1)S(1)}, u32[]{:S(2)}, u32[]{:S(2)}) %collective-permute-start.14) | collective-permute-done | bytes 73760 | tf_op jit(solution)/shard_map/ppermute | solution.py:21
  48.6 0.3 backward_rest.1
  49.0 2.0 %collective-permute-start.22 = (bf16[128,256]{1,0:T(8,128)(2,1)S(1)}, bf16[128,256]{1,0:T(8,128)(2,1)S(1)}, u32[]{:S(2)}, u32[]{:S(2)}) collective-permute-start(bf16[128,256]{1,0:T(8,128)(2,1)S(1)} %get-tuple-element.44), channel_id=1, source_target_pairs={{0,1},{1,0},{2,3},{3,2},{4,5},{5,4},{6,7},{7,6},{8,9},{9,8},{10,11... | collective-permute-start | bytes 196616 | tf_op jit(solution)/shard_map/ppermute | solution.py:21
  51.1 2.3 %collective-permute-done.22.refs_1_ = bf16[128,256]{1,0:T(8,128)(2,1)S(1)} collective-permute-done((bf16[128,256]{1,0:T(8,128)(2,1)S(1)}, bf16[128,256]{1,0:T(8,128)(2,1)S(1)}, u32[]{:S(2)}, u32[]{:S(2)}) %collective-permute-start.22) | collective-permute-done | bytes 65568 | tf_op jit(solution)/shard_map/ppermute | solution.py:21
  53.4 1.4 %collective-permute-done.21.far_ref = bf16[272,256]{1,0:T(8,128)(2,1)S(1)} collective-permute-done((bf16[272,256]{1,0:T(8,128)(2,1)S(1)}, bf16[272,256]{1,0:T(8,128)(2,1)S(1)}, u32[]{:S(2)}, u32[]{:S(2)}) %collective-permute-start.21) | collective-permute-done | bytes 139296 | tf_op jit(solution)/shard_map/ppermute | solution.py:21
  54.7 0.8 %last.1 = (f32[256,256]{1,0:T(8,128)}, f32[1,256]{1,0:T(1,128)}, bf16[128,256]{1,0:T(8,128)(2,1)}) custom-call(bf16[272,256]{1,0:T(8,128)(2,1)S(1)} %halves.1.near_ref, bf16[272,256]{1,0:T(8,128)(2,1)S(1)} %collective-permute-done.21.far_ref, f32[128,256]{1,0:T(8,128)S(1)} %get-tuple-element.42.refs_0_, bf16[128,256]{1,0:T(8,128)(2,1)S(1)} %collective-permute-done.22.refs_1_), custom_call_target="tpu_custom_call" | custom-call | bytes 803840 | tf_op jit(solution)/shard_map/last/pallas_call | solution.py:221
  (30 shorter events, 1.4 us)
Async XLA Ops:
  0.6 8.0 %collective-permute-start = (bf16[128,256]{1,0:T(8,128)(2,1)}, bf16[128,256]{1,0:T(8,128)(2,1)S(1)}, u32[]{:S(2)}, u32[]{:S(2)}) collective-permute-start(bf16[128,256]{1,0:T(8,128)(2,1)} %f_hbm.1), channel_id=1, source_target_pairs={{0,16},{8,24},{16,0},{24,8},{1,17},{9,25},{17,1},{25,9},{2,18},{10... | collective-permute-start | bytes 196616 | tf_op jit(solution)/shard_map/ppermute | solution.py:21
  8.6 5.0 %collective-permute-start.1 = (bf16[256,256]{1,0:T(8,128)(2,1)S(1)}, bf16[256,256]{1,0:T(8,128)(2,1)S(1)}, u32[]{:S(2)}, u32[]{:S(2)}) collective-permute-start(bf16[256,256]{1,0:T(8,128)(2,1)S(1)} %pack.1.refs_0_), channel_id=1, source_target_pairs={{0,8},{8,0},{16,24},{24,16},{1,9},{9,1},{17,25},{25,17},{2,10},{10... | collective-permute-start | bytes 393224 | tf_op jit(solution)/shard_map/ppermute | solution.py:21
  9.3 6.5 %collective-permute-start.4 = (bf16[256,256]{1,0:T(8,128)(2,1)S(1)}, bf16[256,256]{1,0:T(8,128)(2,1)S(1)}, u32[]{:S(2)}, u32[]{:S(2)}) collective-permute-start(bf16[256,256]{1,0:T(8,128)(2,1)S(1)} %pack.1.refs_0_), channel_id=1, source_target_pairs={{0,4},{4,0},{1,5},{5,1},{2,6},{6,2},{3,7},{7,3},{8,12},{12,8},{9,1... | collective-permute-start | bytes 393224 | tf_op jit(solution)/shard_map/ppermute | solution.py:21
  13.6 5.0 %collective-permute-start.5 = (bf16[256,256]{1,0:T(8,128)(2,1)S(1)}, bf16[256,256]{1,0:T(8,128)(2,1)S(1)}, u32[]{:S(2)}, u32[]{:S(2)}) collective-permute-start(bf16[256,256]{1,0:T(8,128)(2,1)S(1)} %collective-permute-done.1.refs_1_), channel_id=1, source_target_pairs={{0,4},{4,0},{1,5},{5,1},{2,6},{6,2},{3,7},{7,3},{8,12},{12,8},{9,1... | collective-permute-start | bytes 393224 | tf_op jit(solution)/shard_map/ppermute | solution.py:21
  15.3 3.3 %collective-permute-start.2 = (bf16[256,256]{1,0:T(8,128)(2,1)S(1)}, bf16[256,256]{1,0:T(8,128)(2,1)S(1)}, u32[]{:S(2)}, u32[]{:S(2)}) collective-permute-start(bf16[256,256]{1,0:T(8,128)(2,1)S(1)} %pack.1.refs_0_), channel_id=1, source_target_pairs={{0,2},{2,0},{1,3},{3,1},{4,6},{6,4},{5,7},{7,5},{8,10},{10,8},{9,1... | collective-permute-start | bytes 393224 | tf_op jit(solution)/shard_map/ppermute | solution.py:21
  15.3 3.3 %collective-permute-start.3 = (bf16[256,256]{1,0:T(8,128)(2,1)S(1)}, bf16[256,256]{1,0:T(8,128)(2,1)S(1)}, u32[]{:S(2)}, u32[]{:S(2)}) collective-permute-start(bf16[256,256]{1,0:T(8,128)(2,1)S(1)} %collective-permute-done.1.refs_1_), channel_id=1, source_target_pairs={{0,2},{2,0},{1,3},{3,1},{4,6},{6,4},{5,7},{7,5},{8,10},{10,8},{9,1... | collective-permute-start | bytes 393224 | tf_op jit(solution)/shard_map/ppermute | solution.py:21
  15.9 3.1 %collective-permute-start.6 = (bf16[256,256]{1,0:T(8,128)(2,1)S(1)}, bf16[256,256]{1,0:T(8,128)(2,1)S(1)}, u32[]{:S(2)}, u32[]{:S(2)}) collective-permute-start(bf16[256,256]{1,0:T(8,128)(2,1)S(1)} %collective-permute-done.4.refs_0_), channel_id=1, source_target_pairs={{0,2},{2,0},{1,3},{3,1},{4,6},{6,4},{5,7},{7,5},{8,10},{10,8},{9,1... | collective-permute-start | bytes 393224 | tf_op jit(solution)/shard_map/ppermute | solution.py:21
  18.6 1.3 %collective-permute-start.7 = (bf16[256,256]{1,0:T(8,128)(2,1)S(1)}, bf16[256,256]{1,0:T(8,128)(2,1)S(1)}, u32[]{:S(2)}, u32[]{:S(2)}) collective-permute-start(bf16[256,256]{1,0:T(8,128)(2,1)S(1)} %collective-permute-done.5.refs_1_), channel_id=1, source_target_pairs={{0,2},{2,0},{1,3},{3,1},{4,6},{6,4},{5,7},{7,5},{8,10},{10,8},{9,1... | collective-permute-start | bytes 393224 | tf_op jit(solution)/shard_map/ppermute | solution.py:21
  20.3 4.3 %collective-permute-start.8 = (bf16[128,256]{1,0:T(8,128)(2,1)S(1)}, bf16[128,256]{1,0:T(8,128)(2,1)S(1)}, u32[]{:S(2)}, u32[]{:S(2)}) collective-permute-start(bf16[128,256]{1,0:T(8,128)(2,1)S(1)} %get-tuple-element.31), channel_id=1, source_target_pairs={{0,1},{1,0},{2,3},{3,2},{4,5},{5,4},{6,7},{7,6},{8,9},{9,8},{10,11... | collective-permute-start | bytes 196616 | tf_op jit(solution)/shard_map/ppermute | solution.py:21
  25.0 2.5 %collective-permute-start.9 = (bf16[144,256]{1,0:T(8,128)(2,1)S(1)}, bf16[144,256]{1,0:T(8,128)(2,1)S(1)}, u32[]{:S(2)}, u32[]{:S(2)}) collective-permute-start(bf16[144,256]{1,0:T(8,128)(2,1)S(1)} %get-tuple-element.34), channel_id=1, source_target_pairs={{0,2},{2,0},{1,3},{3,1},{4,6},{6,4},{5,7},{7,5},{8,10},{10,8},{9,1... | collective-permute-start | bytes 221192 | tf_op jit(solution)/shard_map/ppermute | solution.py:21
  25.1 7.5 %collective-permute-start.11 = (bf16[160,256]{1,0:T(8,128)(2,1)S(1)}, bf16[160,256]{1,0:T(8,128)(2,1)S(1)}, u32[]{:S(2)}, u32[]{:S(2)}) collective-permute-start(bf16[160,256]{1,0:T(8,128)(2,1)S(1)} %get-tuple-element.35.a_ref), channel_id=1, source_target_pairs={{0,16},{8,24},{16,0},{24,8},{1,17},{9,25},{17,1},{25,9},{2,18},{10... | collective-permute-start | bytes 245768 | tf_op jit(solution)/shard_map/ppermute | solution.py:21
  27.5 4.4 %collective-permute-start.10 = (bf16[144,256]{1,0:T(8,128)(2,1)S(1)}, bf16[144,256]{1,0:T(8,128)(2,1)S(1)}, u32[]{:S(2)}, u32[]{:S(2)}) collective-permute-start(bf16[144,256]{1,0:T(8,128)(2,1)S(1)} %sum_core.1.own_ref), channel_id=1, source_target_pairs={{0,1},{1,0},{2,3},{3,2},{4,5},{5,4},{6,7},{7,6},{8,9},{9,8},{10,11... | collective-permute-start | bytes 221192 | tf_op jit(solution)/shard_map/ppermute | solution.py:21
  32.7 6.7 %collective-permute-start.12 = (bf16[400,256]{1,0:T(8,128)(2,1)S(1)}, bf16[400,256]{1,0:T(8,128)(2,1)S(1)}, u32[]{:S(2)}, u32[]{:S(2)}) collective-permute-start(bf16[400,256]{1,0:T(8,128)(2,1)S(1)} %get-tuple-element.37), channel_id=1, source_target_pairs={{0,8},{8,0},{16,24},{24,16},{1,9},{9,1},{17,25},{25,17},{2,10},{10... | collective-permute-start | bytes 614408 | tf_op jit(solution)/shard_map/ppermute | solution.py:21
  33.8 10.1 %collective-permute-start.17 = (bf16[256,256]{1,0:T(8,128)(2,1)S(1)}, bf16[256,256]{1,0:T(8,128)(2,1)S(1)}, u32[]{:S(2)}, u32[]{:S(2)}) collective-permute-start(bf16[256,256]{1,0:T(8,128)(2,1)S(1)} %get-tuple-element.40.refs_0_), channel_id=1, source_target_pairs={{0,4},{4,0},{1,5},{5,1},{2,6},{6,2},{3,7},{7,3},{8,12},{12,8},{9,1... | collective-permute-start | bytes 393224 | tf_op jit(solution)/shard_map/ppermute | solution.py:21
  39.4 5.0 %collective-permute-start.18 = (bf16[256,256]{1,0:T(8,128)(2,1)S(1)}, bf16[256,256]{1,0:T(8,128)(2,1)S(1)}, u32[]{:S(2)}, u32[]{:S(2)}) collective-permute-start(bf16[256,256]{1,0:T(8,128)(2,1)S(1)} %get-tuple-element.41.refs_1_), channel_id=1, source_target_pairs={{0,4},{4,0},{1,5},{5,1},{2,6},{6,2},{3,7},{7,3},{8,12},{12,8},{9,1... | collective-permute-start | bytes 393224 | tf_op jit(solution)/shard_map/ppermute | solution.py:21
  41.2 6.0 %collective-permute-start.13 = (bf16[144,256]{1,0:T(8,128)(2,1)S(1)}, bf16[144,256]{1,0:T(8,128)(2,1)S(1)}, u32[]{:S(2)}, u32[]{:S(2)}) collective-permute-start(bf16[144,256]{1,0:T(8,128)(2,1)S(1)} %get-tuple-element.38.own_ref), channel_id=1, source_target_pairs={{0,16},{8,24},{16,0},{24,8},{1,17},{9,25},{17,1},{25,9},{2,18},{10... | collective-permute-start | bytes 221192 | tf_op jit(solution)/shard_map/ppermute | solution.py:21
  43.4 3.9 %collective-permute-start.15 = (bf16[256,256]{1,0:T(8,128)(2,1)S(1)}, bf16[256,256]{1,0:T(8,128)(2,1)S(1)}, u32[]{:S(2)}, u32[]{:S(2)}) collective-permute-start(bf16[256,256]{1,0:T(8,128)(2,1)S(1)} %get-tuple-element.40.refs_0_), channel_id=1, source_target_pairs={{0,2},{2,0},{1,3},{3,1},{4,6},{6,4},{5,7},{7,5},{8,10},{10,8},{9,1... | collective-permute-start | bytes 393224 | tf_op jit(solution)/shard_map/ppermute | solution.py:21
  43.4 3.9 %collective-permute-start.16 = (bf16[256,256]{1,0:T(8,128)(2,1)S(1)}, bf16[256,256]{1,0:T(8,128)(2,1)S(1)}, u32[]{:S(2)}, u32[]{:S(2)}) collective-permute-start(bf16[256,256]{1,0:T(8,128)(2,1)S(1)} %get-tuple-element.41.refs_1_), channel_id=1, source_target_pairs={{0,2},{2,0},{1,3},{3,1},{4,6},{6,4},{5,7},{7,5},{8,10},{10,8},{9,1... | collective-permute-start | bytes 393224 | tf_op jit(solution)/shard_map/ppermute | solution.py:21
  43.9 4.7 %collective-permute-start.19 = (bf16[256,256]{1,0:T(8,128)(2,1)S(1)}, bf16[256,256]{1,0:T(8,128)(2,1)S(1)}, u32[]{:S(2)}, u32[]{:S(2)}) collective-permute-start(bf16[256,256]{1,0:T(8,128)(2,1)S(1)} %collective-permute-done.17.refs_0_), channel_id=1, source_target_pairs={{0,2},{2,0},{1,3},{3,1},{4,6},{6,4},{5,7},{7,5},{8,10},{10,8},{9,1... | collective-permute-start | bytes 393224 | tf_op jit(solution)/shard_map/ppermute | solution.py:21
  44.5 4.2 %collective-permute-start.20 = (bf16[256,256]{1,0:T(8,128)(2,1)S(1)}, bf16[256,256]{1,0:T(8,128)(2,1)S(1)}, u32[]{:S(2)}, u32[]{:S(2)}) collective-permute-start(bf16[256,256]{1,0:T(8,128)(2,1)S(1)} %collective-permute-done.18.refs_1_), channel_id=1, source_target_pairs={{0,2},{2,0},{1,3},{3,1},{4,6},{6,4},{5,7},{7,5},{8,10},{10,8},{9,1... | collective-permute-start | bytes 393224 | tf_op jit(solution)/shard_map/ppermute | solution.py:21
  47.3 1.3 %collective-permute-start.14 = (bf16[144,256]{1,0:T(8,128)(2,1)S(1)}, bf16[144,256]{1,0:T(8,128)(2,1)S(1)}, u32[]{:S(2)}, u32[]{:S(2)}) collective-permute-start(bf16[144,256]{1,0:T(8,128)(2,1)S(1)} %sum_far.1.own_ref), channel_id=1, source_target_pairs={{0,2},{2,0},{1,3},{3,1},{4,6},{6,4},{5,7},{7,5},{8,10},{10,8},{9,1... | collective-permute-start | bytes 221192 | tf_op jit(solution)/shard_map/ppermute | solution.py:21
  48.9 5.8 %collective-permute-start.21 = (bf16[272,256]{1,0:T(8,128)(2,1)S(1)}, bf16[272,256]{1,0:T(8,128)(2,1)S(1)}, u32[]{:S(2)}, u32[]{:S(2)}) collective-permute-start(bf16[272,256]{1,0:T(8,128)(2,1)S(1)} %halves.1.near_ref), channel_id=1, source_target_pairs={{0,4},{4,0},{1,5},{5,1},{2,6},{6,2},{3,7},{7,3},{8,12},{12,8},{9,1... | collective-permute-start | bytes 417800 | tf_op jit(solution)/shard_map/ppermute | solution.py:21
  49.0 4.3 %collective-permute-start.22 = (bf16[128,256]{1,0:T(8,128)(2,1)S(1)}, bf16[128,256]{1,0:T(8,128)(2,1)S(1)}, u32[]{:S(2)}, u32[]{:S(2)}) collective-permute-start(bf16[128,256]{1,0:T(8,128)(2,1)S(1)} %get-tuple-element.44), channel_id=1, source_target_pairs={{0,1},{1,0},{2,3},{3,2},{4,5},{5,4},{6,7},{7,6},{8,9},{9,8},{10,11... | collective-permute-start | bytes 196616 | tf_op jit(solution)/shard_map/ppermute | solution.py:21

commit v12 on v8

--- a/solution.py
+++ b/solution.py
@@ -304,7 +304,7 @@
         ],
         specs=[pl.BlockSpec(memory_space=pltpu.HBM)] * 5,
     )
-    f00 = far_chunks(pack(features, after(other, other_cot)), steps)
+    f00 = far_chunks(after(pack(features, other), other_cot), steps)
     f10 = [swap(chunk, "mid") for chunk in f00]
     cots = far_chunks(pack(cotangent, other_cot), cot_steps)
     f01 = [swap(chunk, "core") for chunk in f00]

time: 52.9 us -> 53 us (level)
  starting transfers between devices: 21.3 us -> 27 us
  waiting for transfers between devices: 25 us -> 19.4 us
    ppermute x23, starting transfers between devices: 21.3 us -> 27 us  [partner(): return lax.ppermute(x, axis, [(i, i ^ mask) for i in range(n)])]
    ppermute x23, waiting for transfers between devices: 25 us -> 19.4 us  [partner(): return lax.ppermute(x, axis, [(i, i ^ mask) for i in range(n)])]
where the time goes in v12:
time: 53 us; the launch traced here: 52.8 us
  starting transfers between devices  27 us (51%)
  waiting for transfers between devices  19.4 us (37%)
  Pallas kernels  5.6 us (11%)
  between operations  0.78 us (1%)
    ppermute x23, starting transfers between devices, partner(): return lax.ppermute(x, axis, [(i, i ^ mask) for i in range(n)])  27 us
    ppermute x23, waiting for transfers between devices, partner(): return lax.ppermute(x, axis, [(i, i ^ mask) for i in range(n)])  19.4 us
    pallas_call x16, Pallas kernels, call(): pl.pallas_call(kernel, name=name, out_shape=outs, in_specs=specs or [VMEM...  5.6 us
  transfers between devices with their start and end apart: 23, of which 13 were waited for; matrix products, arithmetic and copies ran while one was open for 0% of the time, Pallas kernels for 9%

profile of v12, /device:TPU:0, one launch (start us, length us, event | category | flops | bytes accessed | tf_op | source)
XLA Modules:
  0.0 52.8 jit_solution(137884383064417659)
XLA Ops:
  0.6 4.1 %collective-permute-start = (bf16[128,256]{1,0:T(8,128)(2,1)}, bf16[128,256]{1,0:T(8,128)(2,1)S(1)}, u32[]{:S(2)}, u32[]{:S(2)}) collective-permute-start(bf16[128,256]{1,0:T(8,128)(2,1)} %f_hbm.1), channel_id=1, source_target_pairs={{0,16},{8,24},{16,0},{24,8},{1,17},{9,25},{17,1},{25,9},{2,18},{10... | collective-permute-start | bytes 196616 | tf_op jit(solution)/shard_map/ppermute | solution.py:21
  4.7 1.6 %collective-permute-start.1 = (bf16[128,256]{1,0:T(8,128)(2,1)}, bf16[128,256]{1,0:T(8,128)(2,1)S(1)}, u32[]{:S(2)}, u32[]{:S(2)}) collective-permute-start(bf16[128,256]{1,0:T(8,128)(2,1)} %c_hbm.1), channel_id=1, source_target_pairs={{0,8},{8,0},{16,24},{24,16},{1,9},{9,1},{17,25},{25,17},{2,10},{10... | collective-permute-start | bytes 196616 | tf_op jit(solution)/shard_map/ppermute | solution.py:21
  6.3 1.7 %expand.1 = (bf16[256,2048]{1,0:T(8,128)(2,1)S(1)}, bf16[128,256]{1,0:T(8,128)(2,1)S(1)}, bf16[128,256]{1,0:T(8,128)(2,1)S(1)}) custom-call(s32[32]{0:T(128)} %rows_hbm.1, s32[16]{0:T(128)} %counts_hbm.1, bf16[32,128,128]{2,1,0:T(8,128)(2,1)} %tiles_hbm.1, bf16[128,256]{1,0:T(8,128)(2,1)} %f_hbm.1, bf16[128,256]{1,0:T(8,128)(2,1)} %c_hbm.1), custom_call_target="tpu_custom_call" | custom-call | bytes 2359488 | tf_op jit(solution)/shard_map/expand/pallas_call | solution.py:235
  8.0 1.2 %collective-permute-done.1.refs_1_ = bf16[128,256]{1,0:T(8,128)(2,1)S(1)} collective-permute-done((bf16[128,256]{1,0:T(8,128)(2,1)}, bf16[128,256]{1,0:T(8,128)(2,1)S(1)}, u32[]{:S(2)}, u32[]{:S(2)}) %collective-permute-start.1) | collective-permute-done | bytes 65568 | tf_op jit(solution)/shard_map/ppermute | solution.py:21
  9.2 1.6 %collective-permute-start.2 = (bf16[256,256]{1,0:T(8,128)(2,1)S(1)}, bf16[256,256]{1,0:T(8,128)(2,1)S(1)}, u32[]{:S(2)}, u32[]{:S(2)}) collective-permute-start(bf16[256,256]{1,0:T(8,128)(2,1)S(1)} %pack.3.refs_0_), channel_id=1, source_target_pairs={{0,8},{8,0},{16,24},{24,16},{1,9},{9,1},{17,25},{25,17},{2,10},{10... | collective-permute-start | bytes 393224 | tf_op jit(solution)/shard_map/ppermute | solution.py:21
  10.8 1.5 %collective-permute-start.5 = (bf16[256,256]{1,0:T(8,128)(2,1)S(1)}, bf16[256,256]{1,0:T(8,128)(2,1)S(1)}, u32[]{:S(2)}, u32[]{:S(2)}) collective-permute-start(bf16[256,256]{1,0:T(8,128)(2,1)S(1)} %pack.3.refs_0_), channel_id=1, source_target_pairs={{0,4},{4,0},{1,5},{5,1},{2,6},{6,2},{3,7},{7,3},{8,12},{12,8},{9,1... | collective-permute-start | bytes 393224 | tf_op jit(solution)/shard_map/ppermute | solution.py:21
  12.3 1.9 %collective-permute-start.8 = (bf16[256,256]{1,0:T(8,128)(2,1)S(1)}, bf16[256,256]{1,0:T(8,128)(2,1)S(1)}, u32[]{:S(2)}, u32[]{:S(2)}) collective-permute-start(bf16[256,256]{1,0:T(8,128)(2,1)S(1)} %pack.4.c0_ref), channel_id=1, source_target_pairs={{0,16},{8,24},{16,0},{24,8},{1,17},{9,25},{17,1},{25,9},{2,18},{10... | collective-permute-start | bytes 393224 | tf_op jit(solution)/shard_map/ppermute | solution.py:21
  14.2 2.9 %collective-permute-start.6 = (bf16[256,256]{1,0:T(8,128)(2,1)S(1)}, bf16[256,256]{1,0:T(8,128)(2,1)S(1)}, u32[]{:S(2)}, u32[]{:S(2)}) collective-permute-start(bf16[256,256]{1,0:T(8,128)(2,1)S(1)} %collective-permute-done.2.refs_1_), channel_id=1, source_target_pairs={{0,4},{4,0},{1,5},{5,1},{2,6},{6,2},{3,7},{7,3},{8,12},{12,8},{9,1... | collective-permute-start | bytes 393224 | tf_op jit(solution)/shard_map/ppermute | solution.py:21
  17.1 0.5 collective-permute-start.4
  17.6 2.3 %collective-permute-done.8.c1_ref = bf16[256,256]{1,0:T(8,128)(2,1)S(1)} collective-permute-done((bf16[256,256]{1,0:T(8,128)(2,1)S(1)}, bf16[256,256]{1,0:T(8,128)(2,1)S(1)}, u32[]{:S(2)}, u32[]{:S(2)}) %collective-permute-start.8) | collective-permute-done | bytes 131104 | tf_op jit(solution)/shard_map/ppermute | solution.py:21
  20.4 1.0 %collective-permute-done.9.refs_3_ = bf16[256,256]{1,0:T(8,128)(2,1)S(1)} collective-permute-done((bf16[256,256]{1,0:T(8,128)(2,1)S(1)}, bf16[256,256]{1,0:T(8,128)(2,1)S(1)}, u32[]{:S(2)}, u32[]{:S(2)}) %collective-permute-start.9) | collective-permute-done | bytes 131104 | tf_op jit(solution)/shard_map/ppermute | solution.py:21
  21.7 1.6 %collective-permute-start.10 = (bf16[128,256]{1,0:T(8,128)(2,1)S(1)}, bf16[128,256]{1,0:T(8,128)(2,1)S(1)}, u32[]{:S(2)}, u32[]{:S(2)}) collective-permute-start(bf16[128,256]{1,0:T(8,128)(2,1)S(1)} %get-tuple-element.32), channel_id=1, source_target_pairs={{0,1},{1,0},{2,3},{3,2},{4,5},{5,4},{6,7},{7,6},{8,9},{9,8},{10,11... | collective-permute-start | bytes 196616 | tf_op jit(solution)/shard_map/ppermute | solution.py:21
  23.3 2.7 %collective-permute-done.10.refs_0_ = bf16[128,256]{1,0:T(8,128)(2,1)S(1)} collective-permute-done((bf16[128,256]{1,0:T(8,128)(2,1)S(1)}, bf16[128,256]{1,0:T(8,128)(2,1)S(1)}, u32[]{:S(2)}, u32[]{:S(2)}) %collective-permute-start.10) | collective-permute-done | bytes 65568 | tf_op jit(solution)/shard_map/ppermute | solution.py:21
  26.0 1.9 %collective-permute-start.11 = (bf16[128,256]{1,0:T(8,128)(2,1)S(1)}, bf16[128,256]{1,0:T(8,128)(2,1)S(1)}, u32[]{:S(2)}, u32[]{:S(2)}) collective-permute-start(bf16[128,256]{1,0:T(8,128)(2,1)S(1)} %hidden.1.h_ref.refs_0_), channel_id=1, source_target_pairs={{0,16},{8,24},{16,0},{24,8},{1,17},{9,25},{17,1},{25,9},{2,18},{10... | collective-permute-start | bytes 196616 | tf_op jit(solution)/shard_map/ppermute | solution.py:21
  28.0 0.8 %output.1 = bf16[128,256]{1,0:T(8,128)(2,1)} custom-call(bf16[256,256]{1,0:T(8,128)(2,1)S(1)} %copy-done, f32[1,256]{1,0:T(1,128)S(1)} %bitcast.2, bf16[128,256]{1,0:T(8,128)(2,1)S(1)} %hidden.1.h_ref.refs_0_), custom_call_target="tpu_custom_call" | custom-call | bytes 263168 | tf_op jit(solution)/shard_map/output/pallas_call | solution.py:235
  28.8 3.3 %collective-permute-done.11.refs_1_ = bf16[128,256]{1,0:T(8,128)(2,1)S(1)} collective-permute-done((bf16[128,256]{1,0:T(8,128)(2,1)S(1)}, bf16[128,256]{1,0:T(8,128)(2,1)S(1)}, u32[]{:S(2)}, u32[]{:S(2)}) %collective-permute-start.11) | collective-permute-done | bytes 65568 | tf_op jit(solution)/shard_map/ppermute | solution.py:21
  32.1 0.4 collective-permute-start.12
  32.5 0.5 chunk.1
  33.0 2.1 %collective-permute-start.13 = (bf16[256,256]{1,0:T(8,128)(2,1)S(1)}, bf16[256,256]{1,0:T(8,128)(2,1)S(1)}, u32[]{:S(2)}, u32[]{:S(2)}) collective-permute-start(bf16[256,256]{1,0:T(8,128)(2,1)S(1)} %get-tuple-element.40.refs_0_), channel_id=1, source_target_pairs={{0,4},{4,0},{1,5},{5,1},{2,6},{6,2},{3,7},{7,3},{8,12},{12,8},{9,1... | collective-permute-start | bytes 393224 | tf_op jit(solution)/shard_map/ppermute | solution.py:21
  35.1 2.0 %collective-permute-done.12.h_ref = bf16[256,256]{1,0:T(8,128)(2,1)S(1)} collective-permute-done((bf16[256,256]{1,0:T(8,128)(2,1)S(1)}, bf16[256,256]{1,0:T(8,128)(2,1)S(1)}, u32[]{:S(2)}, u32[]{:S(2)}) %collective-permute-start.12) | collective-permute-done | bytes 131104 | tf_op jit(solution)/shard_map/ppermute | solution.py:21
  37.1 0.5 %last_chunk.1 = (bf16[256,256]{1,0:T(8,128)(2,1)S(1)}, bf16[400,256]{1,0:T(8,128)(2,1)S(1)}, bf16[144,256]{1,0:T(8,128)(2,1)S(1)}) custom-call(bf16[256,256]{1,0:T(8,128)(2,1)S(1)} %copy-done, f32[1,256]{1,0:T(1,128)S(1)} %bitcast.4, bf16[256,256]{1,0:T(8,128)(2,1)S(1)} %collective-permute-done.12.h_ref, bf16[256,256]{1,0:T(8,128)(2,1)S(1)} %pack.4.c0_ref, ...), custom_call_target="tpu_custom_call" | custom-call | flops 100663296 | bytes 1205248 | tf_op jit(solution)/shard_map/last_chunk/pallas_call | solution.py:235
  37.7 0.4 collective-permute-done.13.refs_0_
  38.1 2.0 %collective-permute-start.18 = (bf16[256,256]{1,0:T(8,128)(2,1)S(1)}, bf16[256,256]{1,0:T(8,128)(2,1)S(1)}, u32[]{:S(2)}, u32[]{:S(2)}) collective-permute-start(bf16[256,256]{1,0:T(8,128)(2,1)S(1)} %get-tuple-element.41.refs_1_), channel_id=1, source_target_pairs={{0,4},{4,0},{1,5},{5,1},{2,6},{6,2},{3,7},{7,3},{8,12},{12,8},{9,1... | collective-permute-start | bytes 393224 | tf_op jit(solution)/shard_map/ppermute | solution.py:21
  40.3 1.6 %collective-permute-start.15 = (bf16[144,256]{1,0:T(8,128)(2,1)S(1)}, bf16[144,256]{1,0:T(8,128)(2,1)S(1)}, u32[]{:S(2)}, u32[]{:S(2)}) collective-permute-start(bf16[144,256]{1,0:T(8,128)(2,1)S(1)} %sum_core.1.own_ref), channel_id=1, source_target_pairs={{0,1},{1,0},{2,3},{3,2},{4,5},{5,4},{6,7},{7,6},{8,9},{9,8},{10,11... | collective-permute-start | bytes 221192 | tf_op jit(solution)/shard_map/ppermute | solution.py:21
  41.9 2.3 %collective-permute-done.18.refs_1_ = bf16[256,256]{1,0:T(8,128)(2,1)S(1)} collective-permute-done((bf16[256,256]{1,0:T(8,128)(2,1)S(1)}, bf16[256,256]{1,0:T(8,128)(2,1)S(1)}, u32[]{:S(2)}, u32[]{:S(2)}) %collective-permute-start.18) | collective-permute-done | bytes 131104 | tf_op jit(solution)/shard_map/ppermute | solution.py:21
  44.2 0.6 %collective-permute-done.15.other_ref = bf16[144,256]{1,0:T(8,128)(2,1)S(1)} collective-permute-done((bf16[144,256]{1,0:T(8,128)(2,1)S(1)}, bf16[144,256]{1,0:T(8,128)(2,1)S(1)}, u32[]{:S(2)}, u32[]{:S(2)}) %collective-permute-start.15) | collective-permute-done | bytes 73760 | tf_op jit(solution)/shard_map/ppermute | solution.py:21
  45.0 0.3 backward_near.1.half_ref
  45.9 0.3 collective-permute-done.16.other_ref
  46.2 1.5 %collective-permute-start.21 = (bf16[272,256]{1,0:T(8,128)(2,1)S(1)}, bf16[272,256]{1,0:T(8,128)(2,1)S(1)}, u32[]{:S(2)}, u32[]{:S(2)}) collective-permute-start(bf16[272,256]{1,0:T(8,128)(2,1)S(1)} %halves.1.near_ref), channel_id=1, source_target_pairs={{0,4},{4,0},{1,5},{5,1},{2,6},{6,2},{3,7},{7,3},{8,12},{12,8},{9,1... | collective-permute-start | bytes 417800 | tf_op jit(solution)/shard_map/ppermute | solution.py:21
  47.8 1.5 %collective-permute-start.22 = (bf16[128,256]{1,0:T(8,128)(2,1)S(1)}, bf16[128,256]{1,0:T(8,128)(2,1)S(1)}, u32[]{:S(2)}, u32[]{:S(2)}) collective-permute-start(bf16[128,256]{1,0:T(8,128)(2,1)S(1)} %get-tuple-element.44), channel_id=1, source_target_pairs={{0,1},{1,0},{2,3},{3,2},{4,5},{5,4},{6,7},{7,6},{8,9},{9,8},{10,11... | collective-permute-start | bytes 196616 | tf_op jit(solution)/shard_map/ppermute | solution.py:21
  49.3 2.8 %collective-permute-done.22.refs_1_ = bf16[128,256]{1,0:T(8,128)(2,1)S(1)} collective-permute-done((bf16[128,256]{1,0:T(8,128)(2,1)S(1)}, bf16[128,256]{1,0:T(8,128)(2,1)S(1)}, u32[]{:S(2)}, u32[]{:S(2)}) %collective-permute-start.22) | collective-permute-done | bytes 65568 | tf_op jit(solution)/shard_map/ppermute | solution.py:21
  52.0 0.8 %last.1 = (f32[256,256]{1,0:T(8,128)}, f32[1,256]{1,0:T(1,128)}, bf16[128,256]{1,0:T(8,128)(2,1)}) custom-call(bf16[272,256]{1,0:T(8,128)(2,1)S(1)} %halves.1.near_ref, bf16[272,256]{1,0:T(8,128)(2,1)S(1)} %collective-permute-done.21.far_ref, f32[128,256]{1,0:T(8,128)S(1)} %get-tuple-element.42.refs_0_, bf16[128,256]{1,0:T(8,128)(2,1)S(1)} %collective-permute-done.22.refs_1_), custom_call_target="tpu_custom_call" | custom-call | bytes 803840 | tf_op jit(solution)/shard_map/last/pallas_call | solution.py:235
  (34 shorter events, 1.9 us)
Async XLA Ops:
  0.6 7.4 %collective-permute-start = (bf16[128,256]{1,0:T(8,128)(2,1)}, bf16[128,256]{1,0:T(8,128)(2,1)S(1)}, u32[]{:S(2)}, u32[]{:S(2)}) collective-permute-start(bf16[128,256]{1,0:T(8,128)(2,1)} %f_hbm.1), channel_id=1, source_target_pairs={{0,16},{8,24},{16,0},{24,8},{1,17},{9,25},{17,1},{25,9},{2,18},{10... | collective-permute-start | bytes 196616 | tf_op jit(solution)/shard_map/ppermute | solution.py:21
  4.7 4.5 %collective-permute-start.1 = (bf16[128,256]{1,0:T(8,128)(2,1)}, bf16[128,256]{1,0:T(8,128)(2,1)S(1)}, u32[]{:S(2)}, u32[]{:S(2)}) collective-permute-start(bf16[128,256]{1,0:T(8,128)(2,1)} %c_hbm.1), channel_id=1, source_target_pairs={{0,8},{8,0},{16,24},{24,16},{1,9},{9,1},{17,25},{25,17},{2,10},{10... | collective-permute-start | bytes 196616 | tf_op jit(solution)/shard_map/ppermute | solution.py:21
  9.2 5.0 %collective-permute-start.2 = (bf16[256,256]{1,0:T(8,128)(2,1)S(1)}, bf16[256,256]{1,0:T(8,128)(2,1)S(1)}, u32[]{:S(2)}, u32[]{:S(2)}) collective-permute-start(bf16[256,256]{1,0:T(8,128)(2,1)S(1)} %pack.3.refs_0_), channel_id=1, source_target_pairs={{0,8},{8,0},{16,24},{24,16},{1,9},{9,1},{17,25},{25,17},{2,10},{10... | collective-permute-start | bytes 393224 | tf_op jit(solution)/shard_map/ppermute | solution.py:21
  10.8 6.8 %collective-permute-start.5 = (bf16[256,256]{1,0:T(8,128)(2,1)S(1)}, bf16[256,256]{1,0:T(8,128)(2,1)S(1)}, u32[]{:S(2)}, u32[]{:S(2)}) collective-permute-start(bf16[256,256]{1,0:T(8,128)(2,1)S(1)} %pack.3.refs_0_), channel_id=1, source_target_pairs={{0,4},{4,0},{1,5},{5,1},{2,6},{6,2},{3,7},{7,3},{8,12},{12,8},{9,1... | collective-permute-start | bytes 393224 | tf_op jit(solution)/shard_map/ppermute | solution.py:21
  12.3 7.6 %collective-permute-start.8 = (bf16[256,256]{1,0:T(8,128)(2,1)S(1)}, bf16[256,256]{1,0:T(8,128)(2,1)S(1)}, u32[]{:S(2)}, u32[]{:S(2)}) collective-permute-start(bf16[256,256]{1,0:T(8,128)(2,1)S(1)} %pack.4.c0_ref), channel_id=1, source_target_pairs={{0,16},{8,24},{16,0},{24,8},{1,17},{9,25},{17,1},{25,9},{2,18},{10... | collective-permute-start | bytes 393224 | tf_op jit(solution)/shard_map/ppermute | solution.py:21
  14.2 5.8 %collective-permute-start.6 = (bf16[256,256]{1,0:T(8,128)(2,1)S(1)}, bf16[256,256]{1,0:T(8,128)(2,1)S(1)}, u32[]{:S(2)}, u32[]{:S(2)}) collective-permute-start(bf16[256,256]{1,0:T(8,128)(2,1)S(1)} %collective-permute-done.2.refs_1_), channel_id=1, source_target_pairs={{0,4},{4,0},{1,5},{5,1},{2,6},{6,2},{3,7},{7,3},{8,12},{12,8},{9,1... | collective-permute-start | bytes 393224 | tf_op jit(solution)/shard_map/ppermute | solution.py:21
  17.1 3.0 %collective-permute-start.3 = (bf16[256,256]{1,0:T(8,128)(2,1)S(1)}, bf16[256,256]{1,0:T(8,128)(2,1)S(1)}, u32[]{:S(2)}, u32[]{:S(2)}) collective-permute-start(bf16[256,256]{1,0:T(8,128)(2,1)S(1)} %pack.3.refs_0_), channel_id=1, source_target_pairs={{0,2},{2,0},{1,3},{3,1},{4,6},{6,4},{5,7},{7,5},{8,10},{10,8},{9,1... | collective-permute-start | bytes 393224 | tf_op jit(solution)/shard_map/ppermute | solution.py:21
  17.1 3.0 %collective-permute-start.4 = (bf16[256,256]{1,0:T(8,128)(2,1)S(1)}, bf16[256,256]{1,0:T(8,128)(2,1)S(1)}, u32[]{:S(2)}, u32[]{:S(2)}) collective-permute-start(bf16[256,256]{1,0:T(8,128)(2,1)S(1)} %collective-permute-done.2.refs_1_), channel_id=1, source_target_pairs={{0,2},{2,0},{1,3},{3,1},{4,6},{6,4},{5,7},{7,5},{8,10},{10,8},{9,1... | collective-permute-start | bytes 393224 | tf_op jit(solution)/shard_map/ppermute | solution.py:21
  17.6 2.8 %collective-permute-start.7 = (bf16[256,256]{1,0:T(8,128)(2,1)S(1)}, bf16[256,256]{1,0:T(8,128)(2,1)S(1)}, u32[]{:S(2)}, u32[]{:S(2)}) collective-permute-start(bf16[256,256]{1,0:T(8,128)(2,1)S(1)} %collective-permute-done.5.refs_0_), channel_id=1, source_target_pairs={{0,2},{2,0},{1,3},{3,1},{4,6},{6,4},{5,7},{7,5},{8,10},{10,8},{9,1... | collective-permute-start | bytes 393224 | tf_op jit(solution)/shard_map/ppermute | solution.py:21
  20.0 1.3 %collective-permute-start.9 = (bf16[256,256]{1,0:T(8,128)(2,1)S(1)}, bf16[256,256]{1,0:T(8,128)(2,1)S(1)}, u32[]{:S(2)}, u32[]{:S(2)}) collective-permute-start(bf16[256,256]{1,0:T(8,128)(2,1)S(1)} %collective-permute-done.6.refs_1_), channel_id=1, source_target_pairs={{0,2},{2,0},{1,3},{3,1},{4,6},{6,4},{5,7},{7,5},{8,10},{10,8},{9,1... | collective-permute-start | bytes 393224 | tf_op jit(solution)/shard_map/ppermute | solution.py:21
  21.7 4.3 %collective-permute-start.10 = (bf16[128,256]{1,0:T(8,128)(2,1)S(1)}, bf16[128,256]{1,0:T(8,128)(2,1)S(1)}, u32[]{:S(2)}, u32[]{:S(2)}) collective-permute-start(bf16[128,256]{1,0:T(8,128)(2,1)S(1)} %get-tuple-element.32), channel_id=1, source_target_pairs={{0,1},{1,0},{2,3},{3,2},{4,5},{5,4},{6,7},{7,6},{8,9},{9,8},{10,11... | collective-permute-start | bytes 196616 | tf_op jit(solution)/shard_map/ppermute | solution.py:21
  26.0 2.0 %copy-start = (bf16[256,256]{1,0:T(8,128)(2,1)S(1)}, bf16[256,256]{1,0:T(8,128)(2,1)}, u32[]{:S(2)}) copy-start(bf16[256,256]{1,0:T(8,128)(2,1)} %w_ref.5) | copy-start | bytes 393220
  26.0 2.0 %copy-start.1 = (f32[256]{0:T(256)S(1)}, f32[256]{0:T(256)}, u32[]{:S(2)}) copy-start(f32[256]{0:T(256)} %param.9) | copy-start | bytes 3076
  26.0 6.0 %collective-permute-start.11 = (bf16[128,256]{1,0:T(8,128)(2,1)S(1)}, bf16[128,256]{1,0:T(8,128)(2,1)S(1)}, u32[]{:S(2)}, u32[]{:S(2)}) collective-permute-start(bf16[128,256]{1,0:T(8,128)(2,1)S(1)} %hidden.1.h_ref.refs_0_), channel_id=1, source_target_pairs={{0,16},{8,24},{16,0},{24,8},{1,17},{9,25},{17,1},{25,9},{2,18},{10... | collective-permute-start | bytes 196616 | tf_op jit(solution)/shard_map/ppermute | solution.py:21
  32.1 5.0 %collective-permute-start.12 = (bf16[256,256]{1,0:T(8,128)(2,1)S(1)}, bf16[256,256]{1,0:T(8,128)(2,1)S(1)}, u32[]{:S(2)}, u32[]{:S(2)}) collective-permute-start(bf16[256,256]{1,0:T(8,128)(2,1)S(1)} %pack.5.h_ref), channel_id=1, source_target_pairs={{0,8},{8,0},{16,24},{24,16},{1,9},{9,1},{17,25},{25,17},{2,10},{10... | collective-permute-start | bytes 393224 | tf_op jit(solution)/shard_map/ppermute | solution.py:21
  33.0 5.0 %collective-permute-start.13 = (bf16[256,256]{1,0:T(8,128)(2,1)S(1)}, bf16[256,256]{1,0:T(8,128)(2,1)S(1)}, u32[]{:S(2)}, u32[]{:S(2)}) collective-permute-start(bf16[256,256]{1,0:T(8,128)(2,1)S(1)} %get-tuple-element.40.refs_0_), channel_id=1, source_target_pairs={{0,4},{4,0},{1,5},{5,1},{2,6},{6,2},{3,7},{7,3},{8,12},{12,8},{9,1... | collective-permute-start | bytes 393224 | tf_op jit(solution)/shard_map/ppermute | solution.py:21
  38.1 2.3 %collective-permute-start.14 = (bf16[400,256]{1,0:T(8,128)(2,1)S(1)}, bf16[400,256]{1,0:T(8,128)(2,1)S(1)}, u32[]{:S(2)}, u32[]{:S(2)}) collective-permute-start(bf16[400,256]{1,0:T(8,128)(2,1)S(1)} %get-tuple-element.39), channel_id=1, source_target_pairs={{0,2},{2,0},{1,3},{3,1},{4,6},{6,4},{5,7},{7,5},{8,10},{10,8},{9,1... | collective-permute-start | bytes 614408 | tf_op jit(solution)/shard_map/ppermute | solution.py:21
  38.1 6.2 %collective-permute-start.18 = (bf16[256,256]{1,0:T(8,128)(2,1)S(1)}, bf16[256,256]{1,0:T(8,128)(2,1)S(1)}, u32[]{:S(2)}, u32[]{:S(2)}) collective-permute-start(bf16[256,256]{1,0:T(8,128)(2,1)S(1)} %get-tuple-element.41.refs_1_), channel_id=1, source_target_pairs={{0,4},{4,0},{1,5},{5,1},{2,6},{6,2},{3,7},{7,3},{8,12},{12,8},{9,1... | collective-permute-start | bytes 393224 | tf_op jit(solution)/shard_map/ppermute | solution.py:21
  40.1 4.9 %collective-permute-start.17 = (bf16[256,256]{1,0:T(8,128)(2,1)S(1)}, bf16[256,256]{1,0:T(8,128)(2,1)S(1)}, u32[]{:S(2)}, u32[]{:S(2)}) collective-permute-start(bf16[256,256]{1,0:T(8,128)(2,1)S(1)} %get-tuple-element.40.refs_0_), channel_id=1, source_target_pairs={{0,2},{2,0},{1,3},{3,1},{4,6},{6,4},{5,7},{7,5},{8,10},{10,8},{9,1... | collective-permute-start | bytes 393224 | tf_op jit(solution)/shard_map/ppermute | solution.py:21
  40.3 4.5 %collective-permute-start.15 = (bf16[144,256]{1,0:T(8,128)(2,1)S(1)}, bf16[144,256]{1,0:T(8,128)(2,1)S(1)}, u32[]{:S(2)}, u32[]{:S(2)}) collective-permute-start(bf16[144,256]{1,0:T(8,128)(2,1)S(1)} %sum_core.1.own_ref), channel_id=1, source_target_pairs={{0,1},{1,0},{2,3},{3,2},{4,5},{5,4},{6,7},{7,6},{8,9},{9,8},{10,11... | collective-permute-start | bytes 221192 | tf_op jit(solution)/shard_map/ppermute | solution.py:21
  41.9 3.4 %collective-permute-start.19 = (bf16[256,256]{1,0:T(8,128)(2,1)S(1)}, bf16[256,256]{1,0:T(8,128)(2,1)S(1)}, u32[]{:S(2)}, u32[]{:S(2)}) collective-permute-start(bf16[256,256]{1,0:T(8,128)(2,1)S(1)} %collective-permute-done.13.refs_0_), channel_id=1, source_target_pairs={{0,2},{2,0},{1,3},{3,1},{4,6},{6,4},{5,7},{7,5},{8,10},{10,8},{9,1... | collective-permute-start | bytes 393224 | tf_op jit(solution)/shard_map/ppermute | solution.py:21
  44.2 1.3 %collective-permute-start.20 = (bf16[256,256]{1,0:T(8,128)(2,1)S(1)}, bf16[256,256]{1,0:T(8,128)(2,1)S(1)}, u32[]{:S(2)}, u32[]{:S(2)}) collective-permute-start(bf16[256,256]{1,0:T(8,128)(2,1)S(1)} %collective-permute-done.18.refs_1_), channel_id=1, source_target_pairs={{0,2},{2,0},{1,3},{3,1},{4,6},{6,4},{5,7},{7,5},{8,10},{10,8},{9,1... | collective-permute-start | bytes 393224 | tf_op jit(solution)/shard_map/ppermute | solution.py:21
  44.9 1.3 %collective-permute-start.16 = (bf16[144,256]{1,0:T(8,128)(2,1)S(1)}, bf16[144,256]{1,0:T(8,128)(2,1)S(1)}, u32[]{:S(2)}, u32[]{:S(2)}) collective-permute-start(bf16[144,256]{1,0:T(8,128)(2,1)S(1)} %sum_row.1.own_ref), channel_id=1, source_target_pairs={{0,2},{2,0},{1,3},{3,1},{4,6},{6,4},{5,7},{7,5},{8,10},{10,8},{9,1... | collective-permute-start | bytes 221192 | tf_op jit(solution)/shard_map/ppermute | solution.py:21
  46.2 5.8 %collective-permute-start.21 = (bf16[272,256]{1,0:T(8,128)(2,1)S(1)}, bf16[272,256]{1,0:T(8,128)(2,1)S(1)}, u32[]{:S(2)}, u32[]{:S(2)}) collective-permute-start(bf16[272,256]{1,0:T(8,128)(2,1)S(1)} %halves.1.near_ref), channel_id=1, source_target_pairs={{0,4},{4,0},{1,5},{5,1},{2,6},{6,2},{3,7},{7,3},{8,12},{12,8},{9,1... | collective-permute-start | bytes 417800 | tf_op jit(solution)/shard_map/ppermute | solution.py:21
  47.8 4.3 %collective-permute-start.22 = (bf16[128,256]{1,0:T(8,128)(2,1)S(1)}, bf16[128,256]{1,0:T(8,128)(2,1)S(1)}, u32[]{:S(2)}, u32[]{:S(2)}) collective-permute-start(bf16[128,256]{1,0:T(8,128)(2,1)S(1)} %get-tuple-element.44), channel_id=1, source_target_pairs={{0,1},{1,0},{2,3},{3,2},{4,5},{5,4},{6,7},{7,6},{8,9},{9,8},{10,11... | collective-permute-start | bytes 196616 | tf_op jit(solution)/shard_map/ppermute | solution.py:21

commit v13 on v12

--- a/solution.py
+++ b/solution.py
@@ -306,9 +306,9 @@
     )
     f00 = far_chunks(after(pack(features, other), other_cot), steps)
     f10 = [swap(chunk, "mid") for chunk in f00]
-    cots = far_chunks(pack(cotangent, other_cot), cot_steps)
+    cots = far_chunks(pack(cotangent, after(other_cot, f00[-1])), cot_steps)
     f01 = [swap(chunk, "core") for chunk in f00]
-    f11 = [swap(chunk, "core") for chunk in f10[:-1] + [after(f10[-1], *cots)]]
+    f11 = [swap(chunk, "core") for chunk in f10]
     half = near_product(f00 + f01, "forward")
     own, *parts = rest_product(half, f10 + f11, "forward")
     others = from_row(parts)
@@ -316,7 +316,7 @@
 
     bias_row = bias_vector.reshape(1, width)
     (output,) = call(
-        output_kernel, "output", [shape(tile, width)], [weight, bias_row, hidden]
+        output_kernel, "output", [shape(tile, width)], [weight, bias_row, after(hidden, *cots)]
     )
     other, hidden = far_partner(hidden, steps[0]), after(hidden, output)
     hiddens = far_chunks(pack(hidden, other), steps)

time: 53 us -> 52.9 us (level)
  starting transfers between devices: 27 us -> 25 us
  waiting for transfers between devices: 19.4 us -> 21.4 us
    ppermute x23, waiting for transfers between devices: 19.4 us -> 21.4 us  [partner(): return lax.ppermute(x, axis, [(i, i ^ mask) for i in range(n)])]
    ppermute x23, starting transfers between devices: 27 us -> 25 us  [partner(): return lax.ppermute(x, axis, [(i, i ^ mask) for i in range(n)])]
  transfers between devices with their start and end apart: 23 -> 23, of which waited for: 13 -> 14; matrix products, arithmetic and copies ran while one was open for 0% -> 0% of each run, Pallas kernels for 9% -> 9%
where the time goes in v13:
time: 52.9 us; the launch traced here: 52.8 us
  starting transfers between devices  25 us (47%)
  waiting for transfers between devices  21.4 us (40%)
  Pallas kernels  5.6 us (11%)
  between operations  0.77 us (1%)
    ppermute x23, starting transfers between devices, partner(): return lax.ppermute(x, axis, [(i, i ^ mask) for i in range(n)])  25 us
    ppermute x23, waiting for transfers between devices, partner(): return lax.ppermute(x, axis, [(i, i ^ mask) for i in range(n)])  21.4 us
    pallas_call x16, Pallas kernels, call(): pl.pallas_call(kernel, name=name, out_shape=outs, in_specs=specs or [VMEM...  5.6 us
  transfers between devices with their start and end apart: 23, of which 14 were waited for; matrix products, arithmetic and copies ran while one was open for 0% of the time, Pallas kernels for 9%

profile of v13, /device:TPU:0, one launch (start us, length us, event | category | flops | bytes accessed | tf_op | source)
XLA Modules:
  0.0 52.8 jit_solution(580542016347684748)
XLA Ops:
  0.6 4.1 %collective-permute-start = (bf16[128,256]{1,0:T(8,128)(2,1)}, bf16[128,256]{1,0:T(8,128)(2,1)S(1)}, u32[]{:S(2)}, u32[]{:S(2)}) collective-permute-start(bf16[128,256]{1,0:T(8,128)(2,1)} %f_hbm.1), channel_id=1, source_target_pairs={{0,16},{8,24},{16,0},{24,8},{1,17},{9,25},{17,1},{25,9},{2,18},{10... | collective-permute-start | bytes 196616 | tf_op jit(solution)/shard_map/ppermute | solution.py:21
  4.7 1.6 %collective-permute-start.1 = (bf16[128,256]{1,0:T(8,128)(2,1)}, bf16[128,256]{1,0:T(8,128)(2,1)S(1)}, u32[]{:S(2)}, u32[]{:S(2)}) collective-permute-start(bf16[128,256]{1,0:T(8,128)(2,1)} %c_hbm.1), channel_id=1, source_target_pairs={{0,8},{8,0},{16,24},{24,16},{1,9},{9,1},{17,25},{25,17},{2,10},{10... | collective-permute-start | bytes 196616 | tf_op jit(solution)/shard_map/ppermute | solution.py:21
  6.3 1.7 %expand.1 = (bf16[256,2048]{1,0:T(8,128)(2,1)S(1)}, bf16[128,256]{1,0:T(8,128)(2,1)S(1)}, bf16[128,256]{1,0:T(8,128)(2,1)S(1)}) custom-call(s32[32]{0:T(128)} %rows_hbm.1, s32[16]{0:T(128)} %counts_hbm.1, bf16[32,128,128]{2,1,0:T(8,128)(2,1)} %tiles_hbm.1, bf16[128,256]{1,0:T(8,128)(2,1)} %f_hbm.1, bf16[128,256]{1,0:T(8,128)(2,1)} %c_hbm.1), custom_call_target="tpu_custom_call" | custom-call | bytes 2359488 | tf_op jit(solution)/shard_map/expand/pallas_call | solution.py:235
  8.0 1.2 %collective-permute-done.1.refs_1_ = bf16[128,256]{1,0:T(8,128)(2,1)S(1)} collective-permute-done((bf16[128,256]{1,0:T(8,128)(2,1)}, bf16[128,256]{1,0:T(8,128)(2,1)S(1)}, u32[]{:S(2)}, u32[]{:S(2)}) %collective-permute-start.1) | collective-permute-done | bytes 65568 | tf_op jit(solution)/shard_map/ppermute | solution.py:21
  9.2 1.6 %collective-permute-start.2 = (bf16[256,256]{1,0:T(8,128)(2,1)S(1)}, bf16[256,256]{1,0:T(8,128)(2,1)S(1)}, u32[]{:S(2)}, u32[]{:S(2)}) collective-permute-start(bf16[256,256]{1,0:T(8,128)(2,1)S(1)} %pack.3.refs_0_), channel_id=1, source_target_pairs={{0,8},{8,0},{16,24},{24,16},{1,9},{9,1},{17,25},{25,17},{2,10},{10... | collective-permute-start | bytes 393224 | tf_op jit(solution)/shard_map/ppermute | solution.py:21
  10.8 1.5 %collective-permute-start.5 = (bf16[256,256]{1,0:T(8,128)(2,1)S(1)}, bf16[256,256]{1,0:T(8,128)(2,1)S(1)}, u32[]{:S(2)}, u32[]{:S(2)}) collective-permute-start(bf16[256,256]{1,0:T(8,128)(2,1)S(1)} %pack.3.refs_0_), channel_id=1, source_target_pairs={{0,4},{4,0},{1,5},{5,1},{2,6},{6,2},{3,7},{7,3},{8,12},{12,8},{9,1... | collective-permute-start | bytes 393224 | tf_op jit(solution)/shard_map/ppermute | solution.py:21
  12.3 1.9 %collective-permute-done.2.refs_1_ = bf16[256,256]{1,0:T(8,128)(2,1)S(1)} collective-permute-done((bf16[256,256]{1,0:T(8,128)(2,1)S(1)}, bf16[256,256]{1,0:T(8,128)(2,1)S(1)}, u32[]{:S(2)}, u32[]{:S(2)}) %collective-permute-start.2) | collective-permute-done | bytes 131104 | tf_op jit(solution)/shard_map/ppermute | solution.py:21
  14.2 1.5 %collective-permute-start.6 = (bf16[256,256]{1,0:T(8,128)(2,1)S(1)}, bf16[256,256]{1,0:T(8,128)(2,1)S(1)}, u32[]{:S(2)}, u32[]{:S(2)}) collective-permute-start(bf16[256,256]{1,0:T(8,128)(2,1)S(1)} %collective-permute-done.2.refs_1_), channel_id=1, source_target_pairs={{0,4},{4,0},{1,5},{5,1},{2,6},{6,2},{3,7},{7,3},{8,12},{12,8},{9,1... | collective-permute-start | bytes 393224 | tf_op jit(solution)/shard_map/ppermute | solution.py:21
  15.7 0.5 collective-permute-start.4
  16.2 0.7 %collective-permute-done.5.refs_0_ = bf16[256,256]{1,0:T(8,128)(2,1)S(1)} collective-permute-done((bf16[256,256]{1,0:T(8,128)(2,1)S(1)}, bf16[256,256]{1,0:T(8,128)(2,1)S(1)}, u32[]{:S(2)}, u32[]{:S(2)}) %collective-permute-start.5) | collective-permute-done | bytes 131104 | tf_op jit(solution)/shard_map/ppermute | solution.py:21
  16.9 2.3 %collective-permute-done.6.refs_1_ = bf16[256,256]{1,0:T(8,128)(2,1)S(1)} collective-permute-done((bf16[256,256]{1,0:T(8,128)(2,1)S(1)}, bf16[256,256]{1,0:T(8,128)(2,1)S(1)}, u32[]{:S(2)}, u32[]{:S(2)}) %collective-permute-start.6) | collective-permute-done | bytes 131104 | tf_op jit(solution)/shard_map/ppermute | solution.py:21
  19.2 1.8 %collective-permute-start.10 = (bf16[256,256]{1,0:T(8,128)(2,1)S(1)}, bf16[256,256]{1,0:T(8,128)(2,1)S(1)}, u32[]{:S(2)}, u32[]{:S(2)}) collective-permute-start(bf16[256,256]{1,0:T(8,128)(2,1)S(1)} %pack.4.c0_ref), channel_id=1, source_target_pairs={{0,16},{8,24},{16,0},{24,8},{1,17},{9,25},{17,1},{25,9},{2,18},{10... | collective-permute-start | bytes 393224 | tf_op jit(solution)/shard_map/ppermute | solution.py:21
  21.6 1.6 %collective-permute-start.9 = (bf16[128,256]{1,0:T(8,128)(2,1)S(1)}, bf16[128,256]{1,0:T(8,128)(2,1)S(1)}, u32[]{:S(2)}, u32[]{:S(2)}) collective-permute-start(bf16[128,256]{1,0:T(8,128)(2,1)S(1)} %get-tuple-element.31), channel_id=1, source_target_pairs={{0,1},{1,0},{2,3},{3,2},{4,5},{5,4},{6,7},{7,6},{8,9},{9,8},{10,11... | collective-permute-start | bytes 196616 | tf_op jit(solution)/shard_map/ppermute | solution.py:21
  23.2 2.7 %collective-permute-done.9.refs_0_ = bf16[128,256]{1,0:T(8,128)(2,1)S(1)} collective-permute-done((bf16[128,256]{1,0:T(8,128)(2,1)S(1)}, bf16[128,256]{1,0:T(8,128)(2,1)S(1)}, u32[]{:S(2)}, u32[]{:S(2)}) %collective-permute-start.9) | collective-permute-done | bytes 65568 | tf_op jit(solution)/shard_map/ppermute | solution.py:21
  26.0 1.2 %collective-permute-start.11 = (bf16[128,256]{1,0:T(8,128)(2,1)S(1)}, bf16[128,256]{1,0:T(8,128)(2,1)S(1)}, u32[]{:S(2)}, u32[]{:S(2)}) collective-permute-start(bf16[128,256]{1,0:T(8,128)(2,1)S(1)} %hidden.1.h_ref.refs_0_), channel_id=1, source_target_pairs={{0,16},{8,24},{16,0},{24,8},{1,17},{9,25},{17,1},{25,9},{2,18},{10... | collective-permute-start | bytes 196616 | tf_op jit(solution)/shard_map/ppermute | solution.py:21
  27.2 1.6 %collective-permute-done.10.c1_ref = bf16[256,256]{1,0:T(8,128)(2,1)S(1)} collective-permute-done((bf16[256,256]{1,0:T(8,128)(2,1)S(1)}, bf16[256,256]{1,0:T(8,128)(2,1)S(1)}, u32[]{:S(2)}, u32[]{:S(2)}) %collective-permute-start.10) | collective-permute-done | bytes 131104 | tf_op jit(solution)/shard_map/ppermute | solution.py:21
  28.9 0.8 %output.1 = bf16[128,256]{1,0:T(8,128)(2,1)} custom-call(bf16[256,256]{1,0:T(8,128)(2,1)S(1)} %copy-done, f32[1,256]{1,0:T(1,128)S(1)} %bitcast.2, bf16[128,256]{1,0:T(8,128)(2,1)S(1)} %hidden.1.h_ref.refs_0_), custom_call_target="tpu_custom_call" | custom-call | bytes 263168 | tf_op jit(solution)/shard_map/output/pallas_call | solution.py:235
  29.7 1.8 %collective-permute-done.11.refs_1_ = bf16[128,256]{1,0:T(8,128)(2,1)S(1)} collective-permute-done((bf16[128,256]{1,0:T(8,128)(2,1)S(1)}, bf16[128,256]{1,0:T(8,128)(2,1)S(1)}, u32[]{:S(2)}, u32[]{:S(2)}) %collective-permute-start.11) | collective-permute-done | bytes 65568 | tf_op jit(solution)/shard_map/ppermute | solution.py:21
  31.5 1.5 %collective-permute-start.12 = (bf16[256,256]{1,0:T(8,128)(2,1)S(1)}, bf16[256,256]{1,0:T(8,128)(2,1)S(1)}, u32[]{:S(2)}, u32[]{:S(2)}) collective-permute-start(bf16[256,256]{1,0:T(8,128)(2,1)S(1)} %pack.5.h_ref), channel_id=1, source_target_pairs={{0,8},{8,0},{16,24},{24,16},{1,9},{9,1},{17,25},{25,17},{2,10},{10... | collective-permute-start | bytes 393224 | tf_op jit(solution)/shard_map/ppermute | solution.py:21
  33.1 0.5 chunk.1
  33.5 1.6 %collective-permute-start.13 = (bf16[256,256]{1,0:T(8,128)(2,1)S(1)}, bf16[256,256]{1,0:T(8,128)(2,1)S(1)}, u32[]{:S(2)}, u32[]{:S(2)}) collective-permute-start(bf16[256,256]{1,0:T(8,128)(2,1)S(1)} %get-tuple-element.42.refs_0_), channel_id=1, source_target_pairs={{0,4},{4,0},{1,5},{5,1},{2,6},{6,2},{3,7},{7,3},{8,12},{12,8},{9,1... | collective-permute-start | bytes 393224 | tf_op jit(solution)/shard_map/ppermute | solution.py:21
  35.1 1.5 %collective-permute-done.12.h_ref = bf16[256,256]{1,0:T(8,128)(2,1)S(1)} collective-permute-done((bf16[256,256]{1,0:T(8,128)(2,1)S(1)}, bf16[256,256]{1,0:T(8,128)(2,1)S(1)}, u32[]{:S(2)}, u32[]{:S(2)}) %collective-permute-start.12) | collective-permute-done | bytes 131104 | tf_op jit(solution)/shard_map/ppermute | solution.py:21
  36.6 0.5 %last_chunk.1 = (bf16[256,256]{1,0:T(8,128)(2,1)S(1)}, bf16[400,256]{1,0:T(8,128)(2,1)S(1)}, bf16[144,256]{1,0:T(8,128)(2,1)S(1)}) custom-call(bf16[256,256]{1,0:T(8,128)(2,1)S(1)} %copy-done, f32[1,256]{1,0:T(1,128)S(1)} %bitcast.4, bf16[256,256]{1,0:T(8,128)(2,1)S(1)} %collective-permute-done.12.h_ref, bf16[256,256]{1,0:T(8,128)(2,1)S(1)} %pack.4.c0_ref, ...), custom_call_target="tpu_custom_call" | custom-call | flops 100663296 | bytes 1205248 | tf_op jit(solution)/shard_map/last_chunk/pallas_call | solution.py:235
  37.1 1.5 %collective-permute-done.13.refs_0_ = bf16[256,256]{1,0:T(8,128)(2,1)S(1)} collective-permute-done((bf16[256,256]{1,0:T(8,128)(2,1)S(1)}, bf16[256,256]{1,0:T(8,128)(2,1)S(1)}, u32[]{:S(2)}, u32[]{:S(2)}) %collective-permute-start.13) | collective-permute-done | bytes 131104 | tf_op jit(solution)/shard_map/ppermute | solution.py:21
  38.6 1.5 %collective-permute-start.18 = (bf16[256,256]{1,0:T(8,128)(2,1)S(1)}, bf16[256,256]{1,0:T(8,128)(2,1)S(1)}, u32[]{:S(2)}, u32[]{:S(2)}) collective-permute-start(bf16[256,256]{1,0:T(8,128)(2,1)S(1)} %get-tuple-element.43.refs_1_), channel_id=1, source_target_pairs={{0,4},{4,0},{1,5},{5,1},{2,6},{6,2},{3,7},{7,3},{8,12},{12,8},{9,1... | collective-permute-start | bytes 393224 | tf_op jit(solution)/shard_map/ppermute | solution.py:21
  40.3 1.6 %collective-permute-start.15 = (bf16[144,256]{1,0:T(8,128)(2,1)S(1)}, bf16[144,256]{1,0:T(8,128)(2,1)S(1)}, u32[]{:S(2)}, u32[]{:S(2)}) collective-permute-start(bf16[144,256]{1,0:T(8,128)(2,1)S(1)} %sum_core.1.own_ref), channel_id=1, source_target_pairs={{0,1},{1,0},{2,3},{3,2},{4,5},{5,4},{6,7},{7,6},{8,9},{9,8},{10,11... | collective-permute-start | bytes 221192 | tf_op jit(solution)/shard_map/ppermute | solution.py:21
  41.9 2.6 %collective-permute-done.18.refs_1_ = bf16[256,256]{1,0:T(8,128)(2,1)S(1)} collective-permute-done((bf16[256,256]{1,0:T(8,128)(2,1)S(1)}, bf16[256,256]{1,0:T(8,128)(2,1)S(1)}, u32[]{:S(2)}, u32[]{:S(2)}) %collective-permute-start.18) | collective-permute-done | bytes 131104 | tf_op jit(solution)/shard_map/ppermute | solution.py:21
  45.4 0.4 collective-permute-done.20.refs_3_
  46.2 1.5 %collective-permute-start.21 = (bf16[272,256]{1,0:T(8,128)(2,1)S(1)}, bf16[272,256]{1,0:T(8,128)(2,1)S(1)}, u32[]{:S(2)}, u32[]{:S(2)}) collective-permute-start(bf16[272,256]{1,0:T(8,128)(2,1)S(1)} %halves.1.near_ref), channel_id=1, source_target_pairs={{0,4},{4,0},{1,5},{5,1},{2,6},{6,2},{3,7},{7,3},{8,12},{12,8},{9,1... | collective-permute-start | bytes 417800 | tf_op jit(solution)/shard_map/ppermute | solution.py:21
  47.7 1.5 %collective-permute-start.22 = (bf16[128,256]{1,0:T(8,128)(2,1)S(1)}, bf16[128,256]{1,0:T(8,128)(2,1)S(1)}, u32[]{:S(2)}, u32[]{:S(2)}) collective-permute-start(bf16[128,256]{1,0:T(8,128)(2,1)S(1)} %get-tuple-element.46), channel_id=1, source_target_pairs={{0,1},{1,0},{2,3},{3,2},{4,5},{5,4},{6,7},{7,6},{8,9},{9,8},{10,11... | collective-permute-start | bytes 196616 | tf_op jit(solution)/shard_map/ppermute | solution.py:21
  49.3 2.7 %collective-permute-done.22.refs_1_ = bf16[128,256]{1,0:T(8,128)(2,1)S(1)} collective-permute-done((bf16[128,256]{1,0:T(8,128)(2,1)S(1)}, bf16[128,256]{1,0:T(8,128)(2,1)S(1)}, u32[]{:S(2)}, u32[]{:S(2)}) %collective-permute-start.22) | collective-permute-done | bytes 65568 | tf_op jit(solution)/shard_map/ppermute | solution.py:21
  52.0 0.8 %last.1 = (f32[256,256]{1,0:T(8,128)}, f32[1,256]{1,0:T(1,128)}, bf16[128,256]{1,0:T(8,128)(2,1)}) custom-call(bf16[272,256]{1,0:T(8,128)(2,1)S(1)} %halves.1.near_ref, bf16[272,256]{1,0:T(8,128)(2,1)S(1)} %collective-permute-done.21.far_ref, f32[128,256]{1,0:T(8,128)S(1)} %get-tuple-element.44.refs_0_, bf16[128,256]{1,0:T(8,128)(2,1)S(1)} %collective-permute-done.22.refs_1_), custom_call_target="tpu_custom_call" | custom-call | bytes 803840 | tf_op jit(solution)/shard_map/last/pallas_call | solution.py:235
  (34 shorter events, 2.3 us)
Async XLA Ops:
  0.6 7.4 %collective-permute-start = (bf16[128,256]{1,0:T(8,128)(2,1)}, bf16[128,256]{1,0:T(8,128)(2,1)S(1)}, u32[]{:S(2)}, u32[]{:S(2)}) collective-permute-start(bf16[128,256]{1,0:T(8,128)(2,1)} %f_hbm.1), channel_id=1, source_target_pairs={{0,16},{8,24},{16,0},{24,8},{1,17},{9,25},{17,1},{25,9},{2,18},{10... | collective-permute-start | bytes 196616 | tf_op jit(solution)/shard_map/ppermute | solution.py:21
  4.7 4.5 %collective-permute-start.1 = (bf16[128,256]{1,0:T(8,128)(2,1)}, bf16[128,256]{1,0:T(8,128)(2,1)S(1)}, u32[]{:S(2)}, u32[]{:S(2)}) collective-permute-start(bf16[128,256]{1,0:T(8,128)(2,1)} %c_hbm.1), channel_id=1, source_target_pairs={{0,8},{8,0},{16,24},{24,16},{1,9},{9,1},{17,25},{25,17},{2,10},{10... | collective-permute-start | bytes 196616 | tf_op jit(solution)/shard_map/ppermute | solution.py:21
  9.2 5.0 %collective-permute-start.2 = (bf16[256,256]{1,0:T(8,128)(2,1)S(1)}, bf16[256,256]{1,0:T(8,128)(2,1)S(1)}, u32[]{:S(2)}, u32[]{:S(2)}) collective-permute-start(bf16[256,256]{1,0:T(8,128)(2,1)S(1)} %pack.3.refs_0_), channel_id=1, source_target_pairs={{0,8},{8,0},{16,24},{24,16},{1,9},{9,1},{17,25},{25,17},{2,10},{10... | collective-permute-start | bytes 393224 | tf_op jit(solution)/shard_map/ppermute | solution.py:21
  10.8 6.1 %collective-permute-start.5 = (bf16[256,256]{1,0:T(8,128)(2,1)S(1)}, bf16[256,256]{1,0:T(8,128)(2,1)S(1)}, u32[]{:S(2)}, u32[]{:S(2)}) collective-permute-start(bf16[256,256]{1,0:T(8,128)(2,1)S(1)} %pack.3.refs_0_), channel_id=1, source_target_pairs={{0,4},{4,0},{1,5},{5,1},{2,6},{6,2},{3,7},{7,3},{8,12},{12,8},{9,1... | collective-permute-start | bytes 393224 | tf_op jit(solution)/shard_map/ppermute | solution.py:21
  14.2 5.0 %collective-permute-start.6 = (bf16[256,256]{1,0:T(8,128)(2,1)S(1)}, bf16[256,256]{1,0:T(8,128)(2,1)S(1)}, u32[]{:S(2)}, u32[]{:S(2)}) collective-permute-start(bf16[256,256]{1,0:T(8,128)(2,1)S(1)} %collective-permute-done.2.refs_1_), channel_id=1, source_target_pairs={{0,4},{4,0},{1,5},{5,1},{2,6},{6,2},{3,7},{7,3},{8,12},{12,8},{9,1... | collective-permute-start | bytes 393224 | tf_op jit(solution)/shard_map/ppermute | solution.py:21
  15.7 5.3 %collective-permute-start.3 = (bf16[256,256]{1,0:T(8,128)(2,1)S(1)}, bf16[256,256]{1,0:T(8,128)(2,1)S(1)}, u32[]{:S(2)}, u32[]{:S(2)}) collective-permute-start(bf16[256,256]{1,0:T(8,128)(2,1)S(1)} %pack.3.refs_0_), channel_id=1, source_target_pairs={{0,2},{2,0},{1,3},{3,1},{4,6},{6,4},{5,7},{7,5},{8,10},{10,8},{9,1... | collective-permute-start | bytes 393224 | tf_op jit(solution)/shard_map/ppermute | solution.py:21
  15.7 5.3 %collective-permute-start.4 = (bf16[256,256]{1,0:T(8,128)(2,1)S(1)}, bf16[256,256]{1,0:T(8,128)(2,1)S(1)}, u32[]{:S(2)}, u32[]{:S(2)}) collective-permute-start(bf16[256,256]{1,0:T(8,128)(2,1)S(1)} %collective-permute-done.2.refs_1_), channel_id=1, source_target_pairs={{0,2},{2,0},{1,3},{3,1},{4,6},{6,4},{5,7},{7,5},{8,10},{10,8},{9,1... | collective-permute-start | bytes 393224 | tf_op jit(solution)/shard_map/ppermute | solution.py:21
  16.9 4.4 %collective-permute-start.7 = (bf16[256,256]{1,0:T(8,128)(2,1)S(1)}, bf16[256,256]{1,0:T(8,128)(2,1)S(1)}, u32[]{:S(2)}, u32[]{:S(2)}) collective-permute-start(bf16[256,256]{1,0:T(8,128)(2,1)S(1)} %collective-permute-done.5.refs_0_), channel_id=1, source_target_pairs={{0,2},{2,0},{1,3},{3,1},{4,6},{6,4},{5,7},{7,5},{8,10},{10,8},{9,1... | collective-permute-start | bytes 393224 | tf_op jit(solution)/shard_map/ppermute | solution.py:21
  19.1 2.2 %collective-permute-start.8 = (bf16[256,256]{1,0:T(8,128)(2,1)S(1)}, bf16[256,256]{1,0:T(8,128)(2,1)S(1)}, u32[]{:S(2)}, u32[]{:S(2)}) collective-permute-start(bf16[256,256]{1,0:T(8,128)(2,1)S(1)} %collective-permute-done.6.refs_1_), channel_id=1, source_target_pairs={{0,2},{2,0},{1,3},{3,1},{4,6},{6,4},{5,7},{7,5},{8,10},{10,8},{9,1... | collective-permute-start | bytes 393224 | tf_op jit(solution)/shard_map/ppermute | solution.py:21
  19.2 9.7 %collective-permute-start.10 = (bf16[256,256]{1,0:T(8,128)(2,1)S(1)}, bf16[256,256]{1,0:T(8,128)(2,1)S(1)}, u32[]{:S(2)}, u32[]{:S(2)}) collective-permute-start(bf16[256,256]{1,0:T(8,128)(2,1)S(1)} %pack.4.c0_ref), channel_id=1, source_target_pairs={{0,16},{8,24},{16,0},{24,8},{1,17},{9,25},{17,1},{25,9},{2,18},{10... | collective-permute-start | bytes 393224 | tf_op jit(solution)/shard_map/ppermute | solution.py:21
  21.6 4.3 %collective-permute-start.9 = (bf16[128,256]{1,0:T(8,128)(2,1)S(1)}, bf16[128,256]{1,0:T(8,128)(2,1)S(1)}, u32[]{:S(2)}, u32[]{:S(2)}) collective-permute-start(bf16[128,256]{1,0:T(8,128)(2,1)S(1)} %get-tuple-element.31), channel_id=1, source_target_pairs={{0,1},{1,0},{2,3},{3,2},{4,5},{5,4},{6,7},{7,6},{8,9},{9,8},{10,11... | collective-permute-start | bytes 196616 | tf_op jit(solution)/shard_map/ppermute | solution.py:21
  26.0 2.9 %copy-start = (bf16[256,256]{1,0:T(8,128)(2,1)S(1)}, bf16[256,256]{1,0:T(8,128)(2,1)}, u32[]{:S(2)}) copy-start(bf16[256,256]{1,0:T(8,128)(2,1)} %w_ref.5) | copy-start | bytes 393220
  26.0 2.9 %copy-start.1 = (f32[256]{0:T(256)S(1)}, f32[256]{0:T(256)}, u32[]{:S(2)}) copy-start(f32[256]{0:T(256)} %param.9) | copy-start | bytes 3076
  26.0 5.5 %collective-permute-start.11 = (bf16[128,256]{1,0:T(8,128)(2,1)S(1)}, bf16[128,256]{1,0:T(8,128)(2,1)S(1)}, u32[]{:S(2)}, u32[]{:S(2)}) collective-permute-start(bf16[128,256]{1,0:T(8,128)(2,1)S(1)} %hidden.1.h_ref.refs_0_), channel_id=1, source_target_pairs={{0,16},{8,24},{16,0},{24,8},{1,17},{9,25},{17,1},{25,9},{2,18},{10... | collective-permute-start | bytes 196616 | tf_op jit(solution)/shard_map/ppermute | solution.py:21
  31.5 5.0 %collective-permute-start.12 = (bf16[256,256]{1,0:T(8,128)(2,1)S(1)}, bf16[256,256]{1,0:T(8,128)(2,1)S(1)}, u32[]{:S(2)}, u32[]{:S(2)}) collective-permute-start(bf16[256,256]{1,0:T(8,128)(2,1)S(1)} %pack.5.h_ref), channel_id=1, source_target_pairs={{0,8},{8,0},{16,24},{24,16},{1,9},{9,1},{17,25},{25,17},{2,10},{10... | collective-permute-start | bytes 393224 | tf_op jit(solution)/shard_map/ppermute | solution.py:21
  33.5 5.0 %collective-permute-start.13 = (bf16[256,256]{1,0:T(8,128)(2,1)S(1)}, bf16[256,256]{1,0:T(8,128)(2,1)S(1)}, u32[]{:S(2)}, u32[]{:S(2)}) collective-permute-start(bf16[256,256]{1,0:T(8,128)(2,1)S(1)} %get-tuple-element.42.refs_0_), channel_id=1, source_target_pairs={{0,4},{4,0},{1,5},{5,1},{2,6},{6,2},{3,7},{7,3},{8,12},{12,8},{9,1... | collective-permute-start | bytes 393224 | tf_op jit(solution)/shard_map/ppermute | solution.py:21
  38.6 1.7 %collective-permute-start.14 = (bf16[400,256]{1,0:T(8,128)(2,1)S(1)}, bf16[400,256]{1,0:T(8,128)(2,1)S(1)}, u32[]{:S(2)}, u32[]{:S(2)}) collective-permute-start(bf16[400,256]{1,0:T(8,128)(2,1)S(1)} %get-tuple-element.41), channel_id=1, source_target_pairs={{0,2},{2,0},{1,3},{3,1},{4,6},{6,4},{5,7},{7,5},{8,10},{10,8},{9,1... | collective-permute-start | bytes 614408 | tf_op jit(solution)/shard_map/ppermute | solution.py:21
  38.6 5.9 %collective-permute-start.18 = (bf16[256,256]{1,0:T(8,128)(2,1)S(1)}, bf16[256,256]{1,0:T(8,128)(2,1)S(1)}, u32[]{:S(2)}, u32[]{:S(2)}) collective-permute-start(bf16[256,256]{1,0:T(8,128)(2,1)S(1)} %get-tuple-element.43.refs_1_), channel_id=1, source_target_pairs={{0,4},{4,0},{1,5},{5,1},{2,6},{6,2},{3,7},{7,3},{8,12},{12,8},{9,1... | collective-permute-start | bytes 393224 | tf_op jit(solution)/shard_map/ppermute | solution.py:21
  40.1 5.0 %collective-permute-start.17 = (bf16[256,256]{1,0:T(8,128)(2,1)S(1)}, bf16[256,256]{1,0:T(8,128)(2,1)S(1)}, u32[]{:S(2)}, u32[]{:S(2)}) collective-permute-start(bf16[256,256]{1,0:T(8,128)(2,1)S(1)} %get-tuple-element.42.refs_0_), channel_id=1, source_target_pairs={{0,2},{2,0},{1,3},{3,1},{4,6},{6,4},{5,7},{7,5},{8,10},{10,8},{9,1... | collective-permute-start | bytes 393224 | tf_op jit(solution)/shard_map/ppermute | solution.py:21
  40.3 4.5 %collective-permute-start.15 = (bf16[144,256]{1,0:T(8,128)(2,1)S(1)}, bf16[144,256]{1,0:T(8,128)(2,1)S(1)}, u32[]{:S(2)}, u32[]{:S(2)}) collective-permute-start(bf16[144,256]{1,0:T(8,128)(2,1)S(1)} %sum_core.1.own_ref), channel_id=1, source_target_pairs={{0,1},{1,0},{2,3},{3,2},{4,5},{5,4},{6,7},{7,6},{8,9},{9,8},{10,11... | collective-permute-start | bytes 221192 | tf_op jit(solution)/shard_map/ppermute | solution.py:21
  41.9 3.5 %collective-permute-start.19 = (bf16[256,256]{1,0:T(8,128)(2,1)S(1)}, bf16[256,256]{1,0:T(8,128)(2,1)S(1)}, u32[]{:S(2)}, u32[]{:S(2)}) collective-permute-start(bf16[256,256]{1,0:T(8,128)(2,1)S(1)} %collective-permute-done.13.refs_0_), channel_id=1, source_target_pairs={{0,2},{2,0},{1,3},{3,1},{4,6},{6,4},{5,7},{7,5},{8,10},{10,8},{9,1... | collective-permute-start | bytes 393224 | tf_op jit(solution)/shard_map/ppermute | solution.py:21
  44.5 1.3 %collective-permute-start.20 = (bf16[256,256]{1,0:T(8,128)(2,1)S(1)}, bf16[256,256]{1,0:T(8,128)(2,1)S(1)}, u32[]{:S(2)}, u32[]{:S(2)}) collective-permute-start(bf16[256,256]{1,0:T(8,128)(2,1)S(1)} %collective-permute-done.18.refs_1_), channel_id=1, source_target_pairs={{0,2},{2,0},{1,3},{3,1},{4,6},{6,4},{5,7},{7,5},{8,10},{10,8},{9,1... | collective-permute-start | bytes 393224 | tf_op jit(solution)/shard_map/ppermute | solution.py:21
  44.9 1.3 %collective-permute-start.16 = (bf16[144,256]{1,0:T(8,128)(2,1)S(1)}, bf16[144,256]{1,0:T(8,128)(2,1)S(1)}, u32[]{:S(2)}, u32[]{:S(2)}) collective-permute-start(bf16[144,256]{1,0:T(8,128)(2,1)S(1)} %sum_row.1.own_ref), channel_id=1, source_target_pairs={{0,2},{2,0},{1,3},{3,1},{4,6},{6,4},{5,7},{7,5},{8,10},{10,8},{9,1... | collective-permute-start | bytes 221192 | tf_op jit(solution)/shard_map/ppermute | solution.py:21
  46.2 5.8 %collective-permute-start.21 = (bf16[272,256]{1,0:T(8,128)(2,1)S(1)}, bf16[272,256]{1,0:T(8,128)(2,1)S(1)}, u32[]{:S(2)}, u32[]{:S(2)}) collective-permute-start(bf16[272,256]{1,0:T(8,128)(2,1)S(1)} %halves.1.near_ref), channel_id=1, source_target_pairs={{0,4},{4,0},{1,5},{5,1},{2,6},{6,2},{3,7},{7,3},{8,12},{12,8},{9,1... | collective-permute-start | bytes 417800 | tf_op jit(solution)/shard_map/ppermute | solution.py:21
  47.7 4.3 %collective-permute-start.22 = (bf16[128,256]{1,0:T(8,128)(2,1)S(1)}, bf16[128,256]{1,0:T(8,128)(2,1)S(1)}, u32[]{:S(2)}, u32[]{:S(2)}) collective-permute-start(bf16[128,256]{1,0:T(8,128)(2,1)S(1)} %get-tuple-element.46), channel_id=1, source_target_pairs={{0,1},{1,0},{2,3},{3,2},{4,5},{5,4},{6,7},{7,6},{8,9},{9,8},{10,11... | collective-permute-start | bytes 196616 | tf_op jit(solution)/shard_map/ppermute | solution.py:21

commit v14 on v13

--- a/solution.py
+++ b/solution.py
@@ -304,10 +304,10 @@
         ],
         specs=[pl.BlockSpec(memory_space=pltpu.HBM)] * 5,
     )
-    f00 = far_chunks(after(pack(features, other), other_cot), steps)
+    f00 = far_chunks(pack(features, other), steps)
     f10 = [swap(chunk, "mid") for chunk in f00]
     cots = far_chunks(pack(cotangent, after(other_cot, f00[-1])), cot_steps)
-    f01 = [swap(chunk, "core") for chunk in f00]
+    f01 = [swap(chunk, "core") for chunk in [after(f00[0], other_cot)] + f00[1:]]
     f11 = [swap(chunk, "core") for chunk in f10]
     half = near_product(f00 + f01, "forward")
     own, *parts = rest_product(half, f10 + f11, "forward")

time: 52.9 us -> 54.8 us (1.036)
  waiting for transfers between devices: 21.4 us -> 26.6 us
  starting transfers between devices: 25 us -> 21.7 us
    ppermute x23, waiting for transfers between devices: 21.4 us -> 26.6 us  [partner(): return lax.ppermute(x, axis, [(i, i ^ mask) for i in range(n)])]
    ppermute x23, starting transfers between devices: 25 us -> 21.7 us  [partner(): return lax.ppermute(x, axis, [(i, i ^ mask) for i in range(n)])]
  transfers between devices with their start and end apart: 23 -> 23, of which waited for: 14 -> 13; matrix products, arithmetic and copies ran while one was open for 0% -> 0% of each run, Pallas kernels for 9% -> 9%
where the time goes in v14:
time: 54.8 us; the launch traced here: 54.6 us
  waiting for transfers between devices  26.6 us (49%)
  starting transfers between devices  21.7 us (40%)
  Pallas kernels  5.61 us (10%)
  between operations  0.77 us (1%)
    ppermute x23, waiting for transfers between devices, partner(): return lax.ppermute(x, axis, [(i, i ^ mask) for i in range(n)])  26.6 us
    ppermute x23, starting transfers between devices, partner(): return lax.ppermute(x, axis, [(i, i ^ mask) for i in range(n)])  21.7 us
    pallas_call x16, Pallas kernels, call(): pl.pallas_call(kernel, name=name, out_shape=outs, in_specs=specs or [VMEM...  5.61 us
  transfers between devices with their start and end apart: 23, of which 13 were waited for; matrix products, arithmetic and copies ran while one was open for 0% of the time, Pallas kernels for 9%

profile of v14, /device:TPU:0, one launch (start us, length us, event | category | flops | bytes accessed | tf_op | source)
XLA Modules:
  0.0 54.6 jit_solution(8997030872187927793)
XLA Ops:
  0.6 4.1 %collective-permute-start = (bf16[128,256]{1,0:T(8,128)(2,1)}, bf16[128,256]{1,0:T(8,128)(2,1)S(1)}, u32[]{:S(2)}, u32[]{:S(2)}) collective-permute-start(bf16[128,256]{1,0:T(8,128)(2,1)} %f_hbm.1), channel_id=1, source_target_pairs={{0,16},{8,24},{16,0},{24,8},{1,17},{9,25},{17,1},{25,9},{2,18},{10... | collective-permute-start | bytes 196616 | tf_op jit(solution)/shard_map/ppermute | solution.py:21
  4.7 1.7 %expand.1 = (bf16[256,2048]{1,0:T(8,128)(2,1)S(1)}, bf16[128,256]{1,0:T(8,128)(2,1)S(1)}, bf16[128,256]{1,0:T(8,128)(2,1)S(1)}) custom-call(s32[32]{0:T(128)} %rows_hbm.1, s32[16]{0:T(128)} %counts_hbm.1, bf16[32,128,128]{2,1,0:T(8,128)(2,1)} %tiles_hbm.1, bf16[128,256]{1,0:T(8,128)(2,1)} %f_hbm.1, bf16[128,256]{1,0:T(8,128)(2,1)} %c_hbm.1), custom_call_target="tpu_custom_call" | custom-call | bytes 2359488 | tf_op jit(solution)/shard_map/expand/pallas_call | solution.py:235
  6.4 2.2 %collective-permute-done.refs_1_ = bf16[128,256]{1,0:T(8,128)(2,1)S(1)} collective-permute-done((bf16[128,256]{1,0:T(8,128)(2,1)}, bf16[128,256]{1,0:T(8,128)(2,1)S(1)}, u32[]{:S(2)}, u32[]{:S(2)}) %collective-permute-start) | collective-permute-done | bytes 65568 | tf_op jit(solution)/shard_map/ppermute | solution.py:21
  8.6 0.7 %collective-permute-start.1 = (bf16[256,256]{1,0:T(8,128)(2,1)S(1)}, bf16[256,256]{1,0:T(8,128)(2,1)S(1)}, u32[]{:S(2)}, u32[]{:S(2)}) collective-permute-start(bf16[256,256]{1,0:T(8,128)(2,1)S(1)} %pack.3.refs_0_), channel_id=1, source_target_pairs={{0,8},{8,0},{16,24},{24,16},{1,9},{9,1},{17,25},{25,17},{2,10},{10... | collective-permute-start | bytes 393224 | tf_op jit(solution)/shard_map/ppermute | solution.py:21
  9.3 1.5 %collective-permute-start.5 = (bf16[256,256]{1,0:T(8,128)(2,1)S(1)}, bf16[256,256]{1,0:T(8,128)(2,1)S(1)}, u32[]{:S(2)}, u32[]{:S(2)}) collective-permute-start(bf16[256,256]{1,0:T(8,128)(2,1)S(1)} %pack.3.refs_0_), channel_id=1, source_target_pairs={{0,4},{4,0},{1,5},{5,1},{2,6},{6,2},{3,7},{7,3},{8,12},{12,8},{9,1... | collective-permute-start | bytes 393224 | tf_op jit(solution)/shard_map/ppermute | solution.py:21
  10.8 2.8 %collective-permute-done.1.refs_1_ = bf16[256,256]{1,0:T(8,128)(2,1)S(1)} collective-permute-done((bf16[256,256]{1,0:T(8,128)(2,1)S(1)}, bf16[256,256]{1,0:T(8,128)(2,1)S(1)}, u32[]{:S(2)}, u32[]{:S(2)}) %collective-permute-start.1) | collective-permute-done | bytes 131104 | tf_op jit(solution)/shard_map/ppermute | solution.py:21
  13.6 1.7 %collective-permute-start.6 = (bf16[256,256]{1,0:T(8,128)(2,1)S(1)}, bf16[256,256]{1,0:T(8,128)(2,1)S(1)}, u32[]{:S(2)}, u32[]{:S(2)}) collective-permute-start(bf16[256,256]{1,0:T(8,128)(2,1)S(1)} %collective-permute-done.1.refs_1_), channel_id=1, source_target_pairs={{0,4},{4,0},{1,5},{5,1},{2,6},{6,2},{3,7},{7,3},{8,12},{12,8},{9,1... | collective-permute-start | bytes 393224 | tf_op jit(solution)/shard_map/ppermute | solution.py:21
  15.8 3.8 %collective-permute-done.2.refs_1_ = bf16[128,256]{1,0:T(8,128)(2,1)S(1)} collective-permute-done((bf16[128,256]{1,0:T(8,128)(2,1)S(1)}, bf16[128,256]{1,0:T(8,128)(2,1)S(1)}, u32[]{:S(2)}, u32[]{:S(2)}) %collective-permute-start.2) | collective-permute-done | bytes 65568 | tf_op jit(solution)/shard_map/ppermute | solution.py:21
  19.6 0.5 collective-permute-start.4
  20.1 0.5 collective-permute-start.8
  20.7 2.2 %collective-permute-start.10 = (bf16[256,256]{1,0:T(8,128)(2,1)S(1)}, bf16[256,256]{1,0:T(8,128)(2,1)S(1)}, u32[]{:S(2)}, u32[]{:S(2)}) collective-permute-start(bf16[256,256]{1,0:T(8,128)(2,1)S(1)} %pack.4.c0_ref), channel_id=1, source_target_pairs={{0,16},{8,24},{16,0},{24,8},{1,17},{9,25},{17,1},{25,9},{2,18},{10... | collective-permute-start | bytes 393224 | tf_op jit(solution)/shard_map/ppermute | solution.py:21
  23.5 1.6 %collective-permute-start.9 = (bf16[128,256]{1,0:T(8,128)(2,1)S(1)}, bf16[128,256]{1,0:T(8,128)(2,1)S(1)}, u32[]{:S(2)}, u32[]{:S(2)}) collective-permute-start(bf16[128,256]{1,0:T(8,128)(2,1)S(1)} %get-tuple-element.31), channel_id=1, source_target_pairs={{0,1},{1,0},{2,3},{3,2},{4,5},{5,4},{6,7},{7,6},{8,9},{9,8},{10,11... | collective-permute-start | bytes 196616 | tf_op jit(solution)/shard_map/ppermute | solution.py:21
  25.1 2.7 %collective-permute-done.9.refs_0_ = bf16[128,256]{1,0:T(8,128)(2,1)S(1)} collective-permute-done((bf16[128,256]{1,0:T(8,128)(2,1)S(1)}, bf16[128,256]{1,0:T(8,128)(2,1)S(1)}, u32[]{:S(2)}, u32[]{:S(2)}) %collective-permute-start.9) | collective-permute-done | bytes 65568 | tf_op jit(solution)/shard_map/ppermute | solution.py:21
  27.8 0.9 %collective-permute-start.11 = (bf16[128,256]{1,0:T(8,128)(2,1)S(1)}, bf16[128,256]{1,0:T(8,128)(2,1)S(1)}, u32[]{:S(2)}, u32[]{:S(2)}) collective-permute-start(bf16[128,256]{1,0:T(8,128)(2,1)S(1)} %hidden.1.h_ref.refs_0_), channel_id=1, source_target_pairs={{0,16},{8,24},{16,0},{24,8},{1,17},{9,25},{17,1},{25,9},{2,18},{10... | collective-permute-start | bytes 196616 | tf_op jit(solution)/shard_map/ppermute | solution.py:21
  28.7 1.2 %collective-permute-done.10.c1_ref = bf16[256,256]{1,0:T(8,128)(2,1)S(1)} collective-permute-done((bf16[256,256]{1,0:T(8,128)(2,1)S(1)}, bf16[256,256]{1,0:T(8,128)(2,1)S(1)}, u32[]{:S(2)}, u32[]{:S(2)}) %collective-permute-start.10) | collective-permute-done | bytes 131104 | tf_op jit(solution)/shard_map/ppermute | solution.py:21
  29.9 0.8 %output.1 = bf16[128,256]{1,0:T(8,128)(2,1)} custom-call(bf16[256,256]{1,0:T(8,128)(2,1)S(1)} %copy-done, f32[1,256]{1,0:T(1,128)S(1)} %bitcast.2, bf16[128,256]{1,0:T(8,128)(2,1)S(1)} %hidden.1.h_ref.refs_0_), custom_call_target="tpu_custom_call" | custom-call | bytes 263168 | tf_op jit(solution)/shard_map/output/pallas_call | solution.py:235
  30.7 2.3 %collective-permute-done.11.refs_1_ = bf16[128,256]{1,0:T(8,128)(2,1)S(1)} collective-permute-done((bf16[128,256]{1,0:T(8,128)(2,1)S(1)}, bf16[128,256]{1,0:T(8,128)(2,1)S(1)}, u32[]{:S(2)}, u32[]{:S(2)}) %collective-permute-start.11) | collective-permute-done | bytes 65568 | tf_op jit(solution)/shard_map/ppermute | solution.py:21
  33.1 1.8 %collective-permute-start.12 = (bf16[256,256]{1,0:T(8,128)(2,1)S(1)}, bf16[256,256]{1,0:T(8,128)(2,1)S(1)}, u32[]{:S(2)}, u32[]{:S(2)}) collective-permute-start(bf16[256,256]{1,0:T(8,128)(2,1)S(1)} %pack.5.h_ref), channel_id=1, source_target_pairs={{0,8},{8,0},{16,24},{24,16},{1,9},{9,1},{17,25},{25,17},{2,10},{10... | collective-permute-start | bytes 393224 | tf_op jit(solution)/shard_map/ppermute | solution.py:21
  35.4 0.6 %collective-permute-start.13 = (bf16[256,256]{1,0:T(8,128)(2,1)S(1)}, bf16[256,256]{1,0:T(8,128)(2,1)S(1)}, u32[]{:S(2)}, u32[]{:S(2)}) collective-permute-start(bf16[256,256]{1,0:T(8,128)(2,1)S(1)} %get-tuple-element.42.refs_0_), channel_id=1, source_target_pairs={{0,4},{4,0},{1,5},{5,1},{2,6},{6,2},{3,7},{7,3},{8,12},{12,8},{9,1... | collective-permute-start | bytes 393224 | tf_op jit(solution)/shard_map/ppermute | solution.py:21
  36.0 2.1 %collective-permute-done.12.h_ref = bf16[256,256]{1,0:T(8,128)(2,1)S(1)} collective-permute-done((bf16[256,256]{1,0:T(8,128)(2,1)S(1)}, bf16[256,256]{1,0:T(8,128)(2,1)S(1)}, u32[]{:S(2)}, u32[]{:S(2)}) %collective-permute-start.12) | collective-permute-done | bytes 131104 | tf_op jit(solution)/shard_map/ppermute | solution.py:21
  38.1 0.5 last_chunk.1
  38.7 1.7 %collective-permute-done.13.refs_0_ = bf16[256,256]{1,0:T(8,128)(2,1)S(1)} collective-permute-done((bf16[256,256]{1,0:T(8,128)(2,1)S(1)}, bf16[256,256]{1,0:T(8,128)(2,1)S(1)}, u32[]{:S(2)}, u32[]{:S(2)}) %collective-permute-start.13) | collective-permute-done | bytes 131104 | tf_op jit(solution)/shard_map/ppermute | solution.py:21
  40.4 0.5 collective-permute-start.18
  41.2 0.7 %collective-permute-done.14.other_ref.refs_3_ = bf16[400,256]{1,0:T(8,128)(2,1)S(1)} collective-permute-done((bf16[400,256]{1,0:T(8,128)(2,1)S(1)}, bf16[400,256]{1,0:T(8,128)(2,1)S(1)}, u32[]{:S(2)}, u32[]{:S(2)}) %collective-permute-start.14) | collective-permute-done | bytes 204832 | tf_op jit(solution)/shard_map/ppermute | solution.py:21
  41.9 1.6 %collective-permute-start.15 = (bf16[144,256]{1,0:T(8,128)(2,1)S(1)}, bf16[144,256]{1,0:T(8,128)(2,1)S(1)}, u32[]{:S(2)}, u32[]{:S(2)}) collective-permute-start(bf16[144,256]{1,0:T(8,128)(2,1)S(1)} %sum_core.1.own_ref), channel_id=1, source_target_pairs={{0,1},{1,0},{2,3},{3,2},{4,5},{5,4},{6,7},{7,6},{8,9},{9,8},{10,11... | collective-permute-start | bytes 221192 | tf_op jit(solution)/shard_map/ppermute | solution.py:21
  43.5 2.8 %collective-permute-done.18.refs_1_ = bf16[256,256]{1,0:T(8,128)(2,1)S(1)} collective-permute-done((bf16[256,256]{1,0:T(8,128)(2,1)S(1)}, bf16[256,256]{1,0:T(8,128)(2,1)S(1)}, u32[]{:S(2)}, u32[]{:S(2)}) %collective-permute-start.18) | collective-permute-done | bytes 131104 | tf_op jit(solution)/shard_map/ppermute | solution.py:21
  46.4 0.6 %collective-permute-start.16 = (bf16[144,256]{1,0:T(8,128)(2,1)S(1)}, bf16[144,256]{1,0:T(8,128)(2,1)S(1)}, u32[]{:S(2)}, u32[]{:S(2)}) collective-permute-start(bf16[144,256]{1,0:T(8,128)(2,1)S(1)} %sum_row.1.own_ref), channel_id=1, source_target_pairs={{0,2},{2,0},{1,3},{3,1},{4,6},{6,4},{5,7},{7,5},{8,10},{10,8},{9,1... | collective-permute-start | bytes 221192 | tf_op jit(solution)/shard_map/ppermute | solution.py:21
  48.0 0.6 %collective-permute-start.21 = (bf16[272,256]{1,0:T(8,128)(2,1)S(1)}, bf16[272,256]{1,0:T(8,128)(2,1)S(1)}, u32[]{:S(2)}, u32[]{:S(2)}) collective-permute-start(bf16[272,256]{1,0:T(8,128)(2,1)S(1)} %halves.1.near_ref), channel_id=1, source_target_pairs={{0,4},{4,0},{1,5},{5,1},{2,6},{6,2},{3,7},{7,3},{8,12},{12,8},{9,1... | collective-permute-start | bytes 417800 | tf_op jit(solution)/shard_map/ppermute | solution.py:21
  48.7 1.5 %collective-permute-start.22 = (bf16[128,256]{1,0:T(8,128)(2,1)S(1)}, bf16[128,256]{1,0:T(8,128)(2,1)S(1)}, u32[]{:S(2)}, u32[]{:S(2)}) collective-permute-start(bf16[128,256]{1,0:T(8,128)(2,1)S(1)} %get-tuple-element.46), channel_id=1, source_target_pairs={{0,1},{1,0},{2,3},{3,2},{4,5},{5,4},{6,7},{7,6},{8,9},{9,8},{10,11... | collective-permute-start | bytes 196616 | tf_op jit(solution)/shard_map/ppermute | solution.py:21
  50.2 2.7 %collective-permute-done.22.refs_1_ = bf16[128,256]{1,0:T(8,128)(2,1)S(1)} collective-permute-done((bf16[128,256]{1,0:T(8,128)(2,1)S(1)}, bf16[128,256]{1,0:T(8,128)(2,1)S(1)}, u32[]{:S(2)}, u32[]{:S(2)}) %collective-permute-start.22) | collective-permute-done | bytes 65568 | tf_op jit(solution)/shard_map/ppermute | solution.py:21
  52.9 0.9 %collective-permute-done.21.far_ref = bf16[272,256]{1,0:T(8,128)(2,1)S(1)} collective-permute-done((bf16[272,256]{1,0:T(8,128)(2,1)S(1)}, bf16[272,256]{1,0:T(8,128)(2,1)S(1)}, u32[]{:S(2)}, u32[]{:S(2)}) %collective-permute-start.21) | collective-permute-done | bytes 139296 | tf_op jit(solution)/shard_map/ppermute | solution.py:21
  53.9 0.8 %last.1 = (f32[256,256]{1,0:T(8,128)}, f32[1,256]{1,0:T(1,128)}, bf16[128,256]{1,0:T(8,128)(2,1)}) custom-call(bf16[272,256]{1,0:T(8,128)(2,1)S(1)} %halves.1.near_ref, bf16[272,256]{1,0:T(8,128)(2,1)S(1)} %collective-permute-done.21.far_ref, f32[128,256]{1,0:T(8,128)S(1)} %get-tuple-element.44.refs_0_, bf16[128,256]{1,0:T(8,128)(2,1)S(1)} %collective-permute-done.22.refs_1_), custom_call_target="tpu_custom_call" | custom-call | bytes 803840 | tf_op jit(solution)/shard_map/last/pallas_call | solution.py:235
  (36 shorter events, 3.0 us)
Async XLA Ops:
  0.6 8.0 %collective-permute-start = (bf16[128,256]{1,0:T(8,128)(2,1)}, bf16[128,256]{1,0:T(8,128)(2,1)S(1)}, u32[]{:S(2)}, u32[]{:S(2)}) collective-permute-start(bf16[128,256]{1,0:T(8,128)(2,1)} %f_hbm.1), channel_id=1, source_target_pairs={{0,16},{8,24},{16,0},{24,8},{1,17},{9,25},{17,1},{25,9},{2,18},{10... | collective-permute-start | bytes 196616 | tf_op jit(solution)/shard_map/ppermute | solution.py:21
  8.6 6.8 %copy-start.2 = (bf16[128,256]{1,0:T(8,128)(2,1)S(1)}, bf16[128,256]{1,0:T(8,128)(2,1)}, u32[]{:S(2)}) copy-start(bf16[128,256]{1,0:T(8,128)(2,1)} %c_hbm.1) | copy-start | bytes 196612
  8.6 5.0 %collective-permute-start.1 = (bf16[256,256]{1,0:T(8,128)(2,1)S(1)}, bf16[256,256]{1,0:T(8,128)(2,1)S(1)}, u32[]{:S(2)}, u32[]{:S(2)}) collective-permute-start(bf16[256,256]{1,0:T(8,128)(2,1)S(1)} %pack.3.refs_0_), channel_id=1, source_target_pairs={{0,8},{8,0},{16,24},{24,16},{1,9},{9,1},{17,25},{25,17},{2,10},{10... | collective-permute-start | bytes 393224 | tf_op jit(solution)/shard_map/ppermute | solution.py:21
  9.3 10.8 %collective-permute-start.5 = (bf16[256,256]{1,0:T(8,128)(2,1)S(1)}, bf16[256,256]{1,0:T(8,128)(2,1)S(1)}, u32[]{:S(2)}, u32[]{:S(2)}) collective-permute-start(bf16[256,256]{1,0:T(8,128)(2,1)S(1)} %pack.3.refs_0_), channel_id=1, source_target_pairs={{0,4},{4,0},{1,5},{5,1},{2,6},{6,2},{3,7},{7,3},{8,12},{12,8},{9,1... | collective-permute-start | bytes 393224 | tf_op jit(solution)/shard_map/ppermute | solution.py:21
  13.6 6.5 %collective-permute-start.6 = (bf16[256,256]{1,0:T(8,128)(2,1)S(1)}, bf16[256,256]{1,0:T(8,128)(2,1)S(1)}, u32[]{:S(2)}, u32[]{:S(2)}) collective-permute-start(bf16[256,256]{1,0:T(8,128)(2,1)S(1)} %collective-permute-done.1.refs_1_), channel_id=1, source_target_pairs={{0,4},{4,0},{1,5},{5,1},{2,6},{6,2},{3,7},{7,3},{8,12},{12,8},{9,1... | collective-permute-start | bytes 393224 | tf_op jit(solution)/shard_map/ppermute | solution.py:21
  15.3 4.3 %collective-permute-start.2 = (bf16[128,256]{1,0:T(8,128)(2,1)S(1)}, bf16[128,256]{1,0:T(8,128)(2,1)S(1)}, u32[]{:S(2)}, u32[]{:S(2)}) collective-permute-start(bf16[128,256]{1,0:T(8,128)(2,1)S(1)} %copy-done.2), channel_id=1, source_target_pairs={{0,8},{8,0},{16,24},{24,16},{1,9},{9,1},{17,25},{25,17},{2,10},{10... | collective-permute-start | bytes 196616 | tf_op jit(solution)/shard_map/ppermute | solution.py:21
  19.6 3.2 %collective-permute-start.3 = (bf16[256,256]{1,0:T(8,128)(2,1)S(1)}, bf16[256,256]{1,0:T(8,128)(2,1)S(1)}, u32[]{:S(2)}, u32[]{:S(2)}) collective-permute-start(bf16[256,256]{1,0:T(8,128)(2,1)S(1)} %pack.3.refs_0_), channel_id=1, source_target_pairs={{0,2},{2,0},{1,3},{3,1},{4,6},{6,4},{5,7},{7,5},{8,10},{10,8},{9,1... | collective-permute-start | bytes 393224 | tf_op jit(solution)/shard_map/ppermute | solution.py:21
  19.6 3.2 %collective-permute-start.4 = (bf16[256,256]{1,0:T(8,128)(2,1)S(1)}, bf16[256,256]{1,0:T(8,128)(2,1)S(1)}, u32[]{:S(2)}, u32[]{:S(2)}) collective-permute-start(bf16[256,256]{1,0:T(8,128)(2,1)S(1)} %collective-permute-done.1.refs_1_), channel_id=1, source_target_pairs={{0,2},{2,0},{1,3},{3,1},{4,6},{6,4},{5,7},{7,5},{8,10},{10,8},{9,1... | collective-permute-start | bytes 393224 | tf_op jit(solution)/shard_map/ppermute | solution.py:21
  20.1 3.0 %collective-permute-start.7 = (bf16[256,256]{1,0:T(8,128)(2,1)S(1)}, bf16[256,256]{1,0:T(8,128)(2,1)S(1)}, u32[]{:S(2)}, u32[]{:S(2)}) collective-permute-start(bf16[256,256]{1,0:T(8,128)(2,1)S(1)} %collective-permute-done.5.refs_0_), channel_id=1, source_target_pairs={{0,2},{2,0},{1,3},{3,1},{4,6},{6,4},{5,7},{7,5},{8,10},{10,8},{9,1... | collective-permute-start | bytes 393224 | tf_op jit(solution)/shard_map/ppermute | solution.py:21
  20.1 3.0 %collective-permute-start.8 = (bf16[256,256]{1,0:T(8,128)(2,1)S(1)}, bf16[256,256]{1,0:T(8,128)(2,1)S(1)}, u32[]{:S(2)}, u32[]{:S(2)}) collective-permute-start(bf16[256,256]{1,0:T(8,128)(2,1)S(1)} %collective-permute-done.6.refs_1_), channel_id=1, source_target_pairs={{0,2},{2,0},{1,3},{3,1},{4,6},{6,4},{5,7},{7,5},{8,10},{10,8},{9,1... | collective-permute-start | bytes 393224 | tf_op jit(solution)/shard_map/ppermute | solution.py:21
  20.7 9.2 %collective-permute-start.10 = (bf16[256,256]{1,0:T(8,128)(2,1)S(1)}, bf16[256,256]{1,0:T(8,128)(2,1)S(1)}, u32[]{:S(2)}, u32[]{:S(2)}) collective-permute-start(bf16[256,256]{1,0:T(8,128)(2,1)S(1)} %pack.4.c0_ref), channel_id=1, source_target_pairs={{0,16},{8,24},{16,0},{24,8},{1,17},{9,25},{17,1},{25,9},{2,18},{10... | collective-permute-start | bytes 393224 | tf_op jit(solution)/shard_map/ppermute | solution.py:21
  23.5 4.3 %collective-permute-start.9 = (bf16[128,256]{1,0:T(8,128)(2,1)S(1)}, bf16[128,256]{1,0:T(8,128)(2,1)S(1)}, u32[]{:S(2)}, u32[]{:S(2)}) collective-permute-start(bf16[128,256]{1,0:T(8,128)(2,1)S(1)} %get-tuple-element.31), channel_id=1, source_target_pairs={{0,1},{1,0},{2,3},{3,2},{4,5},{5,4},{6,7},{7,6},{8,9},{9,8},{10,11... | collective-permute-start | bytes 196616 | tf_op jit(solution)/shard_map/ppermute | solution.py:21
  27.8 2.1 %copy-start = (bf16[256,256]{1,0:T(8,128)(2,1)S(1)}, bf16[256,256]{1,0:T(8,128)(2,1)}, u32[]{:S(2)}) copy-start(bf16[256,256]{1,0:T(8,128)(2,1)} %w_ref.5) | copy-start | bytes 393220
  27.8 2.1 %copy-start.1 = (f32[256]{0:T(256)S(1)}, f32[256]{0:T(256)}, u32[]{:S(2)}) copy-start(f32[256]{0:T(256)} %param.9) | copy-start | bytes 3076
  27.8 5.2 %collective-permute-start.11 = (bf16[128,256]{1,0:T(8,128)(2,1)S(1)}, bf16[128,256]{1,0:T(8,128)(2,1)S(1)}, u32[]{:S(2)}, u32[]{:S(2)}) collective-permute-start(bf16[128,256]{1,0:T(8,128)(2,1)S(1)} %hidden.1.h_ref.refs_0_), channel_id=1, source_target_pairs={{0,16},{8,24},{16,0},{24,8},{1,17},{9,25},{17,1},{25,9},{2,18},{10... | collective-permute-start | bytes 196616 | tf_op jit(solution)/shard_map/ppermute | solution.py:21
  33.1 5.0 %collective-permute-start.12 = (bf16[256,256]{1,0:T(8,128)(2,1)S(1)}, bf16[256,256]{1,0:T(8,128)(2,1)S(1)}, u32[]{:S(2)}, u32[]{:S(2)}) collective-permute-start(bf16[256,256]{1,0:T(8,128)(2,1)S(1)} %pack.5.h_ref), channel_id=1, source_target_pairs={{0,8},{8,0},{16,24},{24,16},{1,9},{9,1},{17,25},{25,17},{2,10},{10... | collective-permute-start | bytes 393224 | tf_op jit(solution)/shard_map/ppermute | solution.py:21
  35.4 5.0 %collective-permute-start.13 = (bf16[256,256]{1,0:T(8,128)(2,1)S(1)}, bf16[256,256]{1,0:T(8,128)(2,1)S(1)}, u32[]{:S(2)}, u32[]{:S(2)}) collective-permute-start(bf16[256,256]{1,0:T(8,128)(2,1)S(1)} %get-tuple-element.42.refs_0_), channel_id=1, source_target_pairs={{0,4},{4,0},{1,5},{5,1},{2,6},{6,2},{3,7},{7,3},{8,12},{12,8},{9,1... | collective-permute-start | bytes 393224 | tf_op jit(solution)/shard_map/ppermute | solution.py:21
  40.4 1.5 %collective-permute-start.14 = (bf16[400,256]{1,0:T(8,128)(2,1)S(1)}, bf16[400,256]{1,0:T(8,128)(2,1)S(1)}, u32[]{:S(2)}, u32[]{:S(2)}) collective-permute-start(bf16[400,256]{1,0:T(8,128)(2,1)S(1)} %get-tuple-element.41), channel_id=1, source_target_pairs={{0,2},{2,0},{1,3},{3,1},{4,6},{6,4},{5,7},{7,5},{8,10},{10,8},{9,1... | collective-permute-start | bytes 614408 | tf_op jit(solution)/shard_map/ppermute | solution.py:21
  40.4 5.9 %collective-permute-start.18 = (bf16[256,256]{1,0:T(8,128)(2,1)S(1)}, bf16[256,256]{1,0:T(8,128)(2,1)S(1)}, u32[]{:S(2)}, u32[]{:S(2)}) collective-permute-start(bf16[256,256]{1,0:T(8,128)(2,1)S(1)} %get-tuple-element.43.refs_1_), channel_id=1, source_target_pairs={{0,4},{4,0},{1,5},{5,1},{2,6},{6,2},{3,7},{7,3},{8,12},{12,8},{9,1... | collective-permute-start | bytes 393224 | tf_op jit(solution)/shard_map/ppermute | solution.py:21
  40.9 6.0 %collective-permute-start.17 = (bf16[256,256]{1,0:T(8,128)(2,1)S(1)}, bf16[256,256]{1,0:T(8,128)(2,1)S(1)}, u32[]{:S(2)}, u32[]{:S(2)}) collective-permute-start(bf16[256,256]{1,0:T(8,128)(2,1)S(1)} %get-tuple-element.42.refs_0_), channel_id=1, source_target_pairs={{0,2},{2,0},{1,3},{3,1},{4,6},{6,4},{5,7},{7,5},{8,10},{10,8},{9,1... | collective-permute-start | bytes 393224 | tf_op jit(solution)/shard_map/ppermute | solution.py:21
  41.9 4.4 %collective-permute-start.15 = (bf16[144,256]{1,0:T(8,128)(2,1)S(1)}, bf16[144,256]{1,0:T(8,128)(2,1)S(1)}, u32[]{:S(2)}, u32[]{:S(2)}) collective-permute-start(bf16[144,256]{1,0:T(8,128)(2,1)S(1)} %sum_core.1.own_ref), channel_id=1, source_target_pairs={{0,1},{1,0},{2,3},{3,2},{4,5},{5,4},{6,7},{7,6},{8,9},{9,8},{10,11... | collective-permute-start | bytes 221192 | tf_op jit(solution)/shard_map/ppermute | solution.py:21
  43.5 3.8 %collective-permute-start.19 = (bf16[256,256]{1,0:T(8,128)(2,1)S(1)}, bf16[256,256]{1,0:T(8,128)(2,1)S(1)}, u32[]{:S(2)}, u32[]{:S(2)}) collective-permute-start(bf16[256,256]{1,0:T(8,128)(2,1)S(1)} %collective-permute-done.13.refs_0_), channel_id=1, source_target_pairs={{0,2},{2,0},{1,3},{3,1},{4,6},{6,4},{5,7},{7,5},{8,10},{10,8},{9,1... | collective-permute-start | bytes 393224 | tf_op jit(solution)/shard_map/ppermute | solution.py:21
  46.3 1.3 %collective-permute-start.20 = (bf16[256,256]{1,0:T(8,128)(2,1)S(1)}, bf16[256,256]{1,0:T(8,128)(2,1)S(1)}, u32[]{:S(2)}, u32[]{:S(2)}) collective-permute-start(bf16[256,256]{1,0:T(8,128)(2,1)S(1)} %collective-permute-done.18.refs_1_), channel_id=1, source_target_pairs={{0,2},{2,0},{1,3},{3,1},{4,6},{6,4},{5,7},{7,5},{8,10},{10,8},{9,1... | collective-permute-start | bytes 393224 | tf_op jit(solution)/shard_map/ppermute | solution.py:21
  46.4 1.6 %collective-permute-start.16 = (bf16[144,256]{1,0:T(8,128)(2,1)S(1)}, bf16[144,256]{1,0:T(8,128)(2,1)S(1)}, u32[]{:S(2)}, u32[]{:S(2)}) collective-permute-start(bf16[144,256]{1,0:T(8,128)(2,1)S(1)} %sum_row.1.own_ref), channel_id=1, source_target_pairs={{0,2},{2,0},{1,3},{3,1},{4,6},{6,4},{5,7},{7,5},{8,10},{10,8},{9,1... | collective-permute-start | bytes 221192 | tf_op jit(solution)/shard_map/ppermute | solution.py:21
  48.0 5.8 %collective-permute-start.21 = (bf16[272,256]{1,0:T(8,128)(2,1)S(1)}, bf16[272,256]{1,0:T(8,128)(2,1)S(1)}, u32[]{:S(2)}, u32[]{:S(2)}) collective-permute-start(bf16[272,256]{1,0:T(8,128)(2,1)S(1)} %halves.1.near_ref), channel_id=1, source_target_pairs={{0,4},{4,0},{1,5},{5,1},{2,6},{6,2},{3,7},{7,3},{8,12},{12,8},{9,1... | collective-permute-start | bytes 417800 | tf_op jit(solution)/shard_map/ppermute | solution.py:21
  48.7 4.3 %collective-permute-start.22 = (bf16[128,256]{1,0:T(8,128)(2,1)S(1)}, bf16[128,256]{1,0:T(8,128)(2,1)S(1)}, u32[]{:S(2)}, u32[]{:S(2)}) collective-permute-start(bf16[128,256]{1,0:T(8,128)(2,1)S(1)} %get-tuple-element.46), channel_id=1, source_target_pairs={{0,1},{1,0},{2,3},{3,2},{4,5},{5,4},{6,7},{7,6},{8,9},{9,8},{10,11... | collective-permute-start | bytes 196616 | tf_op jit(solution)/shard_map/ppermute | solution.py:21

commit v15 on v12

--- a/solution.py
+++ b/solution.py
@@ -377,7 +377,7 @@
         [shape(width + PAD, width)],
         [message, swap(message, "core")],
     )
-    message = after(message, own)
+    message = after(message, half)
     messages = [message, swap(message, "mid")]
     weight_grad, bias_grad, grad_features = call(
         functools.partial(last_kernel, 1.0 / nodes**0.5),

time: 53 us -> 53 us (level)
  transfers between devices with their start and end apart: 23 -> 23, of which waited for: 13 -> 11; matrix products, arithmetic and copies ran while one was open for 0% -> 0% of each run, Pallas kernels for 9% -> 9%
where the time goes in v15:
time: 53 us; the launch traced here: 52.8 us
  starting transfers between devices  27.4 us (52%)
  waiting for transfers between devices  19.1 us (36%)
  Pallas kernels  5.61 us (11%)
  between operations  0.77 us (1%)
    ppermute x23, starting transfers between devices, partner(): return lax.ppermute(x, axis, [(i, i ^ mask) for i in range(n)])  27.4 us
    ppermute x23, waiting for transfers between devices, partner(): return lax.ppermute(x, axis, [(i, i ^ mask) for i in range(n)])  19.1 us
    pallas_call x16, Pallas kernels, call(): pl.pallas_call(kernel, name=name, out_shape=outs, in_specs=specs or [VMEM...  5.61 us
  transfers between devices with their start and end apart: 23, of which 11 were waited for; matrix products, arithmetic and copies ran while one was open for 0% of the time, Pallas kernels for 9%

profile of v15, /device:TPU:0, one launch (start us, length us, event | category | flops | bytes accessed | tf_op | source)
XLA Modules:
  0.0 52.8 jit_solution(1018340735539459024)
XLA Ops:
  0.6 4.1 %collective-permute-start = (bf16[128,256]{1,0:T(8,128)(2,1)}, bf16[128,256]{1,0:T(8,128)(2,1)S(1)}, u32[]{:S(2)}, u32[]{:S(2)}) collective-permute-start(bf16[128,256]{1,0:T(8,128)(2,1)} %f_hbm.1), channel_id=1, source_target_pairs={{0,16},{8,24},{16,0},{24,8},{1,17},{9,25},{17,1},{25,9},{2,18},{10... | collective-permute-start | bytes 196616 | tf_op jit(solution)/shard_map/ppermute | solution.py:21
  4.7 1.6 %collective-permute-start.1 = (bf16[128,256]{1,0:T(8,128)(2,1)}, bf16[128,256]{1,0:T(8,128)(2,1)S(1)}, u32[]{:S(2)}, u32[]{:S(2)}) collective-permute-start(bf16[128,256]{1,0:T(8,128)(2,1)} %c_hbm.1), channel_id=1, source_target_pairs={{0,8},{8,0},{16,24},{24,16},{1,9},{9,1},{17,25},{25,17},{2,10},{10... | collective-permute-start | bytes 196616 | tf_op jit(solution)/shard_map/ppermute | solution.py:21
  6.3 1.7 %expand.1 = (bf16[256,2048]{1,0:T(8,128)(2,1)S(1)}, bf16[128,256]{1,0:T(8,128)(2,1)S(1)}, bf16[128,256]{1,0:T(8,128)(2,1)S(1)}) custom-call(s32[32]{0:T(128)} %rows_hbm.1, s32[16]{0:T(128)} %counts_hbm.1, bf16[32,128,128]{2,1,0:T(8,128)(2,1)} %tiles_hbm.1, bf16[128,256]{1,0:T(8,128)(2,1)} %f_hbm.1, bf16[128,256]{1,0:T(8,128)(2,1)} %c_hbm.1), custom_call_target="tpu_custom_call" | custom-call | bytes 2359488 | tf_op jit(solution)/shard_map/expand/pallas_call | solution.py:235
  8.0 1.2 %collective-permute-done.1.refs_1_ = bf16[128,256]{1,0:T(8,128)(2,1)S(1)} collective-permute-done((bf16[128,256]{1,0:T(8,128)(2,1)}, bf16[128,256]{1,0:T(8,128)(2,1)S(1)}, u32[]{:S(2)}, u32[]{:S(2)}) %collective-permute-start.1) | collective-permute-done | bytes 65568 | tf_op jit(solution)/shard_map/ppermute | solution.py:21
  9.2 1.6 %collective-permute-start.2 = (bf16[256,256]{1,0:T(8,128)(2,1)S(1)}, bf16[256,256]{1,0:T(8,128)(2,1)S(1)}, u32[]{:S(2)}, u32[]{:S(2)}) collective-permute-start(bf16[256,256]{1,0:T(8,128)(2,1)S(1)} %pack.3.refs_0_), channel_id=1, source_target_pairs={{0,8},{8,0},{16,24},{24,16},{1,9},{9,1},{17,25},{25,17},{2,10},{10... | collective-permute-start | bytes 393224 | tf_op jit(solution)/shard_map/ppermute | solution.py:21
  10.8 1.5 %collective-permute-start.5 = (bf16[256,256]{1,0:T(8,128)(2,1)S(1)}, bf16[256,256]{1,0:T(8,128)(2,1)S(1)}, u32[]{:S(2)}, u32[]{:S(2)}) collective-permute-start(bf16[256,256]{1,0:T(8,128)(2,1)S(1)} %pack.3.refs_0_), channel_id=1, source_target_pairs={{0,4},{4,0},{1,5},{5,1},{2,6},{6,2},{3,7},{7,3},{8,12},{12,8},{9,1... | collective-permute-start | bytes 393224 | tf_op jit(solution)/shard_map/ppermute | solution.py:21
  12.3 1.9 %collective-permute-start.8 = (bf16[256,256]{1,0:T(8,128)(2,1)S(1)}, bf16[256,256]{1,0:T(8,128)(2,1)S(1)}, u32[]{:S(2)}, u32[]{:S(2)}) collective-permute-start(bf16[256,256]{1,0:T(8,128)(2,1)S(1)} %pack.4.c0_ref), channel_id=1, source_target_pairs={{0,16},{8,24},{16,0},{24,8},{1,17},{9,25},{17,1},{25,9},{2,18},{10... | collective-permute-start | bytes 393224 | tf_op jit(solution)/shard_map/ppermute | solution.py:21
  14.2 2.9 %collective-permute-start.6 = (bf16[256,256]{1,0:T(8,128)(2,1)S(1)}, bf16[256,256]{1,0:T(8,128)(2,1)S(1)}, u32[]{:S(2)}, u32[]{:S(2)}) collective-permute-start(bf16[256,256]{1,0:T(8,128)(2,1)S(1)} %collective-permute-done.2.refs_1_), channel_id=1, source_target_pairs={{0,4},{4,0},{1,5},{5,1},{2,6},{6,2},{3,7},{7,3},{8,12},{12,8},{9,1... | collective-permute-start | bytes 393224 | tf_op jit(solution)/shard_map/ppermute | solution.py:21
  17.1 0.5 collective-permute-start.4
  17.6 2.3 %collective-permute-done.8.c1_ref = bf16[256,256]{1,0:T(8,128)(2,1)S(1)} collective-permute-done((bf16[256,256]{1,0:T(8,128)(2,1)S(1)}, bf16[256,256]{1,0:T(8,128)(2,1)S(1)}, u32[]{:S(2)}, u32[]{:S(2)}) %collective-permute-start.8) | collective-permute-done | bytes 131104 | tf_op jit(solution)/shard_map/ppermute | solution.py:21
  20.4 1.0 %collective-permute-done.9.refs_3_ = bf16[256,256]{1,0:T(8,128)(2,1)S(1)} collective-permute-done((bf16[256,256]{1,0:T(8,128)(2,1)S(1)}, bf16[256,256]{1,0:T(8,128)(2,1)S(1)}, u32[]{:S(2)}, u32[]{:S(2)}) %collective-permute-start.9) | collective-permute-done | bytes 131104 | tf_op jit(solution)/shard_map/ppermute | solution.py:21
  21.7 1.6 %collective-permute-start.10 = (bf16[128,256]{1,0:T(8,128)(2,1)S(1)}, bf16[128,256]{1,0:T(8,128)(2,1)S(1)}, u32[]{:S(2)}, u32[]{:S(2)}) collective-permute-start(bf16[128,256]{1,0:T(8,128)(2,1)S(1)} %get-tuple-element.32), channel_id=1, source_target_pairs={{0,1},{1,0},{2,3},{3,2},{4,5},{5,4},{6,7},{7,6},{8,9},{9,8},{10,11... | collective-permute-start | bytes 196616 | tf_op jit(solution)/shard_map/ppermute | solution.py:21
  23.3 2.7 %collective-permute-done.10.refs_0_ = bf16[128,256]{1,0:T(8,128)(2,1)S(1)} collective-permute-done((bf16[128,256]{1,0:T(8,128)(2,1)S(1)}, bf16[128,256]{1,0:T(8,128)(2,1)S(1)}, u32[]{:S(2)}, u32[]{:S(2)}) %collective-permute-start.10) | collective-permute-done | bytes 65568 | tf_op jit(solution)/shard_map/ppermute | solution.py:21
  26.0 1.9 %collective-permute-start.11 = (bf16[128,256]{1,0:T(8,128)(2,1)S(1)}, bf16[128,256]{1,0:T(8,128)(2,1)S(1)}, u32[]{:S(2)}, u32[]{:S(2)}) collective-permute-start(bf16[128,256]{1,0:T(8,128)(2,1)S(1)} %hidden.1.h_ref.refs_0_), channel_id=1, source_target_pairs={{0,16},{8,24},{16,0},{24,8},{1,17},{9,25},{17,1},{25,9},{2,18},{10... | collective-permute-start | bytes 196616 | tf_op jit(solution)/shard_map/ppermute | solution.py:21
  28.0 0.8 %output.1 = bf16[128,256]{1,0:T(8,128)(2,1)} custom-call(bf16[256,256]{1,0:T(8,128)(2,1)S(1)} %copy-done, f32[1,256]{1,0:T(1,128)S(1)} %bitcast.2, bf16[128,256]{1,0:T(8,128)(2,1)S(1)} %hidden.1.h_ref.refs_0_), custom_call_target="tpu_custom_call" | custom-call | bytes 263168 | tf_op jit(solution)/shard_map/output/pallas_call | solution.py:235
  28.8 3.3 %collective-permute-done.11.refs_1_ = bf16[128,256]{1,0:T(8,128)(2,1)S(1)} collective-permute-done((bf16[128,256]{1,0:T(8,128)(2,1)S(1)}, bf16[128,256]{1,0:T(8,128)(2,1)S(1)}, u32[]{:S(2)}, u32[]{:S(2)}) %collective-permute-start.11) | collective-permute-done | bytes 65568 | tf_op jit(solution)/shard_map/ppermute | solution.py:21
  32.1 0.4 collective-permute-start.12
  32.5 0.5 chunk.1
  33.0 2.1 %collective-permute-start.13 = (bf16[256,256]{1,0:T(8,128)(2,1)S(1)}, bf16[256,256]{1,0:T(8,128)(2,1)S(1)}, u32[]{:S(2)}, u32[]{:S(2)}) collective-permute-start(bf16[256,256]{1,0:T(8,128)(2,1)S(1)} %get-tuple-element.40.refs_0_), channel_id=1, source_target_pairs={{0,4},{4,0},{1,5},{5,1},{2,6},{6,2},{3,7},{7,3},{8,12},{12,8},{9,1... | collective-permute-start | bytes 393224 | tf_op jit(solution)/shard_map/ppermute | solution.py:21
  35.1 2.0 %collective-permute-done.12.h_ref = bf16[256,256]{1,0:T(8,128)(2,1)S(1)} collective-permute-done((bf16[256,256]{1,0:T(8,128)(2,1)S(1)}, bf16[256,256]{1,0:T(8,128)(2,1)S(1)}, u32[]{:S(2)}, u32[]{:S(2)}) %collective-permute-start.12) | collective-permute-done | bytes 131104 | tf_op jit(solution)/shard_map/ppermute | solution.py:21
  37.1 0.5 %last_chunk.1 = (bf16[256,256]{1,0:T(8,128)(2,1)S(1)}, bf16[400,256]{1,0:T(8,128)(2,1)S(1)}, bf16[144,256]{1,0:T(8,128)(2,1)S(1)}) custom-call(bf16[256,256]{1,0:T(8,128)(2,1)S(1)} %copy-done, f32[1,256]{1,0:T(1,128)S(1)} %bitcast.4, bf16[256,256]{1,0:T(8,128)(2,1)S(1)} %collective-permute-done.12.h_ref, bf16[256,256]{1,0:T(8,128)(2,1)S(1)} %pack.4.c0_ref, ...), custom_call_target="tpu_custom_call" | custom-call | flops 100663296 | bytes 1205248 | tf_op jit(solution)/shard_map/last_chunk/pallas_call | solution.py:235
  37.7 0.4 collective-permute-done.13.refs_0_
  38.1 2.0 %collective-permute-start.19 = (bf16[256,256]{1,0:T(8,128)(2,1)S(1)}, bf16[256,256]{1,0:T(8,128)(2,1)S(1)}, u32[]{:S(2)}, u32[]{:S(2)}) collective-permute-start(bf16[256,256]{1,0:T(8,128)(2,1)S(1)} %get-tuple-element.41.refs_1_), channel_id=1, source_target_pairs={{0,4},{4,0},{1,5},{5,1},{2,6},{6,2},{3,7},{7,3},{8,12},{12,8},{9,1... | collective-permute-start | bytes 393224 | tf_op jit(solution)/shard_map/ppermute | solution.py:21
  40.1 1.6 %collective-permute-start.15 = (bf16[144,256]{1,0:T(8,128)(2,1)S(1)}, bf16[144,256]{1,0:T(8,128)(2,1)S(1)}, u32[]{:S(2)}, u32[]{:S(2)}) collective-permute-start(bf16[144,256]{1,0:T(8,128)(2,1)S(1)} %sum_core.1.own_ref), channel_id=1, source_target_pairs={{0,1},{1,0},{2,3},{3,2},{4,5},{5,4},{6,7},{7,6},{8,9},{9,8},{10,11... | collective-permute-start | bytes 221192 | tf_op jit(solution)/shard_map/ppermute | solution.py:21
  41.7 2.9 %collective-permute-done.15.other_ref = bf16[144,256]{1,0:T(8,128)(2,1)S(1)} collective-permute-done((bf16[144,256]{1,0:T(8,128)(2,1)S(1)}, bf16[144,256]{1,0:T(8,128)(2,1)S(1)}, u32[]{:S(2)}, u32[]{:S(2)}) %collective-permute-start.15) | collective-permute-done | bytes 73760 | tf_op jit(solution)/shard_map/ppermute | solution.py:21
  44.7 0.5 collective-permute-start.20
  45.6 0.4 collective-permute-done.16.other_ref
  46.0 1.5 %collective-permute-start.18 = (bf16[272,256]{1,0:T(8,128)(2,1)S(1)}, bf16[272,256]{1,0:T(8,128)(2,1)S(1)}, u32[]{:S(2)}, u32[]{:S(2)}) collective-permute-start(bf16[272,256]{1,0:T(8,128)(2,1)S(1)} %halves.1.near_ref), channel_id=1, source_target_pairs={{0,4},{4,0},{1,5},{5,1},{2,6},{6,2},{3,7},{7,3},{8,12},{12,8},{9,1... | collective-permute-start | bytes 417800 | tf_op jit(solution)/shard_map/ppermute | solution.py:21
  47.4 0.3 backward_rest.1
  47.7 1.6 %collective-permute-start.22 = (bf16[128,256]{1,0:T(8,128)(2,1)S(1)}, bf16[128,256]{1,0:T(8,128)(2,1)S(1)}, u32[]{:S(2)}, u32[]{:S(2)}) collective-permute-start(bf16[128,256]{1,0:T(8,128)(2,1)S(1)} %get-tuple-element.44), channel_id=1, source_target_pairs={{0,1},{1,0},{2,3},{3,2},{4,5},{5,4},{6,7},{7,6},{8,9},{9,8},{10,11... | collective-permute-start | bytes 196616 | tf_op jit(solution)/shard_map/ppermute | solution.py:21
  49.3 2.8 %collective-permute-done.22.refs_1_ = bf16[128,256]{1,0:T(8,128)(2,1)S(1)} collective-permute-done((bf16[128,256]{1,0:T(8,128)(2,1)S(1)}, bf16[128,256]{1,0:T(8,128)(2,1)S(1)}, u32[]{:S(2)}, u32[]{:S(2)}) %collective-permute-start.22) | collective-permute-done | bytes 65568 | tf_op jit(solution)/shard_map/ppermute | solution.py:21
  52.1 0.8 %last.1 = (f32[256,256]{1,0:T(8,128)}, f32[1,256]{1,0:T(1,128)}, bf16[128,256]{1,0:T(8,128)(2,1)}) custom-call(bf16[272,256]{1,0:T(8,128)(2,1)S(1)} %halves.1.near_ref, bf16[272,256]{1,0:T(8,128)(2,1)S(1)} %collective-permute-done.18.far_ref, f32[128,256]{1,0:T(8,128)S(1)} %get-tuple-element.43.refs_0_, bf16[128,256]{1,0:T(8,128)(2,1)S(1)} %collective-permute-done.22.refs_1_), custom_call_target="tpu_custom_call" | custom-call | bytes 803840 | tf_op jit(solution)/shard_map/last/pallas_call | solution.py:235
  (34 shorter events, 1.4 us)
Async XLA Ops:
  0.6 7.4 %collective-permute-start = (bf16[128,256]{1,0:T(8,128)(2,1)}, bf16[128,256]{1,0:T(8,128)(2,1)S(1)}, u32[]{:S(2)}, u32[]{:S(2)}) collective-permute-start(bf16[128,256]{1,0:T(8,128)(2,1)} %f_hbm.1), channel_id=1, source_target_pairs={{0,16},{8,24},{16,0},{24,8},{1,17},{9,25},{17,1},{25,9},{2,18},{10... | collective-permute-start | bytes 196616 | tf_op jit(solution)/shard_map/ppermute | solution.py:21
  4.7 4.5 %collective-permute-start.1 = (bf16[128,256]{1,0:T(8,128)(2,1)}, bf16[128,256]{1,0:T(8,128)(2,1)S(1)}, u32[]{:S(2)}, u32[]{:S(2)}) collective-permute-start(bf16[128,256]{1,0:T(8,128)(2,1)} %c_hbm.1), channel_id=1, source_target_pairs={{0,8},{8,0},{16,24},{24,16},{1,9},{9,1},{17,25},{25,17},{2,10},{10... | collective-permute-start | bytes 196616 | tf_op jit(solution)/shard_map/ppermute | solution.py:21
  9.2 5.0 %collective-permute-start.2 = (bf16[256,256]{1,0:T(8,128)(2,1)S(1)}, bf16[256,256]{1,0:T(8,128)(2,1)S(1)}, u32[]{:S(2)}, u32[]{:S(2)}) collective-permute-start(bf16[256,256]{1,0:T(8,128)(2,1)S(1)} %pack.3.refs_0_), channel_id=1, source_target_pairs={{0,8},{8,0},{16,24},{24,16},{1,9},{9,1},{17,25},{25,17},{2,10},{10... | collective-permute-start | bytes 393224 | tf_op jit(solution)/shard_map/ppermute | solution.py:21
  10.8 6.8 %collective-permute-start.5 = (bf16[256,256]{1,0:T(8,128)(2,1)S(1)}, bf16[256,256]{1,0:T(8,128)(2,1)S(1)}, u32[]{:S(2)}, u32[]{:S(2)}) collective-permute-start(bf16[256,256]{1,0:T(8,128)(2,1)S(1)} %pack.3.refs_0_), channel_id=1, source_target_pairs={{0,4},{4,0},{1,5},{5,1},{2,6},{6,2},{3,7},{7,3},{8,12},{12,8},{9,1... | collective-permute-start | bytes 393224 | tf_op jit(solution)/shard_map/ppermute | solution.py:21
  12.3 7.6 %collective-permute-start.8 = (bf16[256,256]{1,0:T(8,128)(2,1)S(1)}, bf16[256,256]{1,0:T(8,128)(2,1)S(1)}, u32[]{:S(2)}, u32[]{:S(2)}) collective-permute-start(bf16[256,256]{1,0:T(8,128)(2,1)S(1)} %pack.4.c0_ref), channel_id=1, source_target_pairs={{0,16},{8,24},{16,0},{24,8},{1,17},{9,25},{17,1},{25,9},{2,18},{10... | collective-permute-start | bytes 393224 | tf_op jit(solution)/shard_map/ppermute | solution.py:21
  14.2 5.8 %collective-permute-start.6 = (bf16[256,256]{1,0:T(8,128)(2,1)S(1)}, bf16[256,256]{1,0:T(8,128)(2,1)S(1)}, u32[]{:S(2)}, u32[]{:S(2)}) collective-permute-start(bf16[256,256]{1,0:T(8,128)(2,1)S(1)} %collective-permute-done.2.refs_1_), channel_id=1, source_target_pairs={{0,4},{4,0},{1,5},{5,1},{2,6},{6,2},{3,7},{7,3},{8,12},{12,8},{9,1... | collective-permute-start | bytes 393224 | tf_op jit(solution)/shard_map/ppermute | solution.py:21
  17.1 3.0 %collective-permute-start.3 = (bf16[256,256]{1,0:T(8,128)(2,1)S(1)}, bf16[256,256]{1,0:T(8,128)(2,1)S(1)}, u32[]{:S(2)}, u32[]{:S(2)}) collective-permute-start(bf16[256,256]{1,0:T(8,128)(2,1)S(1)} %pack.3.refs_0_), channel_id=1, source_target_pairs={{0,2},{2,0},{1,3},{3,1},{4,6},{6,4},{5,7},{7,5},{8,10},{10,8},{9,1... | collective-permute-start | bytes 393224 | tf_op jit(solution)/shard_map/ppermute | solution.py:21
  17.1 3.0 %collective-permute-start.4 = (bf16[256,256]{1,0:T(8,128)(2,1)S(1)}, bf16[256,256]{1,0:T(8,128)(2,1)S(1)}, u32[]{:S(2)}, u32[]{:S(2)}) collective-permute-start(bf16[256,256]{1,0:T(8,128)(2,1)S(1)} %collective-permute-done.2.refs_1_), channel_id=1, source_target_pairs={{0,2},{2,0},{1,3},{3,1},{4,6},{6,4},{5,7},{7,5},{8,10},{10,8},{9,1... | collective-permute-start | bytes 393224 | tf_op jit(solution)/shard_map/ppermute | solution.py:21
  17.6 2.8 %collective-permute-start.7 = (bf16[256,256]{1,0:T(8,128)(2,1)S(1)}, bf16[256,256]{1,0:T(8,128)(2,1)S(1)}, u32[]{:S(2)}, u32[]{:S(2)}) collective-permute-start(bf16[256,256]{1,0:T(8,128)(2,1)S(1)} %collective-permute-done.5.refs_0_), channel_id=1, source_target_pairs={{0,2},{2,0},{1,3},{3,1},{4,6},{6,4},{5,7},{7,5},{8,10},{10,8},{9,1... | collective-permute-start | bytes 393224 | tf_op jit(solution)/shard_map/ppermute | solution.py:21
  20.0 1.3 %collective-permute-start.9 = (bf16[256,256]{1,0:T(8,128)(2,1)S(1)}, bf16[256,256]{1,0:T(8,128)(2,1)S(1)}, u32[]{:S(2)}, u32[]{:S(2)}) collective-permute-start(bf16[256,256]{1,0:T(8,128)(2,1)S(1)} %collective-permute-done.6.refs_1_), channel_id=1, source_target_pairs={{0,2},{2,0},{1,3},{3,1},{4,6},{6,4},{5,7},{7,5},{8,10},{10,8},{9,1... | collective-permute-start | bytes 393224 | tf_op jit(solution)/shard_map/ppermute | solution.py:21
  21.7 4.3 %collective-permute-start.10 = (bf16[128,256]{1,0:T(8,128)(2,1)S(1)}, bf16[128,256]{1,0:T(8,128)(2,1)S(1)}, u32[]{:S(2)}, u32[]{:S(2)}) collective-permute-start(bf16[128,256]{1,0:T(8,128)(2,1)S(1)} %get-tuple-element.32), channel_id=1, source_target_pairs={{0,1},{1,0},{2,3},{3,2},{4,5},{5,4},{6,7},{7,6},{8,9},{9,8},{10,11... | collective-permute-start | bytes 196616 | tf_op jit(solution)/shard_map/ppermute | solution.py:21
  26.0 2.0 %copy-start = (bf16[256,256]{1,0:T(8,128)(2,1)S(1)}, bf16[256,256]{1,0:T(8,128)(2,1)}, u32[]{:S(2)}) copy-start(bf16[256,256]{1,0:T(8,128)(2,1)} %w_ref.5) | copy-start | bytes 393220
  26.0 2.0 %copy-start.1 = (f32[256]{0:T(256)S(1)}, f32[256]{0:T(256)}, u32[]{:S(2)}) copy-start(f32[256]{0:T(256)} %param.9) | copy-start | bytes 3076
  26.0 6.0 %collective-permute-start.11 = (bf16[128,256]{1,0:T(8,128)(2,1)S(1)}, bf16[128,256]{1,0:T(8,128)(2,1)S(1)}, u32[]{:S(2)}, u32[]{:S(2)}) collective-permute-start(bf16[128,256]{1,0:T(8,128)(2,1)S(1)} %hidden.1.h_ref.refs_0_), channel_id=1, source_target_pairs={{0,16},{8,24},{16,0},{24,8},{1,17},{9,25},{17,1},{25,9},{2,18},{10... | collective-permute-start | bytes 196616 | tf_op jit(solution)/shard_map/ppermute | solution.py:21
  32.1 5.0 %collective-permute-start.12 = (bf16[256,256]{1,0:T(8,128)(2,1)S(1)}, bf16[256,256]{1,0:T(8,128)(2,1)S(1)}, u32[]{:S(2)}, u32[]{:S(2)}) collective-permute-start(bf16[256,256]{1,0:T(8,128)(2,1)S(1)} %pack.5.h_ref), channel_id=1, source_target_pairs={{0,8},{8,0},{16,24},{24,16},{1,9},{9,1},{17,25},{25,17},{2,10},{10... | collective-permute-start | bytes 393224 | tf_op jit(solution)/shard_map/ppermute | solution.py:21
  33.0 5.0 %collective-permute-start.13 = (bf16[256,256]{1,0:T(8,128)(2,1)S(1)}, bf16[256,256]{1,0:T(8,128)(2,1)S(1)}, u32[]{:S(2)}, u32[]{:S(2)}) collective-permute-start(bf16[256,256]{1,0:T(8,128)(2,1)S(1)} %get-tuple-element.40.refs_0_), channel_id=1, source_target_pairs={{0,4},{4,0},{1,5},{5,1},{2,6},{6,2},{3,7},{7,3},{8,12},{12,8},{9,1... | collective-permute-start | bytes 393224 | tf_op jit(solution)/shard_map/ppermute | solution.py:21
  38.1 2.0 %collective-permute-start.14 = (bf16[400,256]{1,0:T(8,128)(2,1)S(1)}, bf16[400,256]{1,0:T(8,128)(2,1)S(1)}, u32[]{:S(2)}, u32[]{:S(2)}) collective-permute-start(bf16[400,256]{1,0:T(8,128)(2,1)S(1)} %get-tuple-element.39), channel_id=1, source_target_pairs={{0,2},{2,0},{1,3},{3,1},{4,6},{6,4},{5,7},{7,5},{8,10},{10,8},{9,1... | collective-permute-start | bytes 614408 | tf_op jit(solution)/shard_map/ppermute | solution.py:21
  38.1 7.1 %collective-permute-start.19 = (bf16[256,256]{1,0:T(8,128)(2,1)S(1)}, bf16[256,256]{1,0:T(8,128)(2,1)S(1)}, u32[]{:S(2)}, u32[]{:S(2)}) collective-permute-start(bf16[256,256]{1,0:T(8,128)(2,1)S(1)} %get-tuple-element.41.refs_1_), channel_id=1, source_target_pairs={{0,4},{4,0},{1,5},{5,1},{2,6},{6,2},{3,7},{7,3},{8,12},{12,8},{9,1... | collective-permute-start | bytes 393224 | tf_op jit(solution)/shard_map/ppermute | solution.py:21
  40.1 4.5 %collective-permute-start.15 = (bf16[144,256]{1,0:T(8,128)(2,1)S(1)}, bf16[144,256]{1,0:T(8,128)(2,1)S(1)}, u32[]{:S(2)}, u32[]{:S(2)}) collective-permute-start(bf16[144,256]{1,0:T(8,128)(2,1)S(1)} %sum_core.1.own_ref), channel_id=1, source_target_pairs={{0,1},{1,0},{2,3},{3,2},{4,5},{5,4},{6,7},{7,6},{8,9},{9,8},{10,11... | collective-permute-start | bytes 221192 | tf_op jit(solution)/shard_map/ppermute | solution.py:21
  41.7 3.6 %collective-permute-start.17 = (bf16[256,256]{1,0:T(8,128)(2,1)S(1)}, bf16[256,256]{1,0:T(8,128)(2,1)S(1)}, u32[]{:S(2)}, u32[]{:S(2)}) collective-permute-start(bf16[256,256]{1,0:T(8,128)(2,1)S(1)} %get-tuple-element.40.refs_0_), channel_id=1, source_target_pairs={{0,2},{2,0},{1,3},{3,1},{4,6},{6,4},{5,7},{7,5},{8,10},{10,8},{9,1... | collective-permute-start | bytes 393224 | tf_op jit(solution)/shard_map/ppermute | solution.py:21
  44.6 1.3 %collective-permute-start.16 = (bf16[144,256]{1,0:T(8,128)(2,1)S(1)}, bf16[144,256]{1,0:T(8,128)(2,1)S(1)}, u32[]{:S(2)}, u32[]{:S(2)}) collective-permute-start(bf16[144,256]{1,0:T(8,128)(2,1)S(1)} %sum_row.1.own_ref), channel_id=1, source_target_pairs={{0,2},{2,0},{1,3},{3,1},{4,6},{6,4},{5,7},{7,5},{8,10},{10,8},{9,1... | collective-permute-start | bytes 221192 | tf_op jit(solution)/shard_map/ppermute | solution.py:21
  44.7 2.7 %collective-permute-start.20 = (bf16[256,256]{1,0:T(8,128)(2,1)S(1)}, bf16[256,256]{1,0:T(8,128)(2,1)S(1)}, u32[]{:S(2)}, u32[]{:S(2)}) collective-permute-start(bf16[256,256]{1,0:T(8,128)(2,1)S(1)} %collective-permute-done.13.refs_0_), channel_id=1, source_target_pairs={{0,2},{2,0},{1,3},{3,1},{4,6},{6,4},{5,7},{7,5},{8,10},{10,8},{9,1... | collective-permute-start | bytes 393224 | tf_op jit(solution)/shard_map/ppermute | solution.py:21
  45.2 2.2 %collective-permute-start.21 = (bf16[256,256]{1,0:T(8,128)(2,1)S(1)}, bf16[256,256]{1,0:T(8,128)(2,1)S(1)}, u32[]{:S(2)}, u32[]{:S(2)}) collective-permute-start(bf16[256,256]{1,0:T(8,128)(2,1)S(1)} %collective-permute-done.19.refs_1_), channel_id=1, source_target_pairs={{0,2},{2,0},{1,3},{3,1},{4,6},{6,4},{5,7},{7,5},{8,10},{10,8},{9,1... | collective-permute-start | bytes 393224 | tf_op jit(solution)/shard_map/ppermute | solution.py:21
  46.0 6.1 %collective-permute-start.18 = (bf16[272,256]{1,0:T(8,128)(2,1)S(1)}, bf16[272,256]{1,0:T(8,128)(2,1)S(1)}, u32[]{:S(2)}, u32[]{:S(2)}) collective-permute-start(bf16[272,256]{1,0:T(8,128)(2,1)S(1)} %halves.1.near_ref), channel_id=1, source_target_pairs={{0,4},{4,0},{1,5},{5,1},{2,6},{6,2},{3,7},{7,3},{8,12},{12,8},{9,1... | collective-permute-start | bytes 417800 | tf_op jit(solution)/shard_map/ppermute | solution.py:21
  47.7 4.3 %collective-permute-start.22 = (bf16[128,256]{1,0:T(8,128)(2,1)S(1)}, bf16[128,256]{1,0:T(8,128)(2,1)S(1)}, u32[]{:S(2)}, u32[]{:S(2)}) collective-permute-start(bf16[128,256]{1,0:T(8,128)(2,1)S(1)} %get-tuple-element.44), channel_id=1, source_target_pairs={{0,1},{1,0},{2,3},{3,2},{4,5},{5,4},{6,7},{7,6},{8,9},{9,8},{10,11... | collective-permute-start | bytes 196616 | tf_op jit(solution)/shard_map/ppermute | solution.py:21
